TPU v7x, 256 devices: a whole 4x4x8 slice. The times are simulated.
256 devices in a mesh: seg: 16 (over y, x), sec: 16 (over z, core).
Axes of the slice: x: 4, y: 4, z: 8, core: 2. Of those that a mesh axis runs over, the one named last changes fastest.
Arguments:
- psi: bfloat16 [16, 16, 16, 128, 128], P('seg', 'sec'), may hold values from -6 to 6
- env_build: bfloat16 [16, 16, 12, 128, 128], P('seg', 'sec'), may hold values from -0.5 to 0.5
- env_right: bfloat16 [16, 16, 12, 128, 128], P('seg', 'sec'), may hold values from -0.5 to 0.5
- site_left: bfloat16 [12, 12, 4, 4], replicated, may hold values from -0.4375 to 0.4375
- site_right: bfloat16 [12, 12, 4, 4], replicated, may hold values from -0.4375 to 0.4375
- charge: int32 [16], replicated, may hold values from 0 to 15
- rank: int32 [16], P('sec'), may hold values from 64 to 128
Outputs:
- state: bfloat16 [16, 16, 16, 128, 128], P('seg', 'sec')
- energy: float32 [16], P('seg')
- sector_weight: float32 [16, 16], P('seg', 'sec')
All inputs are finite; a program needn't handle non-finite values.
Results may differ from a plain program's by a relative error of at most 0.012.
Values may be sent and summed in bfloat16 or wider, within the bound.
No kernel may reach another device: no remote copies, remote signals or barrier semaphores. Data moves between devices by JAX's collectives and lax.ppermute only.
A program may use at most 128 MiB of HBM per device.

v0:
```python
import jax
import jax.numpy as jnp
from jax import lax
from jax.sharding import PartitionSpec as P

ITERS = 2


def from_behind(value, axis, steps):
    count = lax.axis_size(axis)
    initial, last = (max(0, -steps), min(count, count - steps))
    return lax.ppermute(value, axis, [(source, source + steps) for source in range(initial, last)])


def entering(value, axis, join, neutral):
    count, mine = (lax.axis_size(axis), lax.axis_index(axis))
    pieces = lax.all_gather(value, axis)
    total = jnp.full_like(value, 0) + jnp.asarray(neutral, value.dtype)

    def lap(position, total):
        longer = join(total, pieces[position])
        return jnp.where(position < mine, longer, total)

    return lax.fori_loop(0, count - 1, lap, total)


def pair_mpo(site_left, site_right):
    joined = jnp.einsum(
        "lmxs,mwyt->lwxyst", site_left, site_right, preferred_element_type=jnp.float32
    )
    width = joined.shape[0]
    local = joined.shape[2]
    return joined.reshape(width, width, local * local, local * local).astype(jnp.bfloat16)


def apply_local(x_sector, lenv, renv, mpo, left_row):
    rows = x_sector.shape[1]
    blocks = 4
    step_rows = rows // blocks
    total = jnp.zeros(x_sector.shape, jnp.float32)
    for block in range(blocks):
        lo_row = block * step_rows
        piece = x_sector[:, lo_row : lo_row + step_rows, :]
        first = jnp.einsum("pab,wbc->pwac", piece, renv, preferred_element_type=jnp.float32).astype(
            jnp.bfloat16
        )
        third = jnp.einsum(
            "lwqp,pwac->lqac", mpo, first, preferred_element_type=jnp.float32
        ).astype(jnp.bfloat16)
        chosen = jnp.take(lenv[:, :, :, lo_row : lo_row + step_rows], left_row, axis=0)
        total = total + jnp.einsum(
            "qlxa,lqac->qxc", chosen, third, preferred_element_type=jnp.float32
        )
    return total


def shards(psi, env_build, env_right, site_left, site_right, charge, rank):
    nsec = lax.axis_size("sec")
    sector = lax.axis_index("sec")
    segment = lax.axis_index("seg")
    mpo = pair_mpo(site_left, site_right)
    left_row = (sector - charge) % nsec
    own = env_build[0]
    whole = lax.all_gather(own, "sec", axis=0, tiled=True)
    moved = from_behind(whole, "seg", 1)
    lenv = jnp.where(segment == 0, whole, moved)
    renv = env_right[0, 0]
    x = psi[0, 0]
    width = x.shape[2]
    keep = (jnp.arange(width) < rank[0])[None, None, :]
    count = float(nsec * x.shape[0] * x.shape[1] * width)
    energy = jnp.zeros((), jnp.float32)
    squares = jnp.ones((), jnp.float32)
    total = jnp.ones((), jnp.float32)
    for step in range(ITERS):
        h = apply_local(x, lenv, renv, mpo, left_row)
        xf = x.astype(jnp.float32)
        u = jnp.where(keep, xf - 0.5 * h, 0.0)
        squares = jnp.sum(u * u)
        total, inner, self_sum = lax.psum((squares, jnp.sum(xf * h), jnp.sum(xf * xf)), "sec")
        energy = inner / self_sum
        x = (u * lax.rsqrt(total / count + 1e-06)).astype(jnp.bfloat16)
    share = jnp.log(float(nsec) * squares / total)
    before = entering(share, "seg", lambda early, late: early + late, jnp.zeros((), jnp.float32))
    summed = before + share
    return (x[None, None], energy.reshape(1), summed.reshape(1, 1))


def solution(mesh):
    return jax.shard_map(
        shards,
        mesh=mesh,
        in_specs=(
            P("seg", "sec", None, None, None),
            P("seg", "sec", None, None, None),
            P("seg", "sec", None, None, None),
            P(),
            P(),
            P(),
            P("sec"),
        ),
        out_specs=(P("seg", "sec", None, None, None), P("seg"), P("seg", "sec")),
        check_vma=False,
    )
```

profile of v0, /device:TPU:1, one launch (start us, length us, event | category | flops | bytes accessed | tf_op | source)
XLA Modules:
  0.0 390.7 jit_solution(17228802076162054384)
XLA Ops:
  7.9 52.2 %all-gather.3.cloned.1.call-done = bf16[16,1,12,128,128]{4,3,2,1,0:T(8,128)(2,1)} async-done(((bf16[1,1,12,128,128]{4,3,2,1,0:T(8,128)(2,1)}), bf16[16,1,12,128,128]{4,3,2,1,0:T(8,128)(2,1)}) %all-gather.3.cloned.1.call-update) | async-done | bytes 6291472 | tf_op jit(solution)/shard_map/all_gather | solution.py:64
  60.2 5.7 %collective-permute-start = (bf16[16,12,128,128]{3,2,1,0:T(8,128)(2,1)}, bf16[16,12,128,128]{3,2,1,0:T(8,128)(2,1)}, u32[]{:S(2)}, u32[]{:S(2)}) collective-permute-start(bf16[16,12,128,128]{3,2,1,0:T(8,128)(2,1)} %bitcast.206), channel_id=1, source_target_pairs={{0,16},{16,32},{32,48},{48,64},{64,80},{80,96},{96,112},{112,128},... | collective-permute-start | bytes 18874376 | tf_op jit(solution)/shard_map/ppermute | solution.py:12
  67.2 2.3 copy.33
  74.4 2.2 bitcast_convert_fusion.5
  76.7 2.2 bitcast_convert_fusion.6
  78.9 2.3 bitcast_convert_fusion.4
  81.2 2.3 bitcast_convert_fusion.7
  83.5 114.7 %collective-permute-done = bf16[16,12,128,128]{3,2,1,0:T(8,128)(2,1)} collective-permute-done((bf16[16,12,128,128]{3,2,1,0:T(8,128)(2,1)}, bf16[16,12,128,128]{3,2,1,0:T(8,128)(2,1)}, u32[]{:S(2)}, u32[]{:S(2)}) %collective-permute-start) | collective-permute-done | bytes 6291488 | tf_op jit(solution)/shard_map/ppermute | solution.py:12
  198.2 3.4 broadcast_select_fusion.4
  201.6 11.0 %fusion.111 = (bf16[16,12,128,32]{3,2,1,0:T(8,128)(2,1)}, bf16[16,12,128,32]{3,2,1,0:T(8,128)(2,1)}, bf16[16,12,128,32]{3,2,1,0:T(8,128)(2,1)}, bf16[16,12,128,32]{3,2,1,0:T(8,128)(2,1)}) fusion(bf16[16,12,128,128]{3,2,1,0:T(8,128)(2,1)S(1)} %broadcast_select_fusion.4), kind=kLoop, calls=%fused_computation.125 | loop fusion | bytes 12582912 | tf_op jit(solution)/shard_map/slice | solution.py:50
  212.6 6.8 %gather_fusion.2 = bf16[16,12,128,32]{3,2,1,0:T(8,128)(2,1)} fusion(bf16[16,12,128,32]{3,2,1,0:T(8,128)(2,1)} %get-tuple-element.102, s32[1024]{0:T(1024)S(1)} %pad_clamp_fusion), kind=kCustom, calls=%fused_computation.2.clone | custom fusion | bytes 3145792 | tf_op jit(solution)/shard_map/jit(_take)/gather | solution.py:50
  219.4 6.7 %gather_fusion.1 = bf16[16,12,128,32]{3,2,1,0:T(8,128)(2,1)} fusion(bf16[16,12,128,32]{3,2,1,0:T(8,128)(2,1)} %get-tuple-element.103, s32[1024]{0:T(1024)S(1)} %pad_clamp_fusion), kind=kCustom, calls=%fused_computation.1.clone | custom fusion | bytes 3145792 | tf_op jit(solution)/shard_map/jit(_take)/gather | solution.py:50
  226.1 6.7 %gather_fusion.3 = bf16[16,12,128,32]{3,2,1,0:T(8,128)(2,1)} fusion(bf16[16,12,128,32]{3,2,1,0:T(8,128)(2,1)} %get-tuple-element.101, s32[1024]{0:T(1024)S(1)} %pad_clamp_fusion), kind=kCustom, calls=%fused_computation.3.clone | custom fusion | bytes 3145792 | tf_op jit(solution)/shard_map/jit(_take)/gather | solution.py:50
  232.9 6.9 %gather_fusion = bf16[16,12,128,32]{3,2,1,0:T(8,128)(2,1)} fusion(bf16[16,12,128,32]{3,2,1,0:T(8,128)(2,1)} %get-tuple-element.100, s32[1024]{0:T(1024)S(1)} %pad_clamp_fusion), kind=kCustom, calls=%fused_computation.clone | custom fusion | bytes 3145792 | tf_op jit(solution)/shard_map/jit(_take)/gather | solution.py:50
  239.8 5.2 %fusion.43 = f32[16,128,128]{2,1,0:T(8,128)S(1)} fusion(bf16[12,16,32,128]{3,1,2,0:T(8,128)(2,1)} %bitcast_convert_fusion.5, bf16[16,12,128,32]{3,2,1,0:T(8,128)(2,1)} %gather_fusion.2, pred[16]{0:T(512)(128)(4,1)S(1)} %get-tuple-element.98), kind=kOutput, calls=%fused_computation.68 | convolution fusion | flops 202113024 | bytes 4194320 | tf_op jit(solution)/shard_map/qlxa,lqac->qxc/dot_general | solution.py:51
  245.0 1.8 fusion.49
  249.7 3.0 multiply_reduce_fusion.1
  252.6 24.6 %psum.28 = f32[]{:T(128)} all-reduce(f32[]{:T(128)} %get-tuple-element.104), channel_id=1, replica_groups=mesh['seg'=16,'sec'=16] {'sec'}, use_global_device_ids=true, to_apply=%region_1.3 | all-reduce | flops 1 | bytes 8 | tf_op jit(solution)/shard_map/psum | solution.py:80
  286.0 1.8 fusion.46
  291.0 2.1 fusion.40
  293.1 3.2 fusion.89
  297.0 25.1 %all-reduce.1 = (f32[]{:T(128)}, f32[]{:T(128)}, f32[]{:T(128)}) all-reduce(f32[]{:T(128)} %get-tuple-element.85, f32[]{:T(128)} %get-tuple-element.84, f32[]{:T(128)} %get-tuple-element.86), channel_id=1, replica_groups=mesh['seg'=16,'sec'=16] {'sec'}, use_global_device_ids=true, to_apply=%region_3.5 | all-reduce | flops 3 | bytes 24 | tf_op jit(solution)/shard_map/psum | solution.py:80
  324.2 35.9 %all-reduce = f32[16]{0:T(128)S(1)} all-reduce(f32[16]{0:T(128)S(1)} %dynamic-update-slice), channel_id=1, replica_groups=mesh['seg'=16,'sec'=16] {'seg'}, use_global_device_ids=true, to_apply=%add | all-reduce | flops 16 | bytes 128
  360.1 19.0 %while.13 = (s32[]{:T(128)}, f32[]{:T(128)}, s32[]{:T(128)}, f32[16]{0:T(128)S(1)}, s32[]{:T(128)}) while((s32[]{:T(128)}, f32[]{:T(128)}, s32[]{:T(128)}, f32[16]{0:T(128)S(1)}, s32[]{:T(128)}) %tuple.41), condition=%wide.region_9.11_spmd, body=%wide.region_8.10_spmd.sunk | while | flops 5 | bytes 107 | solution.py:24
  (96 shorter events, 31.1 us)
Async XLA Ops:
  7.2 65.0 %copy-start = (bf16[1,1,12,128,128]{4,3,2,1,0:T(8,128)(2,1)S(1)}, bf16[1,1,12,128,128]{4,3,2,1,0:T(8,128)(2,1)}, u32[]{:S(2)}) copy-start(bf16[1,1,12,128,128]{4,3,2,1,0:T(8,128)(2,1)} %param.13) | copy-start | bytes 1179652
  7.2 64.3 %copy-start.6 = (u32[256]{0:T(256)S(1)}, u32[256]{0:T(256)}, u32[]{:S(2)}) copy-start(u32[256]{0:T(256)} %constant.72) | copy-start | bytes 3076
  7.2 64.9 %copy-start.5 = (s32[16]{0:T(128)S(1)}, s32[16]{0:T(128)}, u32[]{:S(2)}) copy-start(s32[16]{0:T(128)} %param.16) | copy-start | bytes 196
  7.2 65.0 %copy-start.3 = (bf16[1,1,16,128,128]{4,3,2,1,0:T(8,128)(2,1)S(1)}, bf16[1,1,16,128,128]{4,3,2,1,0:T(8,128)(2,1)}, u32[]{:S(2)}) copy-start(bf16[1,1,16,128,128]{4,3,2,1,0:T(8,128)(2,1)} %param.11) | copy-start | bytes 1572868
  7.2 53.0 %all-gather.3.cloned.1.call-start = ((), (), s32[]{:S(2)}) async-start(), calls=%async_computation | async-start | bytes 6684672 | tf_op jit(solution)/shard_map/all_gather | solution.py:64
  60.2 138.0 %collective-permute-start = (bf16[16,12,128,128]{3,2,1,0:T(8,128)(2,1)}, bf16[16,12,128,128]{3,2,1,0:T(8,128)(2,1)}, u32[]{:S(2)}, u32[]{:S(2)}) collective-permute-start(bf16[16,12,128,128]{3,2,1,0:T(8,128)(2,1)} %bitcast.206), channel_id=1, source_target_pairs={{0,16},{16,32},{32,48},{48,64},{64,80},{80,96},{96,112},{112,128},... | collective-permute-start | bytes 18874376 | tf_op jit(solution)/shard_map/ppermute | solution.py:12
  70.8 10.4 %copy-start.1 = (bf16[12,12,16,16,1]{3,2,1,4,0:T(8,128)(2,1)}, bf16[12,12,16,16,1]{3,2,1,4,0:T(8,128)(2,1)S(1)}, u32[]{:S(2)}) copy-start(bf16[12,12,16,16,1]{3,2,1,4,0:T(8,128)(2,1)S(1)} %copy.69) | copy-start | bytes 221188
  232.9 12.1 %slice-start.10 = ((s8[6291456]{0:T(1024)(128)(4,1)}), s8[2097152]{0:T(1024)(128)(4,1)S(1)}, s32[]{:S(2)}) async-start(s8[6291456]{0:T(1024)(128)(4,1)} %bitcast.202), calls=%async_computation.11 | async-start | bytes 4194304
  239.8 5.2 %slice-start.11 = ((s8[6291456]{0:T(1024)(128)(4,1)}), s8[4194304]{0:T(1024)(128)(4,1)S(1)}, s32[]{:S(2)}) async-start(s8[6291456]{0:T(1024)(128)(4,1)} %bitcast.202), calls=%async_computation.12 | async-start | bytes 8388608
  239.8 5.2 %copy-start.8 = (bf16[12,16,32,128]{3,1,2,0:T(8,128)(2,1)S(1)}, bf16[12,16,32,128]{3,1,2,0:T(8,128)(2,1)}, u32[]{:S(2)}) copy-start(bf16[12,16,32,128]{3,1,2,0:T(8,128)(2,1)} %bitcast_convert_fusion.6) | copy-start | bytes 4718596
  239.8 7.1 %slice-start.4 = ((s8[6291456]{0:T(1024)(128)(4,1)}), s8[4194304]{0:T(1024)(128)(4,1)S(1)}, s32[]{:S(2)}) async-start(s8[6291456]{0:T(1024)(128)(4,1)} %bitcast.196), calls=%async_computation.5 | async-start | bytes 8388608
  245.0 1.9 slice-start.5
  245.0 2.2 copy-start.9
  245.0 4.1 %slice-start = ((s8[6291456]{0:T(1024)(128)(4,1)}), s8[4194304]{0:T(1024)(128)(4,1)S(1)}, s32[]{:S(2)}) async-start(s8[6291456]{0:T(1024)(128)(4,1)} %bitcast.192), calls=%async_computation.1 | async-start | bytes 8388608
  247.3 1.8 slice-start.1
  247.3 1.9 copy-start.4
  247.3 2.4 copy-start.7
  279.8 2.2 slice-start.12
  280.3 2.4 slice-start.13
  280.3 5.6 %slice-start.8 = ((s8[6291456]{0:T(1024)(128)(4,1)}), s8[4194304]{0:T(1024)(128)(4,1)S(1)}, s32[]{:S(2)}) async-start(s8[6291456]{0:T(1024)(128)(4,1)} %bitcast.200), calls=%async_computation.9 | async-start | bytes 8388608
  282.8 3.2 slice-start.9
  287.8 2.8 slice-start.6
  289.2 3.9 slice-start.2
  291.0 2.1 slice-start.3
  (2 other events, 3.5 us)
Sparse Core Ops, SparseCore 0:
  9.9 50.2 all-gather.2
where the time goes:
time: 396 us; the launch traced here: 391 us
  waiting for transfers between devices  168 us (42%)
  blocking collectives  85.6 us (22%)
  local copies, waits for them, and re-layouts  54.7 us (14%)
  matrix products  41.1 us (10%)
  between operations  21.5 us (5%)
  loops' own time  9.85 us (2%)
  starting transfers between devices  5.73 us (1%)
  other arithmetic  4.6 us (1%)
    ppermute x1, waiting for transfers between devices, from_behind(): lax.ppermute(value, axis, [(source, source + steps) for source in range(i...  115 us
    all_gather x1, waiting for transfers between devices, shards(): whole = lax.all_gather(own, 'sec', axis=0, tiled=True)  52.2 us
    psum x2, blocking collectives, shards(): lax.psum((squares, jnp.sum(xf * h), jnp.sum(xf * xf)), 'sec')  49.7 us
    unnamed x1, blocking collectives  35.9 us
    gather x4, local copies, waits for them, and re-layouts, apply_local(): jnp.take(lenv[:, :, :, lo_row:lo_row + step_rows], left_row, axis=0)  27.2 us
    dot_general x8, matrix products, apply_local(): jnp.einsum('qlxa,lqac->qxc', chosen, third, preferred_element_type=jnp.fl...  20.7 us
    dot_general x8, matrix products, apply_local(): jnp.einsum('lwqp,pwac->lqac', mpo, first, preferred_element_type=jnp.floa...  14.6 us
    slice x1, local copies, waits for them, and re-layouts, apply_local(): lenv[:, :, :, lo_row:lo_row + step_rows]  11 us
  transfers between devices with their start and end apart: 2, of which 2 were waited for; matrix products, arithmetic and copies ran while one was open for 4% of the time, Pallas kernels for 0%

commit v1 on v0

v1 whole, which is shorter than its diff:
```python
import functools

import jax
import jax.numpy as jnp
from jax import lax
from jax.experimental import pallas as pl
from jax.experimental.pallas import tpu as pltpu
from jax.sharding import PartitionSpec as P

F32 = jnp.float32
BF16 = jnp.bfloat16
VMEM_LIMIT = 48 * 2**20


def pair_mpo(site_left, site_right):
    joined = jnp.einsum("lmxs,mwyt->lxywst", site_left, site_right, preferred_element_type=F32)
    rows = joined.shape[0] * joined.shape[1] * joined.shape[2]
    return joined.reshape(rows, rows).astype(BF16)


def spread(xt_ref, renv_ref, mpo_ref, x3_ref):
    states = xt_ref.shape[0]
    pairs = xt_ref.shape[1]
    width = renv_ref.shape[2]
    bonds = renv_ref.shape[0]
    mpo = mpo_ref[...]

    def chunk(j, carry):
        at = pl.multiple_of(j * 16, 16)
        xa = xt_ref[pl.ds(at, 16)].reshape(16 * pairs, width)
        first = []
        for k in range(bonds // 2):
            both = jnp.concatenate([renv_ref[2 * k], renv_ref[2 * k + 1]], axis=1)
            got = jnp.dot(xa, both, preferred_element_type=F32).astype(BF16)
            first.append(got[:, :width])
            first.append(got[:, width:])
        rows = []
        for i in range(8):
            sides = []
            for a in (2 * i, 2 * i + 1):
                sides.append(jnp.concatenate([f[a * pairs : (a + 1) * pairs] for f in first], axis=0))
            rhs = jnp.concatenate(sides, axis=1)
            out = jnp.dot(mpo, rhs, preferred_element_type=F32).astype(BF16)
            rows.append(out[:, :width])
            rows.append(out[:, width:])
        for l in range(bonds):
            block = jnp.stack([row[l * pairs : (l + 1) * pairs] for row in rows], axis=0)
            x3_ref[:, l, pl.ds(at, 16), :] = jnp.swapaxes(block, 0, 1)
        return carry

    lax.fori_loop(0, states // 16, chunk, 0)


def front_kernel(psi_ref, renv_ref, mpo_ref, x3_ref, xt_ref):
    for j in range(psi_ref.shape[1] // 16):
        xt_ref[j * 16 : (j + 1) * 16] = jnp.swapaxes(psi_ref[:, j * 16 : (j + 1) * 16, :], 0, 1)
    spread(xt_ref, renv_ref, mpo_ref, x3_ref)


def contract(lenv_ref, slot, x3_ref, q):
    bonds = lenv_ref.shape[1]
    total = None
    for k in range(bonds // 2):
        lhs = jnp.concatenate([lenv_ref[slot, 2 * k], lenv_ref[slot, 2 * k + 1]], axis=1)
        rhs = jnp.concatenate([x3_ref[q, 2 * k], x3_ref[q, 2 * k + 1]], axis=0)
        part = jnp.dot(lhs, rhs, preferred_element_type=F32)
        total = part if total is None else total + part
    return total


def back_kernel(slot_ref, rank_ref, psi_ref, renv_ref, mpo_ref, x3in_ref, *rest):
    blocks = rest[:16]
    v_ref, stat_ref, lenv_ref, x3_ref, u_ref, xt_ref, sem_ref, sem3_ref = rest[16:]
    pairs, width = psi_ref.shape[0], psi_ref.shape[2]
    copies = [pltpu.make_async_copy(blocks[i], lenv_ref.at[i], sem_ref.at[i]) for i in range(16)]
    for copy in copies:
        copy.start()
    copy3 = pltpu.make_async_copy(x3in_ref, x3_ref, sem3_ref)
    copy3.start()
    keep = lax.broadcasted_iota(jnp.int32, (width, width), 1) < rank_ref[0]
    for copy in copies:
        copy.wait()
    copy3.wait()

    def one(q, acc):
        h = contract(lenv_ref, slot_ref[q], x3_ref, q)
        u = jnp.where(keep, psi_ref[q].astype(F32) - 0.5 * h, 0.0)
        u_ref[q] = u.astype(BF16)
        return acc + u * u

    zero = jnp.zeros((width, width), F32)
    first_sq = lax.fori_loop(0, pairs, one, zero)
    for j in range(width // 16):
        xt_ref[j * 16 : (j + 1) * 16] = jnp.swapaxes(u_ref[:, j * 16 : (j + 1) * 16, :], 0, 1)
    spread(xt_ref, renv_ref, mpo_ref, x3_ref)

    def two(q, accs):
        sq, inner, own = accs
        h = contract(lenv_ref, slot_ref[q], x3_ref, q)
        x = u_ref[q].astype(F32)
        v = jnp.where(keep, x - 0.5 * h, 0.0)
        v_ref[q] = v
        return sq + v * v, inner + x * h, own + x * x

    sq, inner, own = lax.fori_loop(0, pairs, two, (zero, zero, zero))
    row = lax.broadcasted_iota(jnp.int32, (8, width), 0)
    stat = jnp.zeros((8, width), F32)
    for i, part in enumerate((first_sq, sq, inner, own)):
        stat = jnp.where(row == i, jnp.sum(part), stat)
    stat_ref[...] = stat


def front(psi, renv, mpo):
    pairs, width = psi.shape[0], psi.shape[2]
    bonds = renv.shape[0]
    return pl.pallas_call(
        front_kernel,
        out_shape=jax.ShapeDtypeStruct((pairs, bonds, width, width), BF16),
        in_specs=[pl.BlockSpec(memory_space=pltpu.VMEM)] * 3,
        out_specs=pl.BlockSpec(memory_space=pltpu.VMEM),
        scratch_shapes=[pltpu.VMEM((width, pairs, width), BF16)],
        compiler_params=pltpu.CompilerParams(vmem_limit_bytes=VMEM_LIMIT),
        cost_estimate=pl.CostEstimate(flops=2 * 10**9, bytes_accessed=8 * 10**6, transcendentals=0),
        name="front",
    )(psi, renv, mpo)


def back(slot, rank, psi, renv, mpo, x3, blocks):
    pairs, width = psi.shape[0], psi.shape[2]
    bonds = renv.shape[0]
    vmem = pl.BlockSpec(memory_space=pltpu.VMEM)
    smem = pl.BlockSpec(memory_space=pltpu.SMEM)
    anywhere = pl.BlockSpec(memory_space=pl.ANY)
    return pl.pallas_call(
        back_kernel,
        out_shape=(
            jax.ShapeDtypeStruct((pairs, width, width), F32),
            jax.ShapeDtypeStruct((8, width), F32),
        ),
        in_specs=[smem, smem, vmem, vmem, vmem, anywhere] + [anywhere] * 16,
        out_specs=(vmem, vmem),
        scratch_shapes=[
            pltpu.VMEM((16, bonds, width, width), BF16),
            pltpu.VMEM((pairs, bonds, width, width), BF16),
            pltpu.VMEM((pairs, width, width), BF16),
            pltpu.VMEM((width, pairs, width), BF16),
            pltpu.SemaphoreType.DMA((16,)),
            pltpu.SemaphoreType.DMA,
        ],
        compiler_params=pltpu.CompilerParams(vmem_limit_bytes=VMEM_LIMIT),
        cost_estimate=pl.CostEstimate(flops=4 * 10**9, bytes_accessed=16 * 10**6, transcendentals=0),
        name="back",
    )(slot, rank, psi, renv, mpo, x3, *blocks)


def hop(value):
    n = lax.axis_size("sec")
    return lax.ppermute(value, "sec", [(i, (i + (2 if i % 2 == 0 else -2)) % n) for i in range(n)])


def twin(value):
    n = lax.axis_size("sec")
    return lax.ppermute(value, "sec", [(i, i ^ 1) for i in range(n)])


def from_behind(value):
    n = lax.axis_size("seg")
    return lax.ppermute(value, "seg", [(i, i + 1) for i in range(n - 1)])


def shards(psi, env_build, env_right, site_left, site_right, charge, rank):
    nsec = lax.axis_size("sec")
    nseg = lax.axis_size("seg")
    sector = lax.axis_index("sec")
    segment = lax.axis_index("seg")
    x = psi[0, 0]
    renv = env_right[0, 0]
    pairs, width = x.shape[0], x.shape[2]
    count = float(nsec * pairs * width * width)

    env = env_build[0, 0]
    moved = from_behind(env)
    mpo = pair_mpo(site_left, site_right)
    x3 = front(x, renv, mpo)
    moved, x3 = lax.optimization_barrier((moved, x3))
    own = jnp.where(segment == 0, env, moved)

    core = sector % 2
    z = sector // 2
    chips = nsec // 2
    sign = 1 - 2 * core
    blocks = [own]
    holds = [sector]
    other = twin(own)
    blocks.append(other)
    holds.append(sector ^ 1)
    o, t = own, other
    for k in range(1, chips // 2 + 1):
        behind = (z - sign * k) % chips
        ahead = (z + sign * k) % chips
        o = hop(o)
        blocks += [o, twin(o)]
        holds += [2 * behind + core, 2 * ahead + 1 - core]
        if k < chips // 2:
            t = hop(t)
            blocks += [t, twin(t)]
            holds += [2 * behind + 1 - core, 2 * ahead + core]
    holds = jnp.stack(holds).astype(jnp.int32)
    left = (sector - charge) % nsec
    slot = jnp.sum(
        jnp.where(holds[None, :] == left[:, None], jnp.arange(nsec, dtype=jnp.int32)[None, :], 0), axis=1
    ).astype(jnp.int32)

    v, stat = back(slot, rank, x, renv, mpo, x3, blocks)

    mine = stat[1, 0]
    total = stat
    for bit in (1, 2, 4, 8):
        total = total + lax.ppermute(total, "sec", [(i, i ^ bit) for i in range(nsec)])
    scale_one = lax.rsqrt(total[0, 0] / count + 1e-06)
    energy = total[2, 0] / total[3, 0]
    second = (scale_one * scale_one) * total[1, 0]
    scale = scale_one * lax.rsqrt(second / count + 1e-06)
    state = (v * scale).astype(BF16)
    share = jnp.log(float(nsec) * mine / total[1, 0])
    upto = jnp.full((8, width), share, F32)
    whole = upto
    for bit in (1, 2, 4, 8):
        got = lax.ppermute(whole, "seg", [(i, i ^ bit) for i in range(nseg)])
        upto = jnp.where((segment & bit) != 0, upto + got, upto)
        whole = whole + got
    return state[None, None], energy.reshape(1), upto[0, 0].reshape(1, 1)


def solution(mesh):
    return jax.shard_map(
        shards,
        mesh=mesh,
        in_specs=(
            P("seg", "sec", None, None, None),
            P("seg", "sec", None, None, None),
            P("seg", "sec", None, None, None),
            P(),
            P(),
            P(),
            P("sec"),
        ),
        out_specs=(P("seg", "sec", None, None, None), P("seg"), P("seg", "sec")),
        check_vma=False,
    )
```

time: 396 us -> 136 us (0.34)
  the two profiles are of different devices: /device:TPU:1 before, /device:TPU:2 now
where the time goes in v1:
time: 136 us
  waiting for transfers between devices  53.9 us (40%)
  Pallas kernels  31.9 us (23%)
  starting transfers between devices  22.1 us (16%)
  local copies, waits for them, and re-layouts  17.5 us (13%)
  between operations  6.67 us (5%)
  other arithmetic  2.41 us (2%)
    ppermute x7, waiting for transfers between devices, hop(): lax.ppermute(value, 'sec', [(i, (i + (2 if i % 2 == 0 else -2)) % n) for...  35.2 us
    pallas_call x1, Pallas kernels, back(): pl.pallas_call(back_kernel, out_shape=(jax.ShapeDtypeStruct((pairs, width...  22.5 us
    convert_element_type x2, local copies, waits for them, and re-layouts, pair_mpo(): return joined.reshape(rows, rows).astype(BF16)  12.4 us
    ppermute x4, waiting for transfers between devices, shards(): lax.ppermute(total, 'sec', [(i, i ^ bit) for i in range(nsec)])  10.9 us
    pallas_call x1, Pallas kernels, front(): pl.pallas_call(front_kernel, out_shape=jax.ShapeDtypeStruct((pairs, bonds...  9.39 us
    ppermute x4, starting transfers between devices, shards(): got = lax.ppermute(whole, 'seg', [(i, i ^ bit) for i in range(nseg)])  7.56 us
    ppermute x4, waiting for transfers between devices, shards(): got = lax.ppermute(whole, 'seg', [(i, i ^ bit) for i in range(nseg)])  6.75 us
    ppermute x4, starting transfers between devices, shards(): lax.ppermute(total, 'sec', [(i, i ^ bit) for i in range(nsec)])  4.79 us
  transfers between devices with their start and end apart: 24, of which 15 were waited for; matrix products, arithmetic and copies ran while one was open for 12% of the time, Pallas kernels for 7%

profile of v1, /device:TPU:2, one launch (start us, length us, event | category | flops | bytes accessed | tf_op | source)
XLA Modules:
  0.0 135.8 jit_solution(12707965149697096293)
XLA Ops:
  0.6 3.5 %collective-permute-start = (bf16[12,128,128]{2,1,0:T(8,128)(2,1)}, bf16[12,128,128]{2,1,0:T(8,128)(2,1)S(1)}, u32[]{:S(2)}, u32[]{:S(2)}) collective-permute-start(bf16[12,128,128]{2,1,0:T(8,128)(2,1)} %bitcast.35), channel_id=1, source_target_pairs={{0,16},{16,32},{32,48},{48,64},{64,80},{80,96},{96,112},{112,128},... | collective-permute-start | bytes 1179656 | tf_op jit(solution)/shard_map/ppermute | solution.py:168
  5.5 7.1 %copy.18 = bf16[12,4,4,12,4,4]{5,4,3,2,1,0:T(4,128)(2,1)} copy(bf16[12,4,4,12,4,4]{0,3,4,1,5,2:T(8,128)(2,1)S(1)} %fusion) | data formatting | bytes 147456 | tf_op jit(solution)/shard_map/convert_element_type | solution.py:18
  12.6 5.3 %convert_element_type.12.mpo_ref = bf16[192,192]{1,0:T(8,128)(2,1)S(1)} reshape(bf16[12,4,4,12,4,4]{5,4,3,2,1,0:T(4,128)(2,1)} %copy.18) | data formatting | bytes 147456 | tf_op jit(solution)/shard_map/convert_element_type | solution.py:18
  17.9 9.4 %front.1.x3in_ref = bf16[16,12,128,128]{3,2,1,0:T(8,128)(2,1)} custom-call(bf16[16,128,128]{2,1,0:T(8,128)(2,1)S(1)} %bitcast.32, bf16[12,128,128]{2,1,0:T(8,128)(2,1)S(1)} %bitcast.33, bf16[192,192]{1,0:T(8,128)(2,1)S(1)} %convert_element_type.12.mpo_ref), custom_call_target="tpu_custom_call" | custom-call | flops 2000000000 | bytes 8000000 | tf_op jit(solution)/shard_map/front/pallas_call | solution.py:116
  27.4 2.0 %collective-permute-start.2 = (bf16[12,128,128]{2,1,0:T(8,128)(2,1)S(1)}, bf16[12,128,128]{2,1,0:T(8,128)(2,1)S(1)}, u32[]{:S(2)}, u32[]{:S(2)}) collective-permute-start(bf16[12,128,128]{2,1,0:T(8,128)(2,1)S(1)} %broadcast_select_fusion.rest_0_), channel_id=1, source_target_pairs={{0,2},{1,15},{2,4},{3,1},{4,6},{5,3},{6,8},{7,5},{8,10},{9,7},{10,... | collective-permute-start | bytes 1179656 | tf_op jit(solution)/shard_map/ppermute | solution.py:158
  29.4 3.2 %collective-permute-start.1 = (bf16[12,128,128]{2,1,0:T(8,128)(2,1)S(1)}, bf16[12,128,128]{2,1,0:T(8,128)(2,1)S(1)}, u32[]{:S(2)}, u32[]{:S(2)}) collective-permute-start(bf16[12,128,128]{2,1,0:T(8,128)(2,1)S(1)} %broadcast_select_fusion.rest_0_), channel_id=1, source_target_pairs={{0,1},{1,0},{2,3},{3,2},{4,5},{5,4},{6,7},{7,6},{8,9},{9,8},{10,11... | collective-permute-start | bytes 1179656 | tf_op jit(solution)/shard_map/ppermute | solution.py:163
  32.6 6.5 %collective-permute-done.2.rest_2_ = bf16[12,128,128]{2,1,0:T(8,128)(2,1)S(1)} collective-permute-done((bf16[12,128,128]{2,1,0:T(8,128)(2,1)S(1)}, bf16[12,128,128]{2,1,0:T(8,128)(2,1)S(1)}, u32[]{:S(2)}, u32[]{:S(2)}) %collective-permute-start.2) | collective-permute-done | bytes 393248 | tf_op jit(solution)/shard_map/ppermute | solution.py:158
  39.1 9.0 %collective-permute-done.6.rest_6_ = bf16[12,128,128]{2,1,0:T(8,128)(2,1)S(1)} collective-permute-done((bf16[12,128,128]{2,1,0:T(8,128)(2,1)S(1)}, bf16[12,128,128]{2,1,0:T(8,128)(2,1)S(1)}, u32[]{:S(2)}, u32[]{:S(2)}) %collective-permute-start.6) | collective-permute-done | bytes 393248 | tf_op jit(solution)/shard_map/ppermute | solution.py:158
  48.0 4.2 %collective-permute-done.4.rest_4_ = bf16[12,128,128]{2,1,0:T(8,128)(2,1)S(1)} collective-permute-done((bf16[12,128,128]{2,1,0:T(8,128)(2,1)S(1)}, bf16[12,128,128]{2,1,0:T(8,128)(2,1)S(1)}, u32[]{:S(2)}, u32[]{:S(2)}) %collective-permute-start.4) | collective-permute-done | bytes 393248 | tf_op jit(solution)/shard_map/ppermute | solution.py:158
  52.8 4.3 %collective-permute-done.10.rest_10_ = bf16[12,128,128]{2,1,0:T(8,128)(2,1)S(1)} collective-permute-done((bf16[12,128,128]{2,1,0:T(8,128)(2,1)S(1)}, bf16[12,128,128]{2,1,0:T(8,128)(2,1)S(1)}, u32[]{:S(2)}, u32[]{:S(2)}) %collective-permute-start.10) | collective-permute-done | bytes 393248 | tf_op jit(solution)/shard_map/ppermute | solution.py:158
  57.0 4.2 %collective-permute-done.8.rest_8_ = bf16[12,128,128]{2,1,0:T(8,128)(2,1)S(1)} collective-permute-done((bf16[12,128,128]{2,1,0:T(8,128)(2,1)S(1)}, bf16[12,128,128]{2,1,0:T(8,128)(2,1)S(1)}, u32[]{:S(2)}, u32[]{:S(2)}) %collective-permute-start.8) | collective-permute-done | bytes 393248 | tf_op jit(solution)/shard_map/ppermute | solution.py:158
  63.3 2.8 %collective-permute-done.14.rest_14_ = bf16[12,128,128]{2,1,0:T(8,128)(2,1)} collective-permute-done((bf16[12,128,128]{2,1,0:T(8,128)(2,1)S(1)}, bf16[12,128,128]{2,1,0:T(8,128)(2,1)}, u32[]{:S(2)}, u32[]{:S(2)}) %collective-permute-start.14) | collective-permute-done | bytes 393248 | tf_op jit(solution)/shard_map/ppermute | solution.py:158
  66.1 4.2 %collective-permute-done.12.rest_12_ = bf16[12,128,128]{2,1,0:T(8,128)(2,1)} collective-permute-done((bf16[12,128,128]{2,1,0:T(8,128)(2,1)S(1)}, bf16[12,128,128]{2,1,0:T(8,128)(2,1)}, u32[]{:S(2)}, u32[]{:S(2)}) %collective-permute-start.12) | collective-permute-done | bytes 393248 | tf_op jit(solution)/shard_map/ppermute | solution.py:158
  74.4 22.5 %back.1 = (f32[16,128,128]{2,1,0:T(8,128)}, f32[8,128]{1,0:T(8,128)S(1)}) custom-call(s32[16]{0:T(128)S(1)} %select_reduce_fusion.slot_ref, s32[1]{0:T(128)S(6)} %copy.29.rank_ref, bf16[16,128,128]{2,1,0:T(8,128)(2,1)} %bitcast.31, bf16[12,128,128]{2,1,0:T(8,128)(2,1)S(1)} %bitcast.34, bf16[192,192]{1,0:T(8,128)(2,1)S(1)} %convert_element_type.12.mpo_ref, ...), custom_call_target="tpu_custom_call" | custom-call | flops 4000000000 | bytes 16000000 | tf_op jit(solution)/shard_map/back/pallas_call | solution.py:134
  98.2 3.6 %collective-permute-done.17 = f32[8,128]{1,0:T(8,128)S(1)} collective-permute-done((f32[8,128]{1,0:T(8,128)S(1)}, f32[8,128]{1,0:T(8,128)S(1)}, u32[]{:S(2)}, u32[]{:S(2)}) %collective-permute-start.17) | collective-permute-done | bytes 4128 | tf_op jit(solution)/shard_map/ppermute | solution.py:219
  101.8 4.5 %collective-permute-done.18 = f32[8,128]{1,0:T(8,128)S(1)} collective-permute-done((f32[8,128]{1,0:T(8,128)S(1)}, f32[8,128]{1,0:T(8,128)S(1)}, u32[]{:S(2)}, u32[]{:S(2)}) %collective-permute-start.18) | collective-permute-done | bytes 4128 | tf_op jit(solution)/shard_map/ppermute | solution.py:219
  106.3 4.6 %collective-permute-start.19 = (f32[8,128]{1,0:T(8,128)S(1)}, f32[8,128]{1,0:T(8,128)S(1)}, u32[]{:S(2)}, u32[]{:S(2)}) collective-permute-start(f32[8,128]{1,0:T(8,128)S(1)} %add.157), channel_id=1, source_target_pairs={{0,8},{1,9},{2,10},{3,11},{4,12},{5,13},{6,14},{7,15},{8,0},{9,1},... | collective-permute-start | bytes 12296 | tf_op jit(solution)/shard_map/ppermute | solution.py:219
  112.0 1.8 %collective-permute-done.19 = f32[8,128]{1,0:T(8,128)S(1)} collective-permute-done((f32[8,128]{1,0:T(8,128)S(1)}, f32[8,128]{1,0:T(8,128)S(1)}, u32[]{:S(2)}, u32[]{:S(2)}) %collective-permute-start.19) | collective-permute-done | bytes 4128 | tf_op jit(solution)/shard_map/ppermute | solution.py:219
  115.7 3.0 %collective-permute-done.20 = f32[8,128]{1,0:T(8,128)S(1)} collective-permute-done((f32[8,128]{1,0:T(8,128)S(1)}, f32[8,128]{1,0:T(8,128)S(1)}, u32[]{:S(2)}, u32[]{:S(2)}) %collective-permute-start.20) | collective-permute-done | bytes 4128 | tf_op jit(solution)/shard_map/ppermute | solution.py:229
  118.8 2.1 %collective-permute-start.21 = (f32[8,128]{1,0:T(8,128)S(1)}, f32[8,128]{1,0:T(8,128)S(1)}, u32[]{:S(2)}, u32[]{:S(2)}) collective-permute-start(f32[8,128]{1,0:T(8,128)S(1)} %broadcast_add_fusion), channel_id=1, source_target_pairs={{0,32},{16,48},{32,0},{48,16},{64,96},{80,112},{96,64},{112,80},{1... | collective-permute-start | bytes 12296 | tf_op jit(solution)/shard_map/ppermute | solution.py:229
  120.9 3.0 %collective-permute-done.21 = f32[8,128]{1,0:T(8,128)S(1)} collective-permute-done((f32[8,128]{1,0:T(8,128)S(1)}, f32[8,128]{1,0:T(8,128)S(1)}, u32[]{:S(2)}, u32[]{:S(2)}) %collective-permute-start.21) | collective-permute-done | bytes 4128 | tf_op jit(solution)/shard_map/ppermute | solution.py:229
  123.9 1.6 %collective-permute-start.22 = (f32[8,128]{1,0:T(8,128)S(1)}, f32[8,128]{1,0:T(8,128)S(1)}, u32[]{:S(2)}, u32[]{:S(2)}) collective-permute-start(f32[8,128]{1,0:T(8,128)S(1)} %fusion.6), channel_id=1, source_target_pairs={{0,64},{16,80},{32,96},{48,112},{64,0},{80,16},{96,32},{112,48},{1... | collective-permute-start | bytes 12296 | tf_op jit(solution)/shard_map/ppermute | solution.py:229
  127.5 3.2 %collective-permute-start.23 = (f32[8,128]{1,0:T(8,128)S(1)}, f32[8,128]{1,0:T(8,128)S(1)}, u32[]{:S(2)}, u32[]{:S(2)}) collective-permute-start(f32[8,128]{1,0:T(8,128)S(1)} %add.165), channel_id=1, source_target_pairs={{0,128},{16,144},{32,160},{48,176},{64,192},{80,208},{96,224},{112... | collective-permute-start | bytes 12296 | tf_op jit(solution)/shard_map/ppermute | solution.py:229
  130.7 2.1 %fusion.1 = bf16[1,1,16,128,128]{4,3,2,1,0:T(8,128)(2,1)} fusion(f32[16,128,128]{2,1,0:T(8,128)} %get-tuple-element.9, f32[]{:T(128)S(6)} %mul.74), kind=kLoop, calls=%fused_computation.3 | loop fusion | flops 524288 | bytes 1572868 | tf_op jit(solution)/shard_map/broadcast_in_dim | solution.py:232
  (64 shorter events, 11.5 us)
Async XLA Ops:
  0.6 26.7 %collective-permute-start = (bf16[12,128,128]{2,1,0:T(8,128)(2,1)}, bf16[12,128,128]{2,1,0:T(8,128)(2,1)S(1)}, u32[]{:S(2)}, u32[]{:S(2)}) collective-permute-start(bf16[12,128,128]{2,1,0:T(8,128)(2,1)} %bitcast.35), channel_id=1, source_target_pairs={{0,16},{16,32},{32,48},{48,64},{64,80},{80,96},{96,112},{112,128},... | collective-permute-start | bytes 1179656 | tf_op jit(solution)/shard_map/ppermute | solution.py:168
  27.4 11.7 %collective-permute-start.2 = (bf16[12,128,128]{2,1,0:T(8,128)(2,1)S(1)}, bf16[12,128,128]{2,1,0:T(8,128)(2,1)S(1)}, u32[]{:S(2)}, u32[]{:S(2)}) collective-permute-start(bf16[12,128,128]{2,1,0:T(8,128)(2,1)S(1)} %broadcast_select_fusion.rest_0_), channel_id=1, source_target_pairs={{0,2},{1,15},{2,4},{3,1},{4,6},{5,3},{6,8},{7,5},{8,10},{9,7},{10,... | collective-permute-start | bytes 1179656 | tf_op jit(solution)/shard_map/ppermute | solution.py:158
  29.4 9.7 %collective-permute-start.1 = (bf16[12,128,128]{2,1,0:T(8,128)(2,1)S(1)}, bf16[12,128,128]{2,1,0:T(8,128)(2,1)S(1)}, u32[]{:S(2)}, u32[]{:S(2)}) collective-permute-start(bf16[12,128,128]{2,1,0:T(8,128)(2,1)S(1)} %broadcast_select_fusion.rest_0_), channel_id=1, source_target_pairs={{0,1},{1,0},{2,3},{3,2},{4,5},{5,4},{6,7},{7,6},{8,9},{9,8},{10,11... | collective-permute-start | bytes 1179656 | tf_op jit(solution)/shard_map/ppermute | solution.py:163
  39.1 9.0 %collective-permute-start.6 = (bf16[12,128,128]{2,1,0:T(8,128)(2,1)S(1)}, bf16[12,128,128]{2,1,0:T(8,128)(2,1)S(1)}, u32[]{:S(2)}, u32[]{:S(2)}) collective-permute-start(bf16[12,128,128]{2,1,0:T(8,128)(2,1)S(1)} %collective-permute-done.2.rest_2_), channel_id=1, source_target_pairs={{0,2},{1,15},{2,4},{3,1},{4,6},{5,3},{6,8},{7,5},{8,10},{9,7},{10,... | collective-permute-start | bytes 1179656 | tf_op jit(solution)/shard_map/ppermute | solution.py:158
  39.1 13.2 %collective-permute-start.4 = (bf16[12,128,128]{2,1,0:T(8,128)(2,1)S(1)}, bf16[12,128,128]{2,1,0:T(8,128)(2,1)S(1)}, u32[]{:S(2)}, u32[]{:S(2)}) collective-permute-start(bf16[12,128,128]{2,1,0:T(8,128)(2,1)S(1)} %collective-permute-done.1.rest_1_), channel_id=1, source_target_pairs={{0,2},{1,15},{2,4},{3,1},{4,6},{5,3},{6,8},{7,5},{8,10},{9,7},{10,... | collective-permute-start | bytes 1179656 | tf_op jit(solution)/shard_map/ppermute | solution.py:158
  48.0 9.0 %collective-permute-start.10 = (bf16[12,128,128]{2,1,0:T(8,128)(2,1)S(1)}, bf16[12,128,128]{2,1,0:T(8,128)(2,1)S(1)}, u32[]{:S(2)}, u32[]{:S(2)}) collective-permute-start(bf16[12,128,128]{2,1,0:T(8,128)(2,1)S(1)} %collective-permute-done.6.rest_6_), channel_id=1, source_target_pairs={{0,2},{1,15},{2,4},{3,1},{4,6},{5,3},{6,8},{7,5},{8,10},{9,7},{10,... | collective-permute-start | bytes 1179656 | tf_op jit(solution)/shard_map/ppermute | solution.py:158
  52.3 9.0 %collective-permute-start.8 = (bf16[12,128,128]{2,1,0:T(8,128)(2,1)S(1)}, bf16[12,128,128]{2,1,0:T(8,128)(2,1)S(1)}, u32[]{:S(2)}, u32[]{:S(2)}) collective-permute-start(bf16[12,128,128]{2,1,0:T(8,128)(2,1)S(1)} %collective-permute-done.4.rest_4_), channel_id=1, source_target_pairs={{0,2},{1,15},{2,4},{3,1},{4,6},{5,3},{6,8},{7,5},{8,10},{9,7},{10,... | collective-permute-start | bytes 1179656 | tf_op jit(solution)/shard_map/ppermute | solution.py:158
  52.3 9.0 %collective-permute-start.3 = (bf16[12,128,128]{2,1,0:T(8,128)(2,1)S(1)}, bf16[12,128,128]{2,1,0:T(8,128)(2,1)S(1)}, u32[]{:S(2)}, u32[]{:S(2)}) collective-permute-start(bf16[12,128,128]{2,1,0:T(8,128)(2,1)S(1)} %collective-permute-done.2.rest_2_), channel_id=1, source_target_pairs={{0,1},{1,0},{2,3},{3,2},{4,5},{5,4},{6,7},{7,6},{8,9},{9,8},{10,11... | collective-permute-start | bytes 1179656 | tf_op jit(solution)/shard_map/ppermute | solution.py:163
  52.5 10.0 %collective-permute-start.7 = (bf16[12,128,128]{2,1,0:T(8,128)(2,1)S(1)}, bf16[12,128,128]{2,1,0:T(8,128)(2,1)S(1)}, u32[]{:S(2)}, u32[]{:S(2)}) collective-permute-start(bf16[12,128,128]{2,1,0:T(8,128)(2,1)S(1)} %collective-permute-done.6.rest_6_), channel_id=1, source_target_pairs={{0,1},{1,0},{2,3},{3,2},{4,5},{5,4},{6,7},{7,6},{8,9},{9,8},{10,11... | collective-permute-start | bytes 1179656 | tf_op jit(solution)/shard_map/ppermute | solution.py:163
  57.0 9.1 %collective-permute-start.14 = (bf16[12,128,128]{2,1,0:T(8,128)(2,1)S(1)}, bf16[12,128,128]{2,1,0:T(8,128)(2,1)}, u32[]{:S(2)}, u32[]{:S(2)}) collective-permute-start(bf16[12,128,128]{2,1,0:T(8,128)(2,1)S(1)} %collective-permute-done.10.rest_10_), channel_id=1, source_target_pairs={{0,2},{1,15},{2,4},{3,1},{4,6},{5,3},{6,8},{7,5},{8,10},{9,7},{10,... | collective-permute-start | bytes 1179656 | tf_op jit(solution)/shard_map/ppermute | solution.py:158
  61.2 9.1 %collective-permute-start.12 = (bf16[12,128,128]{2,1,0:T(8,128)(2,1)S(1)}, bf16[12,128,128]{2,1,0:T(8,128)(2,1)}, u32[]{:S(2)}, u32[]{:S(2)}) collective-permute-start(bf16[12,128,128]{2,1,0:T(8,128)(2,1)S(1)} %collective-permute-done.8.rest_8_), channel_id=1, source_target_pairs={{0,2},{1,15},{2,4},{3,1},{4,6},{5,3},{6,8},{7,5},{8,10},{9,7},{10,... | collective-permute-start | bytes 1179656 | tf_op jit(solution)/shard_map/ppermute | solution.py:158
  61.3 10.1 %collective-permute-start.5 = (bf16[12,128,128]{2,1,0:T(8,128)(2,1)S(1)}, bf16[12,128,128]{2,1,0:T(8,128)(2,1)}, u32[]{:S(2)}, u32[]{:S(2)}) collective-permute-start(bf16[12,128,128]{2,1,0:T(8,128)(2,1)S(1)} %collective-permute-done.4.rest_4_), channel_id=1, source_target_pairs={{0,1},{1,0},{2,3},{3,2},{4,5},{5,4},{6,7},{7,6},{8,9},{9,8},{10,11... | collective-permute-start | bytes 1179656 | tf_op jit(solution)/shard_map/ppermute | solution.py:163
  62.0 9.3 %collective-permute-start.11 = (bf16[12,128,128]{2,1,0:T(8,128)(2,1)S(1)}, bf16[12,128,128]{2,1,0:T(8,128)(2,1)}, u32[]{:S(2)}, u32[]{:S(2)}) collective-permute-start(bf16[12,128,128]{2,1,0:T(8,128)(2,1)S(1)} %collective-permute-done.10.rest_10_), channel_id=1, source_target_pairs={{0,1},{1,0},{2,3},{3,2},{4,5},{5,4},{6,7},{7,6},{8,9},{9,8},{10,11... | collective-permute-start | bytes 1179656 | tf_op jit(solution)/shard_map/ppermute | solution.py:163
  63.3 8.0 %collective-permute-start.9 = (bf16[12,128,128]{2,1,0:T(8,128)(2,1)S(1)}, bf16[12,128,128]{2,1,0:T(8,128)(2,1)}, u32[]{:S(2)}, u32[]{:S(2)}) collective-permute-start(bf16[12,128,128]{2,1,0:T(8,128)(2,1)S(1)} %collective-permute-done.8.rest_8_), channel_id=1, source_target_pairs={{0,1},{1,0},{2,3},{3,2},{4,5},{5,4},{6,7},{7,6},{8,9},{9,8},{10,11... | collective-permute-start | bytes 1179656 | tf_op jit(solution)/shard_map/ppermute | solution.py:163
  66.1 5.2 %collective-permute-start.15 = (bf16[12,128,128]{2,1,0:T(8,128)(2,1)}, bf16[12,128,128]{2,1,0:T(8,128)(2,1)}, u32[]{:S(2)}, u32[]{:S(2)}) collective-permute-start(bf16[12,128,128]{2,1,0:T(8,128)(2,1)} %collective-permute-done.14.rest_14_), channel_id=1, source_target_pairs={{0,1},{1,0},{2,3},{3,2},{4,5},{5,4},{6,7},{7,6},{8,9},{9,8},{10,11... | collective-permute-start | bytes 1179656 | tf_op jit(solution)/shard_map/ppermute | solution.py:163
  70.3 2.1 %collective-permute-start.13 = (bf16[12,128,128]{2,1,0:T(8,128)(2,1)}, bf16[12,128,128]{2,1,0:T(8,128)(2,1)}, u32[]{:S(2)}, u32[]{:S(2)}) collective-permute-start(bf16[12,128,128]{2,1,0:T(8,128)(2,1)} %collective-permute-done.12.rest_12_), channel_id=1, source_target_pairs={{0,1},{1,0},{2,3},{3,2},{4,5},{5,4},{6,7},{7,6},{8,9},{9,8},{10,11... | collective-permute-start | bytes 1179656 | tf_op jit(solution)/shard_map/ppermute | solution.py:163
  96.9 1.3 collective-permute-start.16
  98.2 3.6 %collective-permute-start.17 = (f32[8,128]{1,0:T(8,128)S(1)}, f32[8,128]{1,0:T(8,128)S(1)}, u32[]{:S(2)}, u32[]{:S(2)}) collective-permute-start(f32[8,128]{1,0:T(8,128)S(1)} %add.155), channel_id=1, source_target_pairs={{0,2},{1,3},{2,0},{3,1},{4,6},{5,7},{6,4},{7,5},{8,10},{9,11},{10,... | collective-permute-start | bytes 12296 | tf_op jit(solution)/shard_map/ppermute | solution.py:219
  101.8 4.5 %collective-permute-start.18 = (f32[8,128]{1,0:T(8,128)S(1)}, f32[8,128]{1,0:T(8,128)S(1)}, u32[]{:S(2)}, u32[]{:S(2)}) collective-permute-start(f32[8,128]{1,0:T(8,128)S(1)} %add.156), channel_id=1, source_target_pairs={{0,4},{1,5},{2,6},{3,7},{4,0},{5,1},{6,2},{7,3},{8,12},{9,13},{10,... | collective-permute-start | bytes 12296 | tf_op jit(solution)/shard_map/ppermute | solution.py:219
  106.3 7.5 %collective-permute-start.19 = (f32[8,128]{1,0:T(8,128)S(1)}, f32[8,128]{1,0:T(8,128)S(1)}, u32[]{:S(2)}, u32[]{:S(2)}) collective-permute-start(f32[8,128]{1,0:T(8,128)S(1)} %add.157), channel_id=1, source_target_pairs={{0,8},{1,9},{2,10},{3,11},{4,12},{5,13},{6,14},{7,15},{8,0},{9,1},... | collective-permute-start | bytes 12296 | tf_op jit(solution)/shard_map/ppermute | solution.py:219
  115.1 3.7 %collective-permute-start.20 = (f32[8,128]{1,0:T(8,128)S(1)}, f32[8,128]{1,0:T(8,128)S(1)}, u32[]{:S(2)}, u32[]{:S(2)}) collective-permute-start(f32[8,128]{1,0:T(8,128)S(1)} %broadcast_in_dim.24), channel_id=1, source_target_pairs={{0,16},{16,0},{32,48},{48,32},{64,80},{80,64},{96,112},{112,96},{1... | collective-permute-start | bytes 12296 | tf_op jit(solution)/shard_map/ppermute | solution.py:229
  118.8 5.1 %collective-permute-start.21 = (f32[8,128]{1,0:T(8,128)S(1)}, f32[8,128]{1,0:T(8,128)S(1)}, u32[]{:S(2)}, u32[]{:S(2)}) collective-permute-start(f32[8,128]{1,0:T(8,128)S(1)} %broadcast_add_fusion), channel_id=1, source_target_pairs={{0,32},{16,48},{32,0},{48,16},{64,96},{80,112},{96,64},{112,80},{1... | collective-permute-start | bytes 12296 | tf_op jit(solution)/shard_map/ppermute | solution.py:229
  123.9 3.6 %collective-permute-start.22 = (f32[8,128]{1,0:T(8,128)S(1)}, f32[8,128]{1,0:T(8,128)S(1)}, u32[]{:S(2)}, u32[]{:S(2)}) collective-permute-start(f32[8,128]{1,0:T(8,128)S(1)} %fusion.6), channel_id=1, source_target_pairs={{0,64},{16,80},{32,96},{48,112},{64,0},{80,16},{96,32},{112,48},{1... | collective-permute-start | bytes 12296 | tf_op jit(solution)/shard_map/ppermute | solution.py:229
  127.5 6.7 %collective-permute-start.23 = (f32[8,128]{1,0:T(8,128)S(1)}, f32[8,128]{1,0:T(8,128)S(1)}, u32[]{:S(2)}, u32[]{:S(2)}) collective-permute-start(f32[8,128]{1,0:T(8,128)S(1)} %add.165), channel_id=1, source_target_pairs={{0,128},{16,144},{32,160},{48,176},{64,192},{80,208},{96,224},{112... | collective-permute-start | bytes 12296 | tf_op jit(solution)/shard_map/ppermute | solution.py:229
  (9 other events, 94.5 us)

commit v2 on v1

v2 whole, which is shorter than its diff:
```python
import jax
import jax.numpy as jnp
import numpy as np
from jax import lax
from jax.experimental import pallas as pl
from jax.experimental.pallas import tpu as pltpu
from jax.sharding import PartitionSpec as P

F32 = jnp.float32
BF16 = jnp.bfloat16


LOCAL = 4
BLOCKS = 16
EARLY = 12
VMEM_LIMIT = 60 * 2**20


def iota(shape, dim):
    return lax.broadcasted_iota(jnp.int32, shape, dim)


def pair_mpo(left_ref, right_ref):
    rows, bonds = left_ref.shape
    pairs = LOCAL * LOCAL
    wide = 256
    over_w = (iota((bonds, wide), 0) == iota((bonds, wide), 1) // pairs).astype(BF16)
    big = jnp.dot(right_ref[...], over_w, preferred_element_type=F32)
    same = (iota((rows, wide), 0) % pairs) == (iota((rows, wide), 1) % pairs)
    big = jnp.where(same, big, 0.0).astype(BF16)
    by_m = (iota((16, rows), 0) == iota((16, rows), 1) // pairs).astype(BF16)
    right = jnp.dot(by_m, big, preferred_element_type=F32).astype(BF16)
    joined = jnp.dot(left_ref[...], right[:bonds], preferred_element_type=F32)
    gap = iota((rows, wide), 0) % LOCAL - (iota((rows, wide), 1) // LOCAL) % LOCAL
    out = jnp.zeros((rows, wide), F32)
    for d in range(1 - LOCAL, LOCAL):
        moved = pltpu.roll(pltpu.roll(joined, d % rows, 0), (-LOCAL * d) % wide, 1)
        out = jnp.where(gap == d, moved, out)
    return out[:, :rows].astype(BF16)


def turn(src_ref, xt_ref):
    for j in range(src_ref.shape[1] // 16):
        xt_ref[j * 16 : (j + 1) * 16] = jnp.swapaxes(src_ref[:, j * 16 : (j + 1) * 16, :], 0, 1)


def spread(xt_ref, renv_ref, mpo, x3_ref, done=None):
    states, pairs, width = xt_ref.shape
    bonds = renv_ref.shape[0]
    for at in range(0, states, 16):
        xa = xt_ref[at : at + 16].reshape(16 * pairs, width)
        first = []
        for k in range(bonds // 2):
            both = jnp.concatenate([renv_ref[2 * k], renv_ref[2 * k + 1]], axis=1)
            got = jnp.dot(xa, both, preferred_element_type=F32).astype(BF16)
            first += [got[:, :width], got[:, width:]]
        rows = []
        for i in range(8):
            sides = []
            for a in (2 * i, 2 * i + 1):
                sides.append(jnp.concatenate([f[a * pairs : (a + 1) * pairs] for f in first], axis=0))
            out = jnp.dot(mpo, jnp.concatenate(sides, axis=1), preferred_element_type=F32).astype(BF16)
            rows += [out[:, :width], out[:, width:]]
        for l in range(bonds):
            block = jnp.stack([row[l * pairs : (l + 1) * pairs] for row in rows], axis=0)
            x3_ref[:, l, at : at + 16, :] = jnp.swapaxes(block, 0, 1)
        if done is not None:
            done(at)


def front_kernel(psi_any, renv_any, left_ref, right_ref, x3_any, mpo_ref, psi_ref, renv_ref, xt_ref, x3_ref, sem_ref, out_sem):
    copies = [
        pltpu.make_async_copy(psi_any, psi_ref, sem_ref.at[0]),
        pltpu.make_async_copy(renv_any, renv_ref, sem_ref.at[1]),
    ]
    for copy in copies:
        copy.start()
    mpo = pair_mpo(left_ref, right_ref)
    mpo_ref[...] = mpo
    for copy in copies:
        copy.wait()
    turn(psi_ref, xt_ref)
    sent = []

    def done(at):
        rows = pl.ds(at, 16)
        sent.append(pltpu.make_async_copy(x3_ref.at[:, :, rows], x3_any.at[:, :, rows], out_sem.at[at // 16]))
        sent[-1].start()

    spread(xt_ref, renv_ref, mpo, x3_ref, done)
    for copy in sent:
        copy.wait()


def contract(lenv_ref, slot, x3_ref, q):
    bonds = lenv_ref.shape[1]
    total = None
    for k in range(bonds // 2):
        lhs = jnp.concatenate([lenv_ref[slot, 2 * k], lenv_ref[slot, 2 * k + 1]], axis=1)
        rhs = jnp.concatenate([x3_ref[q, 2 * k], x3_ref[q, 2 * k + 1]], axis=0)
        part = jnp.dot(lhs, rhs, preferred_element_type=F32)
        total = part if total is None else total + part
    return total


def masked_step(keep, psi_ref, u_ref, sq_ref, lenv_ref, slot, x3_ref, q):
    h = contract(lenv_ref, slot, x3_ref, q)
    u = jnp.where(keep, psi_ref[q].astype(F32) - 0.5 * h, 0.0)
    u_ref[q] = u.astype(BF16)
    sq_ref[...] += u * u


def mid_kernel(slot_ref, rank_ref, psi_any, x3_any, *rest):
    blocks = rest[:EARLY]
    u_ref, sq_ref, psi_ref, lenv_ref, x3_ref, sem_ref, x3_sem = rest[EARLY:]
    pairs, width = psi_ref.shape[0], psi_ref.shape[2]
    copies = [pltpu.make_async_copy(blocks[i], lenv_ref.at[i], sem_ref.at[i]) for i in range(EARLY)]
    copies.append(pltpu.make_async_copy(psi_any, psi_ref, sem_ref.at[EARLY]))
    for copy in copies:
        copy.start()
    loads = [pltpu.make_async_copy(x3_any.at[q], x3_ref.at[q], x3_sem.at[q]) for q in range(pairs)]
    for q in range(pairs):
        pl.when(slot_ref[q] < EARLY)(loads[q].start)
    keep = iota((width, width), 1) < rank_ref[0]
    sq_ref[...] = jnp.zeros_like(sq_ref)
    for copy in copies:
        copy.wait()
    for q in range(pairs):

        @pl.when(slot_ref[q] < EARLY)
        def _():
            loads[q].wait()
            masked_step(keep, psi_ref, u_ref, sq_ref, lenv_ref, slot_ref[q], x3_ref, q)

        @pl.when(slot_ref[q] >= EARLY)
        def _():
            u_ref[q] = jnp.zeros((width, width), BF16)


def back_kernel(slot_ref, rank_ref, psi_any, renv_any, mpo_ref, x3_any, early_u, early_sq, *rest):
    blocks = rest[:BLOCKS]
    v_any, stat_ref, lenv_ref, x3_ref, u_ref, xt_ref, psi_ref, renv_ref, v_ref, sq_ref = rest[BLOCKS:-3]
    sem_ref, x3_sem, v_sem = rest[-3:]
    pairs, width = psi_ref.shape[0], psi_ref.shape[2]
    copies = [pltpu.make_async_copy(blocks[i], lenv_ref.at[i], sem_ref.at[i]) for i in range(BLOCKS)]
    first = copies[EARLY:] + [
        pltpu.make_async_copy(psi_any, psi_ref, sem_ref.at[BLOCKS]),
        pltpu.make_async_copy(early_u, u_ref, sem_ref.at[BLOCKS + 1]),
    ]
    later = pltpu.make_async_copy(renv_any, renv_ref, sem_ref.at[BLOCKS + 2])
    loads = [pltpu.make_async_copy(x3_any.at[q], x3_ref.at[q], x3_sem.at[q]) for q in range(pairs)]
    for copy in first:
        copy.start()
    for q in range(pairs):
        pl.when(slot_ref[q] >= EARLY)(loads[q].start)
    later.start()
    for copy in copies[:EARLY]:
        copy.start()
    keep = iota((width, width), 1) < rank_ref[0]
    sq_ref[...] = early_sq[...]
    for copy in first:
        copy.wait()
    for q in range(pairs):

        @pl.when(slot_ref[q] >= EARLY)
        def _():
            loads[q].wait()
            masked_step(keep, psi_ref, u_ref, sq_ref, lenv_ref, slot_ref[q], x3_ref, q)

    turn(u_ref, xt_ref)
    later.wait()
    spread(xt_ref, renv_ref, mpo_ref[...], x3_ref)
    for copy in copies[:EARLY]:
        copy.wait()
    zero = jnp.zeros((width, width), F32)
    sq, inner, own = zero, zero, zero
    sent = []
    for q in range(pairs):
        h = contract(lenv_ref, slot_ref[q], x3_ref, q)
        x = u_ref[q].astype(F32)
        v = jnp.where(keep, x - 0.5 * h, 0.0)
        v_ref[q] = v
        sent.append(pltpu.make_async_copy(v_ref.at[q], v_any.at[q], v_sem.at[q]))
        sent[-1].start()
        sq, inner, own = sq + v * v, inner + x * h, own + x * x
    row = iota((8, width), 0)
    stat = jnp.zeros((8, width), F32)
    for i, part in enumerate((sq_ref[...], sq, inner, own)):
        stat = jnp.where(row == i, jnp.sum(part), stat)
    stat_ref[...] = stat
    for copy in sent:
        copy.wait()


VMEM_SPEC = pl.BlockSpec(memory_space=pltpu.VMEM)
SMEM_SPEC = pl.BlockSpec(memory_space=pltpu.SMEM)
ANY_SPEC = pl.BlockSpec(memory_space=pl.ANY)


def call(kernel, name, flops, out_shape, in_specs, out_specs, scratch):
    return pl.pallas_call(
        kernel,
        out_shape=out_shape,
        in_specs=in_specs,
        out_specs=out_specs,
        scratch_shapes=scratch,
        compiler_params=pltpu.CompilerParams(vmem_limit_bytes=VMEM_LIMIT),
        cost_estimate=pl.CostEstimate(flops=flops, bytes_accessed=8 * 10**6, transcendentals=0),
        name=name,
    )


def front(psi, renv, left, right):
    pairs, width = psi.shape[0], psi.shape[2]
    bonds = renv.shape[0]
    rows = bonds * pairs
    return call(
        front_kernel,
        "front",
        2 * 10**9,
        (jax.ShapeDtypeStruct((pairs, bonds, width, width), BF16), jax.ShapeDtypeStruct((rows, rows), BF16)),
        [ANY_SPEC, ANY_SPEC, VMEM_SPEC, VMEM_SPEC],
        (ANY_SPEC, VMEM_SPEC),
        [
            pltpu.VMEM((pairs, width, width), BF16),
            pltpu.VMEM((bonds, width, width), BF16),
            pltpu.VMEM((width, pairs, width), BF16),
            pltpu.VMEM((pairs, bonds, width, width), BF16),
            pltpu.SemaphoreType.DMA((2,)),
            pltpu.SemaphoreType.DMA((width // 16,)),
        ],
    )(psi, renv, left, right)


def mid(slot, rank, psi, x3, blocks):
    pairs, width = psi.shape[0], psi.shape[2]
    bonds = x3.shape[1]
    return call(
        mid_kernel,
        "mid",
        10**9,
        (jax.ShapeDtypeStruct((pairs, width, width), BF16), jax.ShapeDtypeStruct((width, width), F32)),
        [SMEM_SPEC, SMEM_SPEC, ANY_SPEC, ANY_SPEC] + [ANY_SPEC] * EARLY,
        (VMEM_SPEC, VMEM_SPEC),
        [
            pltpu.VMEM((pairs, width, width), BF16),
            pltpu.VMEM((EARLY, bonds, width, width), BF16),
            pltpu.VMEM((pairs, bonds, width, width), BF16),
            pltpu.SemaphoreType.DMA((EARLY + 1,)),
            pltpu.SemaphoreType.DMA((pairs,)),
        ],
    )(slot, rank, psi, x3, *blocks)


def back(slot, rank, psi, renv, mpo, x3, early_u, early_sq, blocks):
    pairs, width = psi.shape[0], psi.shape[2]
    bonds = renv.shape[0]
    return call(
        back_kernel,
        "back",
        3 * 10**9,
        (jax.ShapeDtypeStruct((pairs, width, width), F32), jax.ShapeDtypeStruct((8, width), F32)),
        [SMEM_SPEC, SMEM_SPEC, ANY_SPEC, ANY_SPEC, VMEM_SPEC, ANY_SPEC, ANY_SPEC, VMEM_SPEC] + [ANY_SPEC] * BLOCKS,
        (ANY_SPEC, VMEM_SPEC),
        [
            pltpu.VMEM((BLOCKS, bonds, width, width), BF16),
            pltpu.VMEM((pairs, bonds, width, width), BF16),
            pltpu.VMEM((pairs, width, width), BF16),
            pltpu.VMEM((width, pairs, width), BF16),
            pltpu.VMEM((pairs, width, width), BF16),
            pltpu.VMEM((bonds, width, width), BF16),
            pltpu.VMEM((pairs, width, width), F32),
            pltpu.VMEM((width, width), F32),
            pltpu.SemaphoreType.DMA((BLOCKS + 3,)),
            pltpu.SemaphoreType.DMA((pairs,)),
            pltpu.SemaphoreType.DMA((pairs,)),
        ],
    )(slot, rank, psi, renv, mpo, x3, early_u, early_sq, *blocks)


def hop(value):
    n = lax.axis_size("sec")
    return lax.ppermute(value, "sec", [(i, (i + (2 if i % 2 == 0 else -2)) % n) for i in range(n)])


def cross_hop(value):
    n = lax.axis_size("sec")
    return lax.ppermute(value, "sec", [(i, (i + (-2 if i % 2 == 0 else 2)) % n ^ 1) for i in range(n)])


def twin(value):
    n = lax.axis_size("sec")
    return lax.ppermute(value, "sec", [(i, i ^ 1) for i in range(n)])


def from_behind(value):
    n = lax.axis_size("seg")
    return lax.ppermute(value, "seg", [(i, i + 1) for i in range(n - 1)])


def shards(psi, env_build, env_right, site_left, site_right, charge, rank):
    nsec = lax.axis_size("sec")
    nseg = lax.axis_size("seg")
    sector = lax.axis_index("sec")
    segment = lax.axis_index("seg")
    x = psi[0, 0]
    renv = env_right[0, 0]
    pairs, width = x.shape[0], x.shape[2]
    count = float(nsec * pairs * width * width)

    env = env_build[0, 0]
    moved = from_behind(env)
    tall = (site_left.shape[0] * pairs, site_left.shape[1])
    x3, mpo = front(
        x, renv, site_left.transpose(0, 2, 3, 1).reshape(tall), site_right.transpose(0, 2, 3, 1).reshape(tall)
    )
    moved, x3 = lax.optimization_barrier((moved, x3))
    own = jnp.where(segment == 0, env, moved)

    chips = nsec // 2
    held = np.zeros((nsec, nsec), np.int32)
    for s in range(nsec):
        z, c = s // 2, s % 2
        sign = 1 - 2 * c
        order = [s, s ^ 1]
        for k in range(1, chips // 2 + 1):
            behind, ahead = (z - sign * k) % chips, (z + sign * k) % chips
            t_pair = [2 * behind + 1 - c, 2 * ahead + c] if k < chips // 2 else []
            o_pair = [2 * behind + c, 2 * ahead + 1 - c]
            order += o_pair + t_pair
        for i, left in enumerate(order):
            held[s, left] = i
    row = lax.dynamic_index_in_dim(jnp.asarray(held), sector, 0, keepdims=False)
    left = (sector - charge) % nsec
    hits = left[:, None] == jnp.arange(nsec, dtype=jnp.int32)[None, :]
    slot = jnp.sum(jnp.where(hits, row[None, :], 0), axis=1).astype(jnp.int32)

    o1, t1 = hop(own), cross_hop(own)
    o2, t2 = hop(o1), hop(t1)
    o3, t3 = hop(o2), hop(t2)
    o4 = hop(o3)
    blocks = [own, twin(own), o1, twin(o1), t1, twin(t1), o2, twin(o2), t2, twin(t2), o3, twin(o3)]
    early_u, early_sq = mid(slot, rank, x, x3, blocks)
    t3, early_u = lax.optimization_barrier((t3, early_u))
    blocks += [t3, twin(t3), o4, twin(o4)]

    v, stat = back(slot, rank, x, renv, mpo, x3, early_u, early_sq, blocks)

    mine = stat[1, 0]
    total = stat
    for bit in (1, 2, 4, 8):
        total = total + lax.ppermute(total, "sec", [(i, i ^ bit) for i in range(nsec)])
    scale_one = lax.rsqrt(total[0, 0] / count + 1e-06)
    energy = total[2, 0] / total[3, 0]
    second = (scale_one * scale_one) * total[1, 0]
    scale = scale_one * lax.rsqrt(second / count + 1e-06)
    state = (v * scale).astype(BF16)
    share = jnp.log(float(nsec) * mine / total[1, 0])
    upto = jnp.full((8, width), share, F32)
    whole = upto
    for bit in (1, 2, 4, 8):
        got = lax.ppermute(whole, "seg", [(i, i ^ bit) for i in range(nseg)])
        upto = jnp.where((segment & bit) != 0, upto + got, upto)
        whole = whole + got
    return state[None, None], energy.reshape(1), upto[0, 0].reshape(1, 1)


def solution(mesh):
    return jax.shard_map(
        shards,
        mesh=mesh,
        in_specs=(
            P("seg", "sec", None, None, None),
            P("seg", "sec", None, None, None),
            P("seg", "sec", None, None, None),
            P(),
            P(),
            P(),
            P("sec"),
        ),
        out_specs=(P("seg", "sec", None, None, None), P("seg"), P("seg", "sec")),
        check_vma=False,
    )
```

time: 136 us -> 122 us (0.90)
  the two profiles are of different devices: /device:TPU:2 before, /device:TPU:64 now
where the time goes in v2:
time: 122 us; the launch traced here: 121 us
  starting transfers between devices  41.9 us (34%)
  waiting for transfers between devices  32.4 us (27%)
  Pallas kernels  31 us (25%)
  between operations  6.74 us (6%)
  local copies, waits for them, and re-layouts  5.25 us (4%)
  other arithmetic  3.61 us (3%)
    ppermute x6, starting transfers between devices, hop(): lax.ppermute(value, 'sec', [(i, (i + (2 if i % 2 == 0 else -2)) % n) for...  20.5 us
    ppermute x6, waiting for transfers between devices, hop(): lax.ppermute(value, 'sec', [(i, (i + (2 if i % 2 == 0 else -2)) % n) for...  14.5 us
    ppermute x4, starting transfers between devices, shards(): got = lax.ppermute(whole, 'seg', [(i, i ^ bit) for i in range(nseg)])  13.6 us
    pallas_call x1, Pallas kernels, back(): call(back_kernel, 'back', 3 * 10 ** 9, (jax.ShapeDtypeStruct((pairs, widt...  13.4 us
    ppermute x4, waiting for transfers between devices, shards(): lax.ppermute(total, 'sec', [(i, i ^ bit) for i in range(nsec)])  12.6 us
    pallas_call x1, Pallas kernels, front(): call(front_kernel, 'front', 2 * 10 ** 9, (jax.ShapeDtypeStruct((pairs, bo...  8.89 us
    pallas_call x1, Pallas kernels, mid(): call(mid_kernel, 'mid', 10 ** 9, (jax.ShapeDtypeStruct((pairs, width, wid...  8.72 us
    ppermute x1, starting transfers between devices, from_behind(): return lax.ppermute(value, 'seg', [(i, i + 1) for i in range(n - 1)])  3.55 us
  transfers between devices with their start and end apart: 24, of which 12 were waited for; matrix products, arithmetic and copies ran while one was open for 4% of the time, Pallas kernels for 15%

profile of v2, /device:TPU:64, one launch (start us, length us, event | category | flops | bytes accessed | tf_op | source)
XLA Modules:
  0.0 120.9 jit_solution(14592821013818061368)
XLA Ops:
  0.7 3.6 %collective-permute-start = (bf16[12,128,128]{2,1,0:T(8,128)(2,1)}, bf16[12,128,128]{2,1,0:T(8,128)(2,1)S(1)}, u32[]{:S(2)}, u32[]{:S(2)}) collective-permute-start(bf16[12,128,128]{2,1,0:T(8,128)(2,1)} %bitcast.23), channel_id=1, source_target_pairs={{0,16},{16,32},{32,48},{48,64},{64,80},{80,96},{96,112},{112,128},... | collective-permute-start | bytes 1179656 | tf_op jit(solution)/shard_map/ppermute | solution.py:298
  4.2 8.9 %front.1 = (bf16[16,12,128,128]{3,2,1,0:T(8,128)(2,1)}, bf16[192,192]{1,0:T(8,128)(2,1)}) custom-call(bf16[16,128,128]{2,1,0:T(8,128)(2,1)} %bitcast.18, bf16[12,128,128]{2,1,0:T(8,128)(2,1)} %bitcast.21, bf16[192,12]{1,0:T(8,128)(2,1)} %bitcast.24, bf16[192,12]{1,0:T(8,128)(2,1)} %bitcast.25), custom_call_target="tpu_custom_call" | custom-call | flops 2000000000 | bytes 8000000 | tf_op jit(solution)/shard_map/front/pallas_call | solution.py:217
  13.2 2.0 %collective-permute-start.5 = (bf16[12,128,128]{2,1,0:T(8,128)(2,1)S(1)}, bf16[12,128,128]{2,1,0:T(8,128)(2,1)S(1)}, u32[]{:S(2)}, u32[]{:S(2)}) collective-permute-start(bf16[12,128,128]{2,1,0:T(8,128)(2,1)S(1)} %broadcast_select_fusion.rest_0_), channel_id=1, source_target_pairs={{0,2},{1,15},{2,4},{3,1},{4,6},{5,3},{6,8},{7,5},{8,10},{9,7},{10,... | collective-permute-start | bytes 1179656 | tf_op jit(solution)/shard_map/ppermute | solution.py:283
  15.2 8.7 %collective-permute-done.5.rest_2_ = bf16[12,128,128]{2,1,0:T(8,128)(2,1)S(1)} collective-permute-done((bf16[12,128,128]{2,1,0:T(8,128)(2,1)S(1)}, bf16[12,128,128]{2,1,0:T(8,128)(2,1)S(1)}, u32[]{:S(2)}, u32[]{:S(2)}) %collective-permute-start.5) | collective-permute-done | bytes 393248 | tf_op jit(solution)/shard_map/ppermute | solution.py:283
  23.9 3.6 %collective-permute-start.8 = (bf16[12,128,128]{2,1,0:T(8,128)(2,1)S(1)}, bf16[12,128,128]{2,1,0:T(8,128)(2,1)S(1)}, u32[]{:S(2)}, u32[]{:S(2)}) collective-permute-start(bf16[12,128,128]{2,1,0:T(8,128)(2,1)S(1)} %collective-permute-done.5.rest_2_), channel_id=1, source_target_pairs={{0,2},{1,15},{2,4},{3,1},{4,6},{5,3},{6,8},{7,5},{8,10},{9,7},{10,... | collective-permute-start | bytes 1179656 | tf_op jit(solution)/shard_map/ppermute | solution.py:283
  27.5 3.8 %collective-permute-start.2 = (bf16[12,128,128]{2,1,0:T(8,128)(2,1)S(1)}, bf16[12,128,128]{2,1,0:T(8,128)(2,1)S(1)}, u32[]{:S(2)}, u32[]{:S(2)}) collective-permute-start(bf16[12,128,128]{2,1,0:T(8,128)(2,1)S(1)} %collective-permute-done.1.rest_4_), channel_id=1, source_target_pairs={{0,2},{1,15},{2,4},{3,1},{4,6},{5,3},{6,8},{7,5},{8,10},{9,7},{10,... | collective-permute-start | bytes 1179656 | tf_op jit(solution)/shard_map/ppermute | solution.py:283
  31.2 1.5 %collective-permute-done.8.rest_6_ = bf16[12,128,128]{2,1,0:T(8,128)(2,1)S(1)} collective-permute-done((bf16[12,128,128]{2,1,0:T(8,128)(2,1)S(1)}, bf16[12,128,128]{2,1,0:T(8,128)(2,1)S(1)}, u32[]{:S(2)}, u32[]{:S(2)}) %collective-permute-start.8) | collective-permute-done | bytes 393248 | tf_op jit(solution)/shard_map/ppermute | solution.py:283
  32.8 3.7 %collective-permute-start.11 = (bf16[12,128,128]{2,1,0:T(8,128)(2,1)S(1)}, bf16[12,128,128]{2,1,0:T(8,128)(2,1)S(1)}, u32[]{:S(2)}, u32[]{:S(2)}) collective-permute-start(bf16[12,128,128]{2,1,0:T(8,128)(2,1)S(1)} %collective-permute-done.8.rest_6_), channel_id=1, source_target_pairs={{0,2},{1,15},{2,4},{3,1},{4,6},{5,3},{6,8},{7,5},{8,10},{9,7},{10,... | collective-permute-start | bytes 1179656 | tf_op jit(solution)/shard_map/ppermute | solution.py:283
  37.5 4.3 %collective-permute-done.11.rest_10_ = bf16[12,128,128]{2,1,0:T(8,128)(2,1)S(1)} collective-permute-done((bf16[12,128,128]{2,1,0:T(8,128)(2,1)S(1)}, bf16[12,128,128]{2,1,0:T(8,128)(2,1)S(1)}, u32[]{:S(2)}, u32[]{:S(2)}) %collective-permute-start.11) | collective-permute-done | bytes 393248 | tf_op jit(solution)/shard_map/ppermute | solution.py:283
  43.1 3.8 %collective-permute-start.3 = (bf16[12,128,128]{2,1,0:T(8,128)(2,1)S(1)}, bf16[12,128,128]{2,1,0:T(8,128)(2,1)}, u32[]{:S(2)}, u32[]{:S(2)}) collective-permute-start(bf16[12,128,128]{2,1,0:T(8,128)(2,1)S(1)} %collective-permute-done.2.rest_8_), channel_id=1, source_target_pairs={{0,2},{1,15},{2,4},{3,1},{4,6},{5,3},{6,8},{7,5},{8,10},{9,7},{10,... | collective-permute-start | bytes 1179656 | tf_op jit(solution)/shard_map/ppermute | solution.py:283
  46.9 3.7 %collective-permute-start.14 = (bf16[12,128,128]{2,1,0:T(8,128)(2,1)S(1)}, bf16[12,128,128]{2,1,0:T(8,128)(2,1)}, u32[]{:S(2)}, u32[]{:S(2)}) collective-permute-start(bf16[12,128,128]{2,1,0:T(8,128)(2,1)S(1)} %collective-permute-done.11.rest_10_), channel_id=1, source_target_pairs={{0,2},{1,15},{2,4},{3,1},{4,6},{5,3},{6,8},{7,5},{8,10},{9,7},{10,... | collective-permute-start | bytes 1179656 | tf_op jit(solution)/shard_map/ppermute | solution.py:283
  52.9 8.7 %mid.1 = (bf16[16,128,128]{2,1,0:T(8,128)(2,1)}, f32[128,128]{1,0:T(8,128)}) custom-call(s32[16]{0:T(128)} %select_reduce_fusion.slot_ref, s32[1]{0:T(128)S(6)} %copy.11.rank_ref, bf16[16,128,128]{2,1,0:T(8,128)(2,1)} %bitcast.19, bf16[16,12,128,128]{3,2,1,0:T(8,128)(2,1)} %get-tuple-element.15.x3_any, bf16[12,128,128]{2,1,0:T(8,128)(2,1)} %copy-done, ...), custom_call_target="tpu_custom_call" | custom-call | flops 1000000000 | bytes 8000000 | tf_op jit(solution)/shard_map/mid/pallas_call | solution.py:238
  64.9 13.4 %back.1 = (f32[16,128,128]{2,1,0:T(8,128)}, f32[8,128]{1,0:T(8,128)}) custom-call(s32[16]{0:T(128)} %select_reduce_fusion.slot_ref, s32[1]{0:T(128)S(6)} %copy.11.rank_ref, bf16[16,128,128]{2,1,0:T(8,128)(2,1)} %bitcast.20, bf16[12,128,128]{2,1,0:T(8,128)(2,1)} %bitcast.22, bf16[192,192]{1,0:T(8,128)(2,1)} %get-tuple-element.13.mpo_ref, ...), custom_call_target="tpu_custom_call" | custom-call | flops 3000000000 | bytes 8000000 | tf_op jit(solution)/shard_map/back/pallas_call | solution.py:258
  80.6 3.5 %collective-permute-done.17 = f32[8,128]{1,0:T(8,128)S(1)} collective-permute-done((f32[8,128]{1,0:T(8,128)S(1)}, f32[8,128]{1,0:T(8,128)S(1)}, u32[]{:S(2)}, u32[]{:S(2)}) %collective-permute-start.17) | collective-permute-done | bytes 4128 | tf_op jit(solution)/shard_map/ppermute | solution.py:352
  84.1 4.5 %collective-permute-done.18 = f32[8,128]{1,0:T(8,128)S(1)} collective-permute-done((f32[8,128]{1,0:T(8,128)S(1)}, f32[8,128]{1,0:T(8,128)S(1)}, u32[]{:S(2)}, u32[]{:S(2)}) %collective-permute-start.18) | collective-permute-done | bytes 4128 | tf_op jit(solution)/shard_map/ppermute | solution.py:352
  88.6 2.1 %collective-permute-start.19 = (f32[8,128]{1,0:T(8,128)S(1)}, f32[8,128]{1,0:T(8,128)S(1)}, u32[]{:S(2)}, u32[]{:S(2)}) collective-permute-start(f32[8,128]{1,0:T(8,128)S(1)} %add.52), channel_id=1, source_target_pairs={{0,8},{1,9},{2,10},{3,11},{4,12},{5,13},{6,14},{7,15},{8,0},{9,1},... | collective-permute-start | bytes 12296 | tf_op jit(solution)/shard_map/ppermute | solution.py:352
  92.6 3.5 %collective-permute-done.19 = f32[8,128]{1,0:T(8,128)S(1)} collective-permute-done((f32[8,128]{1,0:T(8,128)S(1)}, f32[8,128]{1,0:T(8,128)S(1)}, u32[]{:S(2)}, u32[]{:S(2)}) %collective-permute-start.19) | collective-permute-done | bytes 4128 | tf_op jit(solution)/shard_map/ppermute | solution.py:352
  97.4 2.2 %collective-permute-start.20 = (f32[8,128]{1,0:T(8,128)S(1)}, f32[8,128]{1,0:T(8,128)S(1)}, u32[]{:S(2)}, u32[]{:S(2)}) collective-permute-start(f32[8,128]{1,0:T(8,128)S(1)} %broadcast_in_dim.27), channel_id=1, source_target_pairs={{0,16},{16,0},{32,48},{48,32},{64,80},{80,64},{96,112},{112,96},{1... | collective-permute-start | bytes 12296 | tf_op jit(solution)/shard_map/ppermute | solution.py:362
  99.6 1.6 %collective-permute-done.20 = f32[8,128]{1,0:T(8,128)S(1)} collective-permute-done((f32[8,128]{1,0:T(8,128)S(1)}, f32[8,128]{1,0:T(8,128)S(1)}, u32[]{:S(2)}, u32[]{:S(2)}) %collective-permute-start.20) | collective-permute-done | bytes 4128 | tf_op jit(solution)/shard_map/ppermute | solution.py:362
  101.2 3.6 %collective-permute-start.21 = (f32[8,128]{1,0:T(8,128)S(1)}, f32[8,128]{1,0:T(8,128)S(1)}, u32[]{:S(2)}, u32[]{:S(2)}) collective-permute-start(f32[8,128]{1,0:T(8,128)S(1)} %broadcast_add_fusion), channel_id=1, source_target_pairs={{0,32},{16,48},{32,0},{48,16},{64,96},{80,112},{96,64},{112,80},{1... | collective-permute-start | bytes 12296 | tf_op jit(solution)/shard_map/ppermute | solution.py:362
  104.8 1.6 %collective-permute-done.21 = f32[8,128]{1,0:T(8,128)S(1)} collective-permute-done((f32[8,128]{1,0:T(8,128)S(1)}, f32[8,128]{1,0:T(8,128)S(1)}, u32[]{:S(2)}, u32[]{:S(2)}) %collective-permute-start.21) | collective-permute-done | bytes 4128 | tf_op jit(solution)/shard_map/ppermute | solution.py:362
  106.4 4.2 %collective-permute-start.22 = (f32[8,128]{1,0:T(8,128)S(1)}, f32[8,128]{1,0:T(8,128)S(1)}, u32[]{:S(2)}, u32[]{:S(2)}) collective-permute-start(f32[8,128]{1,0:T(8,128)S(1)} %fusion.3), channel_id=1, source_target_pairs={{0,64},{16,80},{32,96},{48,112},{64,0},{80,16},{96,32},{112,48},{1... | collective-permute-start | bytes 12296 | tf_op jit(solution)/shard_map/ppermute | solution.py:362
  112.1 3.6 %collective-permute-start.23 = (f32[8,128]{1,0:T(8,128)S(1)}, f32[8,128]{1,0:T(8,128)S(1)}, u32[]{:S(2)}, u32[]{:S(2)}) collective-permute-start(f32[8,128]{1,0:T(8,128)S(1)} %add.60), channel_id=1, source_target_pairs={{0,128},{16,144},{32,160},{48,176},{64,192},{80,208},{96,224},{112... | collective-permute-start | bytes 12296 | tf_op jit(solution)/shard_map/ppermute | solution.py:362
  115.8 2.1 %fusion = bf16[1,1,16,128,128]{4,3,2,1,0:T(8,128)(2,1)} fusion(f32[16,128,128]{2,1,0:T(8,128)} %get-tuple-element.21, f32[]{:T(128)S(6)} %mul.17), kind=kLoop, calls=%fused_computation.1 | loop fusion | flops 524288 | bytes 1572868 | tf_op jit(solution)/shard_map/broadcast_in_dim | solution.py:365
  (74 shorter events, 12.1 us)
Async XLA Ops:
  0.7 12.5 %collective-permute-start = (bf16[12,128,128]{2,1,0:T(8,128)(2,1)}, bf16[12,128,128]{2,1,0:T(8,128)(2,1)S(1)}, u32[]{:S(2)}, u32[]{:S(2)}) collective-permute-start(bf16[12,128,128]{2,1,0:T(8,128)(2,1)} %bitcast.23), channel_id=1, source_target_pairs={{0,16},{16,32},{32,48},{48,64},{64,80},{80,96},{96,112},{112,128},... | collective-permute-start | bytes 1179656 | tf_op jit(solution)/shard_map/ppermute | solution.py:298
  13.2 10.7 %collective-permute-start.5 = (bf16[12,128,128]{2,1,0:T(8,128)(2,1)S(1)}, bf16[12,128,128]{2,1,0:T(8,128)(2,1)S(1)}, u32[]{:S(2)}, u32[]{:S(2)}) collective-permute-start(bf16[12,128,128]{2,1,0:T(8,128)(2,1)S(1)} %broadcast_select_fusion.rest_0_), channel_id=1, source_target_pairs={{0,2},{1,15},{2,4},{3,1},{4,6},{5,3},{6,8},{7,5},{8,10},{9,7},{10,... | collective-permute-start | bytes 1179656 | tf_op jit(solution)/shard_map/ppermute | solution.py:283
  15.2 12.3 %collective-permute-start.1 = (bf16[12,128,128]{2,1,0:T(8,128)(2,1)S(1)}, bf16[12,128,128]{2,1,0:T(8,128)(2,1)S(1)}, u32[]{:S(2)}, u32[]{:S(2)}) collective-permute-start(bf16[12,128,128]{2,1,0:T(8,128)(2,1)S(1)} %broadcast_select_fusion.rest_0_), channel_id=1, source_target_pairs={{0,15},{1,2},{2,1},{3,4},{4,3},{5,6},{6,5},{7,8},{8,7},{9,10},{10,... | collective-permute-start | bytes 1179656 | tf_op jit(solution)/shard_map/ppermute | solution.py:288
  23.9 8.9 %collective-permute-start.8 = (bf16[12,128,128]{2,1,0:T(8,128)(2,1)S(1)}, bf16[12,128,128]{2,1,0:T(8,128)(2,1)S(1)}, u32[]{:S(2)}, u32[]{:S(2)}) collective-permute-start(bf16[12,128,128]{2,1,0:T(8,128)(2,1)S(1)} %collective-permute-done.5.rest_2_), channel_id=1, source_target_pairs={{0,2},{1,15},{2,4},{3,1},{4,6},{5,3},{6,8},{7,5},{8,10},{9,7},{10,... | collective-permute-start | bytes 1179656 | tf_op jit(solution)/shard_map/ppermute | solution.py:283
  27.5 9.5 %collective-permute-start.4 = (bf16[12,128,128]{2,1,0:T(8,128)(2,1)S(1)}, bf16[12,128,128]{2,1,0:T(8,128)(2,1)S(1)}, u32[]{:S(2)}, u32[]{:S(2)}) collective-permute-start(bf16[12,128,128]{2,1,0:T(8,128)(2,1)S(1)} %broadcast_select_fusion.rest_0_), channel_id=1, source_target_pairs={{0,1},{1,0},{2,3},{3,2},{4,5},{5,4},{6,7},{7,6},{8,9},{9,8},{10,11... | collective-permute-start | bytes 1179656 | tf_op jit(solution)/shard_map/ppermute | solution.py:293
  27.5 9.6 %collective-permute-start.2 = (bf16[12,128,128]{2,1,0:T(8,128)(2,1)S(1)}, bf16[12,128,128]{2,1,0:T(8,128)(2,1)S(1)}, u32[]{:S(2)}, u32[]{:S(2)}) collective-permute-start(bf16[12,128,128]{2,1,0:T(8,128)(2,1)S(1)} %collective-permute-done.1.rest_4_), channel_id=1, source_target_pairs={{0,2},{1,15},{2,4},{3,1},{4,6},{5,3},{6,8},{7,5},{8,10},{9,7},{10,... | collective-permute-start | bytes 1179656 | tf_op jit(solution)/shard_map/ppermute | solution.py:283
  32.8 9.0 %collective-permute-start.11 = (bf16[12,128,128]{2,1,0:T(8,128)(2,1)S(1)}, bf16[12,128,128]{2,1,0:T(8,128)(2,1)S(1)}, u32[]{:S(2)}, u32[]{:S(2)}) collective-permute-start(bf16[12,128,128]{2,1,0:T(8,128)(2,1)S(1)} %collective-permute-done.8.rest_6_), channel_id=1, source_target_pairs={{0,2},{1,15},{2,4},{3,1},{4,6},{5,3},{6,8},{7,5},{8,10},{9,7},{10,... | collective-permute-start | bytes 1179656 | tf_op jit(solution)/shard_map/ppermute | solution.py:283
  36.5 6.7 %collective-permute-start.6 = (bf16[12,128,128]{2,1,0:T(8,128)(2,1)S(1)}, bf16[12,128,128]{2,1,0:T(8,128)(2,1)S(1)}, u32[]{:S(2)}, u32[]{:S(2)}) collective-permute-start(bf16[12,128,128]{2,1,0:T(8,128)(2,1)S(1)} %collective-permute-done.5.rest_2_), channel_id=1, source_target_pairs={{0,1},{1,0},{2,3},{3,2},{4,5},{5,4},{6,7},{7,6},{8,9},{9,8},{10,11... | collective-permute-start | bytes 1179656 | tf_op jit(solution)/shard_map/ppermute | solution.py:293
  36.5 10.5 %collective-permute-start.7 = (bf16[12,128,128]{2,1,0:T(8,128)(2,1)S(1)}, bf16[12,128,128]{2,1,0:T(8,128)(2,1)S(1)}, u32[]{:S(2)}, u32[]{:S(2)}) collective-permute-start(bf16[12,128,128]{2,1,0:T(8,128)(2,1)S(1)} %collective-permute-done.1.rest_4_), channel_id=1, source_target_pairs={{0,1},{1,0},{2,3},{3,2},{4,5},{5,4},{6,7},{7,6},{8,9},{9,8},{10,11... | collective-permute-start | bytes 1179656 | tf_op jit(solution)/shard_map/ppermute | solution.py:293
  37.0 14.4 %collective-permute-start.9 = (bf16[12,128,128]{2,1,0:T(8,128)(2,1)S(1)}, bf16[12,128,128]{2,1,0:T(8,128)(2,1)S(1)}, u32[]{:S(2)}, u32[]{:S(2)}) collective-permute-start(bf16[12,128,128]{2,1,0:T(8,128)(2,1)S(1)} %collective-permute-done.8.rest_6_), channel_id=1, source_target_pairs={{0,1},{1,0},{2,3},{3,2},{4,5},{5,4},{6,7},{7,6},{8,9},{9,8},{10,11... | collective-permute-start | bytes 1179656 | tf_op jit(solution)/shard_map/ppermute | solution.py:293
  37.1 14.3 %collective-permute-start.10 = (bf16[12,128,128]{2,1,0:T(8,128)(2,1)S(1)}, bf16[12,128,128]{2,1,0:T(8,128)(2,1)S(1)}, u32[]{:S(2)}, u32[]{:S(2)}) collective-permute-start(bf16[12,128,128]{2,1,0:T(8,128)(2,1)S(1)} %collective-permute-done.2.rest_8_), channel_id=1, source_target_pairs={{0,1},{1,0},{2,3},{3,2},{4,5},{5,4},{6,7},{7,6},{8,9},{9,8},{10,11... | collective-permute-start | bytes 1179656 | tf_op jit(solution)/shard_map/ppermute | solution.py:293
  41.8 10.3 %collective-permute-start.12 = (bf16[12,128,128]{2,1,0:T(8,128)(2,1)S(1)}, bf16[12,128,128]{2,1,0:T(8,128)(2,1)}, u32[]{:S(2)}, u32[]{:S(2)}) collective-permute-start(bf16[12,128,128]{2,1,0:T(8,128)(2,1)S(1)} %collective-permute-done.11.rest_10_), channel_id=1, source_target_pairs={{0,1},{1,0},{2,3},{3,2},{4,5},{5,4},{6,7},{7,6},{8,9},{9,8},{10,11... | collective-permute-start | bytes 1179656 | tf_op jit(solution)/shard_map/ppermute | solution.py:293
  43.1 18.4 %collective-permute-start.3 = (bf16[12,128,128]{2,1,0:T(8,128)(2,1)S(1)}, bf16[12,128,128]{2,1,0:T(8,128)(2,1)}, u32[]{:S(2)}, u32[]{:S(2)}) collective-permute-start(bf16[12,128,128]{2,1,0:T(8,128)(2,1)S(1)} %collective-permute-done.2.rest_8_), channel_id=1, source_target_pairs={{0,2},{1,15},{2,4},{3,1},{4,6},{5,3},{6,8},{7,5},{8,10},{9,7},{10,... | collective-permute-start | bytes 1179656 | tf_op jit(solution)/shard_map/ppermute | solution.py:283
  46.9 14.8 %collective-permute-start.14 = (bf16[12,128,128]{2,1,0:T(8,128)(2,1)S(1)}, bf16[12,128,128]{2,1,0:T(8,128)(2,1)}, u32[]{:S(2)}, u32[]{:S(2)}) collective-permute-start(bf16[12,128,128]{2,1,0:T(8,128)(2,1)S(1)} %collective-permute-done.11.rest_10_), channel_id=1, source_target_pairs={{0,2},{1,15},{2,4},{3,1},{4,6},{5,3},{6,8},{7,5},{8,10},{9,7},{10,... | collective-permute-start | bytes 1179656 | tf_op jit(solution)/shard_map/ppermute | solution.py:283
  61.6 2.0 %collective-permute-start.13 = (bf16[12,128,128]{2,1,0:T(8,128)(2,1)}, bf16[12,128,128]{2,1,0:T(8,128)(2,1)S(1)}, u32[]{:S(2)}, u32[]{:S(2)}) collective-permute-start(bf16[12,128,128]{2,1,0:T(8,128)(2,1)} %collective-permute-done.3.rest_12_), channel_id=1, source_target_pairs={{0,1},{1,0},{2,3},{3,2},{4,5},{5,4},{6,7},{7,6},{8,9},{9,8},{10,11... | collective-permute-start | bytes 1179656 | tf_op jit(solution)/shard_map/ppermute | solution.py:293
  61.7 2.5 %collective-permute-start.15 = (bf16[12,128,128]{2,1,0:T(8,128)(2,1)}, bf16[12,128,128]{2,1,0:T(8,128)(2,1)S(1)}, u32[]{:S(2)}, u32[]{:S(2)}) collective-permute-start(bf16[12,128,128]{2,1,0:T(8,128)(2,1)} %collective-permute-done.14.rest_14_), channel_id=1, source_target_pairs={{0,1},{1,0},{2,3},{3,2},{4,5},{5,4},{6,7},{7,6},{8,9},{9,8},{10,11... | collective-permute-start | bytes 1179656 | tf_op jit(solution)/shard_map/ppermute | solution.py:293
  78.3 1.5 %collective-permute-start.16 = (f32[8,128]{1,0:T(8,128)}, f32[8,128]{1,0:T(8,128)S(1)}, u32[]{:S(2)}, u32[]{:S(2)}) collective-permute-start(f32[8,128]{1,0:T(8,128)} %get-tuple-element.22), channel_id=1, source_target_pairs={{0,1},{1,0},{2,3},{3,2},{4,5},{5,4},{6,7},{7,6},{8,9},{9,8},{10,11... | collective-permute-start | bytes 12296 | tf_op jit(solution)/shard_map/ppermute | solution.py:352
  80.5 3.6 %collective-permute-start.17 = (f32[8,128]{1,0:T(8,128)S(1)}, f32[8,128]{1,0:T(8,128)S(1)}, u32[]{:S(2)}, u32[]{:S(2)}) collective-permute-start(f32[8,128]{1,0:T(8,128)S(1)} %add.50), channel_id=1, source_target_pairs={{0,2},{1,3},{2,0},{3,1},{4,6},{5,7},{6,4},{7,5},{8,10},{9,11},{10,... | collective-permute-start | bytes 12296 | tf_op jit(solution)/shard_map/ppermute | solution.py:352
  84.1 4.5 %collective-permute-start.18 = (f32[8,128]{1,0:T(8,128)S(1)}, f32[8,128]{1,0:T(8,128)S(1)}, u32[]{:S(2)}, u32[]{:S(2)}) collective-permute-start(f32[8,128]{1,0:T(8,128)S(1)} %add.51), channel_id=1, source_target_pairs={{0,4},{1,5},{2,6},{3,7},{4,0},{5,1},{6,2},{7,3},{8,12},{9,13},{10,... | collective-permute-start | bytes 12296 | tf_op jit(solution)/shard_map/ppermute | solution.py:352
  88.6 7.5 %collective-permute-start.19 = (f32[8,128]{1,0:T(8,128)S(1)}, f32[8,128]{1,0:T(8,128)S(1)}, u32[]{:S(2)}, u32[]{:S(2)}) collective-permute-start(f32[8,128]{1,0:T(8,128)S(1)} %add.52), channel_id=1, source_target_pairs={{0,8},{1,9},{2,10},{3,11},{4,12},{5,13},{6,14},{7,15},{8,0},{9,1},... | collective-permute-start | bytes 12296 | tf_op jit(solution)/shard_map/ppermute | solution.py:352
  97.4 3.8 %collective-permute-start.20 = (f32[8,128]{1,0:T(8,128)S(1)}, f32[8,128]{1,0:T(8,128)S(1)}, u32[]{:S(2)}, u32[]{:S(2)}) collective-permute-start(f32[8,128]{1,0:T(8,128)S(1)} %broadcast_in_dim.27), channel_id=1, source_target_pairs={{0,16},{16,0},{32,48},{48,32},{64,80},{80,64},{96,112},{112,96},{1... | collective-permute-start | bytes 12296 | tf_op jit(solution)/shard_map/ppermute | solution.py:362
  101.2 5.1 %collective-permute-start.21 = (f32[8,128]{1,0:T(8,128)S(1)}, f32[8,128]{1,0:T(8,128)S(1)}, u32[]{:S(2)}, u32[]{:S(2)}) collective-permute-start(f32[8,128]{1,0:T(8,128)S(1)} %broadcast_add_fusion), channel_id=1, source_target_pairs={{0,32},{16,48},{32,0},{48,16},{64,96},{80,112},{96,64},{112,80},{1... | collective-permute-start | bytes 12296 | tf_op jit(solution)/shard_map/ppermute | solution.py:362
  106.4 5.8 %collective-permute-start.22 = (f32[8,128]{1,0:T(8,128)S(1)}, f32[8,128]{1,0:T(8,128)S(1)}, u32[]{:S(2)}, u32[]{:S(2)}) collective-permute-start(f32[8,128]{1,0:T(8,128)S(1)} %fusion.3), channel_id=1, source_target_pairs={{0,64},{16,80},{32,96},{48,112},{64,0},{80,16},{96,32},{112,48},{1... | collective-permute-start | bytes 12296 | tf_op jit(solution)/shard_map/ppermute | solution.py:362
  112.1 7.1 %collective-permute-start.23 = (f32[8,128]{1,0:T(8,128)S(1)}, f32[8,128]{1,0:T(8,128)S(1)}, u32[]{:S(2)}, u32[]{:S(2)}) collective-permute-start(f32[8,128]{1,0:T(8,128)S(1)} %add.60), channel_id=1, source_target_pairs={{0,128},{16,144},{32,160},{48,176},{64,192},{80,208},{96,224},{112... | collective-permute-start | bytes 12296 | tf_op jit(solution)/shard_map/ppermute | solution.py:362
  (15 other events, 231.5 us)

commit v3 on v2

--- a/solution.py
+++ b/solution.py
@@ -1,6 +1,7 @@
+import functools
+
 import jax
 import jax.numpy as jnp
-import numpy as np
 from jax import lax
 from jax.experimental import pallas as pl
 from jax.experimental.pallas import tpu as pltpu
@@ -12,7 +13,7 @@
 
 LOCAL = 4
 BLOCKS = 16
-EARLY = 12
+LATE = range(8, 12)
 VMEM_LIMIT = 60 * 2**20
 
 
@@ -103,6 +104,19 @@
     return total
 
 
+def slot_of(charge_ref, q):
+    sector = lax.axis_index("sec")
+    left = (sector - charge_ref[q]) & 15
+    core = sector & 1
+    ahead = (sector >> 1) - (left >> 1)
+    hops = jnp.where(core == 0, ahead, -ahead) & 7
+    return 2 * hops + ((left ^ sector) & 1)
+
+
+def is_late(slot):
+    return jnp.logical_and(slot >= LATE.start, slot < LATE.stop)
+
+
 def masked_step(keep, psi_ref, u_ref, sq_ref, lenv_ref, slot, x3_ref, q):
     h = contract(lenv_ref, slot, x3_ref, q)
     u = jnp.where(keep, psi_ref[q].astype(F32) - 0.5 * h, 0.0)
@@ -110,86 +124,102 @@
     sq_ref[...] += u * u
 
 
-def mid_kernel(slot_ref, rank_ref, psi_any, x3_any, *rest):
-    blocks = rest[:EARLY]
-    u_ref, sq_ref, psi_ref, lenv_ref, x3_ref, sem_ref, x3_sem = rest[EARLY:]
+def mid_kernel(charge_ref, rank_ref, psi_any, x3_any, *rest):
+    early = [i for i in range(BLOCKS) if i not in LATE]
+    blocks = rest[: len(early)]
+    u_ref, sq_ref, psi_ref, lenv_ref, x3_ref, sem_ref, x3_sem = rest[len(early) :]
     pairs, width = psi_ref.shape[0], psi_ref.shape[2]
-    copies = [pltpu.make_async_copy(blocks[i], lenv_ref.at[i], sem_ref.at[i]) for i in range(EARLY)]
-    copies.append(pltpu.make_async_copy(psi_any, psi_ref, sem_ref.at[EARLY]))
+    copies = [pltpu.make_async_copy(b, lenv_ref.at[i], sem_ref.at[i]) for i, b in zip(early, blocks)]
+    copies.append(pltpu.make_async_copy(psi_any, psi_ref, sem_ref.at[BLOCKS]))
     for copy in copies:
         copy.start()
+    slots = [slot_of(charge_ref, q) for q in range(pairs)]
     loads = [pltpu.make_async_copy(x3_any.at[q], x3_ref.at[q], x3_sem.at[q]) for q in range(pairs)]
     for q in range(pairs):
-        pl.when(slot_ref[q] < EARLY)(loads[q].start)
+        pl.when(jnp.logical_not(is_late(slots[q])))(loads[q].start)
     keep = iota((width, width), 1) < rank_ref[0]
     sq_ref[...] = jnp.zeros_like(sq_ref)
     for copy in copies:
         copy.wait()
     for q in range(pairs):
 
-        @pl.when(slot_ref[q] < EARLY)
+        @pl.when(jnp.logical_not(is_late(slots[q])))
         def _():
             loads[q].wait()
-            masked_step(keep, psi_ref, u_ref, sq_ref, lenv_ref, slot_ref[q], x3_ref, q)
-
-        @pl.when(slot_ref[q] >= EARLY)
+            masked_step(keep, psi_ref, u_ref, sq_ref, lenv_ref, slots[q], x3_ref, q)
+
+        @pl.when(is_late(slots[q]))
         def _():
             u_ref[q] = jnp.zeros((width, width), BF16)
 
 
-def back_kernel(slot_ref, rank_ref, psi_any, renv_any, mpo_ref, x3_any, early_u, early_sq, *rest):
+def back_kernel(charge_ref, rank_ref, psi_any, renv_any, mpo_ref, x3_any, early_u, early_sq, *rest):
     blocks = rest[:BLOCKS]
     v_any, stat_ref, lenv_ref, x3_ref, u_ref, xt_ref, psi_ref, renv_ref, v_ref, sq_ref = rest[BLOCKS:-3]
     sem_ref, x3_sem, v_sem = rest[-3:]
     pairs, width = psi_ref.shape[0], psi_ref.shape[2]
     copies = [pltpu.make_async_copy(blocks[i], lenv_ref.at[i], sem_ref.at[i]) for i in range(BLOCKS)]
-    first = copies[EARLY:] + [
+    first = [copies[i] for i in LATE] + [
         pltpu.make_async_copy(psi_any, psi_ref, sem_ref.at[BLOCKS]),
         pltpu.make_async_copy(early_u, u_ref, sem_ref.at[BLOCKS + 1]),
     ]
     later = pltpu.make_async_copy(renv_any, renv_ref, sem_ref.at[BLOCKS + 2])
+    last = [copies[i] for i in range(BLOCKS) if i not in LATE]
+    slots = [slot_of(charge_ref, q) for q in range(pairs)]
     loads = [pltpu.make_async_copy(x3_any.at[q], x3_ref.at[q], x3_sem.at[q]) for q in range(pairs)]
     for copy in first:
         copy.start()
     for q in range(pairs):
-        pl.when(slot_ref[q] >= EARLY)(loads[q].start)
+        pl.when(is_late(slots[q]))(loads[q].start)
     later.start()
-    for copy in copies[:EARLY]:
-        copy.start()
     keep = iota((width, width), 1) < rank_ref[0]
     sq_ref[...] = early_sq[...]
     for copy in first:
         copy.wait()
+    for copy in last:
+        copy.start()
     for q in range(pairs):
 
-        @pl.when(slot_ref[q] >= EARLY)
+        @pl.when(is_late(slots[q]))
         def _():
             loads[q].wait()
-            masked_step(keep, psi_ref, u_ref, sq_ref, lenv_ref, slot_ref[q], x3_ref, q)
+            masked_step(keep, psi_ref, u_ref, sq_ref, lenv_ref, slots[q], x3_ref, q)
 
     turn(u_ref, xt_ref)
     later.wait()
     spread(xt_ref, renv_ref, mpo_ref[...], x3_ref)
-    for copy in copies[:EARLY]:
+    for copy in last:
         copy.wait()
     zero = jnp.zeros((width, width), F32)
     sq, inner, own = zero, zero, zero
     sent = []
     for q in range(pairs):
-        h = contract(lenv_ref, slot_ref[q], x3_ref, q)
+        h = contract(lenv_ref, slots[q], x3_ref, q)
         x = u_ref[q].astype(F32)
         v = jnp.where(keep, x - 0.5 * h, 0.0)
         v_ref[q] = v
         sent.append(pltpu.make_async_copy(v_ref.at[q], v_any.at[q], v_sem.at[q]))
         sent[-1].start()
         sq, inner, own = sq + v * v, inner + x * h, own + x * x
+    for i, part in enumerate((sq_ref[...], sq, inner, own)):
+        stat_ref[i : i + 1] = jnp.sum(part, axis=0, keepdims=True)
+    for copy in sent:
+        copy.wait()
+
+
+def settle_kernel(count, total_ref, mine_ref, twin_ref, share_ref, out_ref):
+    width = total_ref.shape[1]
+    first_sq, sq, inner, own = [jnp.sum(total_ref[i : i + 1], axis=1, keepdims=True) for i in range(4)]
+    one = lax.rsqrt(first_sq / count + 1e-06)
+    scale = one * lax.rsqrt(one * one * sq / count + 1e-06)
     row = iota((8, width), 0)
-    stat = jnp.zeros((8, width), F32)
-    for i, part in enumerate((sq_ref[...], sq, inner, own)):
-        stat = jnp.where(row == i, jnp.sum(part), stat)
-    stat_ref[...] = stat
-    for copy in sent:
-        copy.wait()
+    out_ref[...] = jnp.where(row == 0, scale, inner / own)
+    mine = jnp.sum(mine_ref[1:2], axis=1, keepdims=True)
+    twin = jnp.sum(twin_ref[1:2], axis=1, keepdims=True)
+    row = iota((2, width), 0)
+    here = jnp.where(row == (lax.axis_index("sec") & 1), mine, twin)
+    share = jnp.log(float(lax.axis_size("sec")) * here / sq)
+    share_ref[...] = jnp.where(iota((2, width), 1) == lax.axis_index("seg"), share, 0.0)
 
 
 VMEM_SPEC = pl.BlockSpec(memory_space=pltpu.VMEM)
@@ -232,7 +262,7 @@
     )(psi, renv, left, right)
 
 
-def mid(slot, rank, psi, x3, blocks):
+def mid(charge, rank, psi, x3, blocks):
     pairs, width = psi.shape[0], psi.shape[2]
     bonds = x3.shape[1]
     return call(
@@ -240,26 +270,26 @@
         "mid",
         10**9,
         (jax.ShapeDtypeStruct((pairs, width, width), BF16), jax.ShapeDtypeStruct((width, width), F32)),
-        [SMEM_SPEC, SMEM_SPEC, ANY_SPEC, ANY_SPEC] + [ANY_SPEC] * EARLY,
+        [SMEM_SPEC, SMEM_SPEC, ANY_SPEC, ANY_SPEC] + [ANY_SPEC] * len(blocks),
         (VMEM_SPEC, VMEM_SPEC),
         [
             pltpu.VMEM((pairs, width, width), BF16),
-            pltpu.VMEM((EARLY, bonds, width, width), BF16),
+            pltpu.VMEM((BLOCKS, bonds, width, width), BF16),
             pltpu.VMEM((pairs, bonds, width, width), BF16),
-            pltpu.SemaphoreType.DMA((EARLY + 1,)),
+            pltpu.SemaphoreType.DMA((BLOCKS + 1,)),
             pltpu.SemaphoreType.DMA((pairs,)),
         ],
-    )(slot, rank, psi, x3, *blocks)
-
-
-def back(slot, rank, psi, renv, mpo, x3, early_u, early_sq, blocks):
+    )(charge, rank, psi, x3, *blocks)
+
+
+def back(charge, rank, psi, renv, mpo, x3, early_u, early_sq, blocks):
     pairs, width = psi.shape[0], psi.shape[2]
     bonds = renv.shape[0]
     return call(
         back_kernel,
         "back",
         3 * 10**9,
-        (jax.ShapeDtypeStruct((pairs, width, width), F32), jax.ShapeDtypeStruct((8, width), F32)),
+        (jax.ShapeDtypeStruct((pairs, width, width), F32), jax.ShapeDtypeStruct((4, width), F32)),
         [SMEM_SPEC, SMEM_SPEC, ANY_SPEC, ANY_SPEC, VMEM_SPEC, ANY_SPEC, ANY_SPEC, VMEM_SPEC] + [ANY_SPEC] * BLOCKS,
         (ANY_SPEC, VMEM_SPEC),
         [
@@ -275,7 +305,26 @@
             pltpu.SemaphoreType.DMA((pairs,)),
             pltpu.SemaphoreType.DMA((pairs,)),
         ],
-    )(slot, rank, psi, renv, mpo, x3, early_u, early_sq, *blocks)
+    )(charge, rank, psi, renv, mpo, x3, early_u, early_sq, *blocks)
+
+
+def settle(total, mine, twin_stat, count):
+    width = total.shape[1]
+    return call(
+        functools.partial(settle_kernel, count),
+        "settle",
+        10**4,
+        (jax.ShapeDtypeStruct((2, width), F32), jax.ShapeDtypeStruct((8, width), F32)),
+        [VMEM_SPEC] * 3,
+        (VMEM_SPEC, VMEM_SPEC),
+        [],
+    )(total, mine, twin_stat)
+
+
+def partner(value, bits):
+    axes = ("seg", "sec")
+    n = lax.axis_size(axes)
+    return lax.ppermute(value, axes, [(i, i ^ bits) for i in range(n)])
 
 
 def hop(value):
@@ -300,7 +349,6 @@
 
 def shards(psi, env_build, env_right, site_left, site_right, charge, rank):
     nsec = lax.axis_size("sec")
-    nseg = lax.axis_size("seg")
     sector = lax.axis_index("sec")
     segment = lax.axis_index("seg")
     x = psi[0, 0]
@@ -317,52 +365,28 @@
     moved, x3 = lax.optimization_barrier((moved, x3))
     own = jnp.where(segment == 0, env, moved)
 
-    chips = nsec // 2
-    held = np.zeros((nsec, nsec), np.int32)
-    for s in range(nsec):
-        z, c = s // 2, s % 2
-        sign = 1 - 2 * c
-        order = [s, s ^ 1]
-        for k in range(1, chips // 2 + 1):
-            behind, ahead = (z - sign * k) % chips, (z + sign * k) % chips
-            t_pair = [2 * behind + 1 - c, 2 * ahead + c] if k < chips // 2 else []
-            o_pair = [2 * behind + c, 2 * ahead + 1 - c]
-            order += o_pair + t_pair
-        for i, left in enumerate(order):
-            held[s, left] = i
-    row = lax.dynamic_index_in_dim(jnp.asarray(held), sector, 0, keepdims=False)
-    left = (sector - charge) % nsec
-    hits = left[:, None] == jnp.arange(nsec, dtype=jnp.int32)[None, :]
-    slot = jnp.sum(jnp.where(hits, row[None, :], 0), axis=1).astype(jnp.int32)
-
-    o1, t1 = hop(own), cross_hop(own)
-    o2, t2 = hop(o1), hop(t1)
-    o3, t3 = hop(o2), hop(t2)
+    o1, t1 = lax.optimization_barrier((hop(own), cross_hop(own)))
+    o2, t2 = lax.optimization_barrier((hop(o1), hop(t1)))
+    o3, t3 = lax.optimization_barrier((hop(o2), hop(t2)))
     o4 = hop(o3)
-    blocks = [own, twin(own), o1, twin(o1), t1, twin(t1), o2, twin(o2), t2, twin(t2), o3, twin(o3)]
-    early_u, early_sq = mid(slot, rank, x, x3, blocks)
-    t3, early_u = lax.optimization_barrier((t3, early_u))
-    blocks += [t3, twin(t3), o4, twin(o4)]
-
-    v, stat = back(slot, rank, x, renv, mpo, x3, early_u, early_sq, blocks)
-
-    mine = stat[1, 0]
-    total = stat
-    for bit in (1, 2, 4, 8):
-        total = total + lax.ppermute(total, "sec", [(i, i ^ bit) for i in range(nsec)])
-    scale_one = lax.rsqrt(total[0, 0] / count + 1e-06)
-    energy = total[2, 0] / total[3, 0]
-    second = (scale_one * scale_one) * total[1, 0]
-    scale = scale_one * lax.rsqrt(second / count + 1e-06)
-    state = (v * scale).astype(BF16)
-    share = jnp.log(float(nsec) * mine / total[1, 0])
-    upto = jnp.full((8, width), share, F32)
-    whole = upto
-    for bit in (1, 2, 4, 8):
-        got = lax.ppermute(whole, "seg", [(i, i ^ bit) for i in range(nseg)])
-        upto = jnp.where((segment & bit) != 0, upto + got, upto)
-        whole = whole + got
-    return state[None, None], energy.reshape(1), upto[0, 0].reshape(1, 1)
+    near = [own, twin(own), o1, t1, o2, t2, o3, t3]
+    far = [twin(t2), twin(o2), twin(t1), twin(o1)]
+    early_u, early_sq = mid(charge, rank, x, x3, near + far)
+    o4, early_u = lax.optimization_barrier((o4, early_u))
+    blocks = near + [o4, twin(o4), twin(t3), twin(o3)] + far
+    v, stat = back(charge, rank, x, renv, mpo, x3, early_u, early_sq, blocks)
+
+    twin_stat = partner(stat, 1)
+    total = stat + twin_stat
+    for bits in (3, 5, 13):
+        total = total + partner(total, bits)
+    share, out = settle(total, stat, twin_stat, count)
+    state = (v * out[0, 0]).astype(BF16)
+    for bits in (1, 3, 4, 12):
+        share = share + partner(share, nsec * bits + 1)
+    wanted = (iota(share.shape, 0) == sector % 2) & (iota(share.shape, 1) <= segment)
+    weight = jnp.sum(jnp.where(wanted, share, 0.0))
+    return state[None, None], out[1:2, 0], weight.reshape(1, 1)
 
 
 def solution(mesh):

time: 122 us -> 121 us (level)
  the two profiles are of different devices: /device:TPU:64 before, /device:TPU:1 now
where the time goes in v3:
time: 121 us
  starting transfers between devices  44.7 us (37%)
  waiting for transfers between devices  34.5 us (29%)
  Pallas kernels  32 us (26%)
  other arithmetic  5.42 us (4%)
  local copies, waits for them, and re-layouts  2.85 us (2%)
  between operations  1.5 us (1%)
    ppermute x8, starting transfers between devices, partner(): return lax.ppermute(value, axes, [(i, i ^ bits) for i in range(n)])  18.9 us
    ppermute x6, waiting for transfers between devices, hop(): lax.ppermute(value, 'sec', [(i, (i + (2 if i % 2 == 0 else -2)) % n) for...  17 us
    pallas_call x1, Pallas kernels, back(): call(back_kernel, 'back', 3 * 10 ** 9, (jax.ShapeDtypeStruct((pairs, widt...  13.8 us
    ppermute x8, waiting for transfers between devices, partner(): return lax.ppermute(value, axes, [(i, i ^ bits) for i in range(n)])  10.6 us
    ppermute x6, starting transfers between devices, hop(): lax.ppermute(value, 'sec', [(i, (i + (2 if i % 2 == 0 else -2)) % n) for...  10.2 us
    ppermute x8, starting transfers between devices, twin(): return lax.ppermute(value, 'sec', [(i, i ^ 1) for i in range(n)])  8.97 us
    pallas_call x1, Pallas kernels, front(): call(front_kernel, 'front', 2 * 10 ** 9, (jax.ShapeDtypeStruct((pairs, bo...  8.88 us
    pallas_call x1, Pallas kernels, mid(): call(mid_kernel, 'mid', 10 ** 9, (jax.ShapeDtypeStruct((pairs, width, wid...  7.97 us
  transfers between devices with their start and end apart: 24, of which 13 were waited for; matrix products, arithmetic and copies ran while one was open for 3% of the time, Pallas kernels for 14%

profile of v3, /device:TPU:1, one launch (start us, length us, event | category | flops | bytes accessed | tf_op | source)
XLA Modules:
  0.0 121.0 jit_solution(12275205530172106709)
XLA Ops:
  0.6 4.1 %collective-permute-start = (bf16[12,128,128]{2,1,0:T(8,128)(2,1)}, bf16[12,128,128]{2,1,0:T(8,128)(2,1)S(1)}, u32[]{:S(2)}, u32[]{:S(2)}) collective-permute-start(bf16[12,128,128]{2,1,0:T(8,128)(2,1)} %bitcast.20), channel_id=1, source_target_pairs={{0,16},{16,32},{32,48},{48,64},{64,80},{80,96},{96,112},{112,128},... | collective-permute-start | bytes 1179656 | tf_op jit(solution)/shard_map/ppermute | solution.py:347
  4.8 8.9 %front.1 = (bf16[16,12,128,128]{3,2,1,0:T(8,128)(2,1)}, bf16[192,192]{1,0:T(8,128)(2,1)}) custom-call(bf16[16,128,128]{2,1,0:T(8,128)(2,1)} %bitcast.15, bf16[12,128,128]{2,1,0:T(8,128)(2,1)} %bitcast.18, bf16[192,12]{1,0:T(8,128)(2,1)} %bitcast.21, bf16[192,12]{1,0:T(8,128)(2,1)} %bitcast.22), custom_call_target="tpu_custom_call" | custom-call | flops 2000000000 | bytes 8000000 | tf_op jit(solution)/shard_map/front/pallas_call | solution.py:247
  13.7 2.6 %collective-permute-start.2 = (bf16[12,128,128]{2,1,0:T(8,128)(2,1)S(1)}, bf16[12,128,128]{2,1,0:T(8,128)(2,1)S(1)}, u32[]{:S(2)}, u32[]{:S(2)}) collective-permute-start(bf16[12,128,128]{2,1,0:T(8,128)(2,1)S(1)} %broadcast_select_fusion.rest_0_), channel_id=1, source_target_pairs={{0,15},{1,2},{2,1},{3,4},{4,3},{5,6},{6,5},{7,8},{8,7},{9,10},{10,... | collective-permute-start | bytes 1179656 | tf_op jit(solution)/shard_map/ppermute | solution.py:337
  16.3 3.2 %collective-permute-start.1 = (bf16[12,128,128]{2,1,0:T(8,128)(2,1)S(1)}, bf16[12,128,128]{2,1,0:T(8,128)(2,1)S(1)}, u32[]{:S(2)}, u32[]{:S(2)}) collective-permute-start(bf16[12,128,128]{2,1,0:T(8,128)(2,1)S(1)} %broadcast_select_fusion.rest_0_), channel_id=1, source_target_pairs={{0,2},{1,15},{2,4},{3,1},{4,6},{5,3},{6,8},{7,5},{8,10},{9,7},{10,... | collective-permute-start | bytes 1179656 | tf_op jit(solution)/shard_map/ppermute | solution.py:332
  19.5 5.4 %collective-permute-done.2.rest_3_ = bf16[12,128,128]{2,1,0:T(8,128)(2,1)S(1)} collective-permute-done((bf16[12,128,128]{2,1,0:T(8,128)(2,1)S(1)}, bf16[12,128,128]{2,1,0:T(8,128)(2,1)S(1)}, u32[]{:S(2)}, u32[]{:S(2)}) %collective-permute-start.2) | collective-permute-done | bytes 393248 | tf_op jit(solution)/shard_map/ppermute | solution.py:337
  24.9 3.1 %collective-permute-done.1.rest_2_ = bf16[12,128,128]{2,1,0:T(8,128)(2,1)S(1)} collective-permute-done((bf16[12,128,128]{2,1,0:T(8,128)(2,1)S(1)}, bf16[12,128,128]{2,1,0:T(8,128)(2,1)S(1)}, u32[]{:S(2)}, u32[]{:S(2)}) %collective-permute-start.1) | collective-permute-done | bytes 393248 | tf_op jit(solution)/shard_map/ppermute | solution.py:332
  28.0 3.6 %collective-permute-start.3 = (bf16[12,128,128]{2,1,0:T(8,128)(2,1)S(1)}, bf16[12,128,128]{2,1,0:T(8,128)(2,1)S(1)}, u32[]{:S(2)}, u32[]{:S(2)}) collective-permute-start(bf16[12,128,128]{2,1,0:T(8,128)(2,1)S(1)} %collective-permute-done.1.rest_2_), channel_id=1, source_target_pairs={{0,2},{1,15},{2,4},{3,1},{4,6},{5,3},{6,8},{7,5},{8,10},{9,7},{10,... | collective-permute-start | bytes 1179656 | tf_op jit(solution)/shard_map/ppermute | solution.py:332
  31.8 4.5 %collective-permute-done.3.rest_4_ = bf16[12,128,128]{2,1,0:T(8,128)(2,1)S(1)} collective-permute-done((bf16[12,128,128]{2,1,0:T(8,128)(2,1)S(1)}, bf16[12,128,128]{2,1,0:T(8,128)(2,1)S(1)}, u32[]{:S(2)}, u32[]{:S(2)}) %collective-permute-start.3) | collective-permute-done | bytes 393248 | tf_op jit(solution)/shard_map/ppermute | solution.py:332
  36.3 4.2 %collective-permute-done.4.rest_5_ = bf16[12,128,128]{2,1,0:T(8,128)(2,1)S(1)} collective-permute-done((bf16[12,128,128]{2,1,0:T(8,128)(2,1)S(1)}, bf16[12,128,128]{2,1,0:T(8,128)(2,1)S(1)}, u32[]{:S(2)}, u32[]{:S(2)}) %collective-permute-start.4) | collective-permute-done | bytes 393248 | tf_op jit(solution)/shard_map/ppermute | solution.py:332
  40.6 3.1 %collective-permute-start.5 = (bf16[12,128,128]{2,1,0:T(8,128)(2,1)S(1)}, bf16[12,128,128]{2,1,0:T(8,128)(2,1)S(1)}, u32[]{:S(2)}, u32[]{:S(2)}) collective-permute-start(bf16[12,128,128]{2,1,0:T(8,128)(2,1)S(1)} %collective-permute-done.3.rest_4_), channel_id=1, source_target_pairs={{0,2},{1,15},{2,4},{3,1},{4,6},{5,3},{6,8},{7,5},{8,10},{9,7},{10,... | collective-permute-start | bytes 1179656 | tf_op jit(solution)/shard_map/ppermute | solution.py:332
  44.2 4.2 %collective-permute-done.5.rest_6_ = bf16[12,128,128]{2,1,0:T(8,128)(2,1)S(1)} collective-permute-done((bf16[12,128,128]{2,1,0:T(8,128)(2,1)S(1)}, bf16[12,128,128]{2,1,0:T(8,128)(2,1)S(1)}, u32[]{:S(2)}, u32[]{:S(2)}) %collective-permute-start.5) | collective-permute-done | bytes 393248 | tf_op jit(solution)/shard_map/ppermute | solution.py:332
  48.4 3.3 %collective-permute-start.10 = (bf16[12,128,128]{2,1,0:T(8,128)(2,1)S(1)}, bf16[12,128,128]{2,1,0:T(8,128)(2,1)S(1)}, u32[]{:S(2)}, u32[]{:S(2)}) collective-permute-start(bf16[12,128,128]{2,1,0:T(8,128)(2,1)S(1)} %collective-permute-done.3.rest_4_), channel_id=1, source_target_pairs={{0,1},{1,0},{2,3},{3,2},{4,5},{5,4},{6,7},{7,6},{8,9},{9,8},{10,11... | collective-permute-start | bytes 1179656 | tf_op jit(solution)/shard_map/ppermute | solution.py:342
  52.6 3.3 %collective-permute-start.9 = (bf16[12,128,128]{2,1,0:T(8,128)(2,1)S(1)}, bf16[12,128,128]{2,1,0:T(8,128)(2,1)}, u32[]{:S(2)}, u32[]{:S(2)}) collective-permute-start(bf16[12,128,128]{2,1,0:T(8,128)(2,1)S(1)} %collective-permute-done.4.rest_5_), channel_id=1, source_target_pairs={{0,1},{1,0},{2,3},{3,2},{4,5},{5,4},{6,7},{7,6},{8,9},{9,8},{10,11... | collective-permute-start | bytes 1179656 | tf_op jit(solution)/shard_map/ppermute | solution.py:342
  58.0 8.0 %mid.1 = (bf16[16,128,128]{2,1,0:T(8,128)(2,1)}, f32[128,128]{1,0:T(8,128)}) custom-call(s32[16]{0:T(128)} %charge_ref.3, s32[1]{0:T(128)S(6)} %copy.10.rank_ref, bf16[16,128,128]{2,1,0:T(8,128)(2,1)} %bitcast.16, bf16[16,12,128,128]{3,2,1,0:T(8,128)(2,1)} %get-tuple-element.23.x3_any, bf16[12,128,128]{2,1,0:T(8,128)(2,1)} %copy-done, ...), custom_call_target="tpu_custom_call" | custom-call | flops 1000000000 | bytes 8000000 | tf_op jit(solution)/shard_map/mid/pallas_call | solution.py:268
  67.3 1.6 %collective-permute-done.13.rest_9_ = bf16[12,128,128]{2,1,0:T(8,128)(2,1)S(1)} collective-permute-done((bf16[12,128,128]{2,1,0:T(8,128)(2,1)}, bf16[12,128,128]{2,1,0:T(8,128)(2,1)S(1)}, u32[]{:S(2)}, u32[]{:S(2)}) %collective-permute-start.13) | collective-permute-done | bytes 393248 | tf_op jit(solution)/shard_map/ppermute | solution.py:342
  69.7 13.8 %back.1 = (f32[16,128,128]{2,1,0:T(8,128)}, f32[4,128]{1,0:T(4,128)}) custom-call(s32[16]{0:T(128)} %charge_ref.3, s32[1]{0:T(128)S(6)} %copy.10.rank_ref, bf16[16,128,128]{2,1,0:T(8,128)(2,1)} %bitcast.17, bf16[12,128,128]{2,1,0:T(8,128)(2,1)} %bitcast.19, bf16[192,192]{1,0:T(8,128)(2,1)} %get-tuple-element.21.mpo_ref, ...), custom_call_target="tpu_custom_call" | custom-call | flops 3000000000 | bytes 8000000 | tf_op jit(solution)/shard_map/back/pallas_call | solution.py:288
  85.4 1.5 %collective-permute-start.17 = (f32[4,128]{1,0:T(4,128)S(1)}, f32[4,128]{1,0:T(4,128)S(1)}, u32[]{:S(2)}, u32[]{:S(2)}) collective-permute-start(f32[4,128]{1,0:T(4,128)S(1)} %add.28), channel_id=1, source_target_pairs={{0,3},{1,2},{2,1},{3,0},{4,7},{5,6},{6,5},{7,4},{8,11},{9,10},{10,... | collective-permute-start | bytes 6152 | tf_op jit(solution)/shard_map/ppermute | solution.py:327
  88.4 4.2 %collective-permute-start.18 = (f32[4,128]{1,0:T(4,128)S(1)}, f32[4,128]{1,0:T(4,128)S(1)}, u32[]{:S(2)}, u32[]{:S(2)}) collective-permute-start(f32[4,128]{1,0:T(4,128)S(1)} %add.29), channel_id=1, source_target_pairs={{0,5},{1,4},{2,7},{3,6},{4,1},{5,0},{6,3},{7,2},{8,13},{9,12},{10,... | collective-permute-start | bytes 6152 | tf_op jit(solution)/shard_map/ppermute | solution.py:327
  95.2 3.9 %collective-permute-done.19 = f32[4,128]{1,0:T(4,128)S(1)} collective-permute-done((f32[4,128]{1,0:T(4,128)S(1)}, f32[4,128]{1,0:T(4,128)S(1)}, u32[]{:S(2)}, u32[]{:S(2)}) %collective-permute-start.19) | collective-permute-done | bytes 2080 | tf_op jit(solution)/shard_map/ppermute | solution.py:327
  101.0 1.9 %collective-permute-start.20 = (f32[2,128]{1,0:T(2,128)}, f32[2,128]{1,0:T(2,128)S(1)}, u32[]{:S(2)}, u32[]{:S(2)}) collective-permute-start(f32[2,128]{1,0:T(2,128)} %get-tuple-element.38), channel_id=1, source_target_pairs={{0,17},{1,16},{2,19},{3,18},{4,21},{5,20},{6,23},{7,22},{8,25},{9,... | collective-permute-start | bytes 3080 | tf_op jit(solution)/shard_map/ppermute | solution.py:327
  105.0 3.0 %collective-permute-start.21 = (f32[2,128]{1,0:T(2,128)S(1)}, f32[2,128]{1,0:T(2,128)S(1)}, u32[]{:S(2)}, u32[]{:S(2)}) collective-permute-start(f32[2,128]{1,0:T(2,128)S(1)} %add.33), channel_id=1, source_target_pairs={{0,49},{1,48},{2,51},{3,50},{4,53},{5,52},{6,55},{7,54},{8,57},{9,... | collective-permute-start | bytes 3080 | tf_op jit(solution)/shard_map/ppermute | solution.py:327
  109.3 3.9 %collective-permute-start.22 = (f32[2,128]{1,0:T(2,128)S(1)}, f32[2,128]{1,0:T(2,128)S(1)}, u32[]{:S(2)}, u32[]{:S(2)}) collective-permute-start(f32[2,128]{1,0:T(2,128)S(1)} %add.34), channel_id=1, source_target_pairs={{0,65},{1,64},{2,67},{3,66},{4,69},{5,68},{6,71},{7,70},{8,73},{9,... | collective-permute-start | bytes 3080 | tf_op jit(solution)/shard_map/ppermute | solution.py:327
  114.4 3.1 %collective-permute-start.23 = (f32[2,128]{1,0:T(2,128)S(1)}, f32[2,128]{1,0:T(2,128)S(1)}, u32[]{:S(2)}, u32[]{:S(2)}) collective-permute-start(f32[2,128]{1,0:T(2,128)S(1)} %add.35), channel_id=1, source_target_pairs={{0,193},{1,192},{2,195},{3,194},{4,197},{5,196},{6,199},{7,198},{8... | collective-permute-start | bytes 3080 | tf_op jit(solution)/shard_map/ppermute | solution.py:327
  117.6 2.8 %fusion = bf16[1,1,16,128,128]{4,3,2,1,0:T(8,128)(2,1)} fusion(f32[16,128,128]{2,1,0:T(8,128)} %get-tuple-element.35, f32[]{:T(128)} %bitcast.7), kind=kLoop, calls=%fused_computation.1 | loop fusion | flops 524288 | bytes 1572868 | tf_op jit(solution)/shard_map/broadcast_in_dim | solution.py:389
  (69 shorter events, 18.5 us)
Async XLA Ops:
  0.6 13.0 %collective-permute-start = (bf16[12,128,128]{2,1,0:T(8,128)(2,1)}, bf16[12,128,128]{2,1,0:T(8,128)(2,1)S(1)}, u32[]{:S(2)}, u32[]{:S(2)}) collective-permute-start(bf16[12,128,128]{2,1,0:T(8,128)(2,1)} %bitcast.20), channel_id=1, source_target_pairs={{0,16},{16,32},{32,48},{48,64},{64,80},{80,96},{96,112},{112,128},... | collective-permute-start | bytes 1179656 | tf_op jit(solution)/shard_map/ppermute | solution.py:347
  13.7 11.2 %collective-permute-start.2 = (bf16[12,128,128]{2,1,0:T(8,128)(2,1)S(1)}, bf16[12,128,128]{2,1,0:T(8,128)(2,1)S(1)}, u32[]{:S(2)}, u32[]{:S(2)}) collective-permute-start(bf16[12,128,128]{2,1,0:T(8,128)(2,1)S(1)} %broadcast_select_fusion.rest_0_), channel_id=1, source_target_pairs={{0,15},{1,2},{2,1},{3,4},{4,3},{5,6},{6,5},{7,8},{8,7},{9,10},{10,... | collective-permute-start | bytes 1179656 | tf_op jit(solution)/shard_map/ppermute | solution.py:337
  16.3 11.7 %collective-permute-start.1 = (bf16[12,128,128]{2,1,0:T(8,128)(2,1)S(1)}, bf16[12,128,128]{2,1,0:T(8,128)(2,1)S(1)}, u32[]{:S(2)}, u32[]{:S(2)}) collective-permute-start(bf16[12,128,128]{2,1,0:T(8,128)(2,1)S(1)} %broadcast_select_fusion.rest_0_), channel_id=1, source_target_pairs={{0,2},{1,15},{2,4},{3,1},{4,6},{5,3},{6,8},{7,5},{8,10},{9,7},{10,... | collective-permute-start | bytes 1179656 | tf_op jit(solution)/shard_map/ppermute | solution.py:332
  28.0 8.3 %collective-permute-start.3 = (bf16[12,128,128]{2,1,0:T(8,128)(2,1)S(1)}, bf16[12,128,128]{2,1,0:T(8,128)(2,1)S(1)}, u32[]{:S(2)}, u32[]{:S(2)}) collective-permute-start(bf16[12,128,128]{2,1,0:T(8,128)(2,1)S(1)} %collective-permute-done.1.rest_2_), channel_id=1, source_target_pairs={{0,2},{1,15},{2,4},{3,1},{4,6},{5,3},{6,8},{7,5},{8,10},{9,7},{10,... | collective-permute-start | bytes 1179656 | tf_op jit(solution)/shard_map/ppermute | solution.py:332
  31.6 8.9 %collective-permute-start.4 = (bf16[12,128,128]{2,1,0:T(8,128)(2,1)S(1)}, bf16[12,128,128]{2,1,0:T(8,128)(2,1)S(1)}, u32[]{:S(2)}, u32[]{:S(2)}) collective-permute-start(bf16[12,128,128]{2,1,0:T(8,128)(2,1)S(1)} %collective-permute-done.2.rest_3_), channel_id=1, source_target_pairs={{0,2},{1,15},{2,4},{3,1},{4,6},{5,3},{6,8},{7,5},{8,10},{9,7},{10,... | collective-permute-start | bytes 1179656 | tf_op jit(solution)/shard_map/ppermute | solution.py:332
  40.6 7.8 %collective-permute-start.5 = (bf16[12,128,128]{2,1,0:T(8,128)(2,1)S(1)}, bf16[12,128,128]{2,1,0:T(8,128)(2,1)S(1)}, u32[]{:S(2)}, u32[]{:S(2)}) collective-permute-start(bf16[12,128,128]{2,1,0:T(8,128)(2,1)S(1)} %collective-permute-done.3.rest_4_), channel_id=1, source_target_pairs={{0,2},{1,15},{2,4},{3,1},{4,6},{5,3},{6,8},{7,5},{8,10},{9,7},{10,... | collective-permute-start | bytes 1179656 | tf_op jit(solution)/shard_map/ppermute | solution.py:332
  43.7 8.9 %collective-permute-start.6 = (bf16[12,128,128]{2,1,0:T(8,128)(2,1)S(1)}, bf16[12,128,128]{2,1,0:T(8,128)(2,1)S(1)}, u32[]{:S(2)}, u32[]{:S(2)}) collective-permute-start(bf16[12,128,128]{2,1,0:T(8,128)(2,1)S(1)} %collective-permute-done.4.rest_5_), channel_id=1, source_target_pairs={{0,2},{1,15},{2,4},{3,1},{4,6},{5,3},{6,8},{7,5},{8,10},{9,7},{10,... | collective-permute-start | bytes 1179656 | tf_op jit(solution)/shard_map/ppermute | solution.py:332
  43.7 12.2 %collective-permute-start.8 = (bf16[12,128,128]{2,1,0:T(8,128)(2,1)S(1)}, bf16[12,128,128]{2,1,0:T(8,128)(2,1)S(1)}, u32[]{:S(2)}, u32[]{:S(2)}) collective-permute-start(bf16[12,128,128]{2,1,0:T(8,128)(2,1)S(1)} %broadcast_select_fusion.rest_0_), channel_id=1, source_target_pairs={{0,1},{1,0},{2,3},{3,2},{4,5},{5,4},{6,7},{7,6},{8,9},{9,8},{10,11... | collective-permute-start | bytes 1179656 | tf_op jit(solution)/shard_map/ppermute | solution.py:342
  43.7 12.8 %collective-permute-start.12 = (bf16[12,128,128]{2,1,0:T(8,128)(2,1)S(1)}, bf16[12,128,128]{2,1,0:T(8,128)(2,1)S(1)}, u32[]{:S(2)}, u32[]{:S(2)}) collective-permute-start(bf16[12,128,128]{2,1,0:T(8,128)(2,1)S(1)} %collective-permute-done.1.rest_2_), channel_id=1, source_target_pairs={{0,1},{1,0},{2,3},{3,2},{4,5},{5,4},{6,7},{7,6},{8,9},{9,8},{10,11... | collective-permute-start | bytes 1179656 | tf_op jit(solution)/shard_map/ppermute | solution.py:342
  44.2 12.6 %collective-permute-start.11 = (bf16[12,128,128]{2,1,0:T(8,128)(2,1)S(1)}, bf16[12,128,128]{2,1,0:T(8,128)(2,1)S(1)}, u32[]{:S(2)}, u32[]{:S(2)}) collective-permute-start(bf16[12,128,128]{2,1,0:T(8,128)(2,1)S(1)} %collective-permute-done.2.rest_3_), channel_id=1, source_target_pairs={{0,1},{1,0},{2,3},{3,2},{4,5},{5,4},{6,7},{7,6},{8,9},{9,8},{10,11... | collective-permute-start | bytes 1179656 | tf_op jit(solution)/shard_map/ppermute | solution.py:342
  48.4 8.8 %collective-permute-start.10 = (bf16[12,128,128]{2,1,0:T(8,128)(2,1)S(1)}, bf16[12,128,128]{2,1,0:T(8,128)(2,1)S(1)}, u32[]{:S(2)}, u32[]{:S(2)}) collective-permute-start(bf16[12,128,128]{2,1,0:T(8,128)(2,1)S(1)} %collective-permute-done.3.rest_4_), channel_id=1, source_target_pairs={{0,1},{1,0},{2,3},{3,2},{4,5},{5,4},{6,7},{7,6},{8,9},{9,8},{10,11... | collective-permute-start | bytes 1179656 | tf_op jit(solution)/shard_map/ppermute | solution.py:342
  52.6 5.3 %collective-permute-start.9 = (bf16[12,128,128]{2,1,0:T(8,128)(2,1)S(1)}, bf16[12,128,128]{2,1,0:T(8,128)(2,1)}, u32[]{:S(2)}, u32[]{:S(2)}) collective-permute-start(bf16[12,128,128]{2,1,0:T(8,128)(2,1)S(1)} %collective-permute-done.4.rest_5_), channel_id=1, source_target_pairs={{0,1},{1,0},{2,3},{3,2},{4,5},{5,4},{6,7},{7,6},{8,9},{9,8},{10,11... | collective-permute-start | bytes 1179656 | tf_op jit(solution)/shard_map/ppermute | solution.py:342
  55.9 10.1 %collective-permute-start.7 = (bf16[12,128,128]{2,1,0:T(8,128)(2,1)S(1)}, bf16[12,128,128]{2,1,0:T(8,128)(2,1)}, u32[]{:S(2)}, u32[]{:S(2)}) collective-permute-start(bf16[12,128,128]{2,1,0:T(8,128)(2,1)S(1)} %collective-permute-done.5.rest_6_), channel_id=1, source_target_pairs={{0,2},{1,15},{2,4},{3,1},{4,6},{5,3},{6,8},{7,5},{8,10},{9,7},{10,... | collective-permute-start | bytes 1179656 | tf_op jit(solution)/shard_map/ppermute | solution.py:332
  56.6 10.8 %collective-permute-start.15 = (bf16[12,128,128]{2,1,0:T(8,128)(2,1)S(1)}, bf16[12,128,128]{2,1,0:T(8,128)(2,1)}, u32[]{:S(2)}, u32[]{:S(2)}) collective-permute-start(bf16[12,128,128]{2,1,0:T(8,128)(2,1)S(1)} %collective-permute-done.5.rest_6_), channel_id=1, source_target_pairs={{0,1},{1,0},{2,3},{3,2},{4,5},{5,4},{6,7},{7,6},{8,9},{9,8},{10,11... | collective-permute-start | bytes 1179656 | tf_op jit(solution)/shard_map/ppermute | solution.py:342
  56.8 10.5 %collective-permute-start.14 = (bf16[12,128,128]{2,1,0:T(8,128)(2,1)S(1)}, bf16[12,128,128]{2,1,0:T(8,128)(2,1)}, u32[]{:S(2)}, u32[]{:S(2)}) collective-permute-start(bf16[12,128,128]{2,1,0:T(8,128)(2,1)S(1)} %collective-permute-done.6.rest_7_), channel_id=1, source_target_pairs={{0,1},{1,0},{2,3},{3,2},{4,5},{5,4},{6,7},{7,6},{8,9},{9,8},{10,11... | collective-permute-start | bytes 1179656 | tf_op jit(solution)/shard_map/ppermute | solution.py:342
  66.0 2.9 %collective-permute-start.13 = (bf16[12,128,128]{2,1,0:T(8,128)(2,1)}, bf16[12,128,128]{2,1,0:T(8,128)(2,1)S(1)}, u32[]{:S(2)}, u32[]{:S(2)}) collective-permute-start(bf16[12,128,128]{2,1,0:T(8,128)(2,1)} %collective-permute-done.7.rest_8_), channel_id=1, source_target_pairs={{0,1},{1,0},{2,3},{3,2},{4,5},{5,4},{6,7},{7,6},{8,9},{9,8},{10,11... | collective-permute-start | bytes 1179656 | tf_op jit(solution)/shard_map/ppermute | solution.py:342
  83.4 1.3 %collective-permute-start.16 = (f32[4,128]{1,0:T(4,128)}, f32[4,128]{1,0:T(4,128)S(1)}, u32[]{:S(2)}, u32[]{:S(2)}) collective-permute-start(f32[4,128]{1,0:T(4,128)} %get-tuple-element.36.mine_ref), channel_id=1, source_target_pairs={{0,1},{1,0},{2,3},{3,2},{4,5},{5,4},{6,7},{7,6},{8,9},{9,8},{10,11... | collective-permute-start | bytes 6152 | tf_op jit(solution)/shard_map/ppermute | solution.py:327
  85.4 3.0 %collective-permute-start.17 = (f32[4,128]{1,0:T(4,128)S(1)}, f32[4,128]{1,0:T(4,128)S(1)}, u32[]{:S(2)}, u32[]{:S(2)}) collective-permute-start(f32[4,128]{1,0:T(4,128)S(1)} %add.28), channel_id=1, source_target_pairs={{0,3},{1,2},{2,1},{3,0},{4,7},{5,6},{6,5},{7,4},{8,11},{9,10},{10,... | collective-permute-start | bytes 6152 | tf_op jit(solution)/shard_map/ppermute | solution.py:327
  88.4 5.5 %collective-permute-start.18 = (f32[4,128]{1,0:T(4,128)S(1)}, f32[4,128]{1,0:T(4,128)S(1)}, u32[]{:S(2)}, u32[]{:S(2)}) collective-permute-start(f32[4,128]{1,0:T(4,128)S(1)} %add.29), channel_id=1, source_target_pairs={{0,5},{1,4},{2,7},{3,6},{4,1},{5,0},{6,3},{7,2},{8,13},{9,12},{10,... | collective-permute-start | bytes 6152 | tf_op jit(solution)/shard_map/ppermute | solution.py:327
  93.9 5.1 %collective-permute-start.19 = (f32[4,128]{1,0:T(4,128)S(1)}, f32[4,128]{1,0:T(4,128)S(1)}, u32[]{:S(2)}, u32[]{:S(2)}) collective-permute-start(f32[4,128]{1,0:T(4,128)S(1)} %add.30), channel_id=1, source_target_pairs={{0,13},{1,12},{2,15},{3,14},{4,9},{5,8},{6,11},{7,10},{8,5},{9,4},... | collective-permute-start | bytes 6152 | tf_op jit(solution)/shard_map/ppermute | solution.py:327
  101.0 3.3 %collective-permute-start.20 = (f32[2,128]{1,0:T(2,128)}, f32[2,128]{1,0:T(2,128)S(1)}, u32[]{:S(2)}, u32[]{:S(2)}) collective-permute-start(f32[2,128]{1,0:T(2,128)} %get-tuple-element.38), channel_id=1, source_target_pairs={{0,17},{1,16},{2,19},{3,18},{4,21},{5,20},{6,23},{7,22},{8,25},{9,... | collective-permute-start | bytes 3080 | tf_op jit(solution)/shard_map/ppermute | solution.py:327
  105.0 4.3 %collective-permute-start.21 = (f32[2,128]{1,0:T(2,128)S(1)}, f32[2,128]{1,0:T(2,128)S(1)}, u32[]{:S(2)}, u32[]{:S(2)}) collective-permute-start(f32[2,128]{1,0:T(2,128)S(1)} %add.33), channel_id=1, source_target_pairs={{0,49},{1,48},{2,51},{3,50},{4,53},{5,52},{6,55},{7,54},{8,57},{9,... | collective-permute-start | bytes 3080 | tf_op jit(solution)/shard_map/ppermute | solution.py:327
  109.3 5.2 %collective-permute-start.22 = (f32[2,128]{1,0:T(2,128)S(1)}, f32[2,128]{1,0:T(2,128)S(1)}, u32[]{:S(2)}, u32[]{:S(2)}) collective-permute-start(f32[2,128]{1,0:T(2,128)S(1)} %add.34), channel_id=1, source_target_pairs={{0,65},{1,64},{2,67},{3,66},{4,69},{5,68},{6,71},{7,70},{8,73},{9,... | collective-permute-start | bytes 3080 | tf_op jit(solution)/shard_map/ppermute | solution.py:327
  114.4 5.9 %collective-permute-start.23 = (f32[2,128]{1,0:T(2,128)S(1)}, f32[2,128]{1,0:T(2,128)S(1)}, u32[]{:S(2)}, u32[]{:S(2)}) collective-permute-start(f32[2,128]{1,0:T(2,128)S(1)} %add.35), channel_id=1, source_target_pairs={{0,193},{1,192},{2,195},{3,194},{4,197},{5,196},{6,199},{7,198},{8... | collective-permute-start | bytes 3080 | tf_op jit(solution)/shard_map/ppermute | solution.py:327
  (14 other events, 195.3 us)

commit v4 on v3

--- a/solution.py
+++ b/solution.py
@@ -13,7 +13,6 @@
 
 LOCAL = 4
 BLOCKS = 16
-LATE = range(8, 12)
 VMEM_LIMIT = 60 * 2**20
 
 
@@ -69,9 +68,9 @@
             done(at)
 
 
-def front_kernel(psi_any, renv_any, left_ref, right_ref, x3_any, mpo_ref, psi_ref, renv_ref, xt_ref, x3_ref, sem_ref, out_sem):
+def front_kernel(start, psi_any, renv_any, left_ref, right_ref, x3_any, mpo_ref, psi_ref, renv_ref, xt_ref, x3_ref, sem_ref, out_sem):
     copies = [
-        pltpu.make_async_copy(psi_any, psi_ref, sem_ref.at[0]),
+        pltpu.make_async_copy(psi_any.at[:, pl.ds(start, psi_ref.shape[1])], psi_ref, sem_ref.at[0]),
         pltpu.make_async_copy(renv_any, renv_ref, sem_ref.at[1]),
     ]
     for copy in copies:
@@ -113,84 +112,45 @@
     return 2 * hops + ((left ^ sector) & 1)
 
 
-def is_late(slot):
-    return jnp.logical_and(slot >= LATE.start, slot < LATE.stop)
-
-
-def masked_step(keep, psi_ref, u_ref, sq_ref, lenv_ref, slot, x3_ref, q):
-    h = contract(lenv_ref, slot, x3_ref, q)
-    u = jnp.where(keep, psi_ref[q].astype(F32) - 0.5 * h, 0.0)
-    u_ref[q] = u.astype(BF16)
-    sq_ref[...] += u * u
-
-
-def mid_kernel(charge_ref, rank_ref, psi_any, x3_any, *rest):
-    early = [i for i in range(BLOCKS) if i not in LATE]
-    blocks = rest[: len(early)]
-    u_ref, sq_ref, psi_ref, lenv_ref, x3_ref, sem_ref, x3_sem = rest[len(early) :]
-    pairs, width = psi_ref.shape[0], psi_ref.shape[2]
-    copies = [pltpu.make_async_copy(b, lenv_ref.at[i], sem_ref.at[i]) for i, b in zip(early, blocks)]
-    copies.append(pltpu.make_async_copy(psi_any, psi_ref, sem_ref.at[BLOCKS]))
-    for copy in copies:
-        copy.start()
-    slots = [slot_of(charge_ref, q) for q in range(pairs)]
-    loads = [pltpu.make_async_copy(x3_any.at[q], x3_ref.at[q], x3_sem.at[q]) for q in range(pairs)]
-    for q in range(pairs):
-        pl.when(jnp.logical_not(is_late(slots[q])))(loads[q].start)
-    keep = iota((width, width), 1) < rank_ref[0]
-    sq_ref[...] = jnp.zeros_like(sq_ref)
-    for copy in copies:
-        copy.wait()
-    for q in range(pairs):
-
-        @pl.when(jnp.logical_not(is_late(slots[q])))
-        def _():
-            loads[q].wait()
-            masked_step(keep, psi_ref, u_ref, sq_ref, lenv_ref, slots[q], x3_ref, q)
-
-        @pl.when(is_late(slots[q]))
-        def _():
-            u_ref[q] = jnp.zeros((width, width), BF16)
-
-
-def back_kernel(charge_ref, rank_ref, psi_any, renv_any, mpo_ref, x3_any, early_u, early_sq, *rest):
+def back_kernel(charge_ref, rank_ref, psi_any, renv_any, mpo_ref, x3_low, x3_high, *rest):
     blocks = rest[:BLOCKS]
-    v_any, stat_ref, lenv_ref, x3_ref, u_ref, xt_ref, psi_ref, renv_ref, v_ref, sq_ref = rest[BLOCKS:-3]
+    v_any, stat_ref, lenv_ref, x3_ref, u_ref, xt_ref, psi_ref, renv_ref, v_ref = rest[BLOCKS:-3]
     sem_ref, x3_sem, v_sem = rest[-3:]
     pairs, width = psi_ref.shape[0], psi_ref.shape[2]
-    copies = [pltpu.make_async_copy(blocks[i], lenv_ref.at[i], sem_ref.at[i]) for i in range(BLOCKS)]
-    first = [copies[i] for i in LATE] + [
-        pltpu.make_async_copy(psi_any, psi_ref, sem_ref.at[BLOCKS]),
-        pltpu.make_async_copy(early_u, u_ref, sem_ref.at[BLOCKS + 1]),
-    ]
-    later = pltpu.make_async_copy(renv_any, renv_ref, sem_ref.at[BLOCKS + 2])
-    last = [copies[i] for i in range(BLOCKS) if i not in LATE]
-    slots = [slot_of(charge_ref, q) for q in range(pairs)]
-    loads = [pltpu.make_async_copy(x3_any.at[q], x3_ref.at[q], x3_sem.at[q]) for q in range(pairs)]
+    half = x3_low.shape[2]
+    first = [pltpu.make_async_copy(blocks[i], lenv_ref.at[i], sem_ref.at[i]) for i in range(BLOCKS)]
+    first.append(pltpu.make_async_copy(psi_any, psi_ref, sem_ref.at[BLOCKS]))
+    later = pltpu.make_async_copy(renv_any, renv_ref, sem_ref.at[BLOCKS + 1])
+    loads = []
+    for q in range(pairs):
+        loads.append(
+            (
+                pltpu.make_async_copy(x3_low.at[q], x3_ref.at[q, :, pl.ds(0, half)], x3_sem.at[0, q]),
+                pltpu.make_async_copy(x3_high.at[q], x3_ref.at[q, :, pl.ds(half, half)], x3_sem.at[1, q]),
+            )
+        )
     for copy in first:
         copy.start()
-    for q in range(pairs):
-        pl.when(is_late(slots[q]))(loads[q].start)
+    for low, high in loads:
+        low.start()
+        high.start()
     later.start()
+    slots = [slot_of(charge_ref, q) for q in range(pairs)]
     keep = iota((width, width), 1) < rank_ref[0]
-    sq_ref[...] = early_sq[...]
+    zero = jnp.zeros((width, width), F32)
     for copy in first:
         copy.wait()
-    for copy in last:
-        copy.start()
+    first_sq = zero
     for q in range(pairs):
-
-        @pl.when(is_late(slots[q]))
-        def _():
-            loads[q].wait()
-            masked_step(keep, psi_ref, u_ref, sq_ref, lenv_ref, slots[q], x3_ref, q)
-
+        loads[q][0].wait()
+        loads[q][1].wait()
+        h = contract(lenv_ref, slots[q], x3_ref, q)
+        u = jnp.where(keep, psi_ref[q].astype(F32) - 0.5 * h, 0.0)
+        u_ref[q] = u.astype(BF16)
+        first_sq = first_sq + u * u
+    later.wait()
     turn(u_ref, xt_ref)
-    later.wait()
     spread(xt_ref, renv_ref, mpo_ref[...], x3_ref)
-    for copy in last:
-        copy.wait()
-    zero = jnp.zeros((width, width), F32)
     sq, inner, own = zero, zero, zero
     sent = []
     for q in range(pairs):
@@ -201,7 +161,7 @@
         sent.append(pltpu.make_async_copy(v_ref.at[q], v_any.at[q], v_sem.at[q]))
         sent[-1].start()
         sq, inner, own = sq + v * v, inner + x * h, own + x * x
-    for i, part in enumerate((sq_ref[...], sq, inner, own)):
+    for i, part in enumerate((first_sq, sq, inner, own)):
         stat_ref[i : i + 1] = jnp.sum(part, axis=0, keepdims=True)
     for copy in sent:
         copy.wait()
@@ -240,57 +200,38 @@
     )
 
 
-def front(psi, renv, left, right):
+def front(psi, renv, left, right, part, parts):
     pairs, width = psi.shape[0], psi.shape[2]
+    states = width // parts
     bonds = renv.shape[0]
     rows = bonds * pairs
     return call(
-        front_kernel,
+        functools.partial(front_kernel, part * states),
         "front",
-        2 * 10**9,
-        (jax.ShapeDtypeStruct((pairs, bonds, width, width), BF16), jax.ShapeDtypeStruct((rows, rows), BF16)),
+        2 * 10**9 // parts,
+        (jax.ShapeDtypeStruct((pairs, bonds, states, width), BF16), jax.ShapeDtypeStruct((rows, rows), BF16)),
         [ANY_SPEC, ANY_SPEC, VMEM_SPEC, VMEM_SPEC],
         (ANY_SPEC, VMEM_SPEC),
         [
-            pltpu.VMEM((pairs, width, width), BF16),
+            pltpu.VMEM((pairs, states, width), BF16),
             pltpu.VMEM((bonds, width, width), BF16),
-            pltpu.VMEM((width, pairs, width), BF16),
-            pltpu.VMEM((pairs, bonds, width, width), BF16),
+            pltpu.VMEM((states, pairs, width), BF16),
+            pltpu.VMEM((pairs, bonds, states, width), BF16),
             pltpu.SemaphoreType.DMA((2,)),
-            pltpu.SemaphoreType.DMA((width // 16,)),
+            pltpu.SemaphoreType.DMA((states // 16,)),
         ],
     )(psi, renv, left, right)
 
 
-def mid(charge, rank, psi, x3, blocks):
-    pairs, width = psi.shape[0], psi.shape[2]
-    bonds = x3.shape[1]
-    return call(
-        mid_kernel,
-        "mid",
-        10**9,
-        (jax.ShapeDtypeStruct((pairs, width, width), BF16), jax.ShapeDtypeStruct((width, width), F32)),
-        [SMEM_SPEC, SMEM_SPEC, ANY_SPEC, ANY_SPEC] + [ANY_SPEC] * len(blocks),
-        (VMEM_SPEC, VMEM_SPEC),
-        [
-            pltpu.VMEM((pairs, width, width), BF16),
-            pltpu.VMEM((BLOCKS, bonds, width, width), BF16),
-            pltpu.VMEM((pairs, bonds, width, width), BF16),
-            pltpu.SemaphoreType.DMA((BLOCKS + 1,)),
-            pltpu.SemaphoreType.DMA((pairs,)),
-        ],
-    )(charge, rank, psi, x3, *blocks)
-
-
-def back(charge, rank, psi, renv, mpo, x3, early_u, early_sq, blocks):
+def back(charge, rank, psi, renv, mpo, x3_low, x3_high, blocks):
     pairs, width = psi.shape[0], psi.shape[2]
     bonds = renv.shape[0]
     return call(
         back_kernel,
         "back",
-        3 * 10**9,
+        4 * 10**9,
         (jax.ShapeDtypeStruct((pairs, width, width), F32), jax.ShapeDtypeStruct((4, width), F32)),
-        [SMEM_SPEC, SMEM_SPEC, ANY_SPEC, ANY_SPEC, VMEM_SPEC, ANY_SPEC, ANY_SPEC, VMEM_SPEC] + [ANY_SPEC] * BLOCKS,
+        [SMEM_SPEC, SMEM_SPEC, ANY_SPEC, ANY_SPEC, VMEM_SPEC, ANY_SPEC, ANY_SPEC] + [ANY_SPEC] * BLOCKS,
         (ANY_SPEC, VMEM_SPEC),
         [
             pltpu.VMEM((BLOCKS, bonds, width, width), BF16),
@@ -300,12 +241,11 @@
             pltpu.VMEM((pairs, width, width), BF16),
             pltpu.VMEM((bonds, width, width), BF16),
             pltpu.VMEM((pairs, width, width), F32),
-            pltpu.VMEM((width, width), F32),
-            pltpu.SemaphoreType.DMA((BLOCKS + 3,)),
-            pltpu.SemaphoreType.DMA((pairs,)),
+            pltpu.SemaphoreType.DMA((BLOCKS + 2,)),
+            pltpu.SemaphoreType.DMA((2, pairs)),
             pltpu.SemaphoreType.DMA((pairs,)),
         ],
-    )(charge, rank, psi, renv, mpo, x3, early_u, early_sq, *blocks)
+    )(charge, rank, psi, renv, mpo, x3_low, x3_high, *blocks)
 
 
 def settle(total, mine, twin_stat, count):
@@ -359,22 +299,24 @@
     env = env_build[0, 0]
     moved = from_behind(env)
     tall = (site_left.shape[0] * pairs, site_left.shape[1])
-    x3, mpo = front(
-        x, renv, site_left.transpose(0, 2, 3, 1).reshape(tall), site_right.transpose(0, 2, 3, 1).reshape(tall)
-    )
-    moved, x3 = lax.optimization_barrier((moved, x3))
+    ends = (site_left.transpose(0, 2, 3, 1).reshape(tall), site_right.transpose(0, 2, 3, 1).reshape(tall))
+    x3_low, mpo = front(x, renv, *ends, 0, 2)
+    moved, x3_low = lax.optimization_barrier((moved, x3_low))
     own = jnp.where(segment == 0, env, moved)
 
-    o1, t1 = lax.optimization_barrier((hop(own), cross_hop(own)))
-    o2, t2 = lax.optimization_barrier((hop(o1), hop(t1)))
-    o3, t3 = lax.optimization_barrier((hop(o2), hop(t2)))
+    o1 = hop(own)
+    waited, x_then = lax.optimization_barrier((own, x))
+    x3_high, _ = front(x_then, renv, *ends, 1, 2)
+    waited, x3_high = lax.optimization_barrier((waited, x3_high))
+    t1 = cross_hop(waited)
+    o2 = hop(o1)
+    t2 = hop(t1)
+    o3 = hop(o2)
+    t3 = hop(t2)
     o4 = hop(o3)
-    near = [own, twin(own), o1, t1, o2, t2, o3, t3]
-    far = [twin(t2), twin(o2), twin(t1), twin(o1)]
-    early_u, early_sq = mid(charge, rank, x, x3, near + far)
-    o4, early_u = lax.optimization_barrier((o4, early_u))
-    blocks = near + [o4, twin(o4), twin(t3), twin(o3)] + far
-    v, stat = back(charge, rank, x, renv, mpo, x3, early_u, early_sq, blocks)
+    blocks = [own, twin(own), o1, t1, o2, t2, o3, t3]
+    blocks += [o4, twin(o4), twin(t3), twin(o3), twin(t2), twin(o2), twin(t1), twin(o1)]
+    v, stat = back(charge, rank, x, renv, mpo, x3_low, x3_high, blocks)
 
     twin_stat = partner(stat, 1)
     total = stat + twin_stat

time: 121 us -> 115 us (0.950)
  starting transfers between devices: 44.7 us -> 39.8 us
  waiting for transfers between devices: 34.5 us -> 33.2 us
    ppermute x6, waiting for transfers between devices: 17 us -> 7.73 us  [hop(): lax.ppermute(value, 'sec', [(i, (i + (2 if i % 2 == 0 else -2)) % n) for...]
    ppermute x6, starting transfers between devices: 10.2 us -> 15.7 us  [hop(): lax.ppermute(value, 'sec', [(i, (i + (2 if i % 2 == 0 else -2)) % n) for...]
    ppermute x8, starting transfers between devices: 18.9 us -> 14.7 us  [partner(): return lax.ppermute(value, axes, [(i, i ^ bits) for i in range(n)])]
    ppermute x1, waiting for transfers between devices: 5.4 us -> 9.46 us  [cross_hop(): lax.ppermute(value, 'sec', [(i, (i + (-2 if i % 2 == 0 else 2)) % n ^ 1)...]
    ppermute x8, starting transfers between devices: 8.97 us -> 5.29 us  [twin(): return lax.ppermute(value, 'sec', [(i, i ^ 1) for i in range(n)])]
    ppermute x8, waiting for transfers between devices: 10.6 us -> 13.6 us  [partner(): return lax.ppermute(value, axes, [(i, i ^ bits) for i in range(n)])]
    ppermute x1, starting transfers between devices: 2.57 us -> 0.09 us  [cross_hop(): lax.ppermute(value, 'sec', [(i, (i + (-2 if i % 2 == 0 else 2)) % n ^ 1)...]
    ppermute x1, waiting for transfers between devices: 0.01 us -> 1.82 us  [from_behind(): return lax.ppermute(value, 'seg', [(i, i + 1) for i in range(n - 1)])]
  transfers between devices with their start and end apart: 24 -> 24, of which waited for: 13 -> 14; matrix products, arithmetic and copies ran while one was open for 3% -> 4% of each run, Pallas kernels for 14% -> 11%
where the time goes in v4:
time: 115 us
  starting transfers between devices  39.8 us (35%)
  waiting for transfers between devices  33.2 us (29%)
  Pallas kernels  32.3 us (28%)
  other arithmetic  5.41 us (5%)
  local copies, waits for them, and re-layouts  2.57 us (2%)
  between operations  1.55 us (1%)
    pallas_call x1, Pallas kernels, back(): call(back_kernel, 'back', 4 * 10 ** 9, (jax.ShapeDtypeStruct((pairs, widt...  18.5 us
    ppermute x6, starting transfers between devices, hop(): lax.ppermute(value, 'sec', [(i, (i + (2 if i % 2 == 0 else -2)) % n) for...  15.7 us
    ppermute x8, starting transfers between devices, partner(): return lax.ppermute(value, axes, [(i, i ^ bits) for i in range(n)])  14.7 us
    ppermute x8, waiting for transfers between devices, partner(): return lax.ppermute(value, axes, [(i, i ^ bits) for i in range(n)])  13.6 us
    pallas_call x2, Pallas kernels, front(): call(functools.partial(front_kernel, part * states), 'front', 2 * 10 ** 9...  12.5 us
    ppermute x1, waiting for transfers between devices, cross_hop(): lax.ppermute(value, 'sec', [(i, (i + (-2 if i % 2 == 0 else 2)) % n ^ 1)...  9.46 us
    ppermute x6, waiting for transfers between devices, hop(): lax.ppermute(value, 'sec', [(i, (i + (2 if i % 2 == 0 else -2)) % n) for...  7.73 us
    ppermute x8, starting transfers between devices, twin(): return lax.ppermute(value, 'sec', [(i, i ^ 1) for i in range(n)])  5.29 us
  transfers between devices with their start and end apart: 24, of which 14 were waited for; matrix products, arithmetic and copies ran while one was open for 4% of the time, Pallas kernels for 11%

profile of v4, /device:TPU:1, one launch (start us, length us, event | category | flops | bytes accessed | tf_op | source)
XLA Modules:
  0.0 114.9 jit_solution(3996737091051509945)
XLA Ops:
  0.6 4.1 %collective-permute-start = (bf16[12,128,128]{2,1,0:T(8,128)(2,1)}, bf16[12,128,128]{2,1,0:T(8,128)(2,1)S(1)}, u32[]{:S(2)}, u32[]{:S(2)}) collective-permute-start(bf16[12,128,128]{2,1,0:T(8,128)(2,1)} %bitcast.15), channel_id=1, source_target_pairs={{0,16},{16,32},{32,48},{48,64},{64,80},{80,96},{96,112},{112,128},... | collective-permute-start | bytes 1179656 | tf_op jit(solution)/shard_map/ppermute | solution.py:287
  4.8 6.2 %front.2 = (bf16[16,12,64,128]{3,2,1,0:T(8,128)(2,1)}, bf16[192,192]{1,0:T(8,128)(2,1)}) custom-call(bf16[16,128,128]{2,1,0:T(8,128)(2,1)} %bitcast.16, bf16[12,128,128]{2,1,0:T(8,128)(2,1)} %bitcast.19, bf16[192,12]{1,0:T(8,128)(2,1)} %bitcast.22, bf16[192,12]{1,0:T(8,128)(2,1)} %bitcast.24), custom_call_target="tpu_custom_call" | custom-call | flops 1000000000 | bytes 8000000 | tf_op jit(solution)/shard_map/front/pallas_call | solution.py:208
  11.0 1.8 %collective-permute-done = bf16[12,128,128]{2,1,0:T(8,128)(2,1)S(1)} collective-permute-done((bf16[12,128,128]{2,1,0:T(8,128)(2,1)}, bf16[12,128,128]{2,1,0:T(8,128)(2,1)S(1)}, u32[]{:S(2)}, u32[]{:S(2)}) %collective-permute-start) | collective-permute-done | bytes 393248 | tf_op jit(solution)/shard_map/ppermute | solution.py:287
  12.9 5.7 %collective-permute-start.2 = (bf16[12,128,128]{2,1,0:T(8,128)(2,1)S(1)}, bf16[12,128,128]{2,1,0:T(8,128)(2,1)S(1)}, u32[]{:S(2)}, u32[]{:S(2)}) collective-permute-start(bf16[12,128,128]{2,1,0:T(8,128)(2,1)S(1)} %broadcast_select_fusion.rest_0_), channel_id=1, source_target_pairs={{0,2},{1,15},{2,4},{3,1},{4,6},{5,3},{6,8},{7,5},{8,10},{9,7},{10,... | collective-permute-start | bytes 1179656 | tf_op jit(solution)/shard_map/ppermute | solution.py:272
  18.5 6.2 %front.3 = (bf16[16,12,64,128]{3,2,1,0:T(8,128)(2,1)}, bf16[192,192]{1,0:T(8,128)(2,1)}) custom-call(bf16[16,128,128]{2,1,0:T(8,128)(2,1)} %bitcast.17, bf16[12,128,128]{2,1,0:T(8,128)(2,1)} %bitcast.20, bf16[192,12]{1,0:T(8,128)(2,1)} %bitcast.23, bf16[192,12]{1,0:T(8,128)(2,1)} %bitcast.25), custom_call_target="tpu_custom_call" | custom-call | flops 1000000000 | bytes 8000000 | tf_op jit(solution)/shard_map/front/pallas_call | solution.py:208
  24.9 1.5 %collective-permute-start.4 = (bf16[12,128,128]{2,1,0:T(8,128)(2,1)S(1)}, bf16[12,128,128]{2,1,0:T(8,128)(2,1)S(1)}, u32[]{:S(2)}, u32[]{:S(2)}) collective-permute-start(bf16[12,128,128]{2,1,0:T(8,128)(2,1)S(1)} %collective-permute-done.2.rest_2_), channel_id=1, source_target_pairs={{0,2},{1,15},{2,4},{3,1},{4,6},{5,3},{6,8},{7,5},{8,10},{9,7},{10,... | collective-permute-start | bytes 1179656 | tf_op jit(solution)/shard_map/ppermute | solution.py:272
  26.4 9.5 %collective-permute-done.3.rest_3_ = bf16[12,128,128]{2,1,0:T(8,128)(2,1)S(1)} collective-permute-done((bf16[12,128,128]{2,1,0:T(8,128)(2,1)S(1)}, bf16[12,128,128]{2,1,0:T(8,128)(2,1)S(1)}, u32[]{:S(2)}, u32[]{:S(2)}) %collective-permute-start.3) | collective-permute-done | bytes 393248 | tf_op jit(solution)/shard_map/ppermute | solution.py:277
  35.8 2.2 %collective-permute-start.5 = (bf16[12,128,128]{2,1,0:T(8,128)(2,1)S(1)}, bf16[12,128,128]{2,1,0:T(8,128)(2,1)S(1)}, u32[]{:S(2)}, u32[]{:S(2)}) collective-permute-start(bf16[12,128,128]{2,1,0:T(8,128)(2,1)S(1)} %collective-permute-done.3.rest_3_), channel_id=1, source_target_pairs={{0,2},{1,15},{2,4},{3,1},{4,6},{5,3},{6,8},{7,5},{8,10},{9,7},{10,... | collective-permute-start | bytes 1179656 | tf_op jit(solution)/shard_map/ppermute | solution.py:272
  38.7 4.0 %collective-permute-done.5.rest_5_ = bf16[12,128,128]{2,1,0:T(8,128)(2,1)S(1)} collective-permute-done((bf16[12,128,128]{2,1,0:T(8,128)(2,1)S(1)}, bf16[12,128,128]{2,1,0:T(8,128)(2,1)S(1)}, u32[]{:S(2)}, u32[]{:S(2)}) %collective-permute-start.5) | collective-permute-done | bytes 393248 | tf_op jit(solution)/shard_map/ppermute | solution.py:272
  42.7 3.1 %collective-permute-start.7 = (bf16[12,128,128]{2,1,0:T(8,128)(2,1)S(1)}, bf16[12,128,128]{2,1,0:T(8,128)(2,1)S(1)}, u32[]{:S(2)}, u32[]{:S(2)}) collective-permute-start(bf16[12,128,128]{2,1,0:T(8,128)(2,1)S(1)} %collective-permute-done.5.rest_5_), channel_id=1, source_target_pairs={{0,2},{1,15},{2,4},{3,1},{4,6},{5,3},{6,8},{7,5},{8,10},{9,7},{10,... | collective-permute-start | bytes 1179656 | tf_op jit(solution)/shard_map/ppermute | solution.py:272
  47.0 3.1 %collective-permute-start.8 = (bf16[12,128,128]{2,1,0:T(8,128)(2,1)S(1)}, bf16[12,128,128]{2,1,0:T(8,128)(2,1)S(1)}, u32[]{:S(2)}, u32[]{:S(2)}) collective-permute-start(bf16[12,128,128]{2,1,0:T(8,128)(2,1)S(1)} %collective-permute-done.6.rest_6_), channel_id=1, source_target_pairs={{0,2},{1,15},{2,4},{3,1},{4,6},{5,3},{6,8},{7,5},{8,10},{9,7},{10,... | collective-permute-start | bytes 1179656 | tf_op jit(solution)/shard_map/ppermute | solution.py:272
  51.2 2.1 %collective-permute-start.10 = (bf16[12,128,128]{2,1,0:T(8,128)(2,1)S(1)}, bf16[12,128,128]{2,1,0:T(8,128)(2,1)S(1)}, u32[]{:S(2)}, u32[]{:S(2)}) collective-permute-start(bf16[12,128,128]{2,1,0:T(8,128)(2,1)S(1)} %collective-permute-done.7.rest_7_), channel_id=1, source_target_pairs={{0,1},{1,0},{2,3},{3,2},{4,5},{5,4},{6,7},{7,6},{8,9},{9,8},{10,11... | collective-permute-start | bytes 1179656 | tf_op jit(solution)/shard_map/ppermute | solution.py:282
  53.3 2.1 %collective-permute-done.8.rest_8_ = bf16[12,128,128]{2,1,0:T(8,128)(2,1)S(1)} collective-permute-done((bf16[12,128,128]{2,1,0:T(8,128)(2,1)S(1)}, bf16[12,128,128]{2,1,0:T(8,128)(2,1)S(1)}, u32[]{:S(2)}, u32[]{:S(2)}) %collective-permute-start.8) | collective-permute-done | bytes 393248 | tf_op jit(solution)/shard_map/ppermute | solution.py:272
  55.4 2.1 %collective-permute-start.9 = (bf16[12,128,128]{2,1,0:T(8,128)(2,1)S(1)}, bf16[12,128,128]{2,1,0:T(8,128)(2,1)S(1)}, u32[]{:S(2)}, u32[]{:S(2)}) collective-permute-start(bf16[12,128,128]{2,1,0:T(8,128)(2,1)S(1)} %collective-permute-done.8.rest_8_), channel_id=1, source_target_pairs={{0,1},{1,0},{2,3},{3,2},{4,5},{5,4},{6,7},{7,6},{8,9},{9,8},{10,11... | collective-permute-start | bytes 1179656 | tf_op jit(solution)/shard_map/ppermute | solution.py:282
  60.1 18.5 %back.1 = (f32[16,128,128]{2,1,0:T(8,128)}, f32[4,128]{1,0:T(4,128)}) custom-call(s32[16]{0:T(128)} %charge_ref.1, s32[1]{0:T(128)S(6)} %copy.10.rank_ref, bf16[16,128,128]{2,1,0:T(8,128)(2,1)} %bitcast.18, bf16[12,128,128]{2,1,0:T(8,128)(2,1)} %bitcast.21, bf16[192,192]{1,0:T(8,128)(2,1)} %get-tuple-element.16.mpo_ref, ...), custom_call_target="tpu_custom_call" | custom-call | flops 4000000000 | bytes 8000000 | tf_op jit(solution)/shard_map/back/pallas_call | solution.py:229
  80.7 3.0 %collective-permute-done.17 = f32[4,128]{1,0:T(4,128)S(1)} collective-permute-done((f32[4,128]{1,0:T(4,128)S(1)}, f32[4,128]{1,0:T(4,128)S(1)}, u32[]{:S(2)}, u32[]{:S(2)}) %collective-permute-start.17) | collective-permute-done | bytes 2080 | tf_op jit(solution)/shard_map/ppermute | solution.py:267
  84.6 3.0 %collective-permute-done.18 = f32[4,128]{1,0:T(4,128)S(1)} collective-permute-done((f32[4,128]{1,0:T(4,128)S(1)}, f32[4,128]{1,0:T(4,128)S(1)}, u32[]{:S(2)}, u32[]{:S(2)}) %collective-permute-start.18) | collective-permute-done | bytes 2080 | tf_op jit(solution)/shard_map/ppermute | solution.py:267
  87.7 1.8 %collective-permute-start.19 = (f32[4,128]{1,0:T(4,128)S(1)}, f32[4,128]{1,0:T(4,128)S(1)}, u32[]{:S(2)}, u32[]{:S(2)}) collective-permute-start(f32[4,128]{1,0:T(4,128)S(1)} %add.30), channel_id=1, source_target_pairs={{0,13},{1,12},{2,15},{3,14},{4,9},{5,8},{6,11},{7,10},{8,5},{9,4},... | collective-permute-start | bytes 6152 | tf_op jit(solution)/shard_map/ppermute | solution.py:267
  89.5 3.3 %collective-permute-done.19 = f32[4,128]{1,0:T(4,128)S(1)} collective-permute-done((f32[4,128]{1,0:T(4,128)S(1)}, f32[4,128]{1,0:T(4,128)S(1)}, u32[]{:S(2)}, u32[]{:S(2)}) %collective-permute-start.19) | collective-permute-done | bytes 2080 | tf_op jit(solution)/shard_map/ppermute | solution.py:267
  94.8 2.2 %collective-permute-start.20 = (f32[2,128]{1,0:T(2,128)}, f32[2,128]{1,0:T(2,128)S(1)}, u32[]{:S(2)}, u32[]{:S(2)}) collective-permute-start(f32[2,128]{1,0:T(2,128)} %get-tuple-element.28), channel_id=1, source_target_pairs={{0,17},{1,16},{2,19},{3,18},{4,21},{5,20},{6,23},{7,22},{8,25},{9,... | collective-permute-start | bytes 3080 | tf_op jit(solution)/shard_map/ppermute | solution.py:267
  99.0 2.9 %collective-permute-start.21 = (f32[2,128]{1,0:T(2,128)S(1)}, f32[2,128]{1,0:T(2,128)S(1)}, u32[]{:S(2)}, u32[]{:S(2)}) collective-permute-start(f32[2,128]{1,0:T(2,128)S(1)} %add.33), channel_id=1, source_target_pairs={{0,49},{1,48},{2,51},{3,50},{4,53},{5,52},{6,55},{7,54},{8,57},{9,... | collective-permute-start | bytes 3080 | tf_op jit(solution)/shard_map/ppermute | solution.py:267
  103.2 3.8 %collective-permute-start.22 = (f32[2,128]{1,0:T(2,128)S(1)}, f32[2,128]{1,0:T(2,128)S(1)}, u32[]{:S(2)}, u32[]{:S(2)}) collective-permute-start(f32[2,128]{1,0:T(2,128)S(1)} %add.34), channel_id=1, source_target_pairs={{0,65},{1,64},{2,67},{3,66},{4,69},{5,68},{6,71},{7,70},{8,73},{9,... | collective-permute-start | bytes 3080 | tf_op jit(solution)/shard_map/ppermute | solution.py:267
  108.4 3.1 %collective-permute-start.23 = (f32[2,128]{1,0:T(2,128)S(1)}, f32[2,128]{1,0:T(2,128)S(1)}, u32[]{:S(2)}, u32[]{:S(2)}) collective-permute-start(f32[2,128]{1,0:T(2,128)S(1)} %add.35), channel_id=1, source_target_pairs={{0,193},{1,192},{2,195},{3,194},{4,197},{5,196},{6,199},{7,198},{8... | collective-permute-start | bytes 3080 | tf_op jit(solution)/shard_map/ppermute | solution.py:267
  111.5 2.8 %fusion = bf16[1,1,16,128,128]{4,3,2,1,0:T(8,128)(2,1)} fusion(f32[16,128,128]{2,1,0:T(8,128)} %get-tuple-element.25, f32[]{:T(128)} %bitcast.9), kind=kLoop, calls=%fused_computation.1 | loop fusion | flops 524288 | bytes 1572868 | tf_op jit(solution)/shard_map/broadcast_in_dim | solution.py:331
  (77 shorter events, 15.4 us)
Async XLA Ops:
  0.6 12.2 %collective-permute-start = (bf16[12,128,128]{2,1,0:T(8,128)(2,1)}, bf16[12,128,128]{2,1,0:T(8,128)(2,1)S(1)}, u32[]{:S(2)}, u32[]{:S(2)}) collective-permute-start(bf16[12,128,128]{2,1,0:T(8,128)(2,1)} %bitcast.15), channel_id=1, source_target_pairs={{0,16},{16,32},{32,48},{48,64},{64,80},{80,96},{96,112},{112,128},... | collective-permute-start | bytes 1179656 | tf_op jit(solution)/shard_map/ppermute | solution.py:287
  12.9 12.0 %collective-permute-start.2 = (bf16[12,128,128]{2,1,0:T(8,128)(2,1)S(1)}, bf16[12,128,128]{2,1,0:T(8,128)(2,1)S(1)}, u32[]{:S(2)}, u32[]{:S(2)}) collective-permute-start(bf16[12,128,128]{2,1,0:T(8,128)(2,1)S(1)} %broadcast_select_fusion.rest_0_), channel_id=1, source_target_pairs={{0,2},{1,15},{2,4},{3,1},{4,6},{5,3},{6,8},{7,5},{8,10},{9,7},{10,... | collective-permute-start | bytes 1179656 | tf_op jit(solution)/shard_map/ppermute | solution.py:272
  24.8 11.0 %collective-permute-start.3 = (bf16[12,128,128]{2,1,0:T(8,128)(2,1)S(1)}, bf16[12,128,128]{2,1,0:T(8,128)(2,1)S(1)}, u32[]{:S(2)}, u32[]{:S(2)}) collective-permute-start(bf16[12,128,128]{2,1,0:T(8,128)(2,1)S(1)} %broadcast_select_fusion.rest_0_), channel_id=1, source_target_pairs={{0,15},{1,2},{2,1},{3,4},{4,3},{5,6},{6,5},{7,8},{8,7},{9,10},{10,... | collective-permute-start | bytes 1179656 | tf_op jit(solution)/shard_map/ppermute | solution.py:277
  24.9 13.1 %collective-permute-start.4 = (bf16[12,128,128]{2,1,0:T(8,128)(2,1)S(1)}, bf16[12,128,128]{2,1,0:T(8,128)(2,1)S(1)}, u32[]{:S(2)}, u32[]{:S(2)}) collective-permute-start(bf16[12,128,128]{2,1,0:T(8,128)(2,1)S(1)} %collective-permute-done.2.rest_2_), channel_id=1, source_target_pairs={{0,2},{1,15},{2,4},{3,1},{4,6},{5,3},{6,8},{7,5},{8,10},{9,7},{10,... | collective-permute-start | bytes 1179656 | tf_op jit(solution)/shard_map/ppermute | solution.py:272
  35.8 6.9 %collective-permute-start.5 = (bf16[12,128,128]{2,1,0:T(8,128)(2,1)S(1)}, bf16[12,128,128]{2,1,0:T(8,128)(2,1)S(1)}, u32[]{:S(2)}, u32[]{:S(2)}) collective-permute-start(bf16[12,128,128]{2,1,0:T(8,128)(2,1)S(1)} %collective-permute-done.3.rest_3_), channel_id=1, source_target_pairs={{0,2},{1,15},{2,4},{3,1},{4,6},{5,3},{6,8},{7,5},{8,10},{9,7},{10,... | collective-permute-start | bytes 1179656 | tf_op jit(solution)/shard_map/ppermute | solution.py:272
  38.0 8.9 %collective-permute-start.6 = (bf16[12,128,128]{2,1,0:T(8,128)(2,1)S(1)}, bf16[12,128,128]{2,1,0:T(8,128)(2,1)S(1)}, u32[]{:S(2)}, u32[]{:S(2)}) collective-permute-start(bf16[12,128,128]{2,1,0:T(8,128)(2,1)S(1)} %collective-permute-done.4.rest_4_), channel_id=1, source_target_pairs={{0,2},{1,15},{2,4},{3,1},{4,6},{5,3},{6,8},{7,5},{8,10},{9,7},{10,... | collective-permute-start | bytes 1179656 | tf_op jit(solution)/shard_map/ppermute | solution.py:272
  38.2 11.8 %collective-permute-start.1 = (bf16[12,128,128]{2,1,0:T(8,128)(2,1)S(1)}, bf16[12,128,128]{2,1,0:T(8,128)(2,1)S(1)}, u32[]{:S(2)}, u32[]{:S(2)}) collective-permute-start(bf16[12,128,128]{2,1,0:T(8,128)(2,1)S(1)} %broadcast_select_fusion.rest_0_), channel_id=1, source_target_pairs={{0,1},{1,0},{2,3},{3,2},{4,5},{5,4},{6,7},{7,6},{8,9},{9,8},{10,11... | collective-permute-start | bytes 1179656 | tf_op jit(solution)/shard_map/ppermute | solution.py:282
  38.2 11.9 %collective-permute-start.15 = (bf16[12,128,128]{2,1,0:T(8,128)(2,1)S(1)}, bf16[12,128,128]{2,1,0:T(8,128)(2,1)S(1)}, u32[]{:S(2)}, u32[]{:S(2)}) collective-permute-start(bf16[12,128,128]{2,1,0:T(8,128)(2,1)S(1)} %collective-permute-done.2.rest_2_), channel_id=1, source_target_pairs={{0,1},{1,0},{2,3},{3,2},{4,5},{5,4},{6,7},{7,6},{8,9},{9,8},{10,11... | collective-permute-start | bytes 1179656 | tf_op jit(solution)/shard_map/ppermute | solution.py:282
  38.7 11.9 %collective-permute-start.14 = (bf16[12,128,128]{2,1,0:T(8,128)(2,1)S(1)}, bf16[12,128,128]{2,1,0:T(8,128)(2,1)S(1)}, u32[]{:S(2)}, u32[]{:S(2)}) collective-permute-start(bf16[12,128,128]{2,1,0:T(8,128)(2,1)S(1)} %collective-permute-done.3.rest_3_), channel_id=1, source_target_pairs={{0,1},{1,0},{2,3},{3,2},{4,5},{5,4},{6,7},{7,6},{8,9},{9,8},{10,11... | collective-permute-start | bytes 1179656 | tf_op jit(solution)/shard_map/ppermute | solution.py:282
  42.7 8.4 %collective-permute-start.7 = (bf16[12,128,128]{2,1,0:T(8,128)(2,1)S(1)}, bf16[12,128,128]{2,1,0:T(8,128)(2,1)S(1)}, u32[]{:S(2)}, u32[]{:S(2)}) collective-permute-start(bf16[12,128,128]{2,1,0:T(8,128)(2,1)S(1)} %collective-permute-done.5.rest_5_), channel_id=1, source_target_pairs={{0,2},{1,15},{2,4},{3,1},{4,6},{5,3},{6,8},{7,5},{8,10},{9,7},{10,... | collective-permute-start | bytes 1179656 | tf_op jit(solution)/shard_map/ppermute | solution.py:272
  47.0 8.4 %collective-permute-start.8 = (bf16[12,128,128]{2,1,0:T(8,128)(2,1)S(1)}, bf16[12,128,128]{2,1,0:T(8,128)(2,1)S(1)}, u32[]{:S(2)}, u32[]{:S(2)}) collective-permute-start(bf16[12,128,128]{2,1,0:T(8,128)(2,1)S(1)} %collective-permute-done.6.rest_6_), channel_id=1, source_target_pairs={{0,2},{1,15},{2,4},{3,1},{4,6},{5,3},{6,8},{7,5},{8,10},{9,7},{10,... | collective-permute-start | bytes 1179656 | tf_op jit(solution)/shard_map/ppermute | solution.py:272
  50.1 8.1 %collective-permute-start.13 = (bf16[12,128,128]{2,1,0:T(8,128)(2,1)S(1)}, bf16[12,128,128]{2,1,0:T(8,128)(2,1)S(1)}, u32[]{:S(2)}, u32[]{:S(2)}) collective-permute-start(bf16[12,128,128]{2,1,0:T(8,128)(2,1)S(1)} %collective-permute-done.4.rest_4_), channel_id=1, source_target_pairs={{0,1},{1,0},{2,3},{3,2},{4,5},{5,4},{6,7},{7,6},{8,9},{9,8},{10,11... | collective-permute-start | bytes 1179656 | tf_op jit(solution)/shard_map/ppermute | solution.py:282
  50.1 8.1 %collective-permute-start.12 = (bf16[12,128,128]{2,1,0:T(8,128)(2,1)S(1)}, bf16[12,128,128]{2,1,0:T(8,128)(2,1)S(1)}, u32[]{:S(2)}, u32[]{:S(2)}) collective-permute-start(bf16[12,128,128]{2,1,0:T(8,128)(2,1)S(1)} %collective-permute-done.5.rest_5_), channel_id=1, source_target_pairs={{0,1},{1,0},{2,3},{3,2},{4,5},{5,4},{6,7},{7,6},{8,9},{9,8},{10,11... | collective-permute-start | bytes 1179656 | tf_op jit(solution)/shard_map/ppermute | solution.py:282
  50.6 7.6 %collective-permute-start.11 = (bf16[12,128,128]{2,1,0:T(8,128)(2,1)S(1)}, bf16[12,128,128]{2,1,0:T(8,128)(2,1)S(1)}, u32[]{:S(2)}, u32[]{:S(2)}) collective-permute-start(bf16[12,128,128]{2,1,0:T(8,128)(2,1)S(1)} %collective-permute-done.6.rest_6_), channel_id=1, source_target_pairs={{0,1},{1,0},{2,3},{3,2},{4,5},{5,4},{6,7},{7,6},{8,9},{9,8},{10,11... | collective-permute-start | bytes 1179656 | tf_op jit(solution)/shard_map/ppermute | solution.py:282
  51.2 7.0 %collective-permute-start.10 = (bf16[12,128,128]{2,1,0:T(8,128)(2,1)S(1)}, bf16[12,128,128]{2,1,0:T(8,128)(2,1)S(1)}, u32[]{:S(2)}, u32[]{:S(2)}) collective-permute-start(bf16[12,128,128]{2,1,0:T(8,128)(2,1)S(1)} %collective-permute-done.7.rest_7_), channel_id=1, source_target_pairs={{0,1},{1,0},{2,3},{3,2},{4,5},{5,4},{6,7},{7,6},{8,9},{9,8},{10,11... | collective-permute-start | bytes 1179656 | tf_op jit(solution)/shard_map/ppermute | solution.py:282
  55.4 3.4 %collective-permute-start.9 = (bf16[12,128,128]{2,1,0:T(8,128)(2,1)S(1)}, bf16[12,128,128]{2,1,0:T(8,128)(2,1)S(1)}, u32[]{:S(2)}, u32[]{:S(2)}) collective-permute-start(bf16[12,128,128]{2,1,0:T(8,128)(2,1)S(1)} %collective-permute-done.8.rest_8_), channel_id=1, source_target_pairs={{0,1},{1,0},{2,3},{3,2},{4,5},{5,4},{6,7},{7,6},{8,9},{9,8},{10,11... | collective-permute-start | bytes 1179656 | tf_op jit(solution)/shard_map/ppermute | solution.py:282
  78.6 1.5 %collective-permute-start.16 = (f32[4,128]{1,0:T(4,128)}, f32[4,128]{1,0:T(4,128)S(1)}, u32[]{:S(2)}, u32[]{:S(2)}) collective-permute-start(f32[4,128]{1,0:T(4,128)} %get-tuple-element.26.mine_ref), channel_id=1, source_target_pairs={{0,1},{1,0},{2,3},{3,2},{4,5},{5,4},{6,7},{7,6},{8,9},{9,8},{10,11... | collective-permute-start | bytes 6152 | tf_op jit(solution)/shard_map/ppermute | solution.py:267
  80.7 3.0 %collective-permute-start.17 = (f32[4,128]{1,0:T(4,128)S(1)}, f32[4,128]{1,0:T(4,128)S(1)}, u32[]{:S(2)}, u32[]{:S(2)}) collective-permute-start(f32[4,128]{1,0:T(4,128)S(1)} %add.28), channel_id=1, source_target_pairs={{0,3},{1,2},{2,1},{3,0},{4,7},{5,6},{6,5},{7,4},{8,11},{9,10},{10,... | collective-permute-start | bytes 6152 | tf_op jit(solution)/shard_map/ppermute | solution.py:267
  83.8 3.9 %collective-permute-start.18 = (f32[4,128]{1,0:T(4,128)S(1)}, f32[4,128]{1,0:T(4,128)S(1)}, u32[]{:S(2)}, u32[]{:S(2)}) collective-permute-start(f32[4,128]{1,0:T(4,128)S(1)} %add.29), channel_id=1, source_target_pairs={{0,5},{1,4},{2,7},{3,6},{4,1},{5,0},{6,3},{7,2},{8,13},{9,12},{10,... | collective-permute-start | bytes 6152 | tf_op jit(solution)/shard_map/ppermute | solution.py:267
  87.7 5.1 %collective-permute-start.19 = (f32[4,128]{1,0:T(4,128)S(1)}, f32[4,128]{1,0:T(4,128)S(1)}, u32[]{:S(2)}, u32[]{:S(2)}) collective-permute-start(f32[4,128]{1,0:T(4,128)S(1)} %add.30), channel_id=1, source_target_pairs={{0,13},{1,12},{2,15},{3,14},{4,9},{5,8},{6,11},{7,10},{8,5},{9,4},... | collective-permute-start | bytes 6152 | tf_op jit(solution)/shard_map/ppermute | solution.py:267
  94.8 3.6 %collective-permute-start.20 = (f32[2,128]{1,0:T(2,128)}, f32[2,128]{1,0:T(2,128)S(1)}, u32[]{:S(2)}, u32[]{:S(2)}) collective-permute-start(f32[2,128]{1,0:T(2,128)} %get-tuple-element.28), channel_id=1, source_target_pairs={{0,17},{1,16},{2,19},{3,18},{4,21},{5,20},{6,23},{7,22},{8,25},{9,... | collective-permute-start | bytes 3080 | tf_op jit(solution)/shard_map/ppermute | solution.py:267
  99.0 4.2 %collective-permute-start.21 = (f32[2,128]{1,0:T(2,128)S(1)}, f32[2,128]{1,0:T(2,128)S(1)}, u32[]{:S(2)}, u32[]{:S(2)}) collective-permute-start(f32[2,128]{1,0:T(2,128)S(1)} %add.33), channel_id=1, source_target_pairs={{0,49},{1,48},{2,51},{3,50},{4,53},{5,52},{6,55},{7,54},{8,57},{9,... | collective-permute-start | bytes 3080 | tf_op jit(solution)/shard_map/ppermute | solution.py:267
  103.2 5.1 %collective-permute-start.22 = (f32[2,128]{1,0:T(2,128)S(1)}, f32[2,128]{1,0:T(2,128)S(1)}, u32[]{:S(2)}, u32[]{:S(2)}) collective-permute-start(f32[2,128]{1,0:T(2,128)S(1)} %add.34), channel_id=1, source_target_pairs={{0,65},{1,64},{2,67},{3,66},{4,69},{5,68},{6,71},{7,70},{8,73},{9,... | collective-permute-start | bytes 3080 | tf_op jit(solution)/shard_map/ppermute | solution.py:267
  108.4 5.9 %collective-permute-start.23 = (f32[2,128]{1,0:T(2,128)S(1)}, f32[2,128]{1,0:T(2,128)S(1)}, u32[]{:S(2)}, u32[]{:S(2)}) collective-permute-start(f32[2,128]{1,0:T(2,128)S(1)} %add.35), channel_id=1, source_target_pairs={{0,193},{1,192},{2,195},{3,194},{4,197},{5,196},{6,199},{7,198},{8... | collective-permute-start | bytes 3080 | tf_op jit(solution)/shard_map/ppermute | solution.py:267
  (18 other events, 230.5 us)

commit v5 on v4

--- a/solution.py
+++ b/solution.py
@@ -13,6 +13,7 @@
 
 LOCAL = 4
 BLOCKS = 16
+FINISH = 4
 VMEM_LIMIT = 60 * 2**20
 
 
@@ -44,10 +45,10 @@
         xt_ref[j * 16 : (j + 1) * 16] = jnp.swapaxes(src_ref[:, j * 16 : (j + 1) * 16, :], 0, 1)
 
 
-def spread(xt_ref, renv_ref, mpo, x3_ref, done=None):
+def spread(xt_ref, renv_ref, mpo, x3_ref, begin=0, done=None):
     states, pairs, width = xt_ref.shape
     bonds = renv_ref.shape[0]
-    for at in range(0, states, 16):
+    for at in range(begin, states, 16):
         xa = xt_ref[at : at + 16].reshape(16 * pairs, width)
         first = []
         for k in range(bonds // 2):
@@ -68,9 +69,9 @@
             done(at)
 
 
-def front_kernel(start, psi_any, renv_any, left_ref, right_ref, x3_any, mpo_ref, psi_ref, renv_ref, xt_ref, x3_ref, sem_ref, out_sem):
+def front_kernel(psi_any, renv_any, left_ref, right_ref, x3_any, mpo_ref, psi_ref, renv_ref, xt_ref, x3_ref, sem_ref, out_sem):
     copies = [
-        pltpu.make_async_copy(psi_any.at[:, pl.ds(start, psi_ref.shape[1])], psi_ref, sem_ref.at[0]),
+        pltpu.make_async_copy(psi_any.at[:, pl.ds(0, psi_ref.shape[1])], psi_ref, sem_ref.at[0]),
         pltpu.make_async_copy(renv_any, renv_ref, sem_ref.at[1]),
     ]
     for copy in copies:
@@ -87,7 +88,7 @@
         sent.append(pltpu.make_async_copy(x3_ref.at[:, :, rows], x3_any.at[:, :, rows], out_sem.at[at // 16]))
         sent[-1].start()
 
-    spread(xt_ref, renv_ref, mpo, x3_ref, done)
+    spread(xt_ref, renv_ref, mpo, x3_ref, 0, done)
     for copy in sent:
         copy.wait()
 
@@ -112,43 +113,35 @@
     return 2 * hops + ((left ^ sector) & 1)
 
 
-def back_kernel(charge_ref, rank_ref, psi_any, renv_any, mpo_ref, x3_low, x3_high, *rest):
+def back_kernel(charge_ref, rank_ref, psi_any, renv_any, mpo_ref, x3_any, *rest):
     blocks = rest[:BLOCKS]
     v_any, stat_ref, lenv_ref, x3_ref, u_ref, xt_ref, psi_ref, renv_ref, v_ref = rest[BLOCKS:-3]
     sem_ref, x3_sem, v_sem = rest[-3:]
     pairs, width = psi_ref.shape[0], psi_ref.shape[2]
-    half = x3_low.shape[2]
-    first = [pltpu.make_async_copy(blocks[i], lenv_ref.at[i], sem_ref.at[i]) for i in range(BLOCKS)]
-    first.append(pltpu.make_async_copy(psi_any, psi_ref, sem_ref.at[BLOCKS]))
-    later = pltpu.make_async_copy(renv_any, renv_ref, sem_ref.at[BLOCKS + 1])
-    loads = []
-    for q in range(pairs):
-        loads.append(
-            (
-                pltpu.make_async_copy(x3_low.at[q], x3_ref.at[q, :, pl.ds(0, half)], x3_sem.at[0, q]),
-                pltpu.make_async_copy(x3_high.at[q], x3_ref.at[q, :, pl.ds(half, half)], x3_sem.at[1, q]),
-            )
-        )
-    for copy in first:
+    done = x3_any.shape[2]
+    first = [
+        pltpu.make_async_copy(psi_any, psi_ref, sem_ref.at[BLOCKS]),
+        pltpu.make_async_copy(renv_any, renv_ref, sem_ref.at[BLOCKS + 1]),
+    ]
+    second = [pltpu.make_async_copy(blocks[i], lenv_ref.at[i], sem_ref.at[i]) for i in range(BLOCKS)]
+    second.append(pltpu.make_async_copy(x3_any, x3_ref.at[:, :, pl.ds(0, done)], x3_sem))
+    for copy in first + second:
         copy.start()
-    for low, high in loads:
-        low.start()
-        high.start()
-    later.start()
     slots = [slot_of(charge_ref, q) for q in range(pairs)]
     keep = iota((width, width), 1) < rank_ref[0]
     zero = jnp.zeros((width, width), F32)
     for copy in first:
         copy.wait()
+    turn(psi_ref, xt_ref)
+    spread(xt_ref, renv_ref, mpo_ref[...], x3_ref, done)
+    for copy in second:
+        copy.wait()
     first_sq = zero
     for q in range(pairs):
-        loads[q][0].wait()
-        loads[q][1].wait()
         h = contract(lenv_ref, slots[q], x3_ref, q)
         u = jnp.where(keep, psi_ref[q].astype(F32) - 0.5 * h, 0.0)
         u_ref[q] = u.astype(BF16)
         first_sq = first_sq + u * u
-    later.wait()
     turn(u_ref, xt_ref)
     spread(xt_ref, renv_ref, mpo_ref[...], x3_ref)
     sq, inner, own = zero, zero, zero
@@ -172,14 +165,32 @@
     first_sq, sq, inner, own = [jnp.sum(total_ref[i : i + 1], axis=1, keepdims=True) for i in range(4)]
     one = lax.rsqrt(first_sq / count + 1e-06)
     scale = one * lax.rsqrt(one * one * sq / count + 1e-06)
-    row = iota((8, width), 0)
-    out_ref[...] = jnp.where(row == 0, scale, inner / own)
+    out_ref[...] = jnp.where(iota((8, width), 0) == 0, scale, inner / own)
     mine = jnp.sum(mine_ref[1:2], axis=1, keepdims=True)
     twin = jnp.sum(twin_ref[1:2], axis=1, keepdims=True)
     row = iota((2, width), 0)
     here = jnp.where(row == (lax.axis_index("sec") & 1), mine, twin)
     share = jnp.log(float(lax.axis_size("sec")) * here / sq)
     share_ref[...] = jnp.where(iota((2, width), 1) == lax.axis_index("seg"), share, 0.0)
+
+
+def finish_kernel(v_any, out_ref, state_any, v_ref, state_ref, in_sem, out_sem):
+    pairs = v_ref.shape[0]
+    part = pairs // FINISH
+    loads, stores = [], []
+    for i in range(FINISH):
+        rows = pl.ds(i * part, part)
+        loads.append(pltpu.make_async_copy(v_any.at[rows], v_ref.at[rows], in_sem.at[i]))
+        stores.append(pltpu.make_async_copy(state_ref.at[rows], state_any.at[rows], out_sem.at[i]))
+        loads[i].start()
+    scale = out_ref[0:1, :]
+    for i in range(FINISH):
+        loads[i].wait()
+        for q in range(i * part, (i + 1) * part):
+            state_ref[q] = (v_ref[q] * scale).astype(BF16)
+        stores[i].start()
+    for store in stores:
+        store.wait()
 
 
 VMEM_SPEC = pl.BlockSpec(memory_space=pltpu.VMEM)
@@ -200,15 +211,14 @@
     )
 
 
-def front(psi, renv, left, right, part, parts):
+def front(psi, renv, left, right, states):
     pairs, width = psi.shape[0], psi.shape[2]
-    states = width // parts
     bonds = renv.shape[0]
     rows = bonds * pairs
     return call(
-        functools.partial(front_kernel, part * states),
+        front_kernel,
         "front",
-        2 * 10**9 // parts,
+        5 * 10**8,
         (jax.ShapeDtypeStruct((pairs, bonds, states, width), BF16), jax.ShapeDtypeStruct((rows, rows), BF16)),
         [ANY_SPEC, ANY_SPEC, VMEM_SPEC, VMEM_SPEC],
         (ANY_SPEC, VMEM_SPEC),
@@ -223,7 +233,7 @@
     )(psi, renv, left, right)
 
 
-def back(charge, rank, psi, renv, mpo, x3_low, x3_high, blocks):
+def back(charge, rank, psi, renv, mpo, x3, blocks):
     pairs, width = psi.shape[0], psi.shape[2]
     bonds = renv.shape[0]
     return call(
@@ -231,7 +241,7 @@
         "back",
         4 * 10**9,
         (jax.ShapeDtypeStruct((pairs, width, width), F32), jax.ShapeDtypeStruct((4, width), F32)),
-        [SMEM_SPEC, SMEM_SPEC, ANY_SPEC, ANY_SPEC, VMEM_SPEC, ANY_SPEC, ANY_SPEC] + [ANY_SPEC] * BLOCKS,
+        [SMEM_SPEC, SMEM_SPEC, ANY_SPEC, ANY_SPEC, VMEM_SPEC, ANY_SPEC] + [ANY_SPEC] * BLOCKS,
         (ANY_SPEC, VMEM_SPEC),
         [
             pltpu.VMEM((BLOCKS, bonds, width, width), BF16),
@@ -242,10 +252,10 @@
             pltpu.VMEM((bonds, width, width), BF16),
             pltpu.VMEM((pairs, width, width), F32),
             pltpu.SemaphoreType.DMA((BLOCKS + 2,)),
-            pltpu.SemaphoreType.DMA((2, pairs)),
+            pltpu.SemaphoreType.DMA,
             pltpu.SemaphoreType.DMA((pairs,)),
         ],
-    )(charge, rank, psi, renv, mpo, x3_low, x3_high, *blocks)
+    )(charge, rank, psi, renv, mpo, x3, *blocks)
 
 
 def settle(total, mine, twin_stat, count):
@@ -261,6 +271,23 @@
     )(total, mine, twin_stat)
 
 
+def finish(v, out):
+    return call(
+        finish_kernel,
+        "finish",
+        10**6,
+        jax.ShapeDtypeStruct(v.shape, BF16),
+        [ANY_SPEC, VMEM_SPEC],
+        ANY_SPEC,
+        [
+            pltpu.VMEM(v.shape, F32),
+            pltpu.VMEM(v.shape, BF16),
+            pltpu.SemaphoreType.DMA((FINISH,)),
+            pltpu.SemaphoreType.DMA((FINISH,)),
+        ],
+    )(v, out)
+
+
 def partner(value, bits):
     axes = ("seg", "sec")
     n = lax.axis_size(axes)
@@ -300,14 +327,12 @@
     moved = from_behind(env)
     tall = (site_left.shape[0] * pairs, site_left.shape[1])
     ends = (site_left.transpose(0, 2, 3, 1).reshape(tall), site_right.transpose(0, 2, 3, 1).reshape(tall))
-    x3_low, mpo = front(x, renv, *ends, 0, 2)
-    moved, x3_low = lax.optimization_barrier((moved, x3_low))
     own = jnp.where(segment == 0, env, moved)
 
     o1 = hop(own)
     waited, x_then = lax.optimization_barrier((own, x))
-    x3_high, _ = front(x_then, renv, *ends, 1, 2)
-    waited, x3_high = lax.optimization_barrier((waited, x3_high))
+    x3, mpo = front(x_then, renv, *ends, width // 4)
+    waited, x3 = lax.optimization_barrier((waited, x3))
     t1 = cross_hop(waited)
     o2 = hop(o1)
     t2 = hop(t1)
@@ -316,16 +341,18 @@
     o4 = hop(o3)
     blocks = [own, twin(own), o1, t1, o2, t2, o3, t3]
     blocks += [o4, twin(o4), twin(t3), twin(o3), twin(t2), twin(o2), twin(t1), twin(o1)]
-    v, stat = back(charge, rank, x, renv, mpo, x3_low, x3_high, blocks)
+    v, stat = back(charge, rank, x, renv, mpo, x3, blocks)
 
     twin_stat = partner(stat, 1)
     total = stat + twin_stat
     for bits in (3, 5, 13):
         total = total + partner(total, bits)
     share, out = settle(total, stat, twin_stat, count)
-    state = (v * out[0, 0]).astype(BF16)
+    state = finish(v, out)
     for bits in (1, 3, 4, 12):
         share = share + partner(share, nsec * bits + 1)
+        if bits == 1:
+            share, state = lax.optimization_barrier((share, state))
     wanted = (iota(share.shape, 0) == sector % 2) & (iota(share.shape, 1) <= segment)
     weight = jnp.sum(jnp.where(wanted, share, 0.0))
     return state[None, None], out[1:2, 0], weight.reshape(1, 1)

time: 115 us -> 109 us (0.948)
  waiting for transfers between devices: 33.2 us -> 42 us
  Pallas kernels: 32.3 us -> 25.5 us
  starting transfers between devices: 39.8 us -> 34.7 us
  other arithmetic: 5.41 us -> 2.95 us
    ppermute x1, waiting for transfers between devices: 1.82 us -> 8.05 us  [from_behind(): return lax.ppermute(value, 'seg', [(i, i + 1) for i in range(n - 1)])]
    ppermute x6, waiting for transfers between devices: 7.73 us -> 12.7 us  [hop(): lax.ppermute(value, 'sec', [(i, (i + (2 if i % 2 == 0 else -2)) % n) for...]
    pallas_call x2, Pallas kernels: 12.5 us -> 7.54 us  [the longest x1 4.93 us: front(): call(front_kernel, 'front', 5 * 10 ** 8, (jax.ShapeDtypeStruct((pairs, bo...]
    ppermute x8, starting transfers between devices: 5.29 us -> 1.98 us  [twin(): return lax.ppermute(value, 'sec', [(i, i ^ 1) for i in range(n)])]
    broadcast_in_dim x1 -> x0, other arithmetic: 2.79 us -> none  [shards(): return (state[None, None], out[1:2, 0], weight.reshape(1, 1))]
    ppermute x6, starting transfers between devices: 15.7 us -> 13.7 us  [hop(): lax.ppermute(value, 'sec', [(i, (i + (2 if i % 2 == 0 else -2)) % n) for...]
    pallas_call x1, Pallas kernels: 18.5 us -> 16.6 us  [back(): call(back_kernel, 'back', 4 * 10 ** 9, (jax.ShapeDtypeStruct((pairs, widt...]
    ppermute x8, waiting for transfers between devices: 13.6 us -> 12.2 us  [partner(): return lax.ppermute(value, axes, [(i, i ^ bits) for i in range(n)])]
  transfers between devices with their start and end apart: 24 -> 24, of which waited for: 14 -> 13; matrix products, arithmetic and copies ran while one was open for 4% -> 1% of each run, Pallas kernels for 11% -> 7%
where the time goes in v5:
time: 109 us
  waiting for transfers between devices  42 us (39%)
  starting transfers between devices  34.7 us (32%)
  Pallas kernels  25.5 us (23%)
  other arithmetic  2.95 us (3%)
  local copies, waits for them, and re-layouts  2.46 us (2%)
  between operations  1.56 us (1%)
    pallas_call x1, Pallas kernels, back(): call(back_kernel, 'back', 4 * 10 ** 9, (jax.ShapeDtypeStruct((pairs, widt...  16.6 us
    ppermute x8, starting transfers between devices, partner(): return lax.ppermute(value, axes, [(i, i ^ bits) for i in range(n)])  14.9 us
    ppermute x6, starting transfers between devices, hop(): lax.ppermute(value, 'sec', [(i, (i + (2 if i % 2 == 0 else -2)) % n) for...  13.7 us
    ppermute x6, waiting for transfers between devices, hop(): lax.ppermute(value, 'sec', [(i, (i + (2 if i % 2 == 0 else -2)) % n) for...  12.7 us
    ppermute x8, waiting for transfers between devices, partner(): return lax.ppermute(value, axes, [(i, i ^ bits) for i in range(n)])  12.2 us
    ppermute x1, waiting for transfers between devices, cross_hop(): lax.ppermute(value, 'sec', [(i, (i + (-2 if i % 2 == 0 else 2)) % n ^ 1)...  8.43 us
    ppermute x1, waiting for transfers between devices, from_behind(): return lax.ppermute(value, 'seg', [(i, i + 1) for i in range(n - 1)])  8.05 us
    pallas_call x1, Pallas kernels, front(): call(front_kernel, 'front', 5 * 10 ** 8, (jax.ShapeDtypeStruct((pairs, bo...  4.93 us
  transfers between devices with their start and end apart: 24, of which 13 were waited for; matrix products, arithmetic and copies ran while one was open for 1% of the time, Pallas kernels for 7%

profile of v5, /device:TPU:1, one launch (start us, length us, event | category | flops | bytes accessed | tf_op | source)
XLA Modules:
  0.0 109.1 jit_solution(16473153488751493969)
XLA Ops:
  0.6 4.0 %collective-permute-start = (bf16[12,128,128]{2,1,0:T(8,128)(2,1)}, bf16[12,128,128]{2,1,0:T(8,128)(2,1)S(1)}, u32[]{:S(2)}, u32[]{:S(2)}) collective-permute-start(bf16[12,128,128]{2,1,0:T(8,128)(2,1)} %bitcast.14), channel_id=1, source_target_pairs={{0,16},{16,32},{32,48},{48,64},{64,80},{80,96},{96,112},{112,128},... | collective-permute-start | bytes 1179656 | tf_op jit(solution)/shard_map/ppermute | solution.py:314
  4.6 8.0 %collective-permute-done = bf16[12,128,128]{2,1,0:T(8,128)(2,1)S(1)} collective-permute-done((bf16[12,128,128]{2,1,0:T(8,128)(2,1)}, bf16[12,128,128]{2,1,0:T(8,128)(2,1)S(1)}, u32[]{:S(2)}, u32[]{:S(2)}) %collective-permute-start) | collective-permute-done | bytes 393248 | tf_op jit(solution)/shard_map/ppermute | solution.py:314
  13.7 5.7 %collective-permute-start.2 = (bf16[12,128,128]{2,1,0:T(8,128)(2,1)S(1)}, bf16[12,128,128]{2,1,0:T(8,128)(2,1)S(1)}, u32[]{:S(2)}, u32[]{:S(2)}) collective-permute-start(bf16[12,128,128]{2,1,0:T(8,128)(2,1)S(1)} %broadcast_select_fusion.rest_0_), channel_id=1, source_target_pairs={{0,2},{1,15},{2,4},{3,1},{4,6},{5,3},{6,8},{7,5},{8,10},{9,7},{10,... | collective-permute-start | bytes 1179656 | tf_op jit(solution)/shard_map/ppermute | solution.py:299
  19.4 4.9 %front.1 = (bf16[16,12,32,128]{3,2,1,0:T(8,128)(2,1)}, bf16[192,192]{1,0:T(8,128)(2,1)}) custom-call(bf16[16,128,128]{2,1,0:T(8,128)(2,1)} %bitcast.15, bf16[12,128,128]{2,1,0:T(8,128)(2,1)} %bitcast.17, bf16[192,12]{1,0:T(8,128)(2,1)} %bitcast.19, bf16[192,12]{1,0:T(8,128)(2,1)} %bitcast.20), custom_call_target="tpu_custom_call" | custom-call | flops 500000000 | bytes 8000000 | tf_op jit(solution)/shard_map/front/pallas_call | solution.py:218
  24.4 2.8 %collective-permute-start.4 = (bf16[12,128,128]{2,1,0:T(8,128)(2,1)S(1)}, bf16[12,128,128]{2,1,0:T(8,128)(2,1)S(1)}, u32[]{:S(2)}, u32[]{:S(2)}) collective-permute-start(bf16[12,128,128]{2,1,0:T(8,128)(2,1)S(1)} %collective-permute-done.2.rest_2_), channel_id=1, source_target_pairs={{0,2},{1,15},{2,4},{3,1},{4,6},{5,3},{6,8},{7,5},{8,10},{9,7},{10,... | collective-permute-start | bytes 1179656 | tf_op jit(solution)/shard_map/ppermute | solution.py:299
  27.2 8.4 %collective-permute-done.3.rest_3_ = bf16[12,128,128]{2,1,0:T(8,128)(2,1)S(1)} collective-permute-done((bf16[12,128,128]{2,1,0:T(8,128)(2,1)S(1)}, bf16[12,128,128]{2,1,0:T(8,128)(2,1)S(1)}, u32[]{:S(2)}, u32[]{:S(2)}) %collective-permute-start.3) | collective-permute-done | bytes 393248 | tf_op jit(solution)/shard_map/ppermute | solution.py:304
  36.2 1.6 %collective-permute-start.6 = (bf16[12,128,128]{2,1,0:T(8,128)(2,1)S(1)}, bf16[12,128,128]{2,1,0:T(8,128)(2,1)S(1)}, u32[]{:S(2)}, u32[]{:S(2)}) collective-permute-start(bf16[12,128,128]{2,1,0:T(8,128)(2,1)S(1)} %collective-permute-done.4.rest_4_), channel_id=1, source_target_pairs={{0,2},{1,15},{2,4},{3,1},{4,6},{5,3},{6,8},{7,5},{8,10},{9,7},{10,... | collective-permute-start | bytes 1179656 | tf_op jit(solution)/shard_map/ppermute | solution.py:299
  38.3 4.3 %collective-permute-done.5.rest_5_ = bf16[12,128,128]{2,1,0:T(8,128)(2,1)S(1)} collective-permute-done((bf16[12,128,128]{2,1,0:T(8,128)(2,1)S(1)}, bf16[12,128,128]{2,1,0:T(8,128)(2,1)S(1)}, u32[]{:S(2)}, u32[]{:S(2)}) %collective-permute-start.5) | collective-permute-done | bytes 393248 | tf_op jit(solution)/shard_map/ppermute | solution.py:299
  44.0 2.5 %collective-permute-done.6.rest_6_ = bf16[12,128,128]{2,1,0:T(8,128)(2,1)S(1)} collective-permute-done((bf16[12,128,128]{2,1,0:T(8,128)(2,1)S(1)}, bf16[12,128,128]{2,1,0:T(8,128)(2,1)S(1)}, u32[]{:S(2)}, u32[]{:S(2)}) %collective-permute-start.6) | collective-permute-done | bytes 393248 | tf_op jit(solution)/shard_map/ppermute | solution.py:299
  46.5 1.7 %collective-permute-start.8 = (bf16[12,128,128]{2,1,0:T(8,128)(2,1)S(1)}, bf16[12,128,128]{2,1,0:T(8,128)(2,1)S(1)}, u32[]{:S(2)}, u32[]{:S(2)}) collective-permute-start(bf16[12,128,128]{2,1,0:T(8,128)(2,1)S(1)} %collective-permute-done.6.rest_6_), channel_id=1, source_target_pairs={{0,2},{1,15},{2,4},{3,1},{4,6},{5,3},{6,8},{7,5},{8,10},{9,7},{10,... | collective-permute-start | bytes 1179656 | tf_op jit(solution)/shard_map/ppermute | solution.py:299
  48.9 2.1 %collective-permute-done.7.rest_7_ = bf16[12,128,128]{2,1,0:T(8,128)(2,1)S(1)} collective-permute-done((bf16[12,128,128]{2,1,0:T(8,128)(2,1)S(1)}, bf16[12,128,128]{2,1,0:T(8,128)(2,1)S(1)}, u32[]{:S(2)}, u32[]{:S(2)}) %collective-permute-start.7) | collective-permute-done | bytes 393248 | tf_op jit(solution)/shard_map/ppermute | solution.py:299
  51.4 3.8 %collective-permute-done.8.rest_8_ = bf16[12,128,128]{2,1,0:T(8,128)(2,1)S(1)} collective-permute-done((bf16[12,128,128]{2,1,0:T(8,128)(2,1)S(1)}, bf16[12,128,128]{2,1,0:T(8,128)(2,1)S(1)}, u32[]{:S(2)}, u32[]{:S(2)}) %collective-permute-start.8) | collective-permute-done | bytes 393248 | tf_op jit(solution)/shard_map/ppermute | solution.py:299
  58.3 16.6 %back.1 = (f32[16,128,128]{2,1,0:T(8,128)}, f32[4,128]{1,0:T(4,128)}) custom-call(s32[16]{0:T(128)} %charge_ref.1, s32[1]{0:T(128)S(6)} %copy.10.rank_ref, bf16[16,128,128]{2,1,0:T(8,128)(2,1)} %bitcast.16, bf16[12,128,128]{2,1,0:T(8,128)(2,1)} %bitcast.18, bf16[192,192]{1,0:T(8,128)(2,1)} %get-tuple-element.16.mpo_ref, ...), custom_call_target="tpu_custom_call" | custom-call | flops 4000000000 | bytes 8000000 | tf_op jit(solution)/shard_map/back/pallas_call | solution.py:239
  77.1 2.9 %collective-permute-done.17 = f32[4,128]{1,0:T(4,128)S(1)} collective-permute-done((f32[4,128]{1,0:T(4,128)S(1)}, f32[4,128]{1,0:T(4,128)S(1)}, u32[]{:S(2)}, u32[]{:S(2)}) %collective-permute-start.17) | collective-permute-done | bytes 2080 | tf_op jit(solution)/shard_map/ppermute | solution.py:294
  80.0 2.1 %collective-permute-start.18 = (f32[4,128]{1,0:T(4,128)S(1)}, f32[4,128]{1,0:T(4,128)S(1)}, u32[]{:S(2)}, u32[]{:S(2)}) collective-permute-start(f32[4,128]{1,0:T(4,128)S(1)} %add.29), channel_id=1, source_target_pairs={{0,5},{1,4},{2,7},{3,6},{4,1},{5,0},{6,3},{7,2},{8,13},{9,12},{10,... | collective-permute-start | bytes 6152 | tf_op jit(solution)/shard_map/ppermute | solution.py:294
  82.0 1.8 %collective-permute-done.18 = f32[4,128]{1,0:T(4,128)S(1)} collective-permute-done((f32[4,128]{1,0:T(4,128)S(1)}, f32[4,128]{1,0:T(4,128)S(1)}, u32[]{:S(2)}, u32[]{:S(2)}) %collective-permute-start.18) | collective-permute-done | bytes 2080 | tf_op jit(solution)/shard_map/ppermute | solution.py:294
  83.9 2.4 %collective-permute-start.19 = (f32[4,128]{1,0:T(4,128)S(1)}, f32[4,128]{1,0:T(4,128)S(1)}, u32[]{:S(2)}, u32[]{:S(2)}) collective-permute-start(f32[4,128]{1,0:T(4,128)S(1)} %add.30), channel_id=1, source_target_pairs={{0,13},{1,12},{2,15},{3,14},{4,9},{5,8},{6,11},{7,10},{8,5},{9,4},... | collective-permute-start | bytes 6152 | tf_op jit(solution)/shard_map/ppermute | solution.py:294
  86.3 2.7 %collective-permute-done.19 = f32[4,128]{1,0:T(4,128)S(1)} collective-permute-done((f32[4,128]{1,0:T(4,128)S(1)}, f32[4,128]{1,0:T(4,128)S(1)}, u32[]{:S(2)}, u32[]{:S(2)}) %collective-permute-start.19) | collective-permute-done | bytes 2080 | tf_op jit(solution)/shard_map/ppermute | solution.py:294
  91.0 2.2 %collective-permute-start.20 = (f32[2,128]{1,0:T(2,128)}, f32[2,128]{1,0:T(2,128)S(1)}, u32[]{:S(2)}, u32[]{:S(2)}) collective-permute-start(f32[2,128]{1,0:T(2,128)} %get-tuple-element.22), channel_id=1, source_target_pairs={{0,17},{1,16},{2,19},{3,18},{4,21},{5,20},{6,23},{7,22},{8,25},{9,... | collective-permute-start | bytes 3080 | tf_op jit(solution)/shard_map/ppermute | solution.py:294
  93.1 2.6 %finish.1 = bf16[16,128,128]{2,1,0:T(8,128)(2,1)} custom-call(f32[16,128,128]{2,1,0:T(8,128)} %get-tuple-element.23.v_any, f32[8,128]{1,0:T(8,128)} %get-tuple-element.24.out_ref), custom_call_target="tpu_custom_call" | custom-call | flops 1000000 | bytes 8000000 | tf_op jit(solution)/shard_map/finish/pallas_call | solution.py:275
  95.8 2.1 %collective-permute-start.21 = (f32[2,128]{1,0:T(2,128)S(1)}, f32[2,128]{1,0:T(2,128)S(1)}, u32[]{:S(2)}, u32[]{:S(2)}) collective-permute-start(f32[2,128]{1,0:T(2,128)S(1)} %add.32), channel_id=1, source_target_pairs={{0,49},{1,48},{2,51},{3,50},{4,53},{5,52},{6,55},{7,54},{8,57},{9,... | collective-permute-start | bytes 3080 | tf_op jit(solution)/shard_map/ppermute | solution.py:294
  97.9 2.2 %collective-permute-done.21 = f32[2,128]{1,0:T(2,128)S(1)} collective-permute-done((f32[2,128]{1,0:T(2,128)S(1)}, f32[2,128]{1,0:T(2,128)S(1)}, u32[]{:S(2)}, u32[]{:S(2)}) %collective-permute-start.21) | collective-permute-done | bytes 1056 | tf_op jit(solution)/shard_map/ppermute | solution.py:294
  100.1 2.7 %collective-permute-start.22 = (f32[2,128]{1,0:T(2,128)S(1)}, f32[2,128]{1,0:T(2,128)S(1)}, u32[]{:S(2)}, u32[]{:S(2)}) collective-permute-start(f32[2,128]{1,0:T(2,128)S(1)} %add.34), channel_id=1, source_target_pairs={{0,65},{1,64},{2,67},{3,66},{4,69},{5,68},{6,71},{7,70},{8,73},{9,... | collective-permute-start | bytes 3080 | tf_op jit(solution)/shard_map/ppermute | solution.py:294
  104.0 3.2 %collective-permute-start.23 = (f32[2,128]{1,0:T(2,128)S(1)}, f32[2,128]{1,0:T(2,128)S(1)}, u32[]{:S(2)}, u32[]{:S(2)}) collective-permute-start(f32[2,128]{1,0:T(2,128)S(1)} %add.35), channel_id=1, source_target_pairs={{0,193},{1,192},{2,195},{3,194},{4,197},{5,196},{6,199},{7,198},{8... | collective-permute-start | bytes 3080 | tf_op jit(solution)/shard_map/ppermute | solution.py:294
  (76 shorter events, 14.3 us)
Async XLA Ops:
  0.6 12.0 %collective-permute-start = (bf16[12,128,128]{2,1,0:T(8,128)(2,1)}, bf16[12,128,128]{2,1,0:T(8,128)(2,1)S(1)}, u32[]{:S(2)}, u32[]{:S(2)}) collective-permute-start(bf16[12,128,128]{2,1,0:T(8,128)(2,1)} %bitcast.14), channel_id=1, source_target_pairs={{0,16},{16,32},{32,48},{48,64},{64,80},{80,96},{96,112},{112,128},... | collective-permute-start | bytes 1179656 | tf_op jit(solution)/shard_map/ppermute | solution.py:314
  13.7 10.7 %collective-permute-start.2 = (bf16[12,128,128]{2,1,0:T(8,128)(2,1)S(1)}, bf16[12,128,128]{2,1,0:T(8,128)(2,1)S(1)}, u32[]{:S(2)}, u32[]{:S(2)}) collective-permute-start(bf16[12,128,128]{2,1,0:T(8,128)(2,1)S(1)} %broadcast_select_fusion.rest_0_), channel_id=1, source_target_pairs={{0,2},{1,15},{2,4},{3,1},{4,6},{5,3},{6,8},{7,5},{8,10},{9,7},{10,... | collective-permute-start | bytes 1179656 | tf_op jit(solution)/shard_map/ppermute | solution.py:299
  24.3 11.3 %collective-permute-start.3 = (bf16[12,128,128]{2,1,0:T(8,128)(2,1)S(1)}, bf16[12,128,128]{2,1,0:T(8,128)(2,1)S(1)}, u32[]{:S(2)}, u32[]{:S(2)}) collective-permute-start(bf16[12,128,128]{2,1,0:T(8,128)(2,1)S(1)} %broadcast_select_fusion.rest_0_), channel_id=1, source_target_pairs={{0,15},{1,2},{2,1},{3,4},{4,3},{5,6},{6,5},{7,8},{8,7},{9,10},{10,... | collective-permute-start | bytes 1179656 | tf_op jit(solution)/shard_map/ppermute | solution.py:304
  24.4 11.7 %collective-permute-start.4 = (bf16[12,128,128]{2,1,0:T(8,128)(2,1)S(1)}, bf16[12,128,128]{2,1,0:T(8,128)(2,1)S(1)}, u32[]{:S(2)}, u32[]{:S(2)}) collective-permute-start(bf16[12,128,128]{2,1,0:T(8,128)(2,1)S(1)} %collective-permute-done.2.rest_2_), channel_id=1, source_target_pairs={{0,2},{1,15},{2,4},{3,1},{4,6},{5,3},{6,8},{7,5},{8,10},{9,7},{10,... | collective-permute-start | bytes 1179656 | tf_op jit(solution)/shard_map/ppermute | solution.py:299
  35.6 6.9 %collective-permute-start.5 = (bf16[12,128,128]{2,1,0:T(8,128)(2,1)S(1)}, bf16[12,128,128]{2,1,0:T(8,128)(2,1)S(1)}, u32[]{:S(2)}, u32[]{:S(2)}) collective-permute-start(bf16[12,128,128]{2,1,0:T(8,128)(2,1)S(1)} %collective-permute-done.3.rest_3_), channel_id=1, source_target_pairs={{0,2},{1,15},{2,4},{3,1},{4,6},{5,3},{6,8},{7,5},{8,10},{9,7},{10,... | collective-permute-start | bytes 1179656 | tf_op jit(solution)/shard_map/ppermute | solution.py:299
  36.2 10.3 %collective-permute-start.6 = (bf16[12,128,128]{2,1,0:T(8,128)(2,1)S(1)}, bf16[12,128,128]{2,1,0:T(8,128)(2,1)S(1)}, u32[]{:S(2)}, u32[]{:S(2)}) collective-permute-start(bf16[12,128,128]{2,1,0:T(8,128)(2,1)S(1)} %collective-permute-done.4.rest_4_), channel_id=1, source_target_pairs={{0,2},{1,15},{2,4},{3,1},{4,6},{5,3},{6,8},{7,5},{8,10},{9,7},{10,... | collective-permute-start | bytes 1179656 | tf_op jit(solution)/shard_map/ppermute | solution.py:299
  37.8 10.5 %collective-permute-start.1 = (bf16[12,128,128]{2,1,0:T(8,128)(2,1)S(1)}, bf16[12,128,128]{2,1,0:T(8,128)(2,1)S(1)}, u32[]{:S(2)}, u32[]{:S(2)}) collective-permute-start(bf16[12,128,128]{2,1,0:T(8,128)(2,1)S(1)} %broadcast_select_fusion.rest_0_), channel_id=1, source_target_pairs={{0,1},{1,0},{2,3},{3,2},{4,5},{5,4},{6,7},{7,6},{8,9},{9,8},{10,11... | collective-permute-start | bytes 1179656 | tf_op jit(solution)/shard_map/ppermute | solution.py:309
  37.8 10.5 %collective-permute-start.15 = (bf16[12,128,128]{2,1,0:T(8,128)(2,1)S(1)}, bf16[12,128,128]{2,1,0:T(8,128)(2,1)S(1)}, u32[]{:S(2)}, u32[]{:S(2)}) collective-permute-start(bf16[12,128,128]{2,1,0:T(8,128)(2,1)S(1)} %collective-permute-done.2.rest_2_), channel_id=1, source_target_pairs={{0,1},{1,0},{2,3},{3,2},{4,5},{5,4},{6,7},{7,6},{8,9},{9,8},{10,11... | collective-permute-start | bytes 1179656 | tf_op jit(solution)/shard_map/ppermute | solution.py:309
  38.3 10.5 %collective-permute-start.14 = (bf16[12,128,128]{2,1,0:T(8,128)(2,1)S(1)}, bf16[12,128,128]{2,1,0:T(8,128)(2,1)S(1)}, u32[]{:S(2)}, u32[]{:S(2)}) collective-permute-start(bf16[12,128,128]{2,1,0:T(8,128)(2,1)S(1)} %collective-permute-done.3.rest_3_), channel_id=1, source_target_pairs={{0,1},{1,0},{2,3},{3,2},{4,5},{5,4},{6,7},{7,6},{8,9},{9,8},{10,11... | collective-permute-start | bytes 1179656 | tf_op jit(solution)/shard_map/ppermute | solution.py:309
  42.6 8.4 %collective-permute-start.7 = (bf16[12,128,128]{2,1,0:T(8,128)(2,1)S(1)}, bf16[12,128,128]{2,1,0:T(8,128)(2,1)S(1)}, u32[]{:S(2)}, u32[]{:S(2)}) collective-permute-start(bf16[12,128,128]{2,1,0:T(8,128)(2,1)S(1)} %collective-permute-done.5.rest_5_), channel_id=1, source_target_pairs={{0,2},{1,15},{2,4},{3,1},{4,6},{5,3},{6,8},{7,5},{8,10},{9,7},{10,... | collective-permute-start | bytes 1179656 | tf_op jit(solution)/shard_map/ppermute | solution.py:299
  46.5 8.7 %collective-permute-start.8 = (bf16[12,128,128]{2,1,0:T(8,128)(2,1)S(1)}, bf16[12,128,128]{2,1,0:T(8,128)(2,1)S(1)}, u32[]{:S(2)}, u32[]{:S(2)}) collective-permute-start(bf16[12,128,128]{2,1,0:T(8,128)(2,1)S(1)} %collective-permute-done.6.rest_6_), channel_id=1, source_target_pairs={{0,2},{1,15},{2,4},{3,1},{4,6},{5,3},{6,8},{7,5},{8,10},{9,7},{10,... | collective-permute-start | bytes 1179656 | tf_op jit(solution)/shard_map/ppermute | solution.py:299
  48.2 8.1 %collective-permute-start.13 = (bf16[12,128,128]{2,1,0:T(8,128)(2,1)S(1)}, bf16[12,128,128]{2,1,0:T(8,128)(2,1)S(1)}, u32[]{:S(2)}, u32[]{:S(2)}) collective-permute-start(bf16[12,128,128]{2,1,0:T(8,128)(2,1)S(1)} %collective-permute-done.4.rest_4_), channel_id=1, source_target_pairs={{0,1},{1,0},{2,3},{3,2},{4,5},{5,4},{6,7},{7,6},{8,9},{9,8},{10,11... | collective-permute-start | bytes 1179656 | tf_op jit(solution)/shard_map/ppermute | solution.py:309
  48.3 8.1 %collective-permute-start.12 = (bf16[12,128,128]{2,1,0:T(8,128)(2,1)S(1)}, bf16[12,128,128]{2,1,0:T(8,128)(2,1)S(1)}, u32[]{:S(2)}, u32[]{:S(2)}) collective-permute-start(bf16[12,128,128]{2,1,0:T(8,128)(2,1)S(1)} %collective-permute-done.5.rest_5_), channel_id=1, source_target_pairs={{0,1},{1,0},{2,3},{3,2},{4,5},{5,4},{6,7},{7,6},{8,9},{9,8},{10,11... | collective-permute-start | bytes 1179656 | tf_op jit(solution)/shard_map/ppermute | solution.py:309
  48.8 7.6 %collective-permute-start.11 = (bf16[12,128,128]{2,1,0:T(8,128)(2,1)S(1)}, bf16[12,128,128]{2,1,0:T(8,128)(2,1)S(1)}, u32[]{:S(2)}, u32[]{:S(2)}) collective-permute-start(bf16[12,128,128]{2,1,0:T(8,128)(2,1)S(1)} %collective-permute-done.6.rest_6_), channel_id=1, source_target_pairs={{0,1},{1,0},{2,3},{3,2},{4,5},{5,4},{6,7},{7,6},{8,9},{9,8},{10,11... | collective-permute-start | bytes 1179656 | tf_op jit(solution)/shard_map/ppermute | solution.py:309
  51.0 5.4 %collective-permute-start.10 = (bf16[12,128,128]{2,1,0:T(8,128)(2,1)S(1)}, bf16[12,128,128]{2,1,0:T(8,128)(2,1)S(1)}, u32[]{:S(2)}, u32[]{:S(2)}) collective-permute-start(bf16[12,128,128]{2,1,0:T(8,128)(2,1)S(1)} %collective-permute-done.7.rest_7_), channel_id=1, source_target_pairs={{0,1},{1,0},{2,3},{3,2},{4,5},{5,4},{6,7},{7,6},{8,9},{9,8},{10,11... | collective-permute-start | bytes 1179656 | tf_op jit(solution)/shard_map/ppermute | solution.py:309
  55.2 1.8 %collective-permute-start.9 = (bf16[12,128,128]{2,1,0:T(8,128)(2,1)S(1)}, bf16[12,128,128]{2,1,0:T(8,128)(2,1)S(1)}, u32[]{:S(2)}, u32[]{:S(2)}) collective-permute-start(bf16[12,128,128]{2,1,0:T(8,128)(2,1)S(1)} %collective-permute-done.8.rest_8_), channel_id=1, source_target_pairs={{0,1},{1,0},{2,3},{3,2},{4,5},{5,4},{6,7},{7,6},{8,9},{9,8},{10,11... | collective-permute-start | bytes 1179656 | tf_op jit(solution)/shard_map/ppermute | solution.py:309
  74.9 1.5 %collective-permute-start.16 = (f32[4,128]{1,0:T(4,128)}, f32[4,128]{1,0:T(4,128)S(1)}, u32[]{:S(2)}, u32[]{:S(2)}) collective-permute-start(f32[4,128]{1,0:T(4,128)} %get-tuple-element.21.mine_ref), channel_id=1, source_target_pairs={{0,1},{1,0},{2,3},{3,2},{4,5},{5,4},{6,7},{7,6},{8,9},{9,8},{10,11... | collective-permute-start | bytes 6152 | tf_op jit(solution)/shard_map/ppermute | solution.py:294
  76.9 3.0 %collective-permute-start.17 = (f32[4,128]{1,0:T(4,128)S(1)}, f32[4,128]{1,0:T(4,128)S(1)}, u32[]{:S(2)}, u32[]{:S(2)}) collective-permute-start(f32[4,128]{1,0:T(4,128)S(1)} %add.28), channel_id=1, source_target_pairs={{0,3},{1,2},{2,1},{3,0},{4,7},{5,6},{6,5},{7,4},{8,11},{9,10},{10,... | collective-permute-start | bytes 6152 | tf_op jit(solution)/shard_map/ppermute | solution.py:294
  80.0 3.9 %collective-permute-start.18 = (f32[4,128]{1,0:T(4,128)S(1)}, f32[4,128]{1,0:T(4,128)S(1)}, u32[]{:S(2)}, u32[]{:S(2)}) collective-permute-start(f32[4,128]{1,0:T(4,128)S(1)} %add.29), channel_id=1, source_target_pairs={{0,5},{1,4},{2,7},{3,6},{4,1},{5,0},{6,3},{7,2},{8,13},{9,12},{10,... | collective-permute-start | bytes 6152 | tf_op jit(solution)/shard_map/ppermute | solution.py:294
  83.9 5.1 %collective-permute-start.19 = (f32[4,128]{1,0:T(4,128)S(1)}, f32[4,128]{1,0:T(4,128)S(1)}, u32[]{:S(2)}, u32[]{:S(2)}) collective-permute-start(f32[4,128]{1,0:T(4,128)S(1)} %add.30), channel_id=1, source_target_pairs={{0,13},{1,12},{2,15},{3,14},{4,9},{5,8},{6,11},{7,10},{8,5},{9,4},... | collective-permute-start | bytes 6152 | tf_op jit(solution)/shard_map/ppermute | solution.py:294
  91.0 4.8 %collective-permute-start.20 = (f32[2,128]{1,0:T(2,128)}, f32[2,128]{1,0:T(2,128)S(1)}, u32[]{:S(2)}, u32[]{:S(2)}) collective-permute-start(f32[2,128]{1,0:T(2,128)} %get-tuple-element.22), channel_id=1, source_target_pairs={{0,17},{1,16},{2,19},{3,18},{4,21},{5,20},{6,23},{7,22},{8,25},{9,... | collective-permute-start | bytes 3080 | tf_op jit(solution)/shard_map/ppermute | solution.py:294
  95.8 4.3 %collective-permute-start.21 = (f32[2,128]{1,0:T(2,128)S(1)}, f32[2,128]{1,0:T(2,128)S(1)}, u32[]{:S(2)}, u32[]{:S(2)}) collective-permute-start(f32[2,128]{1,0:T(2,128)S(1)} %add.32), channel_id=1, source_target_pairs={{0,49},{1,48},{2,51},{3,50},{4,53},{5,52},{6,55},{7,54},{8,57},{9,... | collective-permute-start | bytes 3080 | tf_op jit(solution)/shard_map/ppermute | solution.py:294
  100.1 3.9 %collective-permute-start.22 = (f32[2,128]{1,0:T(2,128)S(1)}, f32[2,128]{1,0:T(2,128)S(1)}, u32[]{:S(2)}, u32[]{:S(2)}) collective-permute-start(f32[2,128]{1,0:T(2,128)S(1)} %add.34), channel_id=1, source_target_pairs={{0,65},{1,64},{2,67},{3,66},{4,69},{5,68},{6,71},{7,70},{8,73},{9,... | collective-permute-start | bytes 3080 | tf_op jit(solution)/shard_map/ppermute | solution.py:294
  104.0 4.4 %collective-permute-start.23 = (f32[2,128]{1,0:T(2,128)S(1)}, f32[2,128]{1,0:T(2,128)S(1)}, u32[]{:S(2)}, u32[]{:S(2)}) collective-permute-start(f32[2,128]{1,0:T(2,128)S(1)} %add.35), channel_id=1, source_target_pairs={{0,193},{1,192},{2,195},{3,194},{4,197},{5,196},{6,199},{7,198},{8... | collective-permute-start | bytes 3080 | tf_op jit(solution)/shard_map/ppermute | solution.py:294
  (18 other events, 210.7 us)

commit v6 on v5

--- a/solution.py
+++ b/solution.py
@@ -13,7 +13,9 @@
 
 LOCAL = 4
 BLOCKS = 16
+CHUNK = 32
 FINISH = 4
+LATEST = (9, 10)
 VMEM_LIMIT = 60 * 2**20
 
 
@@ -48,28 +50,31 @@
 def spread(xt_ref, renv_ref, mpo, x3_ref, begin=0, done=None):
     states, pairs, width = xt_ref.shape
     bonds = renv_ref.shape[0]
-    for at in range(begin, states, 16):
-        xa = xt_ref[at : at + 16].reshape(16 * pairs, width)
-        first = []
-        for k in range(bonds // 2):
-            both = jnp.concatenate([renv_ref[2 * k], renv_ref[2 * k + 1]], axis=1)
-            got = jnp.dot(xa, both, preferred_element_type=F32).astype(BF16)
-            first += [got[:, :width], got[:, width:]]
-        rows = []
-        for i in range(8):
-            sides = []
-            for a in (2 * i, 2 * i + 1):
-                sides.append(jnp.concatenate([f[a * pairs : (a + 1) * pairs] for f in first], axis=0))
-            out = jnp.dot(mpo, jnp.concatenate(sides, axis=1), preferred_element_type=F32).astype(BF16)
-            rows += [out[:, :width], out[:, width:]]
-        for l in range(bonds):
-            block = jnp.stack([row[l * pairs : (l + 1) * pairs] for row in rows], axis=0)
-            x3_ref[:, l, at : at + 16, :] = jnp.swapaxes(block, 0, 1)
+    beside = jnp.concatenate([renv_ref[w] for w in range(bonds)], axis=1)
+    for start in range(begin, states, CHUNK):
+        xa = xt_ref[start : start + CHUNK].reshape(CHUNK * pairs, width)
+        first = jnp.dot(xa, beside, preferred_element_type=F32).astype(BF16)
+        for at in range(0, CHUNK, 16):
+            rows = []
+            for i in range(at, at + 16, 2):
+                sides = []
+                for a in (i, i + 1):
+                    row = first[a * pairs : (a + 1) * pairs]
+                    sides.append(jnp.concatenate([row[:, w * width : (w + 1) * width] for w in range(bonds)], axis=0))
+                out = jnp.dot(mpo, jnp.concatenate(sides, axis=1), preferred_element_type=F32).astype(BF16)
+                rows += [out[:, :width], out[:, width:]]
+            for l in range(bonds):
+                block = jnp.stack([row[l * pairs : (l + 1) * pairs] for row in rows], axis=0)
+                x3_ref[:, l, start + at : start + at + 16, :] = jnp.swapaxes(block, 0, 1)
         if done is not None:
-            done(at)
-
-
-def front_kernel(psi_any, renv_any, left_ref, right_ref, x3_any, mpo_ref, psi_ref, renv_ref, xt_ref, x3_ref, sem_ref, out_sem):
+            done(start)
+
+
+def operators_kernel(left_ref, right_ref, mpo_ref):
+    mpo_ref[...] = pair_mpo(left_ref, right_ref)
+
+
+def front_kernel(psi_any, renv_any, left_ref, right_ref, x3_any, psi_ref, renv_ref, xt_ref, x3_ref, sem_ref, out_sem):
     copies = [
         pltpu.make_async_copy(psi_any.at[:, pl.ds(0, psi_ref.shape[1])], psi_ref, sem_ref.at[0]),
         pltpu.make_async_copy(renv_any, renv_ref, sem_ref.at[1]),
@@ -77,15 +82,14 @@
     for copy in copies:
         copy.start()
     mpo = pair_mpo(left_ref, right_ref)
-    mpo_ref[...] = mpo
     for copy in copies:
         copy.wait()
     turn(psi_ref, xt_ref)
     sent = []
 
     def done(at):
-        rows = pl.ds(at, 16)
-        sent.append(pltpu.make_async_copy(x3_ref.at[:, :, rows], x3_any.at[:, :, rows], out_sem.at[at // 16]))
+        rows = pl.ds(at, CHUNK)
+        sent.append(pltpu.make_async_copy(x3_ref.at[:, :, rows], x3_any.at[:, :, rows], out_sem.at[at // CHUNK]))
         sent[-1].start()
 
     spread(xt_ref, renv_ref, mpo, x3_ref, 0, done)
@@ -95,13 +99,13 @@
 
 def contract(lenv_ref, slot, x3_ref, q):
     bonds = lenv_ref.shape[1]
-    total = None
-    for k in range(bonds // 2):
-        lhs = jnp.concatenate([lenv_ref[slot, 2 * k], lenv_ref[slot, 2 * k + 1]], axis=1)
-        rhs = jnp.concatenate([x3_ref[q, 2 * k], x3_ref[q, 2 * k + 1]], axis=0)
-        part = jnp.dot(lhs, rhs, preferred_element_type=F32)
-        total = part if total is None else total + part
-    return total
+    lhs = jnp.concatenate([lenv_ref[slot, l] for l in range(bonds)], axis=1)
+    rhs = jnp.concatenate([x3_ref[q, l] for l in range(bonds)], axis=0)
+    return jnp.dot(lhs, rhs, preferred_element_type=F32)
+
+
+def folded(value):
+    return jnp.sum(value.reshape(value.shape[0] // 8, 8, value.shape[1]), axis=0)
 
 
 def slot_of(charge_ref, q):
@@ -129,7 +133,7 @@
         copy.start()
     slots = [slot_of(charge_ref, q) for q in range(pairs)]
     keep = iota((width, width), 1) < rank_ref[0]
-    zero = jnp.zeros((width, width), F32)
+    zero = jnp.zeros((8, width), F32)
     for copy in first:
         copy.wait()
     turn(psi_ref, xt_ref)
@@ -141,7 +145,7 @@
         h = contract(lenv_ref, slots[q], x3_ref, q)
         u = jnp.where(keep, psi_ref[q].astype(F32) - 0.5 * h, 0.0)
         u_ref[q] = u.astype(BF16)
-        first_sq = first_sq + u * u
+        first_sq = first_sq + folded(u * u)
     turn(u_ref, xt_ref)
     spread(xt_ref, renv_ref, mpo_ref[...], x3_ref)
     sq, inner, own = zero, zero, zero
@@ -153,16 +157,17 @@
         v_ref[q] = v
         sent.append(pltpu.make_async_copy(v_ref.at[q], v_any.at[q], v_sem.at[q]))
         sent[-1].start()
-        sq, inner, own = sq + v * v, inner + x * h, own + x * x
+        sq, inner, own = sq + folded(v * v), inner + folded(x * h), own + folded(x * x)
     for i, part in enumerate((first_sq, sq, inner, own)):
         stat_ref[i : i + 1] = jnp.sum(part, axis=0, keepdims=True)
     for copy in sent:
         copy.wait()
 
 
-def settle_kernel(count, total_ref, mine_ref, twin_ref, share_ref, out_ref):
-    width = total_ref.shape[1]
-    first_sq, sq, inner, own = [jnp.sum(total_ref[i : i + 1], axis=1, keepdims=True) for i in range(4)]
+def settle_kernel(count, half_ref, other_ref, mine_ref, twin_ref, share_ref, out_ref):
+    width = half_ref.shape[1]
+    total = jnp.sum(half_ref[...] + other_ref[...], axis=1, keepdims=True)
+    first_sq, sq, inner, own = [total[i : i + 1] for i in range(4)]
     one = lax.rsqrt(first_sq / count + 1e-06)
     scale = one * lax.rsqrt(one * one * sq / count + 1e-06)
     out_ref[...] = jnp.where(iota((8, width), 0) == 0, scale, inner / own)
@@ -211,24 +216,36 @@
     )
 
 
+def operators(left, right):
+    rows = left.shape[0]
+    return call(
+        operators_kernel,
+        "operators",
+        10**8,
+        jax.ShapeDtypeStruct((rows, rows), BF16),
+        [VMEM_SPEC, VMEM_SPEC],
+        VMEM_SPEC,
+        [],
+    )(left, right)
+
+
 def front(psi, renv, left, right, states):
     pairs, width = psi.shape[0], psi.shape[2]
     bonds = renv.shape[0]
-    rows = bonds * pairs
     return call(
         front_kernel,
         "front",
         5 * 10**8,
-        (jax.ShapeDtypeStruct((pairs, bonds, states, width), BF16), jax.ShapeDtypeStruct((rows, rows), BF16)),
+        jax.ShapeDtypeStruct((pairs, bonds, states, width), BF16),
         [ANY_SPEC, ANY_SPEC, VMEM_SPEC, VMEM_SPEC],
-        (ANY_SPEC, VMEM_SPEC),
+        ANY_SPEC,
         [
             pltpu.VMEM((pairs, states, width), BF16),
             pltpu.VMEM((bonds, width, width), BF16),
             pltpu.VMEM((states, pairs, width), BF16),
             pltpu.VMEM((pairs, bonds, states, width), BF16),
             pltpu.SemaphoreType.DMA((2,)),
-            pltpu.SemaphoreType.DMA((states // 16,)),
+            pltpu.SemaphoreType.DMA((states // CHUNK,)),
         ],
     )(psi, renv, left, right)
 
@@ -241,7 +258,8 @@
         "back",
         4 * 10**9,
         (jax.ShapeDtypeStruct((pairs, width, width), F32), jax.ShapeDtypeStruct((4, width), F32)),
-        [SMEM_SPEC, SMEM_SPEC, ANY_SPEC, ANY_SPEC, VMEM_SPEC, ANY_SPEC] + [ANY_SPEC] * BLOCKS,
+        [SMEM_SPEC, SMEM_SPEC, ANY_SPEC, ANY_SPEC, VMEM_SPEC, ANY_SPEC]
+        + [VMEM_SPEC if i in LATEST else ANY_SPEC for i in range(BLOCKS)],
         (ANY_SPEC, VMEM_SPEC),
         [
             pltpu.VMEM((BLOCKS, bonds, width, width), BF16),
@@ -258,17 +276,17 @@
     )(charge, rank, psi, renv, mpo, x3, *blocks)
 
 
-def settle(total, mine, twin_stat, count):
-    width = total.shape[1]
+def settle(half, other, mine, twin_stat, count):
+    width = half.shape[1]
     return call(
         functools.partial(settle_kernel, count),
         "settle",
         10**4,
         (jax.ShapeDtypeStruct((2, width), F32), jax.ShapeDtypeStruct((8, width), F32)),
-        [VMEM_SPEC] * 3,
+        [VMEM_SPEC] * 4,
         (VMEM_SPEC, VMEM_SPEC),
         [],
-    )(total, mine, twin_stat)
+    )(half, other, mine, twin_stat)
 
 
 def finish(v, out):
@@ -327,12 +345,14 @@
     moved = from_behind(env)
     tall = (site_left.shape[0] * pairs, site_left.shape[1])
     ends = (site_left.transpose(0, 2, 3, 1).reshape(tall), site_right.transpose(0, 2, 3, 1).reshape(tall))
+    x3 = front(x, renv, *ends, width // 4)
+    moved, x3 = lax.optimization_barrier((moved, x3))
     own = jnp.where(segment == 0, env, moved)
 
     o1 = hop(own)
-    waited, x_then = lax.optimization_barrier((own, x))
-    x3, mpo = front(x_then, renv, *ends, width // 4)
-    waited, x3 = lax.optimization_barrier((waited, x3))
+    waited, ends = lax.optimization_barrier((own, ends))
+    mpo = operators(*ends)
+    waited, mpo = lax.optimization_barrier((waited, mpo))
     t1 = cross_hop(waited)
     o2 = hop(o1)
     t2 = hop(t1)
@@ -345,9 +365,9 @@
 
     twin_stat = partner(stat, 1)
     total = stat + twin_stat
-    for bits in (3, 5, 13):
+    for bits in (3, 5):
         total = total + partner(total, bits)
-    share, out = settle(total, stat, twin_stat, count)
+    share, out = settle(total, partner(total, 13), stat, twin_stat, count)
     state = finish(v, out)
     for bits in (1, 3, 4, 12):
         share = share + partner(share, nsec * bits + 1)

time: 109 us -> 109 us (level)
  waiting for transfers between devices: 42 us -> 27.3 us
  starting transfers between devices: 34.7 us -> 48.8 us
  other arithmetic: 2.95 us -> 1.42 us
    ppermute x8, starting transfers between devices: 1.98 us -> 16.5 us  [twin(): return lax.ppermute(value, 'sec', [(i, i ^ 1) for i in range(n)])]
    ppermute x6, waiting for transfers between devices: 12.7 us -> 4.74 us  [hop(): lax.ppermute(value, 'sec', [(i, (i + (2 if i % 2 == 0 else -2)) % n) for...]
    ppermute x1, waiting for transfers between devices: 8.43 us -> 2.74 us  [cross_hop(): lax.ppermute(value, 'sec', [(i, (i + (-2 if i % 2 == 0 else 2)) % n ^ 1)...]
    ppermute x1, waiting for transfers between devices: 8.05 us -> 3.66 us  [from_behind(): return lax.ppermute(value, 'seg', [(i, i + 1) for i in range(n - 1)])]
    ppermute x8, waiting for transfers between devices: 12.2 us -> 16.1 us  [partner(): return lax.ppermute(value, axes, [(i, i ^ bits) for i in range(n)])]
    ppermute x8, starting transfers between devices: 14.9 us -> 11.2 us  [partner(): return lax.ppermute(value, axes, [(i, i ^ bits) for i in range(n)])]
    ppermute x6, starting transfers between devices: 13.7 us -> 17 us  [hop(): lax.ppermute(value, 'sec', [(i, (i + (2 if i % 2 == 0 else -2)) % n) for...]
    pallas_call x1 -> x2, Pallas kernels: 4.93 us -> 6.57 us  [the longest x1 4.38 us: front(): call(front_kernel, 'front', 5 * 10 ** 8, jax.ShapeDtypeStruct((pairs, bon...]
  transfers between devices with their start and end apart: 24 -> 24, of which waited for: 13 -> 11; matrix products, arithmetic and copies ran while one was open for 1% -> 1% of each run, Pallas kernels for 7% -> 8%
where the time goes in v6:
time: 109 us
  starting transfers between devices  48.8 us (45%)
  waiting for transfers between devices  27.3 us (25%)
  Pallas kernels  26.1 us (24%)
  local copies, waits for them, and re-layouts  3.53 us (3%)
  between operations  1.54 us (1%)
  other arithmetic  1.42 us (1%)
    ppermute x6, starting transfers between devices, hop(): lax.ppermute(value, 'sec', [(i, (i + (2 if i % 2 == 0 else -2)) % n) for...  17 us
    ppermute x8, starting transfers between devices, twin(): return lax.ppermute(value, 'sec', [(i, i ^ 1) for i in range(n)])  16.5 us
    ppermute x8, waiting for transfers between devices, partner(): return lax.ppermute(value, axes, [(i, i ^ bits) for i in range(n)])  16.1 us
    pallas_call x1, Pallas kernels, back(): call(back_kernel, 'back', 4 * 10 ** 9, (jax.ShapeDtypeStruct((pairs, widt...  15.5 us
    ppermute x8, starting transfers between devices, partner(): return lax.ppermute(value, axes, [(i, i ^ bits) for i in range(n)])  11.2 us
    ppermute x6, waiting for transfers between devices, hop(): lax.ppermute(value, 'sec', [(i, (i + (2 if i % 2 == 0 else -2)) % n) for...  4.74 us
    pallas_call x1, Pallas kernels, front(): call(front_kernel, 'front', 5 * 10 ** 8, jax.ShapeDtypeStruct((pairs, bon...  4.38 us
    ppermute x1, starting transfers between devices, from_behind(): return lax.ppermute(value, 'seg', [(i, i + 1) for i in range(n - 1)])  4.1 us
  transfers between devices with their start and end apart: 24, of which 11 were waited for; matrix products, arithmetic and copies ran while one was open for 1% of the time, Pallas kernels for 8%

profile of v6, /device:TPU:1, one launch (start us, length us, event | category | flops | bytes accessed | tf_op | source)
XLA Modules:
  0.0 108.7 jit_solution(8895690641710248358)
XLA Ops:
  0.6 4.1 %collective-permute-start = (bf16[12,128,128]{2,1,0:T(8,128)(2,1)}, bf16[12,128,128]{2,1,0:T(8,128)(2,1)S(1)}, u32[]{:S(2)}, u32[]{:S(2)}) collective-permute-start(bf16[12,128,128]{2,1,0:T(8,128)(2,1)} %bitcast.18), channel_id=1, source_target_pairs={{0,16},{16,32},{32,48},{48,64},{64,80},{80,96},{96,112},{112,128},... | collective-permute-start | bytes 1179656 | tf_op jit(solution)/shard_map/ppermute | solution.py:332
  4.8 4.4 %front.1.x3_any = bf16[16,12,32,128]{3,2,1,0:T(8,128)(2,1)} custom-call(bf16[16,128,128]{2,1,0:T(8,128)(2,1)} %bitcast.13, bf16[12,128,128]{2,1,0:T(8,128)(2,1)} %bitcast.16, bf16[192,12]{1,0:T(8,128)(2,1)} %bitcast.19, bf16[192,12]{1,0:T(8,128)(2,1)} %bitcast.21), custom_call_target="tpu_custom_call" | custom-call | flops 500000000 | bytes 8000000 | tf_op jit(solution)/shard_map/front/pallas_call | solution.py:235
  9.1 3.7 %collective-permute-done = bf16[12,128,128]{2,1,0:T(8,128)(2,1)S(1)} collective-permute-done((bf16[12,128,128]{2,1,0:T(8,128)(2,1)}, bf16[12,128,128]{2,1,0:T(8,128)(2,1)S(1)}, u32[]{:S(2)}, u32[]{:S(2)}) %collective-permute-start) | collective-permute-done | bytes 393248 | tf_op jit(solution)/shard_map/ppermute | solution.py:332
  12.9 5.7 %collective-permute-start.2 = (bf16[12,128,128]{2,1,0:T(8,128)(2,1)S(1)}, bf16[12,128,128]{2,1,0:T(8,128)(2,1)S(1)}, u32[]{:S(2)}, u32[]{:S(2)}) collective-permute-start(bf16[12,128,128]{2,1,0:T(8,128)(2,1)S(1)} %broadcast_select_fusion.rest_0_), channel_id=1, source_target_pairs={{0,2},{1,15},{2,4},{3,1},{4,6},{5,3},{6,8},{7,5},{8,10},{9,7},{10,... | collective-permute-start | bytes 1179656 | tf_op jit(solution)/shard_map/ppermute | solution.py:317
  18.5 2.2 %operators.1.mpo_ref = bf16[192,192]{1,0:T(8,128)(2,1)} custom-call(bf16[192,12]{1,0:T(8,128)(2,1)} %bitcast.20, bf16[192,12]{1,0:T(8,128)(2,1)} %bitcast.22), custom_call_target="tpu_custom_call" | custom-call | flops 100000000 | bytes 8000000 | tf_op jit(solution)/shard_map/operators/pallas_call | solution.py:221
  20.7 3.2 %collective-permute-done.2.rest_2_ = bf16[12,128,128]{2,1,0:T(8,128)(2,1)S(1)} collective-permute-done((bf16[12,128,128]{2,1,0:T(8,128)(2,1)S(1)}, bf16[12,128,128]{2,1,0:T(8,128)(2,1)S(1)}, u32[]{:S(2)}, u32[]{:S(2)}) %collective-permute-start.2) | collective-permute-done | bytes 393248 | tf_op jit(solution)/shard_map/ppermute | solution.py:317
  23.9 3.1 %collective-permute-start.4 = (bf16[12,128,128]{2,1,0:T(8,128)(2,1)S(1)}, bf16[12,128,128]{2,1,0:T(8,128)(2,1)S(1)}, u32[]{:S(2)}, u32[]{:S(2)}) collective-permute-start(bf16[12,128,128]{2,1,0:T(8,128)(2,1)S(1)} %collective-permute-done.2.rest_2_), channel_id=1, source_target_pairs={{0,2},{1,15},{2,4},{3,1},{4,6},{5,3},{6,8},{7,5},{8,10},{9,7},{10,... | collective-permute-start | bytes 1179656 | tf_op jit(solution)/shard_map/ppermute | solution.py:317
  27.0 2.7 %collective-permute-done.3.rest_3_ = bf16[12,128,128]{2,1,0:T(8,128)(2,1)S(1)} collective-permute-done((bf16[12,128,128]{2,1,0:T(8,128)(2,1)S(1)}, bf16[12,128,128]{2,1,0:T(8,128)(2,1)S(1)}, u32[]{:S(2)}, u32[]{:S(2)}) %collective-permute-start.3) | collective-permute-done | bytes 393248 | tf_op jit(solution)/shard_map/ppermute | solution.py:322
  32.1 2.7 %collective-permute-start.6 = (bf16[12,128,128]{2,1,0:T(8,128)(2,1)S(1)}, bf16[12,128,128]{2,1,0:T(8,128)(2,1)S(1)}, u32[]{:S(2)}, u32[]{:S(2)}) collective-permute-start(bf16[12,128,128]{2,1,0:T(8,128)(2,1)S(1)} %collective-permute-done.4.rest_4_), channel_id=1, source_target_pairs={{0,2},{1,15},{2,4},{3,1},{4,6},{5,3},{6,8},{7,5},{8,10},{9,7},{10,... | collective-permute-start | bytes 1179656 | tf_op jit(solution)/shard_map/ppermute | solution.py:317
  34.8 3.2 %collective-permute-start.1 = (bf16[12,128,128]{2,1,0:T(8,128)(2,1)S(1)}, bf16[12,128,128]{2,1,0:T(8,128)(2,1)S(1)}, u32[]{:S(2)}, u32[]{:S(2)}) collective-permute-start(bf16[12,128,128]{2,1,0:T(8,128)(2,1)S(1)} %broadcast_select_fusion.rest_0_), channel_id=1, source_target_pairs={{0,1},{1,0},{2,3},{3,2},{4,5},{5,4},{6,7},{7,6},{8,9},{9,8},{10,11... | collective-permute-start | bytes 1179656 | tf_op jit(solution)/shard_map/ppermute | solution.py:327
  38.6 3.0 %collective-permute-start.7 = (bf16[12,128,128]{2,1,0:T(8,128)(2,1)S(1)}, bf16[12,128,128]{2,1,0:T(8,128)(2,1)S(1)}, u32[]{:S(2)}, u32[]{:S(2)}) collective-permute-start(bf16[12,128,128]{2,1,0:T(8,128)(2,1)S(1)} %collective-permute-done.5.rest_5_), channel_id=1, source_target_pairs={{0,2},{1,15},{2,4},{3,1},{4,6},{5,3},{6,8},{7,5},{8,10},{9,7},{10,... | collective-permute-start | bytes 1179656 | tf_op jit(solution)/shard_map/ppermute | solution.py:317
  43.3 3.9 %collective-permute-start.12 = (bf16[12,128,128]{2,1,0:T(8,128)(2,1)S(1)}, bf16[12,128,128]{2,1,0:T(8,128)(2,1)S(1)}, u32[]{:S(2)}, u32[]{:S(2)}) collective-permute-start(bf16[12,128,128]{2,1,0:T(8,128)(2,1)S(1)} %collective-permute-done.5.rest_5_), channel_id=1, source_target_pairs={{0,1},{1,0},{2,3},{3,2},{4,5},{5,4},{6,7},{7,6},{8,9},{9,8},{10,11... | collective-permute-start | bytes 1179656 | tf_op jit(solution)/shard_map/ppermute | solution.py:327
  47.7 3.6 %collective-permute-start.10 = (bf16[12,128,128]{2,1,0:T(8,128)(2,1)S(1)}, bf16[12,128,128]{2,1,0:T(8,128)(2,1)S(1)}, u32[]{:S(2)}, u32[]{:S(2)}) collective-permute-start(bf16[12,128,128]{2,1,0:T(8,128)(2,1)S(1)} %collective-permute-done.7.rest_7_), channel_id=1, source_target_pairs={{0,1},{1,0},{2,3},{3,2},{4,5},{5,4},{6,7},{7,6},{8,9},{9,8},{10,11... | collective-permute-start | bytes 1179656 | tf_op jit(solution)/shard_map/ppermute | solution.py:327
  51.3 4.8 %collective-permute-start.9 = (bf16[12,128,128]{2,1,0:T(8,128)(2,1)S(1)}, bf16[12,128,128]{2,1,0:T(8,128)(2,1)}, u32[]{:S(2)}, u32[]{:S(2)}) collective-permute-start(bf16[12,128,128]{2,1,0:T(8,128)(2,1)S(1)} %collective-permute-done.8.rest_8_), channel_id=1, source_target_pairs={{0,1},{1,0},{2,3},{3,2},{4,5},{5,4},{6,7},{7,6},{8,9},{9,8},{10,11... | collective-permute-start | bytes 1179656 | tf_op jit(solution)/shard_map/ppermute | solution.py:327
  58.6 15.5 %back.1 = (f32[16,128,128]{2,1,0:T(8,128)}, f32[4,128]{1,0:T(4,128)}) custom-call(s32[16]{0:T(128)} %charge_ref.1, s32[1]{0:T(128)S(6)} %copy.10.rank_ref, bf16[16,128,128]{2,1,0:T(8,128)(2,1)} %bitcast.14, bf16[12,128,128]{2,1,0:T(8,128)(2,1)} %bitcast.17, bf16[192,192]{1,0:T(8,128)(2,1)} %operators.1.mpo_ref, bf16[16,12,32,128]{3,2,1,0:T(8,128)(2,1)} %front.1.x3_any, ...), custom_call_target="tpu_custom_call" | custom-call | flops 4000000000 | bytes 8000000 | tf_op jit(solution)/shard_map/back/pallas_call | solution.py:256
  76.5 3.0 %collective-permute-done.17 = f32[4,128]{1,0:T(4,128)S(1)} collective-permute-done((f32[4,128]{1,0:T(4,128)S(1)}, f32[4,128]{1,0:T(4,128)S(1)}, u32[]{:S(2)}, u32[]{:S(2)}) %collective-permute-start.17) | collective-permute-done | bytes 2080 | tf_op jit(solution)/shard_map/ppermute | solution.py:312
  79.5 3.9 %collective-permute-done.18 = f32[4,128]{1,0:T(4,128)S(1)} collective-permute-done((f32[4,128]{1,0:T(4,128)S(1)}, f32[4,128]{1,0:T(4,128)S(1)}, u32[]{:S(2)}, u32[]{:S(2)}) %collective-permute-start.18) | collective-permute-done | bytes 2080 | tf_op jit(solution)/shard_map/ppermute | solution.py:312
  84.2 4.4 %collective-permute-done.19.other_ref = f32[4,128]{1,0:T(4,128)S(1)} collective-permute-done((f32[4,128]{1,0:T(4,128)S(1)}, f32[4,128]{1,0:T(4,128)S(1)}, u32[]{:S(2)}, u32[]{:S(2)}) %collective-permute-start.19) | collective-permute-done | bytes 2080 | tf_op jit(solution)/shard_map/ppermute | solution.py:312
  90.5 2.2 %collective-permute-start.20 = (f32[2,128]{1,0:T(2,128)}, f32[2,128]{1,0:T(2,128)S(1)}, u32[]{:S(2)}, u32[]{:S(2)}) collective-permute-start(f32[2,128]{1,0:T(2,128)} %get-tuple-element.24), channel_id=1, source_target_pairs={{0,17},{1,16},{2,19},{3,18},{4,21},{5,20},{6,23},{7,22},{8,25},{9,... | collective-permute-start | bytes 3080 | tf_op jit(solution)/shard_map/ppermute | solution.py:312
  92.7 2.6 %finish.1 = bf16[16,128,128]{2,1,0:T(8,128)(2,1)} custom-call(f32[16,128,128]{2,1,0:T(8,128)} %get-tuple-element.25.v_any, f32[8,128]{1,0:T(8,128)} %get-tuple-element.26.out_ref), custom_call_target="tpu_custom_call" | custom-call | flops 1000000 | bytes 8000000 | tf_op jit(solution)/shard_map/finish/pallas_call | solution.py:293
  95.4 2.1 %collective-permute-start.21 = (f32[2,128]{1,0:T(2,128)S(1)}, f32[2,128]{1,0:T(2,128)S(1)}, u32[]{:S(2)}, u32[]{:S(2)}) collective-permute-start(f32[2,128]{1,0:T(2,128)S(1)} %add.28), channel_id=1, source_target_pairs={{0,49},{1,48},{2,51},{3,50},{4,53},{5,52},{6,55},{7,54},{8,57},{9,... | collective-permute-start | bytes 3080 | tf_op jit(solution)/shard_map/ppermute | solution.py:312
  97.5 2.2 %collective-permute-done.21 = f32[2,128]{1,0:T(2,128)S(1)} collective-permute-done((f32[2,128]{1,0:T(2,128)S(1)}, f32[2,128]{1,0:T(2,128)S(1)}, u32[]{:S(2)}, u32[]{:S(2)}) %collective-permute-start.21) | collective-permute-done | bytes 1056 | tf_op jit(solution)/shard_map/ppermute | solution.py:312
  99.7 2.7 %collective-permute-start.22 = (f32[2,128]{1,0:T(2,128)S(1)}, f32[2,128]{1,0:T(2,128)S(1)}, u32[]{:S(2)}, u32[]{:S(2)}) collective-permute-start(f32[2,128]{1,0:T(2,128)S(1)} %add.30), channel_id=1, source_target_pairs={{0,65},{1,64},{2,67},{3,66},{4,69},{5,68},{6,71},{7,70},{8,73},{9,... | collective-permute-start | bytes 3080 | tf_op jit(solution)/shard_map/ppermute | solution.py:312
  103.6 3.2 %collective-permute-start.23 = (f32[2,128]{1,0:T(2,128)S(1)}, f32[2,128]{1,0:T(2,128)S(1)}, u32[]{:S(2)}, u32[]{:S(2)}) collective-permute-start(f32[2,128]{1,0:T(2,128)S(1)} %add.31), channel_id=1, source_target_pairs={{0,193},{1,192},{2,195},{3,194},{4,197},{5,196},{6,199},{7,198},{8... | collective-permute-start | bytes 3080 | tf_op jit(solution)/shard_map/ppermute | solution.py:312
  (80 shorter events, 15.3 us)
Async XLA Ops:
  0.6 12.2 %collective-permute-start = (bf16[12,128,128]{2,1,0:T(8,128)(2,1)}, bf16[12,128,128]{2,1,0:T(8,128)(2,1)S(1)}, u32[]{:S(2)}, u32[]{:S(2)}) collective-permute-start(bf16[12,128,128]{2,1,0:T(8,128)(2,1)} %bitcast.18), channel_id=1, source_target_pairs={{0,16},{16,32},{32,48},{48,64},{64,80},{80,96},{96,112},{112,128},... | collective-permute-start | bytes 1179656 | tf_op jit(solution)/shard_map/ppermute | solution.py:332
  12.9 11.0 %collective-permute-start.2 = (bf16[12,128,128]{2,1,0:T(8,128)(2,1)S(1)}, bf16[12,128,128]{2,1,0:T(8,128)(2,1)S(1)}, u32[]{:S(2)}, u32[]{:S(2)}) collective-permute-start(bf16[12,128,128]{2,1,0:T(8,128)(2,1)S(1)} %broadcast_select_fusion.rest_0_), channel_id=1, source_target_pairs={{0,2},{1,15},{2,4},{3,1},{4,6},{5,3},{6,8},{7,5},{8,10},{9,7},{10,... | collective-permute-start | bytes 1179656 | tf_op jit(solution)/shard_map/ppermute | solution.py:317
  20.7 9.0 %collective-permute-start.3 = (bf16[12,128,128]{2,1,0:T(8,128)(2,1)S(1)}, bf16[12,128,128]{2,1,0:T(8,128)(2,1)S(1)}, u32[]{:S(2)}, u32[]{:S(2)}) collective-permute-start(bf16[12,128,128]{2,1,0:T(8,128)(2,1)S(1)} %broadcast_select_fusion.rest_0_), channel_id=1, source_target_pairs={{0,15},{1,2},{2,1},{3,4},{4,3},{5,6},{6,5},{7,8},{8,7},{9,10},{10,... | collective-permute-start | bytes 1179656 | tf_op jit(solution)/shard_map/ppermute | solution.py:322
  23.9 8.2 %collective-permute-start.4 = (bf16[12,128,128]{2,1,0:T(8,128)(2,1)S(1)}, bf16[12,128,128]{2,1,0:T(8,128)(2,1)S(1)}, u32[]{:S(2)}, u32[]{:S(2)}) collective-permute-start(bf16[12,128,128]{2,1,0:T(8,128)(2,1)S(1)} %collective-permute-done.2.rest_2_), channel_id=1, source_target_pairs={{0,2},{1,15},{2,4},{3,1},{4,6},{5,3},{6,8},{7,5},{8,10},{9,7},{10,... | collective-permute-start | bytes 1179656 | tf_op jit(solution)/shard_map/ppermute | solution.py:317
  29.8 8.8 %collective-permute-start.5 = (bf16[12,128,128]{2,1,0:T(8,128)(2,1)S(1)}, bf16[12,128,128]{2,1,0:T(8,128)(2,1)S(1)}, u32[]{:S(2)}, u32[]{:S(2)}) collective-permute-start(bf16[12,128,128]{2,1,0:T(8,128)(2,1)S(1)} %collective-permute-done.3.rest_3_), channel_id=1, source_target_pairs={{0,2},{1,15},{2,4},{3,1},{4,6},{5,3},{6,8},{7,5},{8,10},{9,7},{10,... | collective-permute-start | bytes 1179656 | tf_op jit(solution)/shard_map/ppermute | solution.py:317
  32.1 9.4 %collective-permute-start.6 = (bf16[12,128,128]{2,1,0:T(8,128)(2,1)S(1)}, bf16[12,128,128]{2,1,0:T(8,128)(2,1)S(1)}, u32[]{:S(2)}, u32[]{:S(2)}) collective-permute-start(bf16[12,128,128]{2,1,0:T(8,128)(2,1)S(1)} %collective-permute-done.4.rest_4_), channel_id=1, source_target_pairs={{0,2},{1,15},{2,4},{3,1},{4,6},{5,3},{6,8},{7,5},{8,10},{9,7},{10,... | collective-permute-start | bytes 1179656 | tf_op jit(solution)/shard_map/ppermute | solution.py:317
  34.8 8.4 %collective-permute-start.1 = (bf16[12,128,128]{2,1,0:T(8,128)(2,1)S(1)}, bf16[12,128,128]{2,1,0:T(8,128)(2,1)S(1)}, u32[]{:S(2)}, u32[]{:S(2)}) collective-permute-start(bf16[12,128,128]{2,1,0:T(8,128)(2,1)S(1)} %broadcast_select_fusion.rest_0_), channel_id=1, source_target_pairs={{0,1},{1,0},{2,3},{3,2},{4,5},{5,4},{6,7},{7,6},{8,9},{9,8},{10,11... | collective-permute-start | bytes 1179656 | tf_op jit(solution)/shard_map/ppermute | solution.py:327
  38.1 9.1 %collective-permute-start.14 = (bf16[12,128,128]{2,1,0:T(8,128)(2,1)S(1)}, bf16[12,128,128]{2,1,0:T(8,128)(2,1)S(1)}, u32[]{:S(2)}, u32[]{:S(2)}) collective-permute-start(bf16[12,128,128]{2,1,0:T(8,128)(2,1)S(1)} %collective-permute-done.3.rest_3_), channel_id=1, source_target_pairs={{0,1},{1,0},{2,3},{3,2},{4,5},{5,4},{6,7},{7,6},{8,9},{9,8},{10,11... | collective-permute-start | bytes 1179656 | tf_op jit(solution)/shard_map/ppermute | solution.py:327
  38.2 9.1 %collective-permute-start.15 = (bf16[12,128,128]{2,1,0:T(8,128)(2,1)S(1)}, bf16[12,128,128]{2,1,0:T(8,128)(2,1)S(1)}, u32[]{:S(2)}, u32[]{:S(2)}) collective-permute-start(bf16[12,128,128]{2,1,0:T(8,128)(2,1)S(1)} %collective-permute-done.2.rest_2_), channel_id=1, source_target_pairs={{0,1},{1,0},{2,3},{3,2},{4,5},{5,4},{6,7},{7,6},{8,9},{9,8},{10,11... | collective-permute-start | bytes 1179656 | tf_op jit(solution)/shard_map/ppermute | solution.py:327
  38.6 9.1 %collective-permute-start.7 = (bf16[12,128,128]{2,1,0:T(8,128)(2,1)S(1)}, bf16[12,128,128]{2,1,0:T(8,128)(2,1)S(1)}, u32[]{:S(2)}, u32[]{:S(2)}) collective-permute-start(bf16[12,128,128]{2,1,0:T(8,128)(2,1)S(1)} %collective-permute-done.5.rest_5_), channel_id=1, source_target_pairs={{0,2},{1,15},{2,4},{3,1},{4,6},{5,3},{6,8},{7,5},{8,10},{9,7},{10,... | collective-permute-start | bytes 1179656 | tf_op jit(solution)/shard_map/ppermute | solution.py:317
  41.6 9.7 %collective-permute-start.8 = (bf16[12,128,128]{2,1,0:T(8,128)(2,1)S(1)}, bf16[12,128,128]{2,1,0:T(8,128)(2,1)S(1)}, u32[]{:S(2)}, u32[]{:S(2)}) collective-permute-start(bf16[12,128,128]{2,1,0:T(8,128)(2,1)S(1)} %collective-permute-done.6.rest_6_), channel_id=1, source_target_pairs={{0,2},{1,15},{2,4},{3,1},{4,6},{5,3},{6,8},{7,5},{8,10},{9,7},{10,... | collective-permute-start | bytes 1179656 | tf_op jit(solution)/shard_map/ppermute | solution.py:317
  43.3 13.4 %collective-permute-start.12 = (bf16[12,128,128]{2,1,0:T(8,128)(2,1)S(1)}, bf16[12,128,128]{2,1,0:T(8,128)(2,1)S(1)}, u32[]{:S(2)}, u32[]{:S(2)}) collective-permute-start(bf16[12,128,128]{2,1,0:T(8,128)(2,1)S(1)} %collective-permute-done.5.rest_5_), channel_id=1, source_target_pairs={{0,1},{1,0},{2,3},{3,2},{4,5},{5,4},{6,7},{7,6},{8,9},{9,8},{10,11... | collective-permute-start | bytes 1179656 | tf_op jit(solution)/shard_map/ppermute | solution.py:327
  47.2 9.6 %collective-permute-start.13 = (bf16[12,128,128]{2,1,0:T(8,128)(2,1)S(1)}, bf16[12,128,128]{2,1,0:T(8,128)(2,1)S(1)}, u32[]{:S(2)}, u32[]{:S(2)}) collective-permute-start(bf16[12,128,128]{2,1,0:T(8,128)(2,1)S(1)} %collective-permute-done.4.rest_4_), channel_id=1, source_target_pairs={{0,1},{1,0},{2,3},{3,2},{4,5},{5,4},{6,7},{7,6},{8,9},{9,8},{10,11... | collective-permute-start | bytes 1179656 | tf_op jit(solution)/shard_map/ppermute | solution.py:327
  47.3 9.5 %collective-permute-start.11 = (bf16[12,128,128]{2,1,0:T(8,128)(2,1)S(1)}, bf16[12,128,128]{2,1,0:T(8,128)(2,1)S(1)}, u32[]{:S(2)}, u32[]{:S(2)}) collective-permute-start(bf16[12,128,128]{2,1,0:T(8,128)(2,1)S(1)} %collective-permute-done.6.rest_6_), channel_id=1, source_target_pairs={{0,1},{1,0},{2,3},{3,2},{4,5},{5,4},{6,7},{7,6},{8,9},{9,8},{10,11... | collective-permute-start | bytes 1179656 | tf_op jit(solution)/shard_map/ppermute | solution.py:327
  47.7 9.1 %collective-permute-start.10 = (bf16[12,128,128]{2,1,0:T(8,128)(2,1)S(1)}, bf16[12,128,128]{2,1,0:T(8,128)(2,1)S(1)}, u32[]{:S(2)}, u32[]{:S(2)}) collective-permute-start(bf16[12,128,128]{2,1,0:T(8,128)(2,1)S(1)} %collective-permute-done.7.rest_7_), channel_id=1, source_target_pairs={{0,1},{1,0},{2,3},{3,2},{4,5},{5,4},{6,7},{7,6},{8,9},{9,8},{10,11... | collective-permute-start | bytes 1179656 | tf_op jit(solution)/shard_map/ppermute | solution.py:327
  51.3 7.2 %collective-permute-start.9 = (bf16[12,128,128]{2,1,0:T(8,128)(2,1)S(1)}, bf16[12,128,128]{2,1,0:T(8,128)(2,1)}, u32[]{:S(2)}, u32[]{:S(2)}) collective-permute-start(bf16[12,128,128]{2,1,0:T(8,128)(2,1)S(1)} %collective-permute-done.8.rest_8_), channel_id=1, source_target_pairs={{0,1},{1,0},{2,3},{3,2},{4,5},{5,4},{6,7},{7,6},{8,9},{9,8},{10,11... | collective-permute-start | bytes 1179656 | tf_op jit(solution)/shard_map/ppermute | solution.py:327
  74.1 1.7 %collective-permute-start.16 = (f32[4,128]{1,0:T(4,128)}, f32[4,128]{1,0:T(4,128)S(1)}, u32[]{:S(2)}, u32[]{:S(2)}) collective-permute-start(f32[4,128]{1,0:T(4,128)} %get-tuple-element.23.mine_ref), channel_id=1, source_target_pairs={{0,1},{1,0},{2,3},{3,2},{4,5},{5,4},{6,7},{7,6},{8,9},{9,8},{10,11... | collective-permute-start | bytes 6152 | tf_op jit(solution)/shard_map/ppermute | solution.py:312
  76.5 3.0 %collective-permute-start.17 = (f32[4,128]{1,0:T(4,128)S(1)}, f32[4,128]{1,0:T(4,128)S(1)}, u32[]{:S(2)}, u32[]{:S(2)}) collective-permute-start(f32[4,128]{1,0:T(4,128)S(1)} %add.25), channel_id=1, source_target_pairs={{0,3},{1,2},{2,1},{3,0},{4,7},{5,6},{6,5},{7,4},{8,11},{9,10},{10,... | collective-permute-start | bytes 6152 | tf_op jit(solution)/shard_map/ppermute | solution.py:312
  79.5 3.9 %collective-permute-start.18 = (f32[4,128]{1,0:T(4,128)S(1)}, f32[4,128]{1,0:T(4,128)S(1)}, u32[]{:S(2)}, u32[]{:S(2)}) collective-permute-start(f32[4,128]{1,0:T(4,128)S(1)} %add.26), channel_id=1, source_target_pairs={{0,5},{1,4},{2,7},{3,6},{4,1},{5,0},{6,3},{7,2},{8,13},{9,12},{10,... | collective-permute-start | bytes 6152 | tf_op jit(solution)/shard_map/ppermute | solution.py:312
  83.4 5.1 %collective-permute-start.19 = (f32[4,128]{1,0:T(4,128)S(1)}, f32[4,128]{1,0:T(4,128)S(1)}, u32[]{:S(2)}, u32[]{:S(2)}) collective-permute-start(f32[4,128]{1,0:T(4,128)S(1)} %add.27.half_ref), channel_id=1, source_target_pairs={{0,13},{1,12},{2,15},{3,14},{4,9},{5,8},{6,11},{7,10},{8,5},{9,4},... | collective-permute-start | bytes 6152 | tf_op jit(solution)/shard_map/ppermute | solution.py:312
  90.5 4.8 %collective-permute-start.20 = (f32[2,128]{1,0:T(2,128)}, f32[2,128]{1,0:T(2,128)S(1)}, u32[]{:S(2)}, u32[]{:S(2)}) collective-permute-start(f32[2,128]{1,0:T(2,128)} %get-tuple-element.24), channel_id=1, source_target_pairs={{0,17},{1,16},{2,19},{3,18},{4,21},{5,20},{6,23},{7,22},{8,25},{9,... | collective-permute-start | bytes 3080 | tf_op jit(solution)/shard_map/ppermute | solution.py:312
  95.4 4.3 %collective-permute-start.21 = (f32[2,128]{1,0:T(2,128)S(1)}, f32[2,128]{1,0:T(2,128)S(1)}, u32[]{:S(2)}, u32[]{:S(2)}) collective-permute-start(f32[2,128]{1,0:T(2,128)S(1)} %add.28), channel_id=1, source_target_pairs={{0,49},{1,48},{2,51},{3,50},{4,53},{5,52},{6,55},{7,54},{8,57},{9,... | collective-permute-start | bytes 3080 | tf_op jit(solution)/shard_map/ppermute | solution.py:312
  99.7 3.9 %collective-permute-start.22 = (f32[2,128]{1,0:T(2,128)S(1)}, f32[2,128]{1,0:T(2,128)S(1)}, u32[]{:S(2)}, u32[]{:S(2)}) collective-permute-start(f32[2,128]{1,0:T(2,128)S(1)} %add.30), channel_id=1, source_target_pairs={{0,65},{1,64},{2,67},{3,66},{4,69},{5,68},{6,71},{7,70},{8,73},{9,... | collective-permute-start | bytes 3080 | tf_op jit(solution)/shard_map/ppermute | solution.py:312
  103.6 4.4 %collective-permute-start.23 = (f32[2,128]{1,0:T(2,128)S(1)}, f32[2,128]{1,0:T(2,128)S(1)}, u32[]{:S(2)}, u32[]{:S(2)}) collective-permute-start(f32[2,128]{1,0:T(2,128)S(1)} %add.31), channel_id=1, source_target_pairs={{0,193},{1,192},{2,195},{3,194},{4,197},{5,196},{6,199},{7,198},{8... | collective-permute-start | bytes 3080 | tf_op jit(solution)/shard_map/ppermute | solution.py:312
  (20 other events, 265.4 us)

commit v7 on v6

--- a/solution.py
+++ b/solution.py
@@ -15,8 +15,7 @@
 BLOCKS = 16
 CHUNK = 32
 FINISH = 4
-LATEST = (9, 10)
-VMEM_LIMIT = 60 * 2**20
+VMEM_LIMIT = 40 * 2**20
 
 
 def iota(shape, dim):
@@ -258,8 +257,7 @@
         "back",
         4 * 10**9,
         (jax.ShapeDtypeStruct((pairs, width, width), F32), jax.ShapeDtypeStruct((4, width), F32)),
-        [SMEM_SPEC, SMEM_SPEC, ANY_SPEC, ANY_SPEC, VMEM_SPEC, ANY_SPEC]
-        + [VMEM_SPEC if i in LATEST else ANY_SPEC for i in range(BLOCKS)],
+        [SMEM_SPEC, SMEM_SPEC, ANY_SPEC, ANY_SPEC, VMEM_SPEC, ANY_SPEC] + [ANY_SPEC] * BLOCKS,
         (ANY_SPEC, VMEM_SPEC),
         [
             pltpu.VMEM((BLOCKS, bonds, width, width), BF16),

time: 109 us -> 111 us (1.018)
  starting transfers between devices: 48.8 us -> 53.1 us
  Pallas kernels: 26.1 us -> 24.4 us
    pallas_call x1, Pallas kernels: 15.5 us -> 20.3 us  [back(): call(back_kernel, 'back', 4 * 10 ** 9, (jax.ShapeDtypeStruct((pairs, widt...]
    ppermute x6, waiting for transfers between devices: 4.74 us -> 8.44 us  [hop(): lax.ppermute(value, 'sec', [(i, (i + (2 if i % 2 == 0 else -2)) % n) for...]
    ppermute x8, starting transfers between devices: 11.2 us -> 14.1 us  [partner(): return lax.ppermute(value, axes, [(i, i ^ bits) for i in range(n)])]
    ppermute x1, waiting for transfers between devices: 2.74 us -> 0.01 us  [cross_hop(): lax.ppermute(value, 'sec', [(i, (i + (-2 if i % 2 == 0 else 2)) % n ^ 1)...]
    ppermute x6, starting transfers between devices: 17 us -> 19.1 us  [hop(): lax.ppermute(value, 'sec', [(i, (i + (2 if i % 2 == 0 else -2)) % n) for...]
    pallas_call x1, Pallas kernels: 4.38 us -> 2.35 us  [front(): call(front_kernel, 'front', 5 * 10 ** 8, jax.ShapeDtypeStruct((pairs, bon...]
    pallas_call x1, Pallas kernels: 2.6 us -> 0.94 us  [finish(): call(finish_kernel, 'finish', 10 ** 6, jax.ShapeDtypeStruct(v.shape, BF16...]
    ppermute x1, waiting for transfers between devices: 3.66 us -> 2.05 us  [from_behind(): return lax.ppermute(value, 'seg', [(i, i + 1) for i in range(n - 1)])]
  transfers between devices with their start and end apart: 24 -> 24, of which waited for: 11 -> 12; matrix products, arithmetic and copies ran while one was open for 1% -> 0% of each run, Pallas kernels for 8% -> 4%
where the time goes in v7:
time: 111 us; the launch traced here: 110 us
  starting transfers between devices  53.1 us (48%)
  waiting for transfers between devices  26.4 us (24%)
  Pallas kernels  24.4 us (22%)
  local copies, waits for them, and re-layouts  4.15 us (4%)
  between operations  1.42 us (1%)
    pallas_call x1, Pallas kernels, back(): call(back_kernel, 'back', 4 * 10 ** 9, (jax.ShapeDtypeStruct((pairs, widt...  20.3 us
    ppermute x6, starting transfers between devices, hop(): lax.ppermute(value, 'sec', [(i, (i + (2 if i % 2 == 0 else -2)) % n) for...  19.1 us
    ppermute x8, starting transfers between devices, twin(): return lax.ppermute(value, 'sec', [(i, i ^ 1) for i in range(n)])  15.9 us
    ppermute x8, waiting for transfers between devices, partner(): return lax.ppermute(value, axes, [(i, i ^ bits) for i in range(n)])  15.3 us
    ppermute x8, starting transfers between devices, partner(): return lax.ppermute(value, axes, [(i, i ^ bits) for i in range(n)])  14.1 us
    ppermute x6, waiting for transfers between devices, hop(): lax.ppermute(value, 'sec', [(i, (i + (2 if i % 2 == 0 else -2)) % n) for...  8.44 us
    ppermute x1, starting transfers between devices, from_behind(): return lax.ppermute(value, 'seg', [(i, i + 1) for i in range(n - 1)])  3.97 us
    unnamed x14, local copies, waits for them, and re-layouts  3.64 us
  transfers between devices with their start and end apart: 24, of which 12 were waited for; matrix products, arithmetic and copies ran while one was open for 0% of the time, Pallas kernels for 4%

profile of v7, /device:TPU:1, one launch (start us, length us, event | category | flops | bytes accessed | tf_op | source)
XLA Modules:
  0.0 110.2 jit_solution(15275144457157345425)
XLA Ops:
  0.6 4.0 %collective-permute-start = (bf16[12,128,128]{2,1,0:T(8,128)(2,1)}, bf16[12,128,128]{2,1,0:T(8,128)(2,1)S(1)}, u32[]{:S(2)}, u32[]{:S(2)}) collective-permute-start(bf16[12,128,128]{2,1,0:T(8,128)(2,1)} %bitcast.22), channel_id=1, source_target_pairs={{0,16},{16,32},{32,48},{48,64},{64,80},{80,96},{96,112},{112,128},... | collective-permute-start | bytes 1179656 | tf_op jit(solution)/shard_map/ppermute | solution.py:330
  8.3 2.4 %front.1.x3_any = bf16[16,12,32,128]{3,2,1,0:T(8,128)(2,1)S(1)} custom-call(bf16[16,128,128]{2,1,0:T(8,128)(2,1)S(1)} %bitcast.13, bf16[12,128,128]{2,1,0:T(8,128)(2,1)S(1)} %bitcast.15, bf16[192,12]{1,0:T(8,128)(2,1)S(1)} %bitcast.17, bf16[192,12]{1,0:T(8,128)(2,1)S(1)} %bitcast.19), custom_call_target="tpu_custom_call" | custom-call | flops 500000000 | bytes 8000000 | tf_op jit(solution)/shard_map/front/pallas_call | solution.py:234
  10.6 2.0 %collective-permute-done = bf16[12,128,128]{2,1,0:T(8,128)(2,1)S(1)} collective-permute-done((bf16[12,128,128]{2,1,0:T(8,128)(2,1)}, bf16[12,128,128]{2,1,0:T(8,128)(2,1)S(1)}, u32[]{:S(2)}, u32[]{:S(2)}) %collective-permute-start) | collective-permute-done | bytes 393248 | tf_op jit(solution)/shard_map/ppermute | solution.py:330
  12.7 5.7 %collective-permute-start.2 = (bf16[12,128,128]{2,1,0:T(8,128)(2,1)S(1)}, bf16[12,128,128]{2,1,0:T(8,128)(2,1)S(1)}, u32[]{:S(2)}, u32[]{:S(2)}) collective-permute-start(bf16[12,128,128]{2,1,0:T(8,128)(2,1)S(1)} %broadcast_select_fusion.rest_0_), channel_id=1, source_target_pairs={{0,2},{1,15},{2,4},{3,1},{4,6},{5,3},{6,8},{7,5},{8,10},{9,7},{10,... | collective-permute-start | bytes 1179656 | tf_op jit(solution)/shard_map/ppermute | solution.py:315
  19.2 5.9 %collective-permute-done.2.rest_2_ = bf16[12,128,128]{2,1,0:T(8,128)(2,1)S(1)} collective-permute-done((bf16[12,128,128]{2,1,0:T(8,128)(2,1)S(1)}, bf16[12,128,128]{2,1,0:T(8,128)(2,1)S(1)}, u32[]{:S(2)}, u32[]{:S(2)}) %collective-permute-start.2) | collective-permute-done | bytes 393248 | tf_op jit(solution)/shard_map/ppermute | solution.py:315
  25.1 3.1 %collective-permute-start.4 = (bf16[12,128,128]{2,1,0:T(8,128)(2,1)S(1)}, bf16[12,128,128]{2,1,0:T(8,128)(2,1)S(1)}, u32[]{:S(2)}, u32[]{:S(2)}) collective-permute-start(bf16[12,128,128]{2,1,0:T(8,128)(2,1)S(1)} %collective-permute-done.2.rest_2_), channel_id=1, source_target_pairs={{0,2},{1,15},{2,4},{3,1},{4,6},{5,3},{6,8},{7,5},{8,10},{9,7},{10,... | collective-permute-start | bytes 1179656 | tf_op jit(solution)/shard_map/ppermute | solution.py:315
  28.2 2.2 %collective-permute-start.5 = (bf16[12,128,128]{2,1,0:T(8,128)(2,1)S(1)}, bf16[12,128,128]{2,1,0:T(8,128)(2,1)S(1)}, u32[]{:S(2)}, u32[]{:S(2)}) collective-permute-start(bf16[12,128,128]{2,1,0:T(8,128)(2,1)S(1)} %collective-permute-done.3.rest_3_), channel_id=1, source_target_pairs={{0,2},{1,15},{2,4},{3,1},{4,6},{5,3},{6,8},{7,5},{8,10},{9,7},{10,... | collective-permute-start | bytes 1179656 | tf_op jit(solution)/shard_map/ppermute | solution.py:315
  30.4 2.5 %collective-permute-done.4.rest_4_ = bf16[12,128,128]{2,1,0:T(8,128)(2,1)S(1)} collective-permute-done((bf16[12,128,128]{2,1,0:T(8,128)(2,1)S(1)}, bf16[12,128,128]{2,1,0:T(8,128)(2,1)S(1)}, u32[]{:S(2)}, u32[]{:S(2)}) %collective-permute-start.4) | collective-permute-done | bytes 393248 | tf_op jit(solution)/shard_map/ppermute | solution.py:315
  32.9 3.1 %collective-permute-start.6 = (bf16[12,128,128]{2,1,0:T(8,128)(2,1)S(1)}, bf16[12,128,128]{2,1,0:T(8,128)(2,1)S(1)}, u32[]{:S(2)}, u32[]{:S(2)}) collective-permute-start(bf16[12,128,128]{2,1,0:T(8,128)(2,1)S(1)} %collective-permute-done.4.rest_4_), channel_id=1, source_target_pairs={{0,2},{1,15},{2,4},{3,1},{4,6},{5,3},{6,8},{7,5},{8,10},{9,7},{10,... | collective-permute-start | bytes 1179656 | tf_op jit(solution)/shard_map/ppermute | solution.py:315
  36.1 2.9 %collective-permute-start.1 = (bf16[12,128,128]{2,1,0:T(8,128)(2,1)S(1)}, bf16[12,128,128]{2,1,0:T(8,128)(2,1)S(1)}, u32[]{:S(2)}, u32[]{:S(2)}) collective-permute-start(bf16[12,128,128]{2,1,0:T(8,128)(2,1)S(1)} %broadcast_select_fusion.rest_0_), channel_id=1, source_target_pairs={{0,1},{1,0},{2,3},{3,2},{4,5},{5,4},{6,7},{7,6},{8,9},{9,8},{10,11... | collective-permute-start | bytes 1179656 | tf_op jit(solution)/shard_map/ppermute | solution.py:325
  39.5 3.0 %collective-permute-start.7 = (bf16[12,128,128]{2,1,0:T(8,128)(2,1)S(1)}, bf16[12,128,128]{2,1,0:T(8,128)(2,1)S(1)}, u32[]{:S(2)}, u32[]{:S(2)}) collective-permute-start(bf16[12,128,128]{2,1,0:T(8,128)(2,1)S(1)} %collective-permute-done.5.rest_5_), channel_id=1, source_target_pairs={{0,2},{1,15},{2,4},{3,1},{4,6},{5,3},{6,8},{7,5},{8,10},{9,7},{10,... | collective-permute-start | bytes 1179656 | tf_op jit(solution)/shard_map/ppermute | solution.py:315
  42.5 2.0 %collective-permute-start.8 = (bf16[12,128,128]{2,1,0:T(8,128)(2,1)S(1)}, bf16[12,128,128]{2,1,0:T(8,128)(2,1)S(1)}, u32[]{:S(2)}, u32[]{:S(2)}) collective-permute-start(bf16[12,128,128]{2,1,0:T(8,128)(2,1)S(1)} %collective-permute-done.6.rest_6_), channel_id=1, source_target_pairs={{0,2},{1,15},{2,4},{3,1},{4,6},{5,3},{6,8},{7,5},{8,10},{9,7},{10,... | collective-permute-start | bytes 1179656 | tf_op jit(solution)/shard_map/ppermute | solution.py:315
  44.5 3.5 %collective-permute-start.12 = (bf16[12,128,128]{2,1,0:T(8,128)(2,1)S(1)}, bf16[12,128,128]{2,1,0:T(8,128)(2,1)S(1)}, u32[]{:S(2)}, u32[]{:S(2)}) collective-permute-start(bf16[12,128,128]{2,1,0:T(8,128)(2,1)S(1)} %collective-permute-done.5.rest_5_), channel_id=1, source_target_pairs={{0,1},{1,0},{2,3},{3,2},{4,5},{5,4},{6,7},{7,6},{8,9},{9,8},{10,11... | collective-permute-start | bytes 1179656 | tf_op jit(solution)/shard_map/ppermute | solution.py:325
  48.5 3.7 %collective-permute-start.10 = (bf16[12,128,128]{2,1,0:T(8,128)(2,1)S(1)}, bf16[12,128,128]{2,1,0:T(8,128)(2,1)S(1)}, u32[]{:S(2)}, u32[]{:S(2)}) collective-permute-start(bf16[12,128,128]{2,1,0:T(8,128)(2,1)S(1)} %collective-permute-done.7.rest_7_), channel_id=1, source_target_pairs={{0,1},{1,0},{2,3},{3,2},{4,5},{5,4},{6,7},{7,6},{8,9},{9,8},{10,11... | collective-permute-start | bytes 1179656 | tf_op jit(solution)/shard_map/ppermute | solution.py:325
  52.2 4.8 %collective-permute-start.9 = (bf16[12,128,128]{2,1,0:T(8,128)(2,1)S(1)}, bf16[12,128,128]{2,1,0:T(8,128)(2,1)S(1)}, u32[]{:S(2)}, u32[]{:S(2)}) collective-permute-start(bf16[12,128,128]{2,1,0:T(8,128)(2,1)S(1)} %collective-permute-done.8.rest_8_), channel_id=1, source_target_pairs={{0,1},{1,0},{2,3},{3,2},{4,5},{5,4},{6,7},{7,6},{8,9},{9,8},{10,11... | collective-permute-start | bytes 1179656 | tf_op jit(solution)/shard_map/ppermute | solution.py:325
  58.3 20.3 %back.1 = (f32[16,128,128]{2,1,0:T(8,128)S(1)}, f32[4,128]{1,0:T(4,128)S(1)}) custom-call(s32[16]{0:T(128)S(1)} %copy-done.5, s32[1]{0:T(128)S(6)} %copy.10.rank_ref, bf16[16,128,128]{2,1,0:T(8,128)(2,1)S(1)} %bitcast.14, bf16[12,128,128]{2,1,0:T(8,128)(2,1)S(1)} %bitcast.16, bf16[192,192]{1,0:T(8,128)(2,1)S(1)} %operators.1.mpo_ref, ...), custom_call_target="tpu_custom_call" | custom-call | flops 4000000000 | bytes 8000000 | tf_op jit(solution)/shard_map/back/pallas_call | solution.py:255
  79.9 3.0 %collective-permute-done.17 = f32[4,128]{1,0:T(4,128)S(1)} collective-permute-done((f32[4,128]{1,0:T(4,128)S(1)}, f32[4,128]{1,0:T(4,128)S(1)}, u32[]{:S(2)}, u32[]{:S(2)}) %collective-permute-start.17) | collective-permute-done | bytes 2080 | tf_op jit(solution)/shard_map/ppermute | solution.py:310
  82.9 3.9 %collective-permute-done.18 = f32[4,128]{1,0:T(4,128)S(1)} collective-permute-done((f32[4,128]{1,0:T(4,128)S(1)}, f32[4,128]{1,0:T(4,128)S(1)}, u32[]{:S(2)}, u32[]{:S(2)}) %collective-permute-start.18) | collective-permute-done | bytes 2080 | tf_op jit(solution)/shard_map/ppermute | solution.py:310
  87.9 4.0 %collective-permute-done.19.other_ref = f32[4,128]{1,0:T(4,128)S(1)} collective-permute-done((f32[4,128]{1,0:T(4,128)S(1)}, f32[4,128]{1,0:T(4,128)S(1)}, u32[]{:S(2)}, u32[]{:S(2)}) %collective-permute-start.19) | collective-permute-done | bytes 2080 | tf_op jit(solution)/shard_map/ppermute | solution.py:310
  92.1 2.4 %collective-permute-start.20 = (f32[2,128]{1,0:T(2,128)S(1)}, f32[2,128]{1,0:T(2,128)S(1)}, u32[]{:S(2)}, u32[]{:S(2)}) collective-permute-start(f32[2,128]{1,0:T(2,128)S(1)} %get-tuple-element.24), channel_id=1, source_target_pairs={{0,17},{1,16},{2,19},{3,18},{4,21},{5,20},{6,23},{7,22},{8,25},{9,... | collective-permute-start | bytes 3080 | tf_op jit(solution)/shard_map/ppermute | solution.py:310
  95.7 3.0 %collective-permute-start.21 = (f32[2,128]{1,0:T(2,128)S(1)}, f32[2,128]{1,0:T(2,128)S(1)}, u32[]{:S(2)}, u32[]{:S(2)}) collective-permute-start(f32[2,128]{1,0:T(2,128)S(1)} %add.28), channel_id=1, source_target_pairs={{0,49},{1,48},{2,51},{3,50},{4,53},{5,52},{6,55},{7,54},{8,57},{9,... | collective-permute-start | bytes 3080 | tf_op jit(solution)/shard_map/ppermute | solution.py:310
  98.7 1.3 %collective-permute-done.21 = f32[2,128]{1,0:T(2,128)S(1)} collective-permute-done((f32[2,128]{1,0:T(2,128)S(1)}, f32[2,128]{1,0:T(2,128)S(1)}, u32[]{:S(2)}, u32[]{:S(2)}) %collective-permute-start.21) | collective-permute-done | bytes 1056 | tf_op jit(solution)/shard_map/ppermute | solution.py:310
  100.0 3.9 %collective-permute-start.22 = (f32[2,128]{1,0:T(2,128)S(1)}, f32[2,128]{1,0:T(2,128)S(1)}, u32[]{:S(2)}, u32[]{:S(2)}) collective-permute-start(f32[2,128]{1,0:T(2,128)S(1)} %add.30), channel_id=1, source_target_pairs={{0,65},{1,64},{2,67},{3,66},{4,69},{5,68},{6,71},{7,70},{8,73},{9,... | collective-permute-start | bytes 3080 | tf_op jit(solution)/shard_map/ppermute | solution.py:310
  105.1 3.2 %collective-permute-start.23 = (f32[2,128]{1,0:T(2,128)S(1)}, f32[2,128]{1,0:T(2,128)S(1)}, u32[]{:S(2)}, u32[]{:S(2)}) collective-permute-start(f32[2,128]{1,0:T(2,128)S(1)} %add.31), channel_id=1, source_target_pairs={{0,193},{1,192},{2,195},{3,194},{4,197},{5,196},{6,199},{7,198},{8... | collective-permute-start | bytes 3080 | tf_op jit(solution)/shard_map/ppermute | solution.py:310
  (54 shorter events, 13.2 us)
Async XLA Ops:
  0.6 12.0 %collective-permute-start = (bf16[12,128,128]{2,1,0:T(8,128)(2,1)}, bf16[12,128,128]{2,1,0:T(8,128)(2,1)S(1)}, u32[]{:S(2)}, u32[]{:S(2)}) collective-permute-start(bf16[12,128,128]{2,1,0:T(8,128)(2,1)} %bitcast.22), channel_id=1, source_target_pairs={{0,16},{16,32},{32,48},{48,64},{64,80},{80,96},{96,112},{112,128},... | collective-permute-start | bytes 1179656 | tf_op jit(solution)/shard_map/ppermute | solution.py:330
  12.7 12.4 %collective-permute-start.2 = (bf16[12,128,128]{2,1,0:T(8,128)(2,1)S(1)}, bf16[12,128,128]{2,1,0:T(8,128)(2,1)S(1)}, u32[]{:S(2)}, u32[]{:S(2)}) collective-permute-start(bf16[12,128,128]{2,1,0:T(8,128)(2,1)S(1)} %broadcast_select_fusion.rest_0_), channel_id=1, source_target_pairs={{0,2},{1,15},{2,4},{3,1},{4,6},{5,3},{6,8},{7,5},{8,10},{9,7},{10,... | collective-permute-start | bytes 1179656 | tf_op jit(solution)/shard_map/ppermute | solution.py:315
  19.1 9.1 %collective-permute-start.3 = (bf16[12,128,128]{2,1,0:T(8,128)(2,1)S(1)}, bf16[12,128,128]{2,1,0:T(8,128)(2,1)S(1)}, u32[]{:S(2)}, u32[]{:S(2)}) collective-permute-start(bf16[12,128,128]{2,1,0:T(8,128)(2,1)S(1)} %broadcast_select_fusion.rest_0_), channel_id=1, source_target_pairs={{0,15},{1,2},{2,1},{3,4},{4,3},{5,6},{6,5},{7,8},{8,7},{9,10},{10,... | collective-permute-start | bytes 1179656 | tf_op jit(solution)/shard_map/ppermute | solution.py:320
  25.1 7.8 %collective-permute-start.4 = (bf16[12,128,128]{2,1,0:T(8,128)(2,1)S(1)}, bf16[12,128,128]{2,1,0:T(8,128)(2,1)S(1)}, u32[]{:S(2)}, u32[]{:S(2)}) collective-permute-start(bf16[12,128,128]{2,1,0:T(8,128)(2,1)S(1)} %collective-permute-done.2.rest_2_), channel_id=1, source_target_pairs={{0,2},{1,15},{2,4},{3,1},{4,6},{5,3},{6,8},{7,5},{8,10},{9,7},{10,... | collective-permute-start | bytes 1179656 | tf_op jit(solution)/shard_map/ppermute | solution.py:315
  28.2 11.3 %collective-permute-start.5 = (bf16[12,128,128]{2,1,0:T(8,128)(2,1)S(1)}, bf16[12,128,128]{2,1,0:T(8,128)(2,1)S(1)}, u32[]{:S(2)}, u32[]{:S(2)}) collective-permute-start(bf16[12,128,128]{2,1,0:T(8,128)(2,1)S(1)} %collective-permute-done.3.rest_3_), channel_id=1, source_target_pairs={{0,2},{1,15},{2,4},{3,1},{4,6},{5,3},{6,8},{7,5},{8,10},{9,7},{10,... | collective-permute-start | bytes 1179656 | tf_op jit(solution)/shard_map/ppermute | solution.py:315
  32.9 9.5 %collective-permute-start.6 = (bf16[12,128,128]{2,1,0:T(8,128)(2,1)S(1)}, bf16[12,128,128]{2,1,0:T(8,128)(2,1)S(1)}, u32[]{:S(2)}, u32[]{:S(2)}) collective-permute-start(bf16[12,128,128]{2,1,0:T(8,128)(2,1)S(1)} %collective-permute-done.4.rest_4_), channel_id=1, source_target_pairs={{0,2},{1,15},{2,4},{3,1},{4,6},{5,3},{6,8},{7,5},{8,10},{9,7},{10,... | collective-permute-start | bytes 1179656 | tf_op jit(solution)/shard_map/ppermute | solution.py:315
  36.1 8.4 %collective-permute-start.1 = (bf16[12,128,128]{2,1,0:T(8,128)(2,1)S(1)}, bf16[12,128,128]{2,1,0:T(8,128)(2,1)S(1)}, u32[]{:S(2)}, u32[]{:S(2)}) collective-permute-start(bf16[12,128,128]{2,1,0:T(8,128)(2,1)S(1)} %broadcast_select_fusion.rest_0_), channel_id=1, source_target_pairs={{0,1},{1,0},{2,3},{3,2},{4,5},{5,4},{6,7},{7,6},{8,9},{9,8},{10,11... | collective-permute-start | bytes 1179656 | tf_op jit(solution)/shard_map/ppermute | solution.py:325
  39.0 9.0 %collective-permute-start.14 = (bf16[12,128,128]{2,1,0:T(8,128)(2,1)S(1)}, bf16[12,128,128]{2,1,0:T(8,128)(2,1)S(1)}, u32[]{:S(2)}, u32[]{:S(2)}) collective-permute-start(bf16[12,128,128]{2,1,0:T(8,128)(2,1)S(1)} %collective-permute-done.3.rest_3_), channel_id=1, source_target_pairs={{0,1},{1,0},{2,3},{3,2},{4,5},{5,4},{6,7},{7,6},{8,9},{9,8},{10,11... | collective-permute-start | bytes 1179656 | tf_op jit(solution)/shard_map/ppermute | solution.py:325
  39.0 9.1 %collective-permute-start.15 = (bf16[12,128,128]{2,1,0:T(8,128)(2,1)S(1)}, bf16[12,128,128]{2,1,0:T(8,128)(2,1)S(1)}, u32[]{:S(2)}, u32[]{:S(2)}) collective-permute-start(bf16[12,128,128]{2,1,0:T(8,128)(2,1)S(1)} %collective-permute-done.2.rest_2_), channel_id=1, source_target_pairs={{0,1},{1,0},{2,3},{3,2},{4,5},{5,4},{6,7},{7,6},{8,9},{9,8},{10,11... | collective-permute-start | bytes 1179656 | tf_op jit(solution)/shard_map/ppermute | solution.py:325
  39.5 9.0 %collective-permute-start.7 = (bf16[12,128,128]{2,1,0:T(8,128)(2,1)S(1)}, bf16[12,128,128]{2,1,0:T(8,128)(2,1)S(1)}, u32[]{:S(2)}, u32[]{:S(2)}) collective-permute-start(bf16[12,128,128]{2,1,0:T(8,128)(2,1)S(1)} %collective-permute-done.5.rest_5_), channel_id=1, source_target_pairs={{0,2},{1,15},{2,4},{3,1},{4,6},{5,3},{6,8},{7,5},{8,10},{9,7},{10,... | collective-permute-start | bytes 1179656 | tf_op jit(solution)/shard_map/ppermute | solution.py:315
  42.5 9.7 %collective-permute-start.8 = (bf16[12,128,128]{2,1,0:T(8,128)(2,1)S(1)}, bf16[12,128,128]{2,1,0:T(8,128)(2,1)S(1)}, u32[]{:S(2)}, u32[]{:S(2)}) collective-permute-start(bf16[12,128,128]{2,1,0:T(8,128)(2,1)S(1)} %collective-permute-done.6.rest_6_), channel_id=1, source_target_pairs={{0,2},{1,15},{2,4},{3,1},{4,6},{5,3},{6,8},{7,5},{8,10},{9,7},{10,... | collective-permute-start | bytes 1179656 | tf_op jit(solution)/shard_map/ppermute | solution.py:315
  44.5 13.1 %collective-permute-start.12 = (bf16[12,128,128]{2,1,0:T(8,128)(2,1)S(1)}, bf16[12,128,128]{2,1,0:T(8,128)(2,1)S(1)}, u32[]{:S(2)}, u32[]{:S(2)}) collective-permute-start(bf16[12,128,128]{2,1,0:T(8,128)(2,1)S(1)} %collective-permute-done.5.rest_5_), channel_id=1, source_target_pairs={{0,1},{1,0},{2,3},{3,2},{4,5},{5,4},{6,7},{7,6},{8,9},{9,8},{10,11... | collective-permute-start | bytes 1179656 | tf_op jit(solution)/shard_map/ppermute | solution.py:325
  48.0 9.6 %collective-permute-start.13 = (bf16[12,128,128]{2,1,0:T(8,128)(2,1)S(1)}, bf16[12,128,128]{2,1,0:T(8,128)(2,1)S(1)}, u32[]{:S(2)}, u32[]{:S(2)}) collective-permute-start(bf16[12,128,128]{2,1,0:T(8,128)(2,1)S(1)} %collective-permute-done.4.rest_4_), channel_id=1, source_target_pairs={{0,1},{1,0},{2,3},{3,2},{4,5},{5,4},{6,7},{7,6},{8,9},{9,8},{10,11... | collective-permute-start | bytes 1179656 | tf_op jit(solution)/shard_map/ppermute | solution.py:325
  48.1 9.6 %collective-permute-start.11 = (bf16[12,128,128]{2,1,0:T(8,128)(2,1)S(1)}, bf16[12,128,128]{2,1,0:T(8,128)(2,1)S(1)}, u32[]{:S(2)}, u32[]{:S(2)}) collective-permute-start(bf16[12,128,128]{2,1,0:T(8,128)(2,1)S(1)} %collective-permute-done.6.rest_6_), channel_id=1, source_target_pairs={{0,1},{1,0},{2,3},{3,2},{4,5},{5,4},{6,7},{7,6},{8,9},{9,8},{10,11... | collective-permute-start | bytes 1179656 | tf_op jit(solution)/shard_map/ppermute | solution.py:325
  48.5 9.1 %collective-permute-start.10 = (bf16[12,128,128]{2,1,0:T(8,128)(2,1)S(1)}, bf16[12,128,128]{2,1,0:T(8,128)(2,1)S(1)}, u32[]{:S(2)}, u32[]{:S(2)}) collective-permute-start(bf16[12,128,128]{2,1,0:T(8,128)(2,1)S(1)} %collective-permute-done.7.rest_7_), channel_id=1, source_target_pairs={{0,1},{1,0},{2,3},{3,2},{4,5},{5,4},{6,7},{7,6},{8,9},{9,8},{10,11... | collective-permute-start | bytes 1179656 | tf_op jit(solution)/shard_map/ppermute | solution.py:325
  52.2 6.1 %collective-permute-start.9 = (bf16[12,128,128]{2,1,0:T(8,128)(2,1)S(1)}, bf16[12,128,128]{2,1,0:T(8,128)(2,1)S(1)}, u32[]{:S(2)}, u32[]{:S(2)}) collective-permute-start(bf16[12,128,128]{2,1,0:T(8,128)(2,1)S(1)} %collective-permute-done.8.rest_8_), channel_id=1, source_target_pairs={{0,1},{1,0},{2,3},{3,2},{4,5},{5,4},{6,7},{7,6},{8,9},{9,8},{10,11... | collective-permute-start | bytes 1179656 | tf_op jit(solution)/shard_map/ppermute | solution.py:325
  78.6 1.3 %collective-permute-start.16 = (f32[4,128]{1,0:T(4,128)S(1)}, f32[4,128]{1,0:T(4,128)S(1)}, u32[]{:S(2)}, u32[]{:S(2)}) collective-permute-start(f32[4,128]{1,0:T(4,128)S(1)} %get-tuple-element.23.mine_ref), channel_id=1, source_target_pairs={{0,1},{1,0},{2,3},{3,2},{4,5},{5,4},{6,7},{7,6},{8,9},{9,8},{10,11... | collective-permute-start | bytes 6152 | tf_op jit(solution)/shard_map/ppermute | solution.py:310
  79.9 3.0 %collective-permute-start.17 = (f32[4,128]{1,0:T(4,128)S(1)}, f32[4,128]{1,0:T(4,128)S(1)}, u32[]{:S(2)}, u32[]{:S(2)}) collective-permute-start(f32[4,128]{1,0:T(4,128)S(1)} %add.25), channel_id=1, source_target_pairs={{0,3},{1,2},{2,1},{3,0},{4,7},{5,6},{6,5},{7,4},{8,11},{9,10},{10,... | collective-permute-start | bytes 6152 | tf_op jit(solution)/shard_map/ppermute | solution.py:310
  82.9 3.9 %collective-permute-start.18 = (f32[4,128]{1,0:T(4,128)S(1)}, f32[4,128]{1,0:T(4,128)S(1)}, u32[]{:S(2)}, u32[]{:S(2)}) collective-permute-start(f32[4,128]{1,0:T(4,128)S(1)} %add.26), channel_id=1, source_target_pairs={{0,5},{1,4},{2,7},{3,6},{4,1},{5,0},{6,3},{7,2},{8,13},{9,12},{10,... | collective-permute-start | bytes 6152 | tf_op jit(solution)/shard_map/ppermute | solution.py:310
  86.8 5.1 %collective-permute-start.19 = (f32[4,128]{1,0:T(4,128)S(1)}, f32[4,128]{1,0:T(4,128)S(1)}, u32[]{:S(2)}, u32[]{:S(2)}) collective-permute-start(f32[4,128]{1,0:T(4,128)S(1)} %add.27.half_ref), channel_id=1, source_target_pairs={{0,13},{1,12},{2,15},{3,14},{4,9},{5,8},{6,11},{7,10},{8,5},{9,4},... | collective-permute-start | bytes 6152 | tf_op jit(solution)/shard_map/ppermute | solution.py:310
  92.1 3.7 %collective-permute-start.20 = (f32[2,128]{1,0:T(2,128)S(1)}, f32[2,128]{1,0:T(2,128)S(1)}, u32[]{:S(2)}, u32[]{:S(2)}) collective-permute-start(f32[2,128]{1,0:T(2,128)S(1)} %get-tuple-element.24), channel_id=1, source_target_pairs={{0,17},{1,16},{2,19},{3,18},{4,21},{5,20},{6,23},{7,22},{8,25},{9,... | collective-permute-start | bytes 3080 | tf_op jit(solution)/shard_map/ppermute | solution.py:310
  95.7 4.3 %collective-permute-start.21 = (f32[2,128]{1,0:T(2,128)S(1)}, f32[2,128]{1,0:T(2,128)S(1)}, u32[]{:S(2)}, u32[]{:S(2)}) collective-permute-start(f32[2,128]{1,0:T(2,128)S(1)} %add.28), channel_id=1, source_target_pairs={{0,49},{1,48},{2,51},{3,50},{4,53},{5,52},{6,55},{7,54},{8,57},{9,... | collective-permute-start | bytes 3080 | tf_op jit(solution)/shard_map/ppermute | solution.py:310
  100.0 5.1 %collective-permute-start.22 = (f32[2,128]{1,0:T(2,128)S(1)}, f32[2,128]{1,0:T(2,128)S(1)}, u32[]{:S(2)}, u32[]{:S(2)}) collective-permute-start(f32[2,128]{1,0:T(2,128)S(1)} %add.30), channel_id=1, source_target_pairs={{0,65},{1,64},{2,67},{3,66},{4,69},{5,68},{6,71},{7,70},{8,73},{9,... | collective-permute-start | bytes 3080 | tf_op jit(solution)/shard_map/ppermute | solution.py:310
  105.1 4.4 %collective-permute-start.23 = (f32[2,128]{1,0:T(2,128)S(1)}, f32[2,128]{1,0:T(2,128)S(1)}, u32[]{:S(2)}, u32[]{:S(2)}) collective-permute-start(f32[2,128]{1,0:T(2,128)S(1)} %add.31), channel_id=1, source_target_pairs={{0,193},{1,192},{2,195},{3,194},{4,197},{5,196},{6,199},{7,198},{8... | collective-permute-start | bytes 3080 | tf_op jit(solution)/shard_map/ppermute | solution.py:310
  (7 other events, 108.2 us)

commit v8 on v7

--- a/solution.py
+++ b/solution.py
@@ -15,7 +15,8 @@
 BLOCKS = 16
 CHUNK = 32
 FINISH = 4
-VMEM_LIMIT = 40 * 2**20
+VMEM_LIMIT = 60 * 2**20
+SMALL_LIMIT = 8 * 2**20
 
 
 def iota(shape, dim):
@@ -202,14 +203,14 @@
 ANY_SPEC = pl.BlockSpec(memory_space=pl.ANY)
 
 
-def call(kernel, name, flops, out_shape, in_specs, out_specs, scratch):
+def call(kernel, name, flops, out_shape, in_specs, out_specs, scratch, limit=SMALL_LIMIT):
     return pl.pallas_call(
         kernel,
         out_shape=out_shape,
         in_specs=in_specs,
         out_specs=out_specs,
         scratch_shapes=scratch,
-        compiler_params=pltpu.CompilerParams(vmem_limit_bytes=VMEM_LIMIT),
+        compiler_params=pltpu.CompilerParams(vmem_limit_bytes=limit),
         cost_estimate=pl.CostEstimate(flops=flops, bytes_accessed=8 * 10**6, transcendentals=0),
         name=name,
     )
@@ -246,6 +247,7 @@
             pltpu.SemaphoreType.DMA((2,)),
             pltpu.SemaphoreType.DMA((states // CHUNK,)),
         ],
+        VMEM_LIMIT,
     )(psi, renv, left, right)
 
 
@@ -271,6 +273,7 @@
             pltpu.SemaphoreType.DMA,
             pltpu.SemaphoreType.DMA((pairs,)),
         ],
+        VMEM_LIMIT,
     )(charge, rank, psi, renv, mpo, x3, *blocks)
 
 

time: 111 us -> 108 us (0.973)
  Pallas kernels: 24.4 us -> 21.5 us
  starting transfers between devices: 53.1 us -> 51.5 us
    pallas_call x1, Pallas kernels: 20.3 us -> 15.3 us  [back(): call(back_kernel, 'back', 4 * 10 ** 9, (jax.ShapeDtypeStruct((pairs, widt...]
    ppermute x8, starting transfers between devices: 14.1 us -> 11.4 us  [partner(): return lax.ppermute(value, axes, [(i, i ^ bits) for i in range(n)])]
    pallas_call x1, Pallas kernels: 2.35 us -> 4.41 us  [front(): call(front_kernel, 'front', 5 * 10 ** 8, jax.ShapeDtypeStruct((pairs, bon...]
    ppermute x6, waiting for transfers between devices: 8.44 us -> 6.78 us  [hop(): lax.ppermute(value, 'sec', [(i, (i + (2 if i % 2 == 0 else -2)) % n) for...]
    ppermute x1, waiting for transfers between devices: 2.05 us -> 3.61 us  [from_behind(): return lax.ppermute(value, 'seg', [(i, i + 1) for i in range(n - 1)])]
    ppermute x8, waiting for transfers between devices: 15.3 us -> 16.7 us  [partner(): return lax.ppermute(value, axes, [(i, i ^ bits) for i in range(n)])]
    unnamed x14 -> x42, local copies, waits for them, and re-layouts: 3.64 us -> 4.31 us
  transfers between devices with their start and end apart: 24 -> 24, of which waited for: 12 -> 10; matrix products, arithmetic and copies ran while one was open for 0% -> 0% of each run, Pallas kernels for 4% -> 6%
where the time goes in v8:
time: 108 us
  starting transfers between devices  51.5 us (48%)
  waiting for transfers between devices  27.2 us (25%)
  Pallas kernels  21.5 us (20%)
  local copies, waits for them, and re-layouts  4.82 us (4%)
  between operations  1.57 us (1%)
  other arithmetic  1.42 us (1%)
    ppermute x6, starting transfers between devices, hop(): lax.ppermute(value, 'sec', [(i, (i + (2 if i % 2 == 0 else -2)) % n) for...  19.2 us
    ppermute x8, waiting for transfers between devices, partner(): return lax.ppermute(value, axes, [(i, i ^ bits) for i in range(n)])  16.7 us
    ppermute x8, starting transfers between devices, twin(): return lax.ppermute(value, 'sec', [(i, i ^ 1) for i in range(n)])  16.7 us
    pallas_call x1, Pallas kernels, back(): call(back_kernel, 'back', 4 * 10 ** 9, (jax.ShapeDtypeStruct((pairs, widt...  15.3 us
    ppermute x8, starting transfers between devices, partner(): return lax.ppermute(value, axes, [(i, i ^ bits) for i in range(n)])  11.4 us
    ppermute x6, waiting for transfers between devices, hop(): lax.ppermute(value, 'sec', [(i, (i + (2 if i % 2 == 0 else -2)) % n) for...  6.78 us
    pallas_call x1, Pallas kernels, front(): call(front_kernel, 'front', 5 * 10 ** 8, jax.ShapeDtypeStruct((pairs, bon...  4.41 us
    unnamed x42, local copies, waits for them, and re-layouts  4.31 us
  transfers between devices with their start and end apart: 24, of which 10 were waited for; matrix products, arithmetic and copies ran while one was open for 0% of the time, Pallas kernels for 6%

profile of v8, /device:TPU:1, one launch (start us, length us, event | category | flops | bytes accessed | tf_op | source)
XLA Modules:
  0.0 107.9 jit_solution(10299044908442858921)
XLA Ops:
  0.6 4.1 %collective-permute-start = (bf16[12,128,128]{2,1,0:T(8,128)(2,1)}, bf16[12,128,128]{2,1,0:T(8,128)(2,1)S(1)}, u32[]{:S(2)}, u32[]{:S(2)}) collective-permute-start(bf16[12,128,128]{2,1,0:T(8,128)(2,1)} %bitcast.22), channel_id=1, source_target_pairs={{0,16},{16,32},{32,48},{48,64},{64,80},{80,96},{96,112},{112,128},... | collective-permute-start | bytes 1179656 | tf_op jit(solution)/shard_map/ppermute | solution.py:333
  4.8 4.4 %front.1.x3_any = bf16[16,12,32,128]{3,2,1,0:T(8,128)(2,1)} custom-call(bf16[16,128,128]{2,1,0:T(8,128)(2,1)} %bitcast.17, bf16[12,128,128]{2,1,0:T(8,128)(2,1)} %bitcast.20, bf16[192,12]{1,0:T(8,128)(2,1)} %bitcast.13, bf16[192,12]{1,0:T(8,128)(2,1)} %bitcast.15), custom_call_target="tpu_custom_call" | custom-call | flops 500000000 | bytes 8000000 | tf_op jit(solution)/shard_map/front/pallas_call | solution.py:235
  9.2 3.6 %collective-permute-done = bf16[12,128,128]{2,1,0:T(8,128)(2,1)S(1)} collective-permute-done((bf16[12,128,128]{2,1,0:T(8,128)(2,1)}, bf16[12,128,128]{2,1,0:T(8,128)(2,1)S(1)}, u32[]{:S(2)}, u32[]{:S(2)}) %collective-permute-start) | collective-permute-done | bytes 393248 | tf_op jit(solution)/shard_map/ppermute | solution.py:333
  12.9 5.7 %collective-permute-start.2 = (bf16[12,128,128]{2,1,0:T(8,128)(2,1)S(1)}, bf16[12,128,128]{2,1,0:T(8,128)(2,1)S(1)}, u32[]{:S(2)}, u32[]{:S(2)}) collective-permute-start(bf16[12,128,128]{2,1,0:T(8,128)(2,1)S(1)} %broadcast_select_fusion.rest_0_), channel_id=1, source_target_pairs={{0,2},{1,15},{2,4},{3,1},{4,6},{5,3},{6,8},{7,5},{8,10},{9,7},{10,... | collective-permute-start | bytes 1179656 | tf_op jit(solution)/shard_map/ppermute | solution.py:318
  19.9 4.8 %collective-permute-done.2.rest_2_ = bf16[12,128,128]{2,1,0:T(8,128)(2,1)S(1)} collective-permute-done((bf16[12,128,128]{2,1,0:T(8,128)(2,1)S(1)}, bf16[12,128,128]{2,1,0:T(8,128)(2,1)S(1)}, u32[]{:S(2)}, u32[]{:S(2)}) %collective-permute-start.2) | collective-permute-done | bytes 393248 | tf_op jit(solution)/shard_map/ppermute | solution.py:318
  24.7 3.1 %collective-permute-start.4 = (bf16[12,128,128]{2,1,0:T(8,128)(2,1)S(1)}, bf16[12,128,128]{2,1,0:T(8,128)(2,1)S(1)}, u32[]{:S(2)}, u32[]{:S(2)}) collective-permute-start(bf16[12,128,128]{2,1,0:T(8,128)(2,1)S(1)} %collective-permute-done.2.rest_2_), channel_id=1, source_target_pairs={{0,2},{1,15},{2,4},{3,1},{4,6},{5,3},{6,8},{7,5},{8,10},{9,7},{10,... | collective-permute-start | bytes 1179656 | tf_op jit(solution)/shard_map/ppermute | solution.py:318
  27.8 2.7 %collective-permute-start.5 = (bf16[12,128,128]{2,1,0:T(8,128)(2,1)S(1)}, bf16[12,128,128]{2,1,0:T(8,128)(2,1)S(1)}, u32[]{:S(2)}, u32[]{:S(2)}) collective-permute-start(bf16[12,128,128]{2,1,0:T(8,128)(2,1)S(1)} %collective-permute-done.3.rest_3_), channel_id=1, source_target_pairs={{0,2},{1,15},{2,4},{3,1},{4,6},{5,3},{6,8},{7,5},{8,10},{9,7},{10,... | collective-permute-start | bytes 1179656 | tf_op jit(solution)/shard_map/ppermute | solution.py:318
  30.6 2.0 %collective-permute-done.4.rest_4_ = bf16[12,128,128]{2,1,0:T(8,128)(2,1)S(1)} collective-permute-done((bf16[12,128,128]{2,1,0:T(8,128)(2,1)S(1)}, bf16[12,128,128]{2,1,0:T(8,128)(2,1)S(1)}, u32[]{:S(2)}, u32[]{:S(2)}) %collective-permute-start.4) | collective-permute-done | bytes 393248 | tf_op jit(solution)/shard_map/ppermute | solution.py:318
  32.5 3.1 %collective-permute-start.6 = (bf16[12,128,128]{2,1,0:T(8,128)(2,1)S(1)}, bf16[12,128,128]{2,1,0:T(8,128)(2,1)S(1)}, u32[]{:S(2)}, u32[]{:S(2)}) collective-permute-start(bf16[12,128,128]{2,1,0:T(8,128)(2,1)S(1)} %collective-permute-done.4.rest_4_), channel_id=1, source_target_pairs={{0,2},{1,15},{2,4},{3,1},{4,6},{5,3},{6,8},{7,5},{8,10},{9,7},{10,... | collective-permute-start | bytes 1179656 | tf_op jit(solution)/shard_map/ppermute | solution.py:318
  35.7 3.4 %collective-permute-start.1 = (bf16[12,128,128]{2,1,0:T(8,128)(2,1)S(1)}, bf16[12,128,128]{2,1,0:T(8,128)(2,1)S(1)}, u32[]{:S(2)}, u32[]{:S(2)}) collective-permute-start(bf16[12,128,128]{2,1,0:T(8,128)(2,1)S(1)} %broadcast_select_fusion.rest_0_), channel_id=1, source_target_pairs={{0,1},{1,0},{2,3},{3,2},{4,5},{5,4},{6,7},{7,6},{8,9},{9,8},{10,11... | collective-permute-start | bytes 1179656 | tf_op jit(solution)/shard_map/ppermute | solution.py:328
  39.5 3.0 %collective-permute-start.7 = (bf16[12,128,128]{2,1,0:T(8,128)(2,1)S(1)}, bf16[12,128,128]{2,1,0:T(8,128)(2,1)S(1)}, u32[]{:S(2)}, u32[]{:S(2)}) collective-permute-start(bf16[12,128,128]{2,1,0:T(8,128)(2,1)S(1)} %collective-permute-done.5.rest_5_), channel_id=1, source_target_pairs={{0,2},{1,15},{2,4},{3,1},{4,6},{5,3},{6,8},{7,5},{8,10},{9,7},{10,... | collective-permute-start | bytes 1179656 | tf_op jit(solution)/shard_map/ppermute | solution.py:318
  42.5 1.6 %collective-permute-start.8 = (bf16[12,128,128]{2,1,0:T(8,128)(2,1)S(1)}, bf16[12,128,128]{2,1,0:T(8,128)(2,1)S(1)}, u32[]{:S(2)}, u32[]{:S(2)}) collective-permute-start(bf16[12,128,128]{2,1,0:T(8,128)(2,1)S(1)} %collective-permute-done.6.rest_6_), channel_id=1, source_target_pairs={{0,2},{1,15},{2,4},{3,1},{4,6},{5,3},{6,8},{7,5},{8,10},{9,7},{10,... | collective-permute-start | bytes 1179656 | tf_op jit(solution)/shard_map/ppermute | solution.py:318
  44.1 4.0 %collective-permute-start.12 = (bf16[12,128,128]{2,1,0:T(8,128)(2,1)S(1)}, bf16[12,128,128]{2,1,0:T(8,128)(2,1)S(1)}, u32[]{:S(2)}, u32[]{:S(2)}) collective-permute-start(bf16[12,128,128]{2,1,0:T(8,128)(2,1)S(1)} %collective-permute-done.5.rest_5_), channel_id=1, source_target_pairs={{0,1},{1,0},{2,3},{3,2},{4,5},{5,4},{6,7},{7,6},{8,9},{9,8},{10,11... | collective-permute-start | bytes 1179656 | tf_op jit(solution)/shard_map/ppermute | solution.py:328
  48.6 3.6 %collective-permute-start.10 = (bf16[12,128,128]{2,1,0:T(8,128)(2,1)S(1)}, bf16[12,128,128]{2,1,0:T(8,128)(2,1)S(1)}, u32[]{:S(2)}, u32[]{:S(2)}) collective-permute-start(bf16[12,128,128]{2,1,0:T(8,128)(2,1)S(1)} %collective-permute-done.7.rest_7_), channel_id=1, source_target_pairs={{0,1},{1,0},{2,3},{3,2},{4,5},{5,4},{6,7},{7,6},{8,9},{9,8},{10,11... | collective-permute-start | bytes 1179656 | tf_op jit(solution)/shard_map/ppermute | solution.py:328
  52.2 4.8 %collective-permute-start.9 = (bf16[12,128,128]{2,1,0:T(8,128)(2,1)S(1)}, bf16[12,128,128]{2,1,0:T(8,128)(2,1)}, u32[]{:S(2)}, u32[]{:S(2)}) collective-permute-start(bf16[12,128,128]{2,1,0:T(8,128)(2,1)S(1)} %collective-permute-done.8.rest_8_), channel_id=1, source_target_pairs={{0,1},{1,0},{2,3},{3,2},{4,5},{5,4},{6,7},{7,6},{8,9},{9,8},{10,11... | collective-permute-start | bytes 1179656 | tf_op jit(solution)/shard_map/ppermute | solution.py:328
  59.5 15.3 %back.1 = (f32[16,128,128]{2,1,0:T(8,128)}, f32[4,128]{1,0:T(4,128)}) custom-call(s32[16]{0:T(128)} %charge_ref.1, s32[1]{0:T(128)S(6)} %copy.10.rank_ref, bf16[16,128,128]{2,1,0:T(8,128)(2,1)} %bitcast.18, bf16[12,128,128]{2,1,0:T(8,128)(2,1)} %bitcast.21, bf16[192,192]{1,0:T(8,128)(2,1)} %copy-done.4, bf16[16,12,32,128]{3,2,1,0:T(8,128)(2,1)} %front.1.x3_any, ...), custom_call_target="tpu_custom_call" | custom-call | flops 4000000000 | bytes 8000000 | tf_op jit(solution)/shard_map/back/pallas_call | solution.py:257
  77.0 3.0 %collective-permute-done.17 = f32[4,128]{1,0:T(4,128)S(1)} collective-permute-done((f32[4,128]{1,0:T(4,128)S(1)}, f32[4,128]{1,0:T(4,128)S(1)}, u32[]{:S(2)}, u32[]{:S(2)}) %collective-permute-start.17) | collective-permute-done | bytes 2080 | tf_op jit(solution)/shard_map/ppermute | solution.py:313
  80.1 3.9 %collective-permute-done.18 = f32[4,128]{1,0:T(4,128)S(1)} collective-permute-done((f32[4,128]{1,0:T(4,128)S(1)}, f32[4,128]{1,0:T(4,128)S(1)}, u32[]{:S(2)}, u32[]{:S(2)}) %collective-permute-start.18) | collective-permute-done | bytes 2080 | tf_op jit(solution)/shard_map/ppermute | solution.py:313
  84.6 4.5 %collective-permute-done.19.other_ref = f32[4,128]{1,0:T(4,128)S(1)} collective-permute-done((f32[4,128]{1,0:T(4,128)S(1)}, f32[4,128]{1,0:T(4,128)S(1)}, u32[]{:S(2)}, u32[]{:S(2)}) %collective-permute-start.19) | collective-permute-done | bytes 2080 | tf_op jit(solution)/shard_map/ppermute | solution.py:313
  89.9 2.3 %collective-permute-start.20 = (f32[2,128]{1,0:T(2,128)S(1)}, f32[2,128]{1,0:T(2,128)S(1)}, u32[]{:S(2)}, u32[]{:S(2)}) collective-permute-start(f32[2,128]{1,0:T(2,128)S(1)} %get-tuple-element.24), channel_id=1, source_target_pairs={{0,17},{1,16},{2,19},{3,18},{4,21},{5,20},{6,23},{7,22},{8,25},{9,... | collective-permute-start | bytes 3080 | tf_op jit(solution)/shard_map/ppermute | solution.py:313
  94.4 2.1 %collective-permute-start.21 = (f32[2,128]{1,0:T(2,128)S(1)}, f32[2,128]{1,0:T(2,128)S(1)}, u32[]{:S(2)}, u32[]{:S(2)}) collective-permute-start(f32[2,128]{1,0:T(2,128)S(1)} %add.28), channel_id=1, source_target_pairs={{0,49},{1,48},{2,51},{3,50},{4,53},{5,52},{6,55},{7,54},{8,57},{9,... | collective-permute-start | bytes 3080 | tf_op jit(solution)/shard_map/ppermute | solution.py:313
  96.5 2.2 %collective-permute-done.21 = f32[2,128]{1,0:T(2,128)S(1)} collective-permute-done((f32[2,128]{1,0:T(2,128)S(1)}, f32[2,128]{1,0:T(2,128)S(1)}, u32[]{:S(2)}, u32[]{:S(2)}) %collective-permute-start.21) | collective-permute-done | bytes 1056 | tf_op jit(solution)/shard_map/ppermute | solution.py:313
  98.7 2.9 %collective-permute-start.22 = (f32[2,128]{1,0:T(2,128)S(1)}, f32[2,128]{1,0:T(2,128)S(1)}, u32[]{:S(2)}, u32[]{:S(2)}) collective-permute-start(f32[2,128]{1,0:T(2,128)S(1)} %add.30), channel_id=1, source_target_pairs={{0,65},{1,64},{2,67},{3,66},{4,69},{5,68},{6,71},{7,70},{8,73},{9,... | collective-permute-start | bytes 3080 | tf_op jit(solution)/shard_map/ppermute | solution.py:313
  102.8 3.2 %collective-permute-start.23 = (f32[2,128]{1,0:T(2,128)S(1)}, f32[2,128]{1,0:T(2,128)S(1)}, u32[]{:S(2)}, u32[]{:S(2)}) collective-permute-start(f32[2,128]{1,0:T(2,128)S(1)} %add.31), channel_id=1, source_target_pairs={{0,193},{1,192},{2,195},{3,194},{4,197},{5,196},{6,199},{7,198},{8... | collective-permute-start | bytes 3080 | tf_op jit(solution)/shard_map/ppermute | solution.py:313
  (82 shorter events, 13.3 us)
Async XLA Ops:
  0.6 12.2 %collective-permute-start = (bf16[12,128,128]{2,1,0:T(8,128)(2,1)}, bf16[12,128,128]{2,1,0:T(8,128)(2,1)S(1)}, u32[]{:S(2)}, u32[]{:S(2)}) collective-permute-start(bf16[12,128,128]{2,1,0:T(8,128)(2,1)} %bitcast.22), channel_id=1, source_target_pairs={{0,16},{16,32},{32,48},{48,64},{64,80},{80,96},{96,112},{112,128},... | collective-permute-start | bytes 1179656 | tf_op jit(solution)/shard_map/ppermute | solution.py:333
  12.9 11.8 %collective-permute-start.2 = (bf16[12,128,128]{2,1,0:T(8,128)(2,1)S(1)}, bf16[12,128,128]{2,1,0:T(8,128)(2,1)S(1)}, u32[]{:S(2)}, u32[]{:S(2)}) collective-permute-start(bf16[12,128,128]{2,1,0:T(8,128)(2,1)S(1)} %broadcast_select_fusion.rest_0_), channel_id=1, source_target_pairs={{0,2},{1,15},{2,4},{3,1},{4,6},{5,3},{6,8},{7,5},{8,10},{9,7},{10,... | collective-permute-start | bytes 1179656 | tf_op jit(solution)/shard_map/ppermute | solution.py:318
  19.9 7.9 %collective-permute-start.3 = (bf16[12,128,128]{2,1,0:T(8,128)(2,1)S(1)}, bf16[12,128,128]{2,1,0:T(8,128)(2,1)S(1)}, u32[]{:S(2)}, u32[]{:S(2)}) collective-permute-start(bf16[12,128,128]{2,1,0:T(8,128)(2,1)S(1)} %broadcast_select_fusion.rest_0_), channel_id=1, source_target_pairs={{0,15},{1,2},{2,1},{3,4},{4,3},{5,6},{6,5},{7,8},{8,7},{9,10},{10,... | collective-permute-start | bytes 1179656 | tf_op jit(solution)/shard_map/ppermute | solution.py:323
  24.7 7.8 %collective-permute-start.4 = (bf16[12,128,128]{2,1,0:T(8,128)(2,1)S(1)}, bf16[12,128,128]{2,1,0:T(8,128)(2,1)S(1)}, u32[]{:S(2)}, u32[]{:S(2)}) collective-permute-start(bf16[12,128,128]{2,1,0:T(8,128)(2,1)S(1)} %collective-permute-done.2.rest_2_), channel_id=1, source_target_pairs={{0,2},{1,15},{2,4},{3,1},{4,6},{5,3},{6,8},{7,5},{8,10},{9,7},{10,... | collective-permute-start | bytes 1179656 | tf_op jit(solution)/shard_map/ppermute | solution.py:318
  27.8 11.7 %collective-permute-start.5 = (bf16[12,128,128]{2,1,0:T(8,128)(2,1)S(1)}, bf16[12,128,128]{2,1,0:T(8,128)(2,1)S(1)}, u32[]{:S(2)}, u32[]{:S(2)}) collective-permute-start(bf16[12,128,128]{2,1,0:T(8,128)(2,1)S(1)} %collective-permute-done.3.rest_3_), channel_id=1, source_target_pairs={{0,2},{1,15},{2,4},{3,1},{4,6},{5,3},{6,8},{7,5},{8,10},{9,7},{10,... | collective-permute-start | bytes 1179656 | tf_op jit(solution)/shard_map/ppermute | solution.py:318
  32.5 9.9 %collective-permute-start.6 = (bf16[12,128,128]{2,1,0:T(8,128)(2,1)S(1)}, bf16[12,128,128]{2,1,0:T(8,128)(2,1)S(1)}, u32[]{:S(2)}, u32[]{:S(2)}) collective-permute-start(bf16[12,128,128]{2,1,0:T(8,128)(2,1)S(1)} %collective-permute-done.4.rest_4_), channel_id=1, source_target_pairs={{0,2},{1,15},{2,4},{3,1},{4,6},{5,3},{6,8},{7,5},{8,10},{9,7},{10,... | collective-permute-start | bytes 1179656 | tf_op jit(solution)/shard_map/ppermute | solution.py:318
  35.7 8.4 %collective-permute-start.1 = (bf16[12,128,128]{2,1,0:T(8,128)(2,1)S(1)}, bf16[12,128,128]{2,1,0:T(8,128)(2,1)S(1)}, u32[]{:S(2)}, u32[]{:S(2)}) collective-permute-start(bf16[12,128,128]{2,1,0:T(8,128)(2,1)S(1)} %broadcast_select_fusion.rest_0_), channel_id=1, source_target_pairs={{0,1},{1,0},{2,3},{3,2},{4,5},{5,4},{6,7},{7,6},{8,9},{9,8},{10,11... | collective-permute-start | bytes 1179656 | tf_op jit(solution)/shard_map/ppermute | solution.py:328
  39.0 9.1 %collective-permute-start.14 = (bf16[12,128,128]{2,1,0:T(8,128)(2,1)S(1)}, bf16[12,128,128]{2,1,0:T(8,128)(2,1)S(1)}, u32[]{:S(2)}, u32[]{:S(2)}) collective-permute-start(bf16[12,128,128]{2,1,0:T(8,128)(2,1)S(1)} %collective-permute-done.3.rest_3_), channel_id=1, source_target_pairs={{0,1},{1,0},{2,3},{3,2},{4,5},{5,4},{6,7},{7,6},{8,9},{9,8},{10,11... | collective-permute-start | bytes 1179656 | tf_op jit(solution)/shard_map/ppermute | solution.py:328
  39.1 9.1 %collective-permute-start.15 = (bf16[12,128,128]{2,1,0:T(8,128)(2,1)S(1)}, bf16[12,128,128]{2,1,0:T(8,128)(2,1)S(1)}, u32[]{:S(2)}, u32[]{:S(2)}) collective-permute-start(bf16[12,128,128]{2,1,0:T(8,128)(2,1)S(1)} %collective-permute-done.2.rest_2_), channel_id=1, source_target_pairs={{0,1},{1,0},{2,3},{3,2},{4,5},{5,4},{6,7},{7,6},{8,9},{9,8},{10,11... | collective-permute-start | bytes 1179656 | tf_op jit(solution)/shard_map/ppermute | solution.py:328
  39.5 9.1 %collective-permute-start.7 = (bf16[12,128,128]{2,1,0:T(8,128)(2,1)S(1)}, bf16[12,128,128]{2,1,0:T(8,128)(2,1)S(1)}, u32[]{:S(2)}, u32[]{:S(2)}) collective-permute-start(bf16[12,128,128]{2,1,0:T(8,128)(2,1)S(1)} %collective-permute-done.5.rest_5_), channel_id=1, source_target_pairs={{0,2},{1,15},{2,4},{3,1},{4,6},{5,3},{6,8},{7,5},{8,10},{9,7},{10,... | collective-permute-start | bytes 1179656 | tf_op jit(solution)/shard_map/ppermute | solution.py:318
  42.5 9.7 %collective-permute-start.8 = (bf16[12,128,128]{2,1,0:T(8,128)(2,1)S(1)}, bf16[12,128,128]{2,1,0:T(8,128)(2,1)S(1)}, u32[]{:S(2)}, u32[]{:S(2)}) collective-permute-start(bf16[12,128,128]{2,1,0:T(8,128)(2,1)S(1)} %collective-permute-done.6.rest_6_), channel_id=1, source_target_pairs={{0,2},{1,15},{2,4},{3,1},{4,6},{5,3},{6,8},{7,5},{8,10},{9,7},{10,... | collective-permute-start | bytes 1179656 | tf_op jit(solution)/shard_map/ppermute | solution.py:318
  44.1 13.6 %collective-permute-start.12 = (bf16[12,128,128]{2,1,0:T(8,128)(2,1)S(1)}, bf16[12,128,128]{2,1,0:T(8,128)(2,1)S(1)}, u32[]{:S(2)}, u32[]{:S(2)}) collective-permute-start(bf16[12,128,128]{2,1,0:T(8,128)(2,1)S(1)} %collective-permute-done.5.rest_5_), channel_id=1, source_target_pairs={{0,1},{1,0},{2,3},{3,2},{4,5},{5,4},{6,7},{7,6},{8,9},{9,8},{10,11... | collective-permute-start | bytes 1179656 | tf_op jit(solution)/shard_map/ppermute | solution.py:328
  48.1 9.6 %collective-permute-start.13 = (bf16[12,128,128]{2,1,0:T(8,128)(2,1)S(1)}, bf16[12,128,128]{2,1,0:T(8,128)(2,1)S(1)}, u32[]{:S(2)}, u32[]{:S(2)}) collective-permute-start(bf16[12,128,128]{2,1,0:T(8,128)(2,1)S(1)} %collective-permute-done.4.rest_4_), channel_id=1, source_target_pairs={{0,1},{1,0},{2,3},{3,2},{4,5},{5,4},{6,7},{7,6},{8,9},{9,8},{10,11... | collective-permute-start | bytes 1179656 | tf_op jit(solution)/shard_map/ppermute | solution.py:328
  48.2 9.5 %collective-permute-start.11 = (bf16[12,128,128]{2,1,0:T(8,128)(2,1)S(1)}, bf16[12,128,128]{2,1,0:T(8,128)(2,1)S(1)}, u32[]{:S(2)}, u32[]{:S(2)}) collective-permute-start(bf16[12,128,128]{2,1,0:T(8,128)(2,1)S(1)} %collective-permute-done.6.rest_6_), channel_id=1, source_target_pairs={{0,1},{1,0},{2,3},{3,2},{4,5},{5,4},{6,7},{7,6},{8,9},{9,8},{10,11... | collective-permute-start | bytes 1179656 | tf_op jit(solution)/shard_map/ppermute | solution.py:328
  48.6 9.1 %collective-permute-start.10 = (bf16[12,128,128]{2,1,0:T(8,128)(2,1)S(1)}, bf16[12,128,128]{2,1,0:T(8,128)(2,1)S(1)}, u32[]{:S(2)}, u32[]{:S(2)}) collective-permute-start(bf16[12,128,128]{2,1,0:T(8,128)(2,1)S(1)} %collective-permute-done.7.rest_7_), channel_id=1, source_target_pairs={{0,1},{1,0},{2,3},{3,2},{4,5},{5,4},{6,7},{7,6},{8,9},{9,8},{10,11... | collective-permute-start | bytes 1179656 | tf_op jit(solution)/shard_map/ppermute | solution.py:328
  52.2 7.2 %collective-permute-start.9 = (bf16[12,128,128]{2,1,0:T(8,128)(2,1)S(1)}, bf16[12,128,128]{2,1,0:T(8,128)(2,1)}, u32[]{:S(2)}, u32[]{:S(2)}) collective-permute-start(bf16[12,128,128]{2,1,0:T(8,128)(2,1)S(1)} %collective-permute-done.8.rest_8_), channel_id=1, source_target_pairs={{0,1},{1,0},{2,3},{3,2},{4,5},{5,4},{6,7},{7,6},{8,9},{9,8},{10,11... | collective-permute-start | bytes 1179656 | tf_op jit(solution)/shard_map/ppermute | solution.py:328
  74.8 1.5 %collective-permute-start.16 = (f32[4,128]{1,0:T(4,128)}, f32[4,128]{1,0:T(4,128)S(1)}, u32[]{:S(2)}, u32[]{:S(2)}) collective-permute-start(f32[4,128]{1,0:T(4,128)} %get-tuple-element.23.mine_ref), channel_id=1, source_target_pairs={{0,1},{1,0},{2,3},{3,2},{4,5},{5,4},{6,7},{7,6},{8,9},{9,8},{10,11... | collective-permute-start | bytes 6152 | tf_op jit(solution)/shard_map/ppermute | solution.py:313
  77.0 3.0 %collective-permute-start.17 = (f32[4,128]{1,0:T(4,128)S(1)}, f32[4,128]{1,0:T(4,128)S(1)}, u32[]{:S(2)}, u32[]{:S(2)}) collective-permute-start(f32[4,128]{1,0:T(4,128)S(1)} %add.25), channel_id=1, source_target_pairs={{0,3},{1,2},{2,1},{3,0},{4,7},{5,6},{6,5},{7,4},{8,11},{9,10},{10,... | collective-permute-start | bytes 6152 | tf_op jit(solution)/shard_map/ppermute | solution.py:313
  80.1 3.9 %collective-permute-start.18 = (f32[4,128]{1,0:T(4,128)S(1)}, f32[4,128]{1,0:T(4,128)S(1)}, u32[]{:S(2)}, u32[]{:S(2)}) collective-permute-start(f32[4,128]{1,0:T(4,128)S(1)} %add.26), channel_id=1, source_target_pairs={{0,5},{1,4},{2,7},{3,6},{4,1},{5,0},{6,3},{7,2},{8,13},{9,12},{10,... | collective-permute-start | bytes 6152 | tf_op jit(solution)/shard_map/ppermute | solution.py:313
  84.0 5.1 %collective-permute-start.19 = (f32[4,128]{1,0:T(4,128)S(1)}, f32[4,128]{1,0:T(4,128)S(1)}, u32[]{:S(2)}, u32[]{:S(2)}) collective-permute-start(f32[4,128]{1,0:T(4,128)S(1)} %add.27.half_ref), channel_id=1, source_target_pairs={{0,13},{1,12},{2,15},{3,14},{4,9},{5,8},{6,11},{7,10},{8,5},{9,4},... | collective-permute-start | bytes 6152 | tf_op jit(solution)/shard_map/ppermute | solution.py:313
  89.9 4.4 %collective-permute-start.20 = (f32[2,128]{1,0:T(2,128)S(1)}, f32[2,128]{1,0:T(2,128)S(1)}, u32[]{:S(2)}, u32[]{:S(2)}) collective-permute-start(f32[2,128]{1,0:T(2,128)S(1)} %get-tuple-element.24), channel_id=1, source_target_pairs={{0,17},{1,16},{2,19},{3,18},{4,21},{5,20},{6,23},{7,22},{8,25},{9,... | collective-permute-start | bytes 3080 | tf_op jit(solution)/shard_map/ppermute | solution.py:313
  94.4 4.3 %collective-permute-start.21 = (f32[2,128]{1,0:T(2,128)S(1)}, f32[2,128]{1,0:T(2,128)S(1)}, u32[]{:S(2)}, u32[]{:S(2)}) collective-permute-start(f32[2,128]{1,0:T(2,128)S(1)} %add.28), channel_id=1, source_target_pairs={{0,49},{1,48},{2,51},{3,50},{4,53},{5,52},{6,55},{7,54},{8,57},{9,... | collective-permute-start | bytes 3080 | tf_op jit(solution)/shard_map/ppermute | solution.py:313
  98.7 4.2 %collective-permute-start.22 = (f32[2,128]{1,0:T(2,128)S(1)}, f32[2,128]{1,0:T(2,128)S(1)}, u32[]{:S(2)}, u32[]{:S(2)}) collective-permute-start(f32[2,128]{1,0:T(2,128)S(1)} %add.30), channel_id=1, source_target_pairs={{0,65},{1,64},{2,67},{3,66},{4,69},{5,68},{6,71},{7,70},{8,73},{9,... | collective-permute-start | bytes 3080 | tf_op jit(solution)/shard_map/ppermute | solution.py:313
  102.8 4.4 %collective-permute-start.23 = (f32[2,128]{1,0:T(2,128)S(1)}, f32[2,128]{1,0:T(2,128)S(1)}, u32[]{:S(2)}, u32[]{:S(2)}) collective-permute-start(f32[2,128]{1,0:T(2,128)S(1)} %add.31), channel_id=1, source_target_pairs={{0,193},{1,192},{2,195},{3,194},{4,197},{5,196},{6,199},{7,198},{8... | collective-permute-start | bytes 3080 | tf_op jit(solution)/shard_map/ppermute | solution.py:313
  (21 other events, 276.9 us)

commit v9 on v8

--- a/solution.py
+++ b/solution.py
@@ -47,14 +47,14 @@
         xt_ref[j * 16 : (j + 1) * 16] = jnp.swapaxes(src_ref[:, j * 16 : (j + 1) * 16, :], 0, 1)
 
 
-def spread(xt_ref, renv_ref, mpo, x3_ref, begin=0, done=None):
+def spread(xt_ref, renv_ref, mpo, x3_ref, chunk, begin=0, done=None):
     states, pairs, width = xt_ref.shape
     bonds = renv_ref.shape[0]
     beside = jnp.concatenate([renv_ref[w] for w in range(bonds)], axis=1)
-    for start in range(begin, states, CHUNK):
-        xa = xt_ref[start : start + CHUNK].reshape(CHUNK * pairs, width)
+    for start in range(begin, states, chunk):
+        xa = xt_ref[start : start + chunk].reshape(chunk * pairs, width)
         first = jnp.dot(xa, beside, preferred_element_type=F32).astype(BF16)
-        for at in range(0, CHUNK, 16):
+        for at in range(0, chunk, 16):
             rows = []
             for i in range(at, at + 16, 2):
                 sides = []
@@ -92,7 +92,7 @@
         sent.append(pltpu.make_async_copy(x3_ref.at[:, :, rows], x3_any.at[:, :, rows], out_sem.at[at // CHUNK]))
         sent[-1].start()
 
-    spread(xt_ref, renv_ref, mpo, x3_ref, 0, done)
+    spread(xt_ref, renv_ref, mpo, x3_ref, CHUNK, 0, done)
     for copy in sent:
         copy.wait()
 
@@ -137,7 +137,7 @@
     for copy in first:
         copy.wait()
     turn(psi_ref, xt_ref)
-    spread(xt_ref, renv_ref, mpo_ref[...], x3_ref, done)
+    spread(xt_ref, renv_ref, mpo_ref[...], x3_ref, CHUNK, done)
     for copy in second:
         copy.wait()
     first_sq = zero
@@ -147,7 +147,7 @@
         u_ref[q] = u.astype(BF16)
         first_sq = first_sq + folded(u * u)
     turn(u_ref, xt_ref)
-    spread(xt_ref, renv_ref, mpo_ref[...], x3_ref)
+    spread(xt_ref, renv_ref, mpo_ref[...], x3_ref, CHUNK)
     sq, inner, own = zero, zero, zero
     sent = []
     for q in range(pairs):
@@ -164,15 +164,15 @@
         copy.wait()
 
 
-def settle_kernel(count, half_ref, other_ref, mine_ref, twin_ref, share_ref, out_ref):
+def settle_kernel(count, half_ref, other_ref, pair_ref, share_ref, out_ref):
     width = half_ref.shape[1]
     total = jnp.sum(half_ref[...] + other_ref[...], axis=1, keepdims=True)
     first_sq, sq, inner, own = [total[i : i + 1] for i in range(4)]
     one = lax.rsqrt(first_sq / count + 1e-06)
     scale = one * lax.rsqrt(one * one * sq / count + 1e-06)
     out_ref[...] = jnp.where(iota((8, width), 0) == 0, scale, inner / own)
-    mine = jnp.sum(mine_ref[1:2], axis=1, keepdims=True)
-    twin = jnp.sum(twin_ref[1:2], axis=1, keepdims=True)
+    mine = jnp.sum(pair_ref[0:1], axis=1, keepdims=True)
+    twin = jnp.sum(pair_ref[1:2], axis=1, keepdims=True)
     row = iota((2, width), 0)
     here = jnp.where(row == (lax.axis_index("sec") & 1), mine, twin)
     share = jnp.log(float(lax.axis_size("sec")) * here / sq)
@@ -277,17 +277,17 @@
     )(charge, rank, psi, renv, mpo, x3, *blocks)
 
 
-def settle(half, other, mine, twin_stat, count):
+def settle(half, other, pair, count):
     width = half.shape[1]
     return call(
         functools.partial(settle_kernel, count),
         "settle",
         10**4,
         (jax.ShapeDtypeStruct((2, width), F32), jax.ShapeDtypeStruct((8, width), F32)),
-        [VMEM_SPEC] * 4,
+        [VMEM_SPEC] * 3,
         (VMEM_SPEC, VMEM_SPEC),
         [],
-    )(half, other, mine, twin_stat)
+    )(half, other, pair)
 
 
 def finish(v, out):
@@ -366,13 +366,15 @@
 
     twin_stat = partner(stat, 1)
     total = stat + twin_stat
-    for bits in (3, 5):
-        total = total + partner(total, bits)
-    share, out = settle(total, partner(total, 13), stat, twin_stat, count)
+    pair = jnp.concatenate([stat[1:2], twin_stat[1:2]], axis=0)
+    got, pair = lax.optimization_barrier((partner(total, 3), pair))
+    total = total + got
+    total = total + partner(total, 5)
+    share, out = settle(total, partner(total, 13), pair, count)
     state = finish(v, out)
     for bits in (1, 3, 4, 12):
         share = share + partner(share, nsec * bits + 1)
-        if bits == 1:
+        if bits == 3:
             share, state = lax.optimization_barrier((share, state))
     wanted = (iota(share.shape, 0) == sector % 2) & (iota(share.shape, 1) <= segment)
     weight = jnp.sum(jnp.where(wanted, share, 0.0))

time: 108 us -> 108 us (level)
  waiting for transfers between devices: 27.2 us -> 25.7 us
    ppermute x8, waiting for transfers between devices: 16.7 us -> 15.3 us  [partner(): return lax.ppermute(value, axes, [(i, i ^ bits) for i in range(n)])]
    unnamed x42 -> x40, local copies, waits for them, and re-layouts: 4.31 us -> 3.61 us
  transfers between devices with their start and end apart: 24 -> 24, of which waited for: 10 -> 10; matrix products, arithmetic and copies ran while one was open for 0% -> 1% of each run, Pallas kernels for 6% -> 6%
where the time goes in v9:
time: 108 us; the launch traced here: 107 us
  starting transfers between devices  52.4 us (49%)
  waiting for transfers between devices  25.7 us (24%)
  Pallas kernels  21.5 us (20%)
  local copies, waits for them, and re-layouts  4.81 us (4%)
  between operations  1.58 us (1%)
  other arithmetic  1.43 us (1%)
    ppermute x6, starting transfers between devices, hop(): lax.ppermute(value, 'sec', [(i, (i + (2 if i % 2 == 0 else -2)) % n) for...  19.2 us
    ppermute x8, starting transfers between devices, twin(): return lax.ppermute(value, 'sec', [(i, i ^ 1) for i in range(n)])  16.7 us
    pallas_call x1, Pallas kernels, back(): call(back_kernel, 'back', 4 * 10 ** 9, (jax.ShapeDtypeStruct((pairs, widt...  15.3 us
    ppermute x8, waiting for transfers between devices, partner(): return lax.ppermute(value, axes, [(i, i ^ bits) for i in range(n)])  15.3 us
    ppermute x8, starting transfers between devices, partner(): return lax.ppermute(value, axes, [(i, i ^ bits) for i in range(n)])  12.4 us
    ppermute x6, waiting for transfers between devices, hop(): lax.ppermute(value, 'sec', [(i, (i + (2 if i % 2 == 0 else -2)) % n) for...  6.78 us
    pallas_call x1, Pallas kernels, front(): call(front_kernel, 'front', 5 * 10 ** 8, jax.ShapeDtypeStruct((pairs, bon...  4.41 us
    ppermute x1, starting transfers between devices, from_behind(): return lax.ppermute(value, 'seg', [(i, i + 1) for i in range(n - 1)])  4.1 us
  transfers between devices with their start and end apart: 24, of which 10 were waited for; matrix products, arithmetic and copies ran while one was open for 1% of the time, Pallas kernels for 6%

profile of v9, /device:TPU:1, one launch (start us, length us, event | category | flops | bytes accessed | tf_op | source)
XLA Modules:
  0.0 107.4 jit_solution(2963999989902721691)
XLA Ops:
  0.6 4.1 %collective-permute-start = (bf16[12,128,128]{2,1,0:T(8,128)(2,1)}, bf16[12,128,128]{2,1,0:T(8,128)(2,1)S(1)}, u32[]{:S(2)}, u32[]{:S(2)}) collective-permute-start(bf16[12,128,128]{2,1,0:T(8,128)(2,1)} %bitcast.22), channel_id=1, source_target_pairs={{0,16},{16,32},{32,48},{48,64},{64,80},{80,96},{96,112},{112,128},... | collective-permute-start | bytes 1179656 | tf_op jit(solution)/shard_map/ppermute | solution.py:333
  4.8 4.4 %front.1.x3_any = bf16[16,12,32,128]{3,2,1,0:T(8,128)(2,1)} custom-call(bf16[16,128,128]{2,1,0:T(8,128)(2,1)} %bitcast.17, bf16[12,128,128]{2,1,0:T(8,128)(2,1)} %bitcast.20, bf16[192,12]{1,0:T(8,128)(2,1)} %bitcast.13, bf16[192,12]{1,0:T(8,128)(2,1)} %bitcast.15), custom_call_target="tpu_custom_call" | custom-call | flops 500000000 | bytes 8000000 | tf_op jit(solution)/shard_map/front/pallas_call | solution.py:235
  9.2 3.6 %collective-permute-done = bf16[12,128,128]{2,1,0:T(8,128)(2,1)S(1)} collective-permute-done((bf16[12,128,128]{2,1,0:T(8,128)(2,1)}, bf16[12,128,128]{2,1,0:T(8,128)(2,1)S(1)}, u32[]{:S(2)}, u32[]{:S(2)}) %collective-permute-start) | collective-permute-done | bytes 393248 | tf_op jit(solution)/shard_map/ppermute | solution.py:333
  12.9 5.7 %collective-permute-start.2 = (bf16[12,128,128]{2,1,0:T(8,128)(2,1)S(1)}, bf16[12,128,128]{2,1,0:T(8,128)(2,1)S(1)}, u32[]{:S(2)}, u32[]{:S(2)}) collective-permute-start(bf16[12,128,128]{2,1,0:T(8,128)(2,1)S(1)} %broadcast_select_fusion.rest_0_), channel_id=1, source_target_pairs={{0,2},{1,15},{2,4},{3,1},{4,6},{5,3},{6,8},{7,5},{8,10},{9,7},{10,... | collective-permute-start | bytes 1179656 | tf_op jit(solution)/shard_map/ppermute | solution.py:318
  19.9 4.8 %collective-permute-done.2.rest_2_ = bf16[12,128,128]{2,1,0:T(8,128)(2,1)S(1)} collective-permute-done((bf16[12,128,128]{2,1,0:T(8,128)(2,1)S(1)}, bf16[12,128,128]{2,1,0:T(8,128)(2,1)S(1)}, u32[]{:S(2)}, u32[]{:S(2)}) %collective-permute-start.2) | collective-permute-done | bytes 393248 | tf_op jit(solution)/shard_map/ppermute | solution.py:318
  24.7 3.1 %collective-permute-start.4 = (bf16[12,128,128]{2,1,0:T(8,128)(2,1)S(1)}, bf16[12,128,128]{2,1,0:T(8,128)(2,1)S(1)}, u32[]{:S(2)}, u32[]{:S(2)}) collective-permute-start(bf16[12,128,128]{2,1,0:T(8,128)(2,1)S(1)} %collective-permute-done.2.rest_2_), channel_id=1, source_target_pairs={{0,2},{1,15},{2,4},{3,1},{4,6},{5,3},{6,8},{7,5},{8,10},{9,7},{10,... | collective-permute-start | bytes 1179656 | tf_op jit(solution)/shard_map/ppermute | solution.py:318
  27.8 2.7 %collective-permute-start.5 = (bf16[12,128,128]{2,1,0:T(8,128)(2,1)S(1)}, bf16[12,128,128]{2,1,0:T(8,128)(2,1)S(1)}, u32[]{:S(2)}, u32[]{:S(2)}) collective-permute-start(bf16[12,128,128]{2,1,0:T(8,128)(2,1)S(1)} %collective-permute-done.3.rest_3_), channel_id=1, source_target_pairs={{0,2},{1,15},{2,4},{3,1},{4,6},{5,3},{6,8},{7,5},{8,10},{9,7},{10,... | collective-permute-start | bytes 1179656 | tf_op jit(solution)/shard_map/ppermute | solution.py:318
  30.6 2.0 %collective-permute-done.4.rest_4_ = bf16[12,128,128]{2,1,0:T(8,128)(2,1)S(1)} collective-permute-done((bf16[12,128,128]{2,1,0:T(8,128)(2,1)S(1)}, bf16[12,128,128]{2,1,0:T(8,128)(2,1)S(1)}, u32[]{:S(2)}, u32[]{:S(2)}) %collective-permute-start.4) | collective-permute-done | bytes 393248 | tf_op jit(solution)/shard_map/ppermute | solution.py:318
  32.5 3.1 %collective-permute-start.6 = (bf16[12,128,128]{2,1,0:T(8,128)(2,1)S(1)}, bf16[12,128,128]{2,1,0:T(8,128)(2,1)S(1)}, u32[]{:S(2)}, u32[]{:S(2)}) collective-permute-start(bf16[12,128,128]{2,1,0:T(8,128)(2,1)S(1)} %collective-permute-done.4.rest_4_), channel_id=1, source_target_pairs={{0,2},{1,15},{2,4},{3,1},{4,6},{5,3},{6,8},{7,5},{8,10},{9,7},{10,... | collective-permute-start | bytes 1179656 | tf_op jit(solution)/shard_map/ppermute | solution.py:318
  35.7 3.4 %collective-permute-start.1 = (bf16[12,128,128]{2,1,0:T(8,128)(2,1)S(1)}, bf16[12,128,128]{2,1,0:T(8,128)(2,1)S(1)}, u32[]{:S(2)}, u32[]{:S(2)}) collective-permute-start(bf16[12,128,128]{2,1,0:T(8,128)(2,1)S(1)} %broadcast_select_fusion.rest_0_), channel_id=1, source_target_pairs={{0,1},{1,0},{2,3},{3,2},{4,5},{5,4},{6,7},{7,6},{8,9},{9,8},{10,11... | collective-permute-start | bytes 1179656 | tf_op jit(solution)/shard_map/ppermute | solution.py:328
  39.5 3.0 %collective-permute-start.7 = (bf16[12,128,128]{2,1,0:T(8,128)(2,1)S(1)}, bf16[12,128,128]{2,1,0:T(8,128)(2,1)S(1)}, u32[]{:S(2)}, u32[]{:S(2)}) collective-permute-start(bf16[12,128,128]{2,1,0:T(8,128)(2,1)S(1)} %collective-permute-done.5.rest_5_), channel_id=1, source_target_pairs={{0,2},{1,15},{2,4},{3,1},{4,6},{5,3},{6,8},{7,5},{8,10},{9,7},{10,... | collective-permute-start | bytes 1179656 | tf_op jit(solution)/shard_map/ppermute | solution.py:318
  42.5 1.6 %collective-permute-start.8 = (bf16[12,128,128]{2,1,0:T(8,128)(2,1)S(1)}, bf16[12,128,128]{2,1,0:T(8,128)(2,1)S(1)}, u32[]{:S(2)}, u32[]{:S(2)}) collective-permute-start(bf16[12,128,128]{2,1,0:T(8,128)(2,1)S(1)} %collective-permute-done.6.rest_6_), channel_id=1, source_target_pairs={{0,2},{1,15},{2,4},{3,1},{4,6},{5,3},{6,8},{7,5},{8,10},{9,7},{10,... | collective-permute-start | bytes 1179656 | tf_op jit(solution)/shard_map/ppermute | solution.py:318
  44.1 4.0 %collective-permute-start.12 = (bf16[12,128,128]{2,1,0:T(8,128)(2,1)S(1)}, bf16[12,128,128]{2,1,0:T(8,128)(2,1)S(1)}, u32[]{:S(2)}, u32[]{:S(2)}) collective-permute-start(bf16[12,128,128]{2,1,0:T(8,128)(2,1)S(1)} %collective-permute-done.5.rest_5_), channel_id=1, source_target_pairs={{0,1},{1,0},{2,3},{3,2},{4,5},{5,4},{6,7},{7,6},{8,9},{9,8},{10,11... | collective-permute-start | bytes 1179656 | tf_op jit(solution)/shard_map/ppermute | solution.py:328
  48.6 3.6 %collective-permute-start.10 = (bf16[12,128,128]{2,1,0:T(8,128)(2,1)S(1)}, bf16[12,128,128]{2,1,0:T(8,128)(2,1)S(1)}, u32[]{:S(2)}, u32[]{:S(2)}) collective-permute-start(bf16[12,128,128]{2,1,0:T(8,128)(2,1)S(1)} %collective-permute-done.7.rest_7_), channel_id=1, source_target_pairs={{0,1},{1,0},{2,3},{3,2},{4,5},{5,4},{6,7},{7,6},{8,9},{9,8},{10,11... | collective-permute-start | bytes 1179656 | tf_op jit(solution)/shard_map/ppermute | solution.py:328
  52.2 4.8 %collective-permute-start.9 = (bf16[12,128,128]{2,1,0:T(8,128)(2,1)S(1)}, bf16[12,128,128]{2,1,0:T(8,128)(2,1)}, u32[]{:S(2)}, u32[]{:S(2)}) collective-permute-start(bf16[12,128,128]{2,1,0:T(8,128)(2,1)S(1)} %collective-permute-done.8.rest_8_), channel_id=1, source_target_pairs={{0,1},{1,0},{2,3},{3,2},{4,5},{5,4},{6,7},{7,6},{8,9},{9,8},{10,11... | collective-permute-start | bytes 1179656 | tf_op jit(solution)/shard_map/ppermute | solution.py:328
  59.5 15.3 %back.1 = (f32[16,128,128]{2,1,0:T(8,128)}, f32[4,128]{1,0:T(4,128)}) custom-call(s32[16]{0:T(128)} %charge_ref.1, s32[1]{0:T(128)S(6)} %copy.10.rank_ref, bf16[16,128,128]{2,1,0:T(8,128)(2,1)} %bitcast.18, bf16[12,128,128]{2,1,0:T(8,128)(2,1)} %bitcast.21, bf16[192,192]{1,0:T(8,128)(2,1)} %copy-done.3, bf16[16,12,32,128]{3,2,1,0:T(8,128)(2,1)} %front.1.x3_any, ...), custom_call_target="tpu_custom_call" | custom-call | flops 4000000000 | bytes 8000000 | tf_op jit(solution)/shard_map/back/pallas_call | solution.py:257
  77.2 3.0 %collective-permute-done.17 = f32[4,128]{1,0:T(4,128)S(1)} collective-permute-done((f32[4,128]{1,0:T(4,128)S(1)}, f32[4,128]{1,0:T(4,128)S(1)}, u32[]{:S(2)}, u32[]{:S(2)}) %collective-permute-start.17) | collective-permute-done | bytes 2080 | tf_op jit(solution)/shard_map/ppermute | solution.py:313
  80.2 3.9 %collective-permute-done.18 = f32[4,128]{1,0:T(4,128)S(1)} collective-permute-done((f32[4,128]{1,0:T(4,128)S(1)}, f32[4,128]{1,0:T(4,128)S(1)}, u32[]{:S(2)}, u32[]{:S(2)}) %collective-permute-start.18) | collective-permute-done | bytes 2080 | tf_op jit(solution)/shard_map/ppermute | solution.py:313
  84.8 4.5 %collective-permute-done.19.other_ref = f32[4,128]{1,0:T(4,128)S(1)} collective-permute-done((f32[4,128]{1,0:T(4,128)S(1)}, f32[4,128]{1,0:T(4,128)S(1)}, u32[]{:S(2)}, u32[]{:S(2)}) %collective-permute-start.19) | collective-permute-done | bytes 2080 | tf_op jit(solution)/shard_map/ppermute | solution.py:313
  89.4 2.3 %collective-permute-start.20 = (f32[2,128]{1,0:T(2,128)S(1)}, f32[2,128]{1,0:T(2,128)S(1)}, u32[]{:S(2)}, u32[]{:S(2)}) collective-permute-start(f32[2,128]{1,0:T(2,128)S(1)} %get-tuple-element.28), channel_id=1, source_target_pairs={{0,17},{1,16},{2,19},{3,18},{4,21},{5,20},{6,23},{7,22},{8,25},{9,... | collective-permute-start | bytes 3080 | tf_op jit(solution)/shard_map/ppermute | solution.py:313
  91.6 1.3 %collective-permute-done.20 = f32[2,128]{1,0:T(2,128)S(1)} collective-permute-done((f32[2,128]{1,0:T(2,128)S(1)}, f32[2,128]{1,0:T(2,128)S(1)}, u32[]{:S(2)}, u32[]{:S(2)}) %collective-permute-start.20) | collective-permute-done | bytes 1056 | tf_op jit(solution)/shard_map/ppermute | solution.py:313
  92.9 3.0 %collective-permute-start.21 = (f32[2,128]{1,0:T(2,128)S(1)}, f32[2,128]{1,0:T(2,128)S(1)}, u32[]{:S(2)}, u32[]{:S(2)}) collective-permute-start(f32[2,128]{1,0:T(2,128)S(1)} %add.28), channel_id=1, source_target_pairs={{0,49},{1,48},{2,51},{3,50},{4,53},{5,52},{6,55},{7,54},{8,57},{9,... | collective-permute-start | bytes 3080 | tf_op jit(solution)/shard_map/ppermute | solution.py:313
  98.1 2.9 %collective-permute-start.22 = (f32[2,128]{1,0:T(2,128)S(1)}, f32[2,128]{1,0:T(2,128)S(1)}, u32[]{:S(2)}, u32[]{:S(2)}) collective-permute-start(f32[2,128]{1,0:T(2,128)S(1)} %add.29), channel_id=1, source_target_pairs={{0,65},{1,64},{2,67},{3,66},{4,69},{5,68},{6,71},{7,70},{8,73},{9,... | collective-permute-start | bytes 3080 | tf_op jit(solution)/shard_map/ppermute | solution.py:313
  102.3 3.2 %collective-permute-start.23 = (f32[2,128]{1,0:T(2,128)S(1)}, f32[2,128]{1,0:T(2,128)S(1)}, u32[]{:S(2)}, u32[]{:S(2)}) collective-permute-start(f32[2,128]{1,0:T(2,128)S(1)} %add.31), channel_id=1, source_target_pairs={{0,193},{1,192},{2,195},{3,194},{4,197},{5,196},{6,199},{7,198},{8... | collective-permute-start | bytes 3080 | tf_op jit(solution)/shard_map/ppermute | solution.py:313
  (83 shorter events, 12.7 us)
Async XLA Ops:
  0.6 12.2 %collective-permute-start = (bf16[12,128,128]{2,1,0:T(8,128)(2,1)}, bf16[12,128,128]{2,1,0:T(8,128)(2,1)S(1)}, u32[]{:S(2)}, u32[]{:S(2)}) collective-permute-start(bf16[12,128,128]{2,1,0:T(8,128)(2,1)} %bitcast.22), channel_id=1, source_target_pairs={{0,16},{16,32},{32,48},{48,64},{64,80},{80,96},{96,112},{112,128},... | collective-permute-start | bytes 1179656 | tf_op jit(solution)/shard_map/ppermute | solution.py:333
  12.9 11.8 %collective-permute-start.2 = (bf16[12,128,128]{2,1,0:T(8,128)(2,1)S(1)}, bf16[12,128,128]{2,1,0:T(8,128)(2,1)S(1)}, u32[]{:S(2)}, u32[]{:S(2)}) collective-permute-start(bf16[12,128,128]{2,1,0:T(8,128)(2,1)S(1)} %broadcast_select_fusion.rest_0_), channel_id=1, source_target_pairs={{0,2},{1,15},{2,4},{3,1},{4,6},{5,3},{6,8},{7,5},{8,10},{9,7},{10,... | collective-permute-start | bytes 1179656 | tf_op jit(solution)/shard_map/ppermute | solution.py:318
  19.9 7.9 %collective-permute-start.3 = (bf16[12,128,128]{2,1,0:T(8,128)(2,1)S(1)}, bf16[12,128,128]{2,1,0:T(8,128)(2,1)S(1)}, u32[]{:S(2)}, u32[]{:S(2)}) collective-permute-start(bf16[12,128,128]{2,1,0:T(8,128)(2,1)S(1)} %broadcast_select_fusion.rest_0_), channel_id=1, source_target_pairs={{0,15},{1,2},{2,1},{3,4},{4,3},{5,6},{6,5},{7,8},{8,7},{9,10},{10,... | collective-permute-start | bytes 1179656 | tf_op jit(solution)/shard_map/ppermute | solution.py:323
  24.7 7.8 %collective-permute-start.4 = (bf16[12,128,128]{2,1,0:T(8,128)(2,1)S(1)}, bf16[12,128,128]{2,1,0:T(8,128)(2,1)S(1)}, u32[]{:S(2)}, u32[]{:S(2)}) collective-permute-start(bf16[12,128,128]{2,1,0:T(8,128)(2,1)S(1)} %collective-permute-done.2.rest_2_), channel_id=1, source_target_pairs={{0,2},{1,15},{2,4},{3,1},{4,6},{5,3},{6,8},{7,5},{8,10},{9,7},{10,... | collective-permute-start | bytes 1179656 | tf_op jit(solution)/shard_map/ppermute | solution.py:318
  27.8 11.7 %collective-permute-start.5 = (bf16[12,128,128]{2,1,0:T(8,128)(2,1)S(1)}, bf16[12,128,128]{2,1,0:T(8,128)(2,1)S(1)}, u32[]{:S(2)}, u32[]{:S(2)}) collective-permute-start(bf16[12,128,128]{2,1,0:T(8,128)(2,1)S(1)} %collective-permute-done.3.rest_3_), channel_id=1, source_target_pairs={{0,2},{1,15},{2,4},{3,1},{4,6},{5,3},{6,8},{7,5},{8,10},{9,7},{10,... | collective-permute-start | bytes 1179656 | tf_op jit(solution)/shard_map/ppermute | solution.py:318
  32.5 9.9 %collective-permute-start.6 = (bf16[12,128,128]{2,1,0:T(8,128)(2,1)S(1)}, bf16[12,128,128]{2,1,0:T(8,128)(2,1)S(1)}, u32[]{:S(2)}, u32[]{:S(2)}) collective-permute-start(bf16[12,128,128]{2,1,0:T(8,128)(2,1)S(1)} %collective-permute-done.4.rest_4_), channel_id=1, source_target_pairs={{0,2},{1,15},{2,4},{3,1},{4,6},{5,3},{6,8},{7,5},{8,10},{9,7},{10,... | collective-permute-start | bytes 1179656 | tf_op jit(solution)/shard_map/ppermute | solution.py:318
  35.7 8.4 %collective-permute-start.1 = (bf16[12,128,128]{2,1,0:T(8,128)(2,1)S(1)}, bf16[12,128,128]{2,1,0:T(8,128)(2,1)S(1)}, u32[]{:S(2)}, u32[]{:S(2)}) collective-permute-start(bf16[12,128,128]{2,1,0:T(8,128)(2,1)S(1)} %broadcast_select_fusion.rest_0_), channel_id=1, source_target_pairs={{0,1},{1,0},{2,3},{3,2},{4,5},{5,4},{6,7},{7,6},{8,9},{9,8},{10,11... | collective-permute-start | bytes 1179656 | tf_op jit(solution)/shard_map/ppermute | solution.py:328
  39.0 9.1 %collective-permute-start.14 = (bf16[12,128,128]{2,1,0:T(8,128)(2,1)S(1)}, bf16[12,128,128]{2,1,0:T(8,128)(2,1)S(1)}, u32[]{:S(2)}, u32[]{:S(2)}) collective-permute-start(bf16[12,128,128]{2,1,0:T(8,128)(2,1)S(1)} %collective-permute-done.3.rest_3_), channel_id=1, source_target_pairs={{0,1},{1,0},{2,3},{3,2},{4,5},{5,4},{6,7},{7,6},{8,9},{9,8},{10,11... | collective-permute-start | bytes 1179656 | tf_op jit(solution)/shard_map/ppermute | solution.py:328
  39.1 9.1 %collective-permute-start.15 = (bf16[12,128,128]{2,1,0:T(8,128)(2,1)S(1)}, bf16[12,128,128]{2,1,0:T(8,128)(2,1)S(1)}, u32[]{:S(2)}, u32[]{:S(2)}) collective-permute-start(bf16[12,128,128]{2,1,0:T(8,128)(2,1)S(1)} %collective-permute-done.2.rest_2_), channel_id=1, source_target_pairs={{0,1},{1,0},{2,3},{3,2},{4,5},{5,4},{6,7},{7,6},{8,9},{9,8},{10,11... | collective-permute-start | bytes 1179656 | tf_op jit(solution)/shard_map/ppermute | solution.py:328
  39.5 9.1 %collective-permute-start.7 = (bf16[12,128,128]{2,1,0:T(8,128)(2,1)S(1)}, bf16[12,128,128]{2,1,0:T(8,128)(2,1)S(1)}, u32[]{:S(2)}, u32[]{:S(2)}) collective-permute-start(bf16[12,128,128]{2,1,0:T(8,128)(2,1)S(1)} %collective-permute-done.5.rest_5_), channel_id=1, source_target_pairs={{0,2},{1,15},{2,4},{3,1},{4,6},{5,3},{6,8},{7,5},{8,10},{9,7},{10,... | collective-permute-start | bytes 1179656 | tf_op jit(solution)/shard_map/ppermute | solution.py:318
  42.5 9.7 %collective-permute-start.8 = (bf16[12,128,128]{2,1,0:T(8,128)(2,1)S(1)}, bf16[12,128,128]{2,1,0:T(8,128)(2,1)S(1)}, u32[]{:S(2)}, u32[]{:S(2)}) collective-permute-start(bf16[12,128,128]{2,1,0:T(8,128)(2,1)S(1)} %collective-permute-done.6.rest_6_), channel_id=1, source_target_pairs={{0,2},{1,15},{2,4},{3,1},{4,6},{5,3},{6,8},{7,5},{8,10},{9,7},{10,... | collective-permute-start | bytes 1179656 | tf_op jit(solution)/shard_map/ppermute | solution.py:318
  44.1 13.6 %collective-permute-start.12 = (bf16[12,128,128]{2,1,0:T(8,128)(2,1)S(1)}, bf16[12,128,128]{2,1,0:T(8,128)(2,1)S(1)}, u32[]{:S(2)}, u32[]{:S(2)}) collective-permute-start(bf16[12,128,128]{2,1,0:T(8,128)(2,1)S(1)} %collective-permute-done.5.rest_5_), channel_id=1, source_target_pairs={{0,1},{1,0},{2,3},{3,2},{4,5},{5,4},{6,7},{7,6},{8,9},{9,8},{10,11... | collective-permute-start | bytes 1179656 | tf_op jit(solution)/shard_map/ppermute | solution.py:328
  48.1 9.6 %collective-permute-start.13 = (bf16[12,128,128]{2,1,0:T(8,128)(2,1)S(1)}, bf16[12,128,128]{2,1,0:T(8,128)(2,1)S(1)}, u32[]{:S(2)}, u32[]{:S(2)}) collective-permute-start(bf16[12,128,128]{2,1,0:T(8,128)(2,1)S(1)} %collective-permute-done.4.rest_4_), channel_id=1, source_target_pairs={{0,1},{1,0},{2,3},{3,2},{4,5},{5,4},{6,7},{7,6},{8,9},{9,8},{10,11... | collective-permute-start | bytes 1179656 | tf_op jit(solution)/shard_map/ppermute | solution.py:328
  48.2 9.5 %collective-permute-start.11 = (bf16[12,128,128]{2,1,0:T(8,128)(2,1)S(1)}, bf16[12,128,128]{2,1,0:T(8,128)(2,1)S(1)}, u32[]{:S(2)}, u32[]{:S(2)}) collective-permute-start(bf16[12,128,128]{2,1,0:T(8,128)(2,1)S(1)} %collective-permute-done.6.rest_6_), channel_id=1, source_target_pairs={{0,1},{1,0},{2,3},{3,2},{4,5},{5,4},{6,7},{7,6},{8,9},{9,8},{10,11... | collective-permute-start | bytes 1179656 | tf_op jit(solution)/shard_map/ppermute | solution.py:328
  48.6 9.1 %collective-permute-start.10 = (bf16[12,128,128]{2,1,0:T(8,128)(2,1)S(1)}, bf16[12,128,128]{2,1,0:T(8,128)(2,1)S(1)}, u32[]{:S(2)}, u32[]{:S(2)}) collective-permute-start(bf16[12,128,128]{2,1,0:T(8,128)(2,1)S(1)} %collective-permute-done.7.rest_7_), channel_id=1, source_target_pairs={{0,1},{1,0},{2,3},{3,2},{4,5},{5,4},{6,7},{7,6},{8,9},{9,8},{10,11... | collective-permute-start | bytes 1179656 | tf_op jit(solution)/shard_map/ppermute | solution.py:328
  52.2 7.2 %collective-permute-start.9 = (bf16[12,128,128]{2,1,0:T(8,128)(2,1)S(1)}, bf16[12,128,128]{2,1,0:T(8,128)(2,1)}, u32[]{:S(2)}, u32[]{:S(2)}) collective-permute-start(bf16[12,128,128]{2,1,0:T(8,128)(2,1)S(1)} %collective-permute-done.8.rest_8_), channel_id=1, source_target_pairs={{0,1},{1,0},{2,3},{3,2},{4,5},{5,4},{6,7},{7,6},{8,9},{9,8},{10,11... | collective-permute-start | bytes 1179656 | tf_op jit(solution)/shard_map/ppermute | solution.py:328
  74.8 1.7 %collective-permute-start.16 = (f32[4,128]{1,0:T(4,128)}, f32[4,128]{1,0:T(4,128)S(1)}, u32[]{:S(2)}, u32[]{:S(2)}) collective-permute-start(f32[4,128]{1,0:T(4,128)} %get-tuple-element.25), channel_id=1, source_target_pairs={{0,1},{1,0},{2,3},{3,2},{4,5},{5,4},{6,7},{7,6},{8,9},{9,8},{10,11... | collective-permute-start | bytes 6152 | tf_op jit(solution)/shard_map/ppermute | solution.py:313
  77.2 3.0 %collective-permute-start.17 = (f32[4,128]{1,0:T(4,128)S(1)}, f32[4,128]{1,0:T(4,128)S(1)}, u32[]{:S(2)}, u32[]{:S(2)}) collective-permute-start(f32[4,128]{1,0:T(4,128)S(1)} %add.25), channel_id=1, source_target_pairs={{0,3},{1,2},{2,1},{3,0},{4,7},{5,6},{6,5},{7,4},{8,11},{9,10},{10,... | collective-permute-start | bytes 6152 | tf_op jit(solution)/shard_map/ppermute | solution.py:313
  80.2 3.9 %collective-permute-start.18 = (f32[4,128]{1,0:T(4,128)S(1)}, f32[4,128]{1,0:T(4,128)S(1)}, u32[]{:S(2)}, u32[]{:S(2)}) collective-permute-start(f32[4,128]{1,0:T(4,128)S(1)} %add.26), channel_id=1, source_target_pairs={{0,5},{1,4},{2,7},{3,6},{4,1},{5,0},{6,3},{7,2},{8,13},{9,12},{10,... | collective-permute-start | bytes 6152 | tf_op jit(solution)/shard_map/ppermute | solution.py:313
  84.1 5.1 %collective-permute-start.19 = (f32[4,128]{1,0:T(4,128)S(1)}, f32[4,128]{1,0:T(4,128)S(1)}, u32[]{:S(2)}, u32[]{:S(2)}) collective-permute-start(f32[4,128]{1,0:T(4,128)S(1)} %add.27.half_ref), channel_id=1, source_target_pairs={{0,13},{1,12},{2,15},{3,14},{4,9},{5,8},{6,11},{7,10},{8,5},{9,4},... | collective-permute-start | bytes 6152 | tf_op jit(solution)/shard_map/ppermute | solution.py:313
  89.4 3.5 %collective-permute-start.20 = (f32[2,128]{1,0:T(2,128)S(1)}, f32[2,128]{1,0:T(2,128)S(1)}, u32[]{:S(2)}, u32[]{:S(2)}) collective-permute-start(f32[2,128]{1,0:T(2,128)S(1)} %get-tuple-element.28), channel_id=1, source_target_pairs={{0,17},{1,16},{2,19},{3,18},{4,21},{5,20},{6,23},{7,22},{8,25},{9,... | collective-permute-start | bytes 3080 | tf_op jit(solution)/shard_map/ppermute | solution.py:313
  92.9 5.2 %collective-permute-start.21 = (f32[2,128]{1,0:T(2,128)S(1)}, f32[2,128]{1,0:T(2,128)S(1)}, u32[]{:S(2)}, u32[]{:S(2)}) collective-permute-start(f32[2,128]{1,0:T(2,128)S(1)} %add.28), channel_id=1, source_target_pairs={{0,49},{1,48},{2,51},{3,50},{4,53},{5,52},{6,55},{7,54},{8,57},{9,... | collective-permute-start | bytes 3080 | tf_op jit(solution)/shard_map/ppermute | solution.py:313
  98.1 4.2 %collective-permute-start.22 = (f32[2,128]{1,0:T(2,128)S(1)}, f32[2,128]{1,0:T(2,128)S(1)}, u32[]{:S(2)}, u32[]{:S(2)}) collective-permute-start(f32[2,128]{1,0:T(2,128)S(1)} %add.29), channel_id=1, source_target_pairs={{0,65},{1,64},{2,67},{3,66},{4,69},{5,68},{6,71},{7,70},{8,73},{9,... | collective-permute-start | bytes 3080 | tf_op jit(solution)/shard_map/ppermute | solution.py:313
  102.3 4.4 %collective-permute-start.23 = (f32[2,128]{1,0:T(2,128)S(1)}, f32[2,128]{1,0:T(2,128)S(1)}, u32[]{:S(2)}, u32[]{:S(2)}) collective-permute-start(f32[2,128]{1,0:T(2,128)S(1)} %add.31), channel_id=1, source_target_pairs={{0,193},{1,192},{2,195},{3,194},{4,197},{5,196},{6,199},{7,198},{8... | collective-permute-start | bytes 3080 | tf_op jit(solution)/shard_map/ppermute | solution.py:313
  (20 other events, 276.1 us)
